TPU v7x, 32 devices: a whole 2x2x4 slice. The times are simulated.
32 devices in a mesh: dp: 16 (over z, x, core), mp: 2 (over y).
Axes of the slice: x: 2, y: 2, z: 4, core: 2. Of those that a mesh axis runs over, the one named last changes fastest.
Arguments:
- tokens: bfloat16 [32, 256, 2048], P('dp'), may hold values from -6 to 6
- mod_table: float32 [32, 6, 2048], replicated, may hold values from -3 to 3
- w_qkv: bfloat16 [3, 2048, 2048], P(None, 'dp', 'mp'), may hold values from -0.125 to 0.125
- w_out_t: bfloat16 [2048, 2048], P('dp', 'mp'), may hold values from -1 to 1
- w_up: bfloat16 [2048, 8192], P('dp', 'mp'), may hold values from -0.125 to 0.125
- w_down: bfloat16 [2048, 8192], P('dp', 'mp'), may hold values from -0.0625 to 0.0625
- bins: int32 [32], P('dp'), may hold values from 0 to 31
- present: int32 [32], P('dp'), may hold values from 0 to 1, as said below
- cotangent: bfloat16 [32, 256, 2048], P('dp'), may hold values from -6 to 6
Outputs:
- block_out: bfloat16 [32, 256, 2048], P('dp')
- input_grad: float32 [32, 256, 2048], P('dp')
- table_grad: float32 [32, 6, 2048], P(None, None, 'dp')
- qkv_grad: float32 [3, 2048, 2048], P(None, 'dp', 'mp')
- out_grad: float32 [2048, 2048], P('dp', 'mp')
- up_grad: float32 [2048, 8192], P('dp', 'mp')
- down_grad: float32 [2048, 8192], P('dp', 'mp')
Inputs may be any that keep to these rules, and one draw needn't show every extreme that they name: `present`: each device's 2 consecutive slots hold its images first and empty slots after; every device holds 1 to 2 images, and some device holds 2, another 1.
All inputs are finite; a program needn't handle non-finite values.
Results may differ from a plain program's by a relative error of at most 0.012.
The roundings to bfloat16 on the way count: a program that leaves them out, or rounds other values in their place, can miss the bound.
Values may be sent and summed in bfloat16 or wider, within the bound.
No kernel may reach another device: no remote copies, remote signals or barrier semaphores. Data moves between devices by JAX's collectives and lax.ppermute only.
A program may use at most 320 MiB of HBM per device.

v0:
```python
import jax
import jax.numpy as jnp
from jax import lax
from jax.sharding import PartitionSpec as P

HEAD_DIM = 128


EPS = 1e-06
HIGH = lax.Precision.HIGHEST


def layer_norm(value):
    centre = value - jnp.mean(value, axis=-1, keepdims=True)
    spread = jnp.mean(centre * centre, axis=-1, keepdims=True)
    return centre * lax.rsqrt(spread + EPS)


def modulate(value, shift, scale):
    return layer_norm(value) * (1.0 + scale) + shift


def body(tokens, mod_table, w_qkv, w_out_t, w_up, w_down, bins, present, cotangent):
    count, length, width = tokens.shape
    rows_all = count * length
    w_q, w_o, w_u, w_d = (
        lax.all_gather(w_qkv, "dp", axis=1, tiled=True),
        lax.all_gather(w_out_t, "dp", axis=0, tiled=True),
        lax.all_gather(w_up, "dp", axis=0, tiled=True),
        lax.all_gather(w_down, "dp", axis=0, tiled=True),
    )
    local_width = w_q.shape[2]
    local_heads = local_width // HEAD_DIM
    factor = HEAD_DIM ** (-0.5)
    onehot = (bins[:, None] == jnp.arange(mod_table.shape[0])[None, :]).astype(jnp.float32)
    mods = jnp.einsum("cb,btd->ctd", onehot, mod_table, precision=HIGH)
    shift1, scale1, gate1 = (mods[:, 0:1], mods[:, 1:2], mods[:, 2:3])
    shift2, scale2, gate2 = (mods[:, 3:4], mods[:, 4:5], mods[:, 5:6])
    mask = present.astype(jnp.float32)[:, None, None]
    inputs = tokens.astype(jnp.float32)
    normed = modulate(inputs, shift1, scale1).astype(jnp.bfloat16).reshape(rows_all, width)
    qkv = jnp.einsum("rd,tde->tre", normed, w_q, preferred_element_type=jnp.float32).astype(
        jnp.bfloat16
    )
    query = qkv[0].reshape(count, length, local_heads, HEAD_DIM)
    keys = qkv[1].reshape(count, length, local_heads, HEAD_DIM)
    values = qkv[2].reshape(count, length, local_heads, HEAD_DIM)
    scores = jnp.einsum("cqhe,ckhe->chqk", query, keys, preferred_element_type=jnp.float32) * factor
    top = jnp.max(scores, axis=-1, keepdims=True)
    expo = jnp.exp(scores - top)
    total = jnp.sum(expo, axis=-1, keepdims=True)
    lse = top + jnp.log(total)
    probs_low = (expo / total).astype(jnp.bfloat16)
    mixed = jnp.einsum("chqk,ckhe->cqhe", probs_low, values, preferred_element_type=jnp.float32)
    mixed = mixed.astype(jnp.bfloat16).reshape(rows_all, local_width)
    att_part = jnp.einsum("re,de->rd", mixed, w_o, preferred_element_type=jnp.float32)
    att = lax.psum(att_part, "mp").reshape(count, length, width)
    hidden = inputs + gate1 * att
    second = modulate(hidden, shift2, scale2).astype(jnp.bfloat16).reshape(rows_all, width)
    up_val = jnp.einsum("rd,df->rf", second, w_u, preferred_element_type=jnp.float32)
    act = jax.nn.gelu(up_val).astype(jnp.bfloat16)
    mlp_part = jnp.einsum("rf,df->rd", act, w_d, preferred_element_type=jnp.float32)
    mlp = (
        lax.psum(mlp_part.astype(jnp.bfloat16), "mp")
        .astype(jnp.float32)
        .reshape(count, length, width)
    )
    block_out = (mask * (hidden + gate2 * mlp)).astype(jnp.bfloat16)
    grad_dy = cotangent.astype(jnp.float32) * mask
    g_gate2 = jnp.sum(grad_dy * mlp, axis=1)
    d_mlp = (gate2 * grad_dy).astype(jnp.bfloat16).reshape(rows_all, width)
    down_grad = jnp.einsum("rd,rf->df", d_mlp, act, preferred_element_type=jnp.float32)
    d_act = jnp.einsum("rd,df->rf", d_mlp, w_d, preferred_element_type=jnp.float32)
    _, gelu_pull = jax.vjp(jax.nn.gelu, up_val)
    d_up = gelu_pull(d_act)[0].astype(jnp.bfloat16)
    up_grad = jnp.einsum("rd,rf->df", second, d_up, preferred_element_type=jnp.float32)
    d_second = lax.psum(
        jnp.einsum("rf,df->rd", d_up, w_u, preferred_element_type=jnp.float32), "mp"
    )
    _, norm_pull2 = jax.vjp(modulate, hidden, shift2, scale2)
    d_hidden_n, g_shift2, g_scale2 = norm_pull2(d_second.reshape(count, length, width))
    d_hidden = grad_dy + d_hidden_n
    g_gate1 = jnp.sum(d_hidden * att, axis=1)
    d_att = (gate1 * d_hidden).astype(jnp.bfloat16).reshape(rows_all, width)
    out_grad = jnp.einsum("rd,re->de", d_att, mixed, preferred_element_type=jnp.float32)
    d_mixed = jnp.einsum("rd,de->re", d_att, w_o, preferred_element_type=jnp.float32).astype(
        jnp.bfloat16
    )
    d_mixed = d_mixed.reshape(count, length, local_heads, HEAD_DIM)
    again = jnp.einsum("cqhe,ckhe->chqk", query, keys, preferred_element_type=jnp.float32) * factor
    probs = jnp.exp(again - lse)
    probs_again = probs.astype(jnp.bfloat16)
    d_probs = jnp.einsum("cqhe,ckhe->chqk", d_mixed, values, preferred_element_type=jnp.float32)
    d_values = jnp.einsum(
        "chqk,cqhe->ckhe", probs_again, d_mixed, preferred_element_type=jnp.float32
    ).astype(jnp.bfloat16)
    delta = jnp.sum(d_probs * probs, axis=-1, keepdims=True)
    d_scores = (probs * (d_probs - delta)).astype(jnp.bfloat16)
    d_query = (
        jnp.einsum("chqk,ckhe->cqhe", d_scores, keys, preferred_element_type=jnp.float32) * factor
    ).astype(jnp.bfloat16)
    d_keys = (
        jnp.einsum("chqk,cqhe->ckhe", d_scores, query, preferred_element_type=jnp.float32) * factor
    ).astype(jnp.bfloat16)
    d_qkv = jnp.stack(
        [
            d_query.reshape(rows_all, local_width),
            d_keys.reshape(rows_all, local_width),
            d_values.reshape(rows_all, local_width),
        ]
    )
    qkv_grad = jnp.einsum("rd,tre->tde", normed, d_qkv, preferred_element_type=jnp.float32)
    d_normed = lax.psum(
        jnp.einsum("tre,tde->rd", d_qkv, w_q, preferred_element_type=jnp.float32), "mp"
    )
    _, norm_pull1 = jax.vjp(modulate, inputs, shift1, scale1)
    d_input_n, g_shift1, g_scale1 = norm_pull1(d_normed.reshape(count, length, width))
    input_grad = d_hidden + d_input_n
    d_mods = jnp.stack(
        [g_shift1[:, 0], g_scale1[:, 0], g_gate1, g_shift2[:, 0], g_scale2[:, 0], g_gate2], axis=1
    )
    table_grad = jnp.einsum("cb,ctd->btd", onehot, d_mods, precision=HIGH)
    qkv_part, out_part, up_part, down_part, table_part = (
        lax.psum_scatter(qkv_grad, "dp", scatter_dimension=1, tiled=True),
        lax.psum_scatter(out_grad, "dp", scatter_dimension=0, tiled=True),
        lax.psum_scatter(up_grad, "dp", scatter_dimension=0, tiled=True),
        lax.psum_scatter(down_grad, "dp", scatter_dimension=0, tiled=True),
        lax.psum_scatter(table_grad, "dp", scatter_dimension=2, tiled=True),
    )
    return (block_out, input_grad, table_part, qkv_part, out_part, up_part, down_part)


def solution(mesh):
    in_specs = (
        P("dp", None, None),
        P(),
        P(None, "dp", "mp"),
        P("dp", "mp"),
        P("dp", "mp"),
        P("dp", "mp"),
        P("dp"),
        P("dp"),
        P("dp", None, None),
    )
    out_specs = (
        P("dp", None, None),
        P("dp", None, None),
        P(None, None, "dp"),
        P(None, "dp", "mp"),
        P("dp", "mp"),
        P("dp", "mp"),
        P("dp", "mp"),
    )
    return jax.shard_map(body, mesh=mesh, in_specs=in_specs, out_specs=out_specs, check_vma=False)
```

profile of v0, /device:TPU:0, one launch (start us, length us, event | category | flops | bytes accessed | tf_op | source)
XLA Modules:
  0.0 2003.8 jit_solution(16918348886612769383)
XLA Ops:
  8.7 2.1 convert_reduce_fusion
  10.8 2.3 fusion.20
  13.9 2.2 fusion.14
  16.1 97.6 %all-gather.5.cloned.1.call-done = bf16[3,2048,1024]{2,1,0:T(8,128)(2,1)} async-done(((bf16[3,128,1024]{2,1,0:T(8,128)(2,1)}), bf16[3,2048,1024]{2,1,0:T(8,128)(2,1)}) %all-gather.5.cloned.1.call-update) | async-done | bytes 12582928 | tf_op jit(solution)/shard_map/all_gather | solution.py:27
  113.7 10.3 convert_bitcast_fusion
  124.0 1.7 slice_bitcast_fusion.2
  125.7 1.3 copy.53
  127.9 2.5 copy.54
  130.4 1.6 copy.40
  132.1 0.8 multiply_reduce_fusion.5
  132.8 0.7 fusion.22
  133.6 1.2 copy-done.4
  134.8 2.0 fusion.34
  136.9 1.7 copy.34
  138.6 26.1 %all-gather.7.cloned.1.call-done = bf16[2048,1024]{1,0:T(8,128)(2,1)} async-done(((bf16[128,1024]{1,0:T(8,128)(2,1)}), bf16[2048,1024]{1,0:T(8,128)(2,1)}) %all-gather.7.cloned.1.call-update) | async-done | bytes 4194320 | tf_op jit(solution)/shard_map/all_gather | solution.py:28
  164.7 6.6 fusion.43
  172.7 105.1 %all-reduce.5.cloned.1.call-done = f32[2,256,2048]{2,1,0:T(8,128)} async-done(((f32[2,256,2048]{2,1,0:T(8,128)}), f32[2,256,2048]{2,1,0:T(8,128)}) %all-reduce.5.cloned.1.call-update) | async-done | bytes 4194320 | tf_op jit(solution)/shard_map/psum | solution.py:57
  277.8 3.5 fusion.64
  281.9 1.5 copy-done.2
  283.4 1.0 copy-done.12
  284.4 4.8 multiply_convert_fusion.3
  289.2 117.7 %all-gather.11.cloned.1.call-done = bf16[2048,4096]{1,0:T(8,128)(2,1)} async-done(((bf16[128,4096]{1,0:T(8,128)(2,1)}), bf16[2048,4096]{1,0:T(8,128)(2,1)}) %all-gather.11.cloned.1.call-update) | async-done | bytes 16777232 | tf_op jit(solution)/shard_map/all_gather | solution.py:30
  407.0 15.1 fusion.65
  422.0 112.2 %all-gather.9.cloned.1.call-done = bf16[2048,4096]{1,0:T(8,128)(2,1)} async-done(((bf16[128,4096]{1,0:T(8,128)(2,1)}), bf16[2048,4096]{1,0:T(8,128)(2,1)}) %all-gather.9.cloned.1.call-update) | async-done | bytes 16777232 | tf_op jit(solution)/shard_map/all_gather | solution.py:29
  534.3 20.9 %fusion.6 = (bf16[512,4096]{1,0:T(8,128)(2,1)S(1)}, f32[512,4096]{1,0:T(8,128)}) fusion(f32[512,4096]{1,0:T(8,128)} %fusion.65, bf16[512,2048]{1,0:T(8,128)(2,1)} %bitcast.125, bf16[2048,4096]{1,0:T(8,128)(2,1)} %all-gather.9.cloned.1.call-done), kind=kOutput, calls=%fused_computation.9 | convolution fusion | flops 8631877632 | bytes 39845888 | tf_op jit(solution)/shard_map/rd,df->rf/dot_general | solution.py:60
  555.2 15.3 fusion.66
  570.5 17.8 convolution_convert_fusion
  588.4 88.3 %all-reduce.9.cloned.1.call-done = f32[2,256,2048]{2,1,0:T(8,128)} async-done(((f32[2,256,2048]{2,1,0:T(8,128)}), f32[2,256,2048]{2,1,0:T(8,128)}) %all-reduce.9.cloned.1.call-update) | async-done | bytes 4194320 | tf_op jit(solution)/shard_map/psum | solution.py:77
  676.7 4.3 multiply_reduce_fusion.3
  681.3 1.3 copy-done.8
  682.6 2.2 multiply_reduce_fusion
  684.8 57.7 %all-reduce.7.cloned.1.call-done = bf16[2,256,2048]{2,1,0:T(8,128)(2,1)} async-done(((bf16[2,256,2048]{2,1,0:T(8,128)(2,1)}), bf16[2,256,2048]{2,1,0:T(8,128)(2,1)}) %all-reduce.7.cloned.1.call-update) | async-done | bytes 2097168 | tf_op jit(solution)/shard_map/psum | solution.py:64
  742.5 8.4 multiply_reduce_fusion.1
  751.5 3.9 copy-done.30
  755.3 2.3 fusion.35
  757.7 1.3 copy.57
  759.0 1.6 copy.43
  760.6 4.2 fusion.36
  764.9 1.1 multiply_reduce_fusion.2
  765.9 1.1 multiply_convert_fusion.1
  767.2 1.8 fusion.40
  769.0 1.4 fusion.39
  770.4 0.7 copy.45
  771.7 2.4 copy.39
  774.1 1.5 stack_reshape.9
  775.7 2.4 copy.42
  778.1 2.3 stack_reshape.10
  780.5 1.3 constant_dynamic-update-slice_fusion.1
  781.8 12.2 fusion.67
  794.1 13.8 convolution_bitcast_fusion
  808.0 94.1 %all-reduce.11.cloned.1.call-done = f32[2,256,2048]{2,1,0:T(8,128)} async-done(((f32[2,256,2048]{2,1,0:T(8,128)}), f32[2,256,2048]{2,1,0:T(8,128)}) %all-reduce.11.cloned.1.call-update) | async-done | bytes 4194320 | tf_op jit(solution)/shard_map/psum | solution.py:113
  902.1 3.8 fusion.21
  906.2 3.4 fusion.15
  909.6 2.0 fusion.53
  911.8 9.4 fusion.41
  921.3 23.3 %fusion.68 = f32[2048,4096]{1,0:T(8,128)} fusion(bf16[512,2048]{1,0:T(8,128)(2,1)} %bitcast.126, bf16[512,4096]{1,0:T(8,128)(2,1)} %copy-done.32), kind=kOutput, calls=%fused_computation.123 | convolution fusion | flops 8589934592 | bytes 39845888 | tf_op jit(solution)/shard_map/rd,rf->df/dot_general | solution.py:76
  944.7 19.3 fusion.63
  964.0 6.4 add_add_fusion.2
  970.4 179.8 %reduce-scatter.8.cloned.1.call-done = f32[3,128,1024]{1,2,0:T(8,128)} async-done(((f32[3,2048,1024]{1,2,0:T(8,128)}), f32[3,128,1024]{1,2,0:T(8,128)}) %reduce-scatter.8.cloned.1.call-update) | async-done | bytes 1572880 | tf_op jit(solution)/shard_map/reduce_scatter | solution.py:124
  1150.2 3.0 copy.47
  1153.2 59.7 %reduce-scatter.6.cloned.1.call-done = f32[32,6,128]{2,0,1:T(8,128)} async-done(((f32[32,6,2048]{2,0,1:T(8,128)}), f32[32,6,128]{2,0,1:T(8,128)}) %reduce-scatter.6.cloned.1.call-update) | async-done | bytes 98320 | tf_op jit(solution)/shard_map/reduce_scatter | solution.py:128
  1212.9 108.9 %reduce-scatter.10.cloned.1.call-done = f32[128,1024]{1,0:T(8,128)} async-done(((f32[2048,1024]{1,0:T(8,128)}), f32[128,1024]{1,0:T(8,128)}) %reduce-scatter.10.cloned.1.call-update) | async-done | bytes 524304 | tf_op jit(solution)/shard_map/reduce_scatter | solution.py:125
  1321.8 337.8 %reduce-scatter.12.cloned.1.call-done = f32[128,4096]{1,0:T(8,128)} async-done(((f32[2048,4096]{1,0:T(8,128)}), f32[128,4096]{1,0:T(8,128)}) %reduce-scatter.12.cloned.1.call-update) | async-done | bytes 2097168 | tf_op jit(solution)/shard_map/reduce_scatter | solution.py:126
  1659.6 337.2 %reduce-scatter.14.cloned.1.call-done = f32[128,4096]{1,0:T(8,128)} async-done(((f32[2048,4096]{1,0:T(8,128)}), f32[128,4096]{1,0:T(8,128)}) %reduce-scatter.14.cloned.1.call-update) | async-done | bytes 2097168 | tf_op jit(solution)/shard_map/reduce_scatter | solution.py:127
  (112 shorter events, 7.6 us)
Async XLA Ops:
  7.2 6.0 copy-start
  7.2 6.0 copy-start.28
  7.2 106.5 %all-gather.5.cloned.1.call-start = ((), (), s32[]{:S(2)}) async-start(), calls=%async_computation.5 | async-start | bytes 13369344 | tf_op jit(solution)/shard_map/all_gather | solution.py:27
  7.9 156.7 %all-gather.7.cloned.1.call-start = ((), (), s32[]{:S(2)}) async-start(), calls=%async_computation.6 | async-start | bytes 4456448 | tf_op jit(solution)/shard_map/all_gather | solution.py:28
  8.7 269.1 %all-reduce.5.cloned.1.call-start = ((), (), s32[]{:S(2)}) async-start(), calls=%async_computation.7 | async-start | bytes 8388608 | tf_op jit(solution)/shard_map/psum | solution.py:57
  8.7 5.2 copy-start.6
  10.8 3.0 copy-start.22
  13.1 0.7 copy-start.26
  13.2 0.7 copy-start.24
  13.8 110.2 %copy-start.19 = (f32[2,2048]{1,0:T(2,128)}, f32[2,2048]{1,0:T(2,128)S(1)}, u32[]{:S(2)}) copy-start(f32[2,2048]{1,0:T(2,128)S(1)} %get-tuple-element.40) | copy-start | bytes 49156
  132.0 1.5 copy-start.10
  132.1 2.8 copy-start.13
  132.8 2.0 copy-start.4
  138.6 32.7 %copy-start.17 = (bf16[2,256,8,128]{3,2,1,0:T(8,128)(2,1)}, bf16[2,256,8,128]{3,2,1,0:T(8,128)(2,1)S(1)}, u32[]{:S(2)}) copy-start(bf16[2,256,8,128]{3,2,1,0:T(8,128)(2,1)S(1)} %copy.34) | copy-start | bytes 3145732
  171.2 1.5 copy-start.31
  171.3 235.7 %all-gather.11.cloned.1.call-start = ((), (), s32[]{:S(2)}) async-start(), calls=%async_computation.9 | async-start | bytes 17825792 | tf_op jit(solution)/shard_map/all_gather | solution.py:30
  171.9 362.4 %all-gather.9.cloned.1.call-start = ((), (), s32[]{:S(2)}) async-start(), calls=%async_computation.8 | async-start | bytes 17825792 | tf_op jit(solution)/shard_map/all_gather | solution.py:29
  172.4 504.2 %all-reduce.9.cloned.1.call-start = ((), (), s32[]{:S(2)}) async-start(), calls=%async_computation.11 | async-start | bytes 8388608 | tf_op jit(solution)/shard_map/psum | solution.py:77
  281.3 2.1 copy-start.2
  281.3 3.1 copy-start.12
  555.2 15.3 copy-start.32
  570.5 172.0 %all-reduce.7.cloned.1.call-start = ((), (), s32[]{:S(2)}) async-start(), calls=%async_computation.10 | async-start | bytes 4194304 | tf_op jit(solution)/shard_map/psum | solution.py:64
  588.3 313.8 %all-reduce.11.cloned.1.call-start = ((), (), s32[]{:S(2)}) async-start(), calls=%async_computation.12 | async-start | bytes 8388608 | tf_op jit(solution)/shard_map/psum | solution.py:113
  676.7 4.6 copy-start.3
  676.7 5.9 copy-start.8
  750.9 6.8 copy-start.9
  750.9 4.4 copy-start.30
  751.5 6.2 copy-start.16
  760.6 4.3 copy-start.5
  760.6 4.3 copy-start.14
  765.9 1.2 copy-start.11
  769.0 1.4 copy-start.15
  781.8 12.2 copy-start.21
  794.1 356.1 %reduce-scatter.8.cloned.1.call-start = ((), (), s32[]{:S(2)}) async-start(), calls=%async_computation.14 | async-start | bytes 26738688 | tf_op jit(solution)/shard_map/reduce_scatter | solution.py:124
  807.9 94.2 %copy-start.20 = (f32[2,2048]{1,0:T(2,128)S(1)}, f32[2,2048]{1,0:T(2,128)}, u32[]{:S(2)}) copy-start(f32[2,2048]{1,0:T(2,128)} %copy-done.19) | copy-start | bytes 49156
  807.9 94.2 %copy-start.23 = (f32[2,256]{1,0:T(2,128)S(1)}, f32[2,256]{1,0:T(2,128)}, u32[]{:S(2)}) copy-start(f32[2,256]{1,0:T(2,128)} %copy-done.22) | copy-start | bytes 6148
  808.0 98.0 %copy-start.27 = (f32[2,256]{1,0:T(2,128)S(1)}, f32[2,256]{1,0:T(2,128)}, u32[]{:S(2)}) copy-start(f32[2,256]{1,0:T(2,128)} %copy-done.26) | copy-start | bytes 6148
  808.0 98.0 %copy-start.25 = (f32[2,256]{1,0:T(2,128)S(1)}, f32[2,256]{1,0:T(2,128)}, u32[]{:S(2)}) copy-start(f32[2,256]{1,0:T(2,128)} %copy-done.24) | copy-start | bytes 6148
  808.0 404.9 %reduce-scatter.6.cloned.1.call-start = ((), (), s32[]{:S(2)}) async-start(), calls=%async_computation.13 | async-start | bytes 1671168 | tf_op jit(solution)/shard_map/reduce_scatter | solution.py:128
  902.1 4.0 copy-start.7
  905.9 3.7 copy-start.29
  906.2 5.6 copy-start.18
  911.7 410.1 %reduce-scatter.10.cloned.1.call-start = ((), (), s32[]{:S(2)}) async-start(), calls=%async_computation.15 | async-start | bytes 8912896 | tf_op jit(solution)/shard_map/reduce_scatter | solution.py:125
  921.2 738.4 %reduce-scatter.12.cloned.1.call-start = ((), (), s32[]{:S(2)}) async-start(), calls=%async_computation.16 | async-start | bytes 35651584 | tf_op jit(solution)/shard_map/reduce_scatter | solution.py:126
  944.6 1052.2 %reduce-scatter.14.cloned.1.call-start = ((), (), s32[]{:S(2)}) async-start(), calls=%async_computation.17 | async-start | bytes 35651584 | tf_op jit(solution)/shard_map/reduce_scatter | solution.py:127
  964.0 1032.8 %copy-start.1 = (f32[32,6,2048]{2,0,1:T(8,128)S(1)}, f32[32,6,2048]{2,0,1:T(8,128)}, u32[]{:S(2)}) copy-start(f32[32,6,2048]{2,0,1:T(8,128)} %param.10) | copy-start | bytes 4718596
Sparse Core Ops, SparseCore 0:
  10.2 103.4 all-gather.4
  115.9 48.7 all-gather.6
  171.4 106.3 all-reduce.4
  280.0 126.8 all-gather.10
  409.2 125.0 all-gather.8
  570.6 106.0 all-reduce.8
  679.5 62.8 all-reduce.6
  794.2 107.8 all-reduce.10
  906.2 243.8 reduce-scatter.7
  1154.2 58.5 reduce-scatter.5
  1218.1 103.6 reduce-scatter.9
  1327.1 332.5 reduce-scatter.11
  1665.0 331.7 reduce-scatter.13
where the time goes:
time: 2010 us; the launch traced here: 2000 us
  waiting for transfers between devices  1720 us (86%)
  matrix products  180 us (9%)
  other arithmetic  46.3 us (2%)
  local copies, waits for them, and re-layouts  36.7 us (2%)
    reduce_scatter x1, waiting for transfers between devices, body(): lax.psum_scatter(up_grad, 'dp', scatter_dimension=0, tiled=True)  338 us
    reduce_scatter x1, waiting for transfers between devices, body(): lax.psum_scatter(down_grad, 'dp', scatter_dimension=0, tiled=True)  337 us
    reduce_scatter x1, waiting for transfers between devices, body(): lax.psum_scatter(qkv_grad, 'dp', scatter_dimension=1, tiled=True)  180 us
    all_gather x1, waiting for transfers between devices, body(): lax.all_gather(w_down, 'dp', axis=0, tiled=True)  118 us
    all_gather x1, waiting for transfers between devices, body(): lax.all_gather(w_up, 'dp', axis=0, tiled=True)  112 us
    reduce_scatter x1, waiting for transfers between devices, body(): lax.psum_scatter(out_grad, 'dp', scatter_dimension=0, tiled=True)  109 us
    psum x1, waiting for transfers between devices, body(): att = lax.psum(att_part, 'mp').reshape(count, length, width)  105 us
    all_gather x1, waiting for transfers between devices, body(): lax.all_gather(w_qkv, 'dp', axis=1, tiled=True)  97.6 us
  transfers between devices with their start and end apart: 13, of which 13 were waited for; matrix products, arithmetic and copies ran while one was open for 8% of the time, Pallas kernels for 0%

commit v1 on v0

v1 whole, which is shorter than its diff:
```python
import jax
import jax.numpy as jnp
from jax import lax
from jax.experimental import pallas as pl
from jax.experimental.pallas import tpu as pltpu
from jax.sharding import PartitionSpec as P

HEAD_DIM = 128
EPS = 1e-06
HIGH = lax.Precision.HIGHEST
F32 = jnp.float32
BF16 = jnp.bfloat16


def layer_norm(value):
    centre = value - jnp.mean(value, axis=-1, keepdims=True)
    spread = jnp.mean(centre * centre, axis=-1, keepdims=True)
    return centre * lax.rsqrt(spread + EPS)


def modulate(value, shift, scale):
    return layer_norm(value) * (1.0 + scale) + shift


class Link:
    def __init__(self, name, perm, depth):
        self.name, self.perm, self.depth, self.done = name, perm, depth, []

    def send(self, value):
        if len(self.done) >= self.depth:
            value, _ = lax.optimization_barrier((value, self.done[-self.depth]))
        out = lax.ppermute(value, self.name, self.perm)
        self.done.append(out)
        return out


class Grid:
    def __init__(self, size):
        self.c = 2 if size % 2 == 0 else 1
        self.z = 4 if (size // self.c) % 4 == 0 else 1
        self.x = size // self.c // self.z
        self.size = size
        self.links = {
            "z": Link("dp", self.ring(1, 0, 0), 2),
            "x": Link("dp", self.ring(0, 1, 0), 2),
            "c": Link("dp", self.ring(0, 0, 1), 2),
        }
        me = lax.axis_index("dp")
        self.me = (me // (self.x * self.c), (me // self.c) % self.x, me % self.c)

    def index(self, z, x, c):
        return (z % self.z * self.x + x % self.x) * self.c + c % self.c

    def ring(self, dz, dx, dc):
        return [
            (self.index(z, x, c), self.index(z + dz, x + dx, c + dc))
            for z in range(self.z)
            for x in range(self.x)
            for c in range(self.c)
        ]

    def to_relative(self):
        z, x, c = self.me
        return jnp.stack(
            [
                self.index(z - kz + self.z, x - kx + self.x, c - kc + self.c)
                for kc in range(self.c)
                for kx in range(self.x)
                for kz in range(self.z)
            ]
        ).astype(jnp.int32)

    def to_absolute(self):
        z, x, c = self.me
        return jnp.stack(
            [
                ((c - oc) % self.c * self.x + (x - ox) % self.x) * self.z + (z - oz) % self.z
                for oz in range(self.z)
                for ox in range(self.x)
                for oc in range(self.c)
            ]
        ).astype(jnp.int32)

    def gather(self, shard, first):
        blocks = {(0, 0, 0): shard}
        place = {"c": 0, "x": 1, "z": 2}
        order = ("z", "x", "c") if first == "z" else ("x", "z", "c")
        for axis in order:
            at, count = place[axis], getattr(self, axis)
            base = list(blocks)
            for k in range(1, count):
                for key in base:
                    source = key[:at] + (k - 1,) + key[at + 1 :]
                    target = key[:at] + (k,) + key[at + 1 :]
                    blocks[target] = self.links[axis].send(blocks[source])
        return blocks

    def whole(self, blocks, axis):
        return jnp.concatenate([blocks[key] for key in sorted(blocks)], axis=axis)

    def reduce(self, lhs, rhs, first):
        width = lhs.shape[1] // (self.c * self.x)
        blk = width // self.z

        def product(kc, kx):
            at = (kc * self.x + kx) * width
            return lax.dot_general(
                lhs[:, at : at + width], rhs, (((0,), (0,)), ((), ())), preferred_element_type=F32
            )

        order = [kx for kx in range(self.x) if kx] + [0]
        kept = {}
        moving = {kx: None for kx in order}
        for kc in list(range(1, self.c)) + [0]:
            for kx in order:
                value = product(kc, kx)
                if moving[kx] is not None:
                    value = value + moving[kx].astype(F32)
                value = value.astype(BF16)
                if kc:
                    moving[kx] = self.links["c"].send(value)
                else:
                    kept[kx] = value
        part = lambda kx, kz: kept[kx][kz * blk : (kz + 1) * blk]
        zorder = list(range(1, self.z)) + [0]
        if first == "x":
            gone = {}
            for kz in zorder:
                gone[kz] = None
            for kx in order:
                for kz in zorder:
                    value = part(kx, kz)
                    if gone[kz] is not None:
                        value = value.astype(F32) + gone[kz].astype(F32)
                        value = value.astype(BF16) if kx else value
                    if kx:
                        gone[kz] = self.links["x"].send(value)
                    else:
                        gone[kz] = value.astype(F32)
            total = None
            for kz in zorder:
                value = gone[kz] if total is None else gone[kz] + total.astype(F32)
                if kz:
                    total = self.links["z"].send(value.astype(BF16))
            return value
        totals = {kx: None for kx in order}
        for kz in zorder:
            for kx in order:
                value = part(kx, kz).astype(F32)
                if totals[kx] is not None:
                    value = value + totals[kx].astype(F32)
                totals[kx] = self.links["z"].send(value.astype(BF16)) if kz else value
        total = None
        for kx in order:
            value = totals[kx] if total is None else totals[kx] + total.astype(F32)
            if kx:
                total = self.links["x"].send(value.astype(BF16))
        return value


def copy_block(order_ref, in_ref, out_ref):
    out_ref[...] = in_ref[...]


def reorder(value, order):
    count = order.shape[0]
    shape = value.shape
    flat = value.reshape(-1, shape[-1])
    blk = shape[-1] // count
    if blk % 128:
        return jnp.take(flat.reshape(-1, count, blk), order, axis=1).reshape(shape)
    out = pl.pallas_call(
        copy_block,
        grid_spec=pltpu.PrefetchScalarGridSpec(
            num_scalar_prefetch=1,
            grid=(count,),
            in_specs=[pl.BlockSpec((flat.shape[0], blk), lambda j, s: (0, s[j]))],
            out_specs=pl.BlockSpec((flat.shape[0], blk), lambda j, s: (0, j)),
        ),
        out_shape=jax.ShapeDtypeStruct(flat.shape, flat.dtype),
    )(order, flat)
    return out.reshape(shape)


def make_body(dp, mp):
    turn = [(i, (i + 1) % mp) for i in range(mp)]

    def across(part):
        total, moving = part.astype(F32), part
        for _ in range(mp - 1):
            moving = lax.ppermute(moving, "mp", turn)
            total = total + moving.astype(F32)
        return total

    def body(tokens, mod_table, w_qkv, w_out_t, w_up, w_down, bins, present, cotangent):
        count, length, width = tokens.shape
        rows_all = count * length
        grid = Grid(dp)
        relative, absolute = grid.to_relative(), grid.to_absolute()

        v_blocks = grid.gather(w_qkv[2], "x")
        o_blocks = grid.gather(w_out_t, "x")
        qk_blocks = grid.gather(w_qkv[:2], "z")
        u_blocks = grid.gather(w_up, "z")
        d_blocks = grid.gather(w_down, "z")
        w_qk, w_v, w_o, w_u, w_d = (
            grid.whole(qk_blocks, 1),
            grid.whole(v_blocks, 0),
            grid.whole(o_blocks, 0),
            grid.whole(u_blocks, 0),
            grid.whole(d_blocks, 0),
        )
        local_width = w_v.shape[1]
        local_heads = local_width // HEAD_DIM
        factor = HEAD_DIM ** (-0.5)

        bins_all = lax.all_gather(bins, "dp", axis=0, tiled=True)
        table_rows = jnp.arange(mod_table.shape[0])[None, :]
        onehot = (bins[:, None] == table_rows).astype(F32)
        onehot_all = (bins_all[:, None] == table_rows).astype(F32)
        mods = jnp.einsum("cb,btd->ctd", onehot, mod_table, precision=HIGH)
        mods = reorder(mods, relative)
        tokens = reorder(tokens, relative)
        cotangent = reorder(cotangent, relative)
        shift1, scale1, gate1 = (mods[:, 0:1], mods[:, 1:2], mods[:, 2:3])
        shift2, scale2, gate2 = (mods[:, 3:4], mods[:, 4:5], mods[:, 5:6])
        mask = present.astype(F32)[:, None, None]
        inputs = tokens.astype(F32)
        grad_dy = cotangent.astype(F32) * mask
        d_mlp = (gate2 * grad_dy).astype(BF16).reshape(rows_all, width)

        normed = modulate(inputs, shift1, scale1).astype(BF16).reshape(rows_all, width)
        qk = jnp.einsum("rd,tde->tre", normed, w_qk, preferred_element_type=F32).astype(BF16)
        val = jnp.einsum("rd,de->re", normed, w_v, preferred_element_type=F32).astype(BF16)
        query = qk[0].reshape(count, length, local_heads, HEAD_DIM)
        keys = qk[1].reshape(count, length, local_heads, HEAD_DIM)
        values = val.reshape(count, length, local_heads, HEAD_DIM)
        scores = jnp.einsum("cqhe,ckhe->chqk", query, keys, preferred_element_type=F32) * factor
        top = jnp.max(scores, axis=-1, keepdims=True)
        expo = jnp.exp(scores - top)
        total = jnp.sum(expo, axis=-1, keepdims=True)
        lse = top + jnp.log(total)
        probs_low = (expo / total).astype(BF16)
        mixed = jnp.einsum("chqk,ckhe->cqhe", probs_low, values, preferred_element_type=F32)
        mixed = mixed.astype(BF16).reshape(rows_all, local_width)
        att_part = jnp.einsum("re,de->rd", mixed, w_o, preferred_element_type=F32).astype(BF16)
        att = across(lax.optimization_barrier(att_part)).reshape(count, length, width)
        hidden = inputs + gate1 * att
        second = modulate(hidden, shift2, scale2).astype(BF16).reshape(rows_all, width)
        up_val = jnp.einsum("rd,df->rf", second, w_u, preferred_element_type=F32)
        act = jax.nn.gelu(up_val).astype(BF16)
        down_part = grid.reduce(d_mlp, act, "x")
        d_act = jnp.einsum("rd,df->rf", d_mlp, w_d, preferred_element_type=F32)
        _, gelu_pull = jax.vjp(jax.nn.gelu, up_val)
        d_up = gelu_pull(d_act)[0].astype(BF16)
        d_second_part = jnp.einsum("rf,df->rd", d_up, w_u, preferred_element_type=F32).astype(BF16)
        d_second = across(lax.optimization_barrier(d_second_part))
        up_part = grid.reduce(second, d_up, "x")
        mlp_part = jnp.einsum("rf,df->rd", act, w_d, preferred_element_type=F32).astype(BF16)
        mlp = across(lax.optimization_barrier(mlp_part)).reshape(count, length, width)
        block_out = (mask * (hidden + gate2 * mlp)).astype(BF16)
        block_out = reorder(block_out, absolute)
        g_gate2 = jnp.sum(grad_dy * mlp, axis=1)
        _, norm_pull2 = jax.vjp(modulate, hidden, shift2, scale2)
        d_hidden_n, g_shift2, g_scale2 = norm_pull2(d_second.reshape(count, length, width))
        d_hidden = grad_dy + d_hidden_n
        g_gate1 = jnp.sum(d_hidden * att, axis=1)
        d_att = (gate1 * d_hidden).astype(BF16).reshape(rows_all, width)
        d_mixed = jnp.einsum("rd,de->re", d_att, w_o, preferred_element_type=F32).astype(BF16)
        out_part = grid.reduce(d_att, mixed, "z")
        d_mixed = d_mixed.reshape(count, length, local_heads, HEAD_DIM)
        again = jnp.einsum("cqhe,ckhe->chqk", query, keys, preferred_element_type=F32) * factor
        probs = jnp.exp(again - lse)
        probs_again = probs.astype(BF16)
        d_probs = jnp.einsum("cqhe,ckhe->chqk", d_mixed, values, preferred_element_type=F32)
        d_values = jnp.einsum(
            "chqk,cqhe->ckhe", probs_again, d_mixed, preferred_element_type=F32
        ).astype(BF16)
        delta = jnp.sum(d_probs * probs, axis=-1, keepdims=True)
        d_scores = (probs * (d_probs - delta)).astype(BF16)
        d_query = (
            jnp.einsum("chqk,ckhe->cqhe", d_scores, keys, preferred_element_type=F32) * factor
        ).astype(BF16)
        d_keys = (
            jnp.einsum("chqk,cqhe->ckhe", d_scores, query, preferred_element_type=F32) * factor
        ).astype(BF16)
        d_query = d_query.reshape(rows_all, local_width)
        d_keys = d_keys.reshape(rows_all, local_width)
        d_values = d_values.reshape(rows_all, local_width)
        d_qk = jnp.stack([d_query, d_keys])
        d_normed_part = (
            jnp.einsum("tre,tde->rd", d_qk, w_qk, preferred_element_type=F32)
            + jnp.einsum("re,de->rd", d_values, w_v, preferred_element_type=F32)
        ).astype(BF16)
        d_normed = across(lax.optimization_barrier(d_normed_part))
        v_part = grid.reduce(normed, d_values, "z")
        qk_part = grid.reduce(normed, jnp.concatenate([d_query, d_keys], axis=1), "x")
        _, norm_pull1 = jax.vjp(modulate, inputs, shift1, scale1)
        d_input_n, g_shift1, g_scale1 = norm_pull1(d_normed.reshape(count, length, width))
        input_grad = reorder(d_hidden + d_input_n, absolute)
        d_mods = jnp.stack(
            [g_shift1[:, 0], g_scale1[:, 0], g_gate1, g_shift2[:, 0], g_scale2[:, 0], g_gate2],
            axis=1,
        )
        d_mods = reorder(d_mods, absolute)
        d_mods = lax.all_to_all(d_mods, "dp", split_axis=2, concat_axis=0, tiled=True)
        table_part = jnp.einsum("sb,std->btd", onehot_all, d_mods, precision=HIGH)
        qkv_part = jnp.stack(
            [qk_part[:, :local_width], qk_part[:, local_width:], v_part], axis=0
        )
        return (block_out, input_grad, table_part, qkv_part, out_part, up_part, down_part)

    return body


def solution(mesh):
    in_specs = (
        P("dp", None, None),
        P(),
        P(None, "dp", "mp"),
        P("dp", "mp"),
        P("dp", "mp"),
        P("dp", "mp"),
        P("dp"),
        P("dp"),
        P("dp", None, None),
    )
    out_specs = (
        P("dp", None, None),
        P("dp", None, None),
        P(None, None, "dp"),
        P(None, "dp", "mp"),
        P("dp", "mp"),
        P("dp", "mp"),
        P("dp", "mp"),
    )
    body = make_body(mesh.shape["dp"], mesh.shape["mp"])
    return jax.shard_map(body, mesh=mesh, in_specs=in_specs, out_specs=out_specs, check_vma=False)
```

time: 2010 us -> 1020 us (0.51)
  waiting for transfers between devices: 1720 us -> 472 us
  local copies, waits for them, and re-layouts: 36.7 us -> 131 us
  starting transfers between devices: 0.74 us -> 77.1 us
  Pallas kernels: 0 us -> 58.5 us
  other arithmetic: 46.3 us -> 76 us
    reduce_scatter x5 -> x0, waiting for transfers between devices: 1020 us -> none  [the longest x1 338 us: body(): lax.psum_scatter(up_grad, 'dp', scatter_dimension=0, tiled=True)]
    ppermute x0 -> x124, waiting for transfers between devices: none -> 472 us  [the longest x120 393 us: send(): out = lax.ppermute(value, self.name, self.perm)]
    all_gather x4 -> x0, waiting for transfers between devices: 354 us -> none  [the longest x1 118 us: body(): lax.all_gather(w_down, 'dp', axis=0, tiled=True)]
    psum x4 -> x0, waiting for transfers between devices: 345 us -> none  [the longest x1 105 us: body(): att = lax.psum(att_part, 'mp').reshape(count, length, width)]
    unnamed x79 -> x312, local copies, waits for them, and re-layouts: 21.1 us -> 93.9 us
    ppermute x0 -> x124, starting transfers between devices: none -> 72.2 us  [the longest x120 67.1 us: send(): out = lax.ppermute(value, self.name, self.perm)]
    pallas_call x0 -> x6, Pallas kernels: none -> 58.5 us  [reorder(): pl.pallas_call(copy_block, grid_spec=pltpu.PrefetchScalarGridSpec(num_sca...]
    dot_general x18 -> x36, matrix products: 175 us -> 175 us  [the longest x20 71.8 us: product(): lax.dot_general(lhs[:, at:at + width], rhs, (((0,), (0,)), ((), ())), pre...]
  transfers between devices with their start and end apart: 13 -> 125, of which waited for: 13 -> 46; matrix products, arithmetic and copies ran while one was open for 8% -> 32% of each run, Pallas kernels for 0% -> 6%
where the time goes in v1:
time: 1020 us; the launch traced here: 1010 us
  waiting for transfers between devices  472 us (46%)
  matrix products  177 us (17%)
  local copies, waits for them, and re-layouts  131 us (13%)
  starting transfers between devices  77.1 us (8%)
  other arithmetic  76 us (7%)
  Pallas kernels  58.5 us (6%)
  blocking collectives  13 us (1%)
    ppermute x120, waiting for transfers between devices, send(): out = lax.ppermute(value, self.name, self.perm)  393 us
    unnamed x312, local copies, waits for them, and re-layouts  93.9 us
    ppermute x4, waiting for transfers between devices, across(): moving = lax.ppermute(moving, 'mp', turn)  78.9 us
    dot_general x20, matrix products, product(): lax.dot_general(lhs[:, at:at + width], rhs, (((0,), (0,)), ((), ())), pre...  71.8 us
    ppermute x120, starting transfers between devices, send(): out = lax.ppermute(value, self.name, self.perm)  67.1 us
    pallas_call x6, Pallas kernels, reorder(): pl.pallas_call(copy_block, grid_spec=pltpu.PrefetchScalarGridSpec(num_sca...  58.5 us
  transfers between devices with their start and end apart: 125, of which 46 were waited for; matrix products, arithmetic and copies ran while one was open for 32% of the time, Pallas kernels for 6%

profile of v1, /device:TPU:0, one launch (start us, length us, event | category | flops | bytes accessed | tf_op | source)
XLA Modules:
  0.0 1008.2 jit_solution(17915703421327176387)
XLA Ops:
  10.5 10.3 %shard_map.144 = bf16[512,2048]{1,0:T(8,128)(2,1)} custom-call(s32[16]{0:T(128)} %stack.159.order_ref, bf16[512,2048]{1,0:T(8,128)(2,1)} %bitcast.267), custom_call_target="tpu_custom_call" | custom-call | tf_op jit(solution)/shard_map/pallas_call | solution.py:172
  26.5 8.5 shard_map.145
  43.8 6.2 collective-permute-done.1
  50.0 5.6 collective-permute-done.4
  57.5 10.4 %shard_map.147 = bf16[512,2048]{1,0:T(8,128)(2,1)} custom-call(s32[16]{0:T(128)} %stack.159.order_ref, bf16[512,2048]{1,0:T(8,128)(2,1)} %bitcast.268), custom_call_target="tpu_custom_call" | custom-call | tf_op jit(solution)/shard_map/pallas_call | solution.py:172
  78.2 13.0 %all-reduce = s32[32]{0:T(128)} all-reduce(s32[32]{0:T(128)S(1)} %dynamic-update-slice), channel_id=1, replica_groups=mesh['dp'=16,'mp'=2] {'dp'}, use_global_device_ids=true, to_apply=%add | all-reduce | flops 32 | bytes 256
  98.6 5.7 collective-permute-done.15
  104.6 5.3 collective-permute-done.6
  119.4 5.2 fusion.44
  135.7 14.9 %collective-permute-done.22 = bf16[128,1024]{1,0:T(8,128)(2,1)S(1)} collective-permute-done((bf16[128,1024]{1,0:T(8,128)(2,1)S(1)}, bf16[128,1024]{1,0:T(8,128)(2,1)S(1)}, u32[]{:S(2)}, u32[]{:S(2)}) %collective-permute-start.22) | collective-permute-done | bytes 262176 | tf_op jit(solution)/shard_map/ppermute | solution.py:32
  153.1 13.0 %collective-permute-done.23 = bf16[2,128,1024]{1,2,0:T(8,128)(2,1)S(1)} collective-permute-done((bf16[2,128,1024]{1,2,0:T(8,128)(2,1)S(1)}, bf16[2,128,1024]{1,2,0:T(8,128)(2,1)S(1)}, u32[]{:S(2)}, u32[]{:S(2)}) %collective-permute-start.23) | collective-permute-done | bytes 524320 | tf_op jit(solution)/shard_map/ppermute | solution.py:32
  166.8 15.9 %collective-permute-done.24 = bf16[2,128,1024]{1,2,0:T(8,128)(2,1)S(1)} collective-permute-done((bf16[2,128,1024]{1,2,0:T(8,128)(2,1)S(1)}, bf16[2,128,1024]{1,2,0:T(8,128)(2,1)S(1)}, u32[]{:S(2)}, u32[]{:S(2)}) %collective-permute-start.24) | collective-permute-done | bytes 524320 | tf_op jit(solution)/shard_map/ppermute | solution.py:32
  186.3 17.0 %collective-permute-done.46 = bf16[128,4096]{1,0:T(8,128)(2,1)} collective-permute-done((bf16[128,4096]{1,0:T(8,128)(2,1)}, bf16[128,4096]{1,0:T(8,128)(2,1)}, u32[]{:S(2)}, u32[]{:S(2)}) %collective-permute-start.46) | collective-permute-done | bytes 1048608 | tf_op jit(solution)/shard_map/ppermute | solution.py:32
  209.0 5.0 convert_bitcast_fusion
  223.8 4.7 collective-permute-done.47
  238.9 17.7 %collective-permute-done.48 = bf16[128,4096]{1,0:T(8,128)(2,1)S(1)} collective-permute-done((bf16[128,4096]{1,0:T(8,128)(2,1)}, bf16[128,4096]{1,0:T(8,128)(2,1)S(1)}, u32[]{:S(2)}, u32[]{:S(2)}) %collective-permute-start.48) | collective-permute-done | bytes 1048608 | tf_op jit(solution)/shard_map/ppermute | solution.py:32
  256.6 18.7 %collective-permute-done.61 = bf16[128,4096]{1,0:T(8,128)(2,1)} collective-permute-done((bf16[128,4096]{1,0:T(8,128)(2,1)S(1)}, bf16[128,4096]{1,0:T(8,128)(2,1)}, u32[]{:S(2)}, u32[]{:S(2)}) %collective-permute-start.61) | collective-permute-done | bytes 1048608 | tf_op jit(solution)/shard_map/ppermute | solution.py:32
  287.1 12.0 %collective-permute-done.62 = bf16[128,4096]{1,0:T(8,128)(2,1)} collective-permute-done((bf16[128,4096]{1,0:T(8,128)(2,1)}, bf16[128,4096]{1,0:T(8,128)(2,1)}, u32[]{:S(2)}, u32[]{:S(2)}) %collective-permute-start.62) | collective-permute-done | bytes 1048608 | tf_op jit(solution)/shard_map/ppermute | solution.py:32
  306.2 21.4 %collective-permute-done.45 = bf16[512,2048]{1,0:T(8,128)(2,1)S(1)} collective-permute-done((bf16[512,2048]{1,0:T(8,128)(2,1)S(1)}, bf16[512,2048]{1,0:T(8,128)(2,1)S(1)}, u32[]{:S(2)}, u32[]{:S(2)}) %collective-permute-start.45) | collective-permute-done | bytes 2097184 | tf_op jit(solution)/shard_map/ppermute | solution.py:191
  344.6 9.4 collective-permute-done.65
  364.2 12.3 %collective-permute-done.66 = bf16[128,4096]{1,0:T(8,128)(2,1)} collective-permute-done((bf16[128,4096]{1,0:T(8,128)(2,1)}, bf16[128,4096]{1,0:T(8,128)(2,1)}, u32[]{:S(2)}, u32[]{:S(2)}) %collective-permute-start.66) | collective-permute-done | bytes 1048608 | tf_op jit(solution)/shard_map/ppermute | solution.py:32
  381.4 12.5 %collective-permute-done.67 = bf16[128,4096]{1,0:T(8,128)(2,1)S(1)} collective-permute-done((bf16[128,4096]{1,0:T(8,128)(2,1)}, bf16[128,4096]{1,0:T(8,128)(2,1)S(1)}, u32[]{:S(2)}, u32[]{:S(2)}) %collective-permute-start.67) | collective-permute-done | bytes 1048608 | tf_op jit(solution)/shard_map/ppermute | solution.py:32
  404.6 14.6 %fusion.150 = f32[512,4096]{1,0:T(8,128)} fusion(bf16[512,2048]{1,0:T(8,128)(2,1)S(1)} %copy-done.32, bf16[2048,4096]{1,0:T(8,128)(2,1)} %constant_dynamic-update-slice_fusion.64), kind=kOutput, calls=%fused_computation.321 | convolution fusion | flops 8589934592 | bytes 27262976 | tf_op jit(solution)/shard_map/rd,df->rf/dot_general | solution.py:253
  419.2 18.9 %fusion.6 = (bf16[512,4096]{1,0:T(8,128)(2,1)S(1)}, bf16[512,4096]{1,0:T(8,128)(2,1)S(1)}) fusion(f32[512,4096]{1,0:T(8,128)} %fusion.150, bf16[512,2048]{1,0:T(8,128)(2,1)S(1)} %fusion.20, bf16[2048,4096]{1,0:T(8,128)(2,1)} %constant_dynamic-update-slice_fusion.48), kind=kOutput, calls=%fused_computation.8 | convolution fusion | flops 8636071936 | bytes 35651584 | tf_op jit(solution)/shard_map/rd,df->rf/dot_general | solution.py:250
  438.1 16.4 %convolution_convert_fusion.8 = bf16[512,2048]{1,0:T(8,128)(2,1)} fusion(bf16[512,4096]{1,0:T(8,128)(2,1)S(1)} %get-tuple-element.248, bf16[2048,4096]{1,0:T(8,128)(2,1)} %constant_dynamic-update-slice_fusion.64), kind=kOutput, calls=%fused_computation.79 | convolution fusion | flops 8590983168 | bytes 23068672 | tf_op jit(solution)/shard_map/rf,df->rd/dot_general | solution.py:259
  456.0 12.9 %convolution_convert_fusion.7 = bf16[512,2048]{1,0:T(8,128)(2,1)S(1)} fusion(bf16[512,4096]{1,0:T(8,128)(2,1)S(1)} %get-tuple-element.247, bf16[2048,4096]{1,0:T(8,128)(2,1)} %constant_dynamic-update-slice_fusion.48), kind=kOutput, calls=%fused_computation.78 | convolution fusion | flops 8590983168 | bytes 23068672 | tf_op jit(solution)/shard_map/rf,df->rd/dot_general | solution.py:256
  469.5 5.5 convolution_convert_fusion
  475.0 5.6 convolution_convert_fusion.2
  489.7 57.5 %collective-permute-done.77 = bf16[512,2048]{1,0:T(8,128)(2,1)S(1)} collective-permute-done((bf16[512,2048]{1,0:T(8,128)(2,1)S(1)}, bf16[512,2048]{1,0:T(8,128)(2,1)S(1)}, u32[]{:S(2)}, u32[]{:S(2)}) %collective-permute-start.77) | collective-permute-done | bytes 2097184 | tf_op jit(solution)/shard_map/ppermute | solution.py:191
  548.5 5.6 fusion.143
  589.5 9.5 fusion.28
  603.5 5.2 fusion.121
  618.6 4.8 add_convert_fusion.1
  633.5 6.1 add_convert_fusion
  639.7 11.9 %collective-permute-done.92 = bf16[128,4096]{1,0:T(8,128)(2,1)S(1)} collective-permute-done((bf16[128,4096]{1,0:T(8,128)(2,1)}, bf16[128,4096]{1,0:T(8,128)(2,1)S(1)}, u32[]{:S(2)}, u32[]{:S(2)}) %collective-permute-start.92) | collective-permute-done | bytes 1048608 | tf_op jit(solution)/shard_map/ppermute | solution.py:32
  651.9 5.1 collective-permute-start.95
  657.0 16.7 %collective-permute-done.89 = bf16[128,4096]{1,0:T(8,128)(2,1)S(1)} collective-permute-done((bf16[128,4096]{1,0:T(8,128)(2,1)}, bf16[128,4096]{1,0:T(8,128)(2,1)S(1)}, u32[]{:S(2)}, u32[]{:S(2)}) %collective-permute-start.89) | collective-permute-done | bytes 1048608 | tf_op jit(solution)/shard_map/ppermute | solution.py:32
  675.8 4.6 add_convert_fusion.2
  682.2 17.6 %collective-permute-done.93 = bf16[128,4096]{1,0:T(8,128)(2,1)S(1)} collective-permute-done((bf16[128,4096]{1,0:T(8,128)(2,1)S(1)}, bf16[128,4096]{1,0:T(8,128)(2,1)S(1)}, u32[]{:S(2)}, u32[]{:S(2)}) %collective-permute-start.93) | collective-permute-done | bytes 1048608 | tf_op jit(solution)/shard_map/ppermute | solution.py:32
  702.0 4.8 collective-permute-start.96
  706.8 15.5 %collective-permute-done.90 = bf16[128,4096]{1,0:T(8,128)(2,1)S(1)} collective-permute-done((bf16[128,4096]{1,0:T(8,128)(2,1)S(1)}, bf16[128,4096]{1,0:T(8,128)(2,1)S(1)}, u32[]{:S(2)}, u32[]{:S(2)}) %collective-permute-start.90) | collective-permute-done | bytes 1048608 | tf_op jit(solution)/shard_map/ppermute | solution.py:32
  726.6 18.1 %collective-permute-done.94 = bf16[128,4096]{1,0:T(8,128)(2,1)S(1)} collective-permute-done((bf16[128,4096]{1,0:T(8,128)(2,1)S(1)}, bf16[128,4096]{1,0:T(8,128)(2,1)S(1)}, u32[]{:S(2)}, u32[]{:S(2)}) %collective-permute-start.94) | collective-permute-done | bytes 1048608 | tf_op jit(solution)/shard_map/ppermute | solution.py:32
  745.9 4.7 collective-permute-start.97
  754.7 10.2 %shard_map.146 = bf16[512,2048]{1,0:T(8,128)(2,1)} custom-call(s32[16]{0:T(128)} %stack.142.order_ref, bf16[512,2048]{1,0:T(8,128)(2,1)} %get-tuple-element.257.in_ref), custom_call_target="tpu_custom_call" | custom-call | tf_op jit(solution)/shard_map/pallas_call | solution.py:172
  767.9 7.1 collective-permute-done.97
  778.3 16.1 %collective-permute-done.98 = bf16[128,4096]{1,0:T(8,128)(2,1)S(1)} collective-permute-done((bf16[128,4096]{1,0:T(8,128)(2,1)}, bf16[128,4096]{1,0:T(8,128)(2,1)S(1)}, u32[]{:S(2)}, u32[]{:S(2)}) %collective-permute-start.98) | collective-permute-done | bytes 1048608 | tf_op jit(solution)/shard_map/ppermute | solution.py:32
  796.6 9.9 fusion.22
  807.5 8.5 shard_map.149
  819.2 5.5 reshape.293
  824.7 4.9 all-to-all-start
  849.7 5.6 collective-permute-done.100
  857.8 24.7 %collective-permute-done.101 = bf16[128,1024]{1,0:T(8,128)(2,1)S(1)} collective-permute-done((bf16[128,1024]{1,0:T(8,128)(2,1)S(1)}, bf16[128,1024]{1,0:T(8,128)(2,1)S(1)}, u32[]{:S(2)}, u32[]{:S(2)}) %collective-permute-start.101) | collective-permute-done | bytes 262176 | tf_op jit(solution)/shard_map/ppermute | solution.py:32
  883.5 8.5 collective-permute-done.102
  894.7 9.3 collective-permute-done.103
  904.2 5.5 collective-permute-done.116
  915.4 5.5 collective-permute-done.117
  921.9 4.6 collective-permute-done.105
  930.4 4.9 collective-permute-done.107
  941.4 5.3 add_add_fusion.3.in_ref
  946.6 10.8 %shard_map.148 = f32[512,2048]{1,0:T(8,128)} custom-call(s32[16]{0:T(128)} %stack.142.order_ref, f32[512,2048]{1,0:T(8,128)} %add_add_fusion.3.in_ref), custom_call_target="tpu_custom_call" | custom-call | tf_op jit(solution)/shard_map/pallas_call | solution.py:172
  958.8 4.6 reshape.294
  969.7 9.5 collective-permute-done.121
  983.4 11.8 %collective-permute-done.122 = bf16[128,2048]{1,0:T(8,128)(2,1)S(1)} collective-permute-done((bf16[128,2048]{1,0:T(8,128)(2,1)S(1)}, bf16[128,2048]{1,0:T(8,128)(2,1)S(1)}, u32[]{:S(2)}, u32[]{:S(2)}) %collective-permute-start.122) | collective-permute-done | bytes 524320 | tf_op jit(solution)/shard_map/ppermute | solution.py:32
  1001.5 4.9 collective-permute-done.123
  (652 shorter events, 320.7 us)
Async XLA Ops:
  2.4 36.3 %collective-permute-start = (bf16[128,1024]{1,0:T(8,128)(2,1)}, bf16[128,1024]{1,0:T(8,128)(2,1)}, u32[]{:S(2)}, u32[]{:S(2)}) collective-permute-start(bf16[128,1024]{1,0:T(8,128)(2,1)} %slice_bitcast_fusion.2), channel_id=1, source_target_pairs={{0,8},{2,10},{4,12},{6,14},{8,16},{10,18},{12,20},{14,22},{16,24},... | collective-permute-start | bytes 786440 | tf_op jit(solution)/shard_map/ppermute | solution.py:32
  5.5 34.9 %collective-permute-start.3 = (bf16[128,1024]{1,0:T(8,128)(2,1)}, bf16[128,1024]{1,0:T(8,128)(2,1)}, u32[]{:S(2)}, u32[]{:S(2)}) collective-permute-start(bf16[128,1024]{1,0:T(8,128)(2,1)} %slice_bitcast_fusion.2), channel_id=1, source_target_pairs={{0,4},{2,6},{4,0},{6,2},{8,12},{10,14},{12,8},{14,10},{16,20},{18,... | collective-permute-start | bytes 786440 | tf_op jit(solution)/shard_map/ppermute | solution.py:32
  7.0 33.5 %collective-permute-start.7 = (bf16[128,1024]{1,0:T(8,128)(2,1)}, bf16[128,1024]{1,0:T(8,128)(2,1)}, u32[]{:S(2)}, u32[]{:S(2)}) collective-permute-start(bf16[128,1024]{1,0:T(8,128)(2,1)} %slice_bitcast_fusion.2), channel_id=1, source_target_pairs={{0,2},{2,0},{4,6},{6,4},{8,10},{10,8},{12,14},{14,12},{16,18},{18,... | collective-permute-start | bytes 786440 | tf_op jit(solution)/shard_map/ppermute | solution.py:32
  7.0 97.6 %collective-permute-start.19 = (bf16[128,1024]{1,0:T(8,128)(2,1)}, bf16[128,1024]{1,0:T(8,128)(2,1)S(1)}, u32[]{:S(2)}, u32[]{:S(2)}) collective-permute-start(bf16[128,1024]{1,0:T(8,128)(2,1)} %param.12), channel_id=1, source_target_pairs={{0,4},{2,6},{4,0},{6,2},{8,12},{10,14},{12,8},{14,10},{16,20},{18,... | collective-permute-start | bytes 786440 | tf_op jit(solution)/shard_map/ppermute | solution.py:32
  50.0 43.7 %collective-permute-start.2 = (bf16[128,1024]{1,0:T(8,128)(2,1)S(1)}, bf16[128,1024]{1,0:T(8,128)(2,1)S(1)}, u32[]{:S(2)}, u32[]{:S(2)}) collective-permute-start(bf16[128,1024]{1,0:T(8,128)(2,1)S(1)} %collective-permute-done.1), channel_id=1, source_target_pairs={{0,8},{2,10},{4,12},{6,14},{8,16},{10,18},{12,20},{14,22},{16,24},... | collective-permute-start | bytes 786440 | tf_op jit(solution)/shard_map/ppermute | solution.py:32
  55.6 38.1 %collective-permute-start.5 = (bf16[128,1024]{1,0:T(8,128)(2,1)S(1)}, bf16[128,1024]{1,0:T(8,128)(2,1)S(1)}, u32[]{:S(2)}, u32[]{:S(2)}) collective-permute-start(bf16[128,1024]{1,0:T(8,128)(2,1)S(1)} %collective-permute-done.4), channel_id=1, source_target_pairs={{0,8},{2,10},{4,12},{6,14},{8,16},{10,18},{12,20},{14,22},{16,24},... | collective-permute-start | bytes 786440 | tf_op jit(solution)/shard_map/ppermute | solution.py:32
  55.6 38.6 %collective-permute-start.9 = (bf16[128,1024]{1,0:T(8,128)(2,1)S(1)}, bf16[128,1024]{1,0:T(8,128)(2,1)S(1)}, u32[]{:S(2)}, u32[]{:S(2)}) collective-permute-start(bf16[128,1024]{1,0:T(8,128)(2,1)S(1)} %collective-permute-done.1), channel_id=1, source_target_pairs={{0,2},{2,0},{4,6},{6,4},{8,10},{10,8},{12,14},{14,12},{16,18},{18,... | collective-permute-start | bytes 786440 | tf_op jit(solution)/shard_map/ppermute | solution.py:32
  55.6 38.6 %collective-permute-start.12 = (bf16[128,1024]{1,0:T(8,128)(2,1)S(1)}, bf16[128,1024]{1,0:T(8,128)(2,1)S(1)}, u32[]{:S(2)}, u32[]{:S(2)}) collective-permute-start(bf16[128,1024]{1,0:T(8,128)(2,1)S(1)} %collective-permute-done.4), channel_id=1, source_target_pairs={{0,2},{2,0},{4,6},{6,4},{8,10},{10,8},{12,14},{14,12},{16,18},{18,... | collective-permute-start | bytes 786440 | tf_op jit(solution)/shard_map/ppermute | solution.py:32
  104.3 61.8 %collective-permute-start.25 = (bf16[2,128,1024]{1,2,0:T(8,128)(2,1)S(1)}, bf16[2,128,1024]{1,2,0:T(8,128)(2,1)S(1)}, u32[]{:S(2)}, u32[]{:S(2)}) collective-permute-start(bf16[2,128,1024]{1,2,0:T(8,128)(2,1)S(1)} %copy.91), channel_id=1, source_target_pairs={{0,4},{2,6},{4,0},{6,2},{8,12},{10,14},{12,8},{14,10},{16,20},{18,... | collective-permute-start | bytes 1572872 | tf_op jit(solution)/shard_map/ppermute | solution.py:32
  128.4 22.2 %collective-permute-start.18 = (bf16[2,128,1024]{1,2,0:T(8,128)(2,1)S(1)}, bf16[2,128,1024]{1,2,0:T(8,128)(2,1)S(1)}, u32[]{:S(2)}, u32[]{:S(2)}) collective-permute-start(bf16[2,128,1024]{1,2,0:T(8,128)(2,1)S(1)} %copy.91), channel_id=1, source_target_pairs={{0,8},{2,10},{4,12},{6,14},{8,16},{10,18},{12,20},{14,22},{16,24},... | collective-permute-start | bytes 1572872 | tf_op jit(solution)/shard_map/ppermute | solution.py:32
  153.0 29.8 %collective-permute-start.38 = (bf16[2,128,1024]{1,2,0:T(8,128)(2,1)S(1)}, bf16[2,128,1024]{1,2,0:T(8,128)(2,1)S(1)}, u32[]{:S(2)}, u32[]{:S(2)}) collective-permute-start(bf16[2,128,1024]{1,2,0:T(8,128)(2,1)S(1)} %collective-permute-done.18), channel_id=1, source_target_pairs={{0,2},{2,0},{4,6},{6,4},{8,10},{10,8},{12,14},{14,12},{16,18},{18,... | collective-permute-start | bytes 1572872 | tf_op jit(solution)/shard_map/ppermute | solution.py:32
  166.1 37.1 %collective-permute-start.46 = (bf16[128,4096]{1,0:T(8,128)(2,1)}, bf16[128,4096]{1,0:T(8,128)(2,1)}, u32[]{:S(2)}, u32[]{:S(2)}) collective-permute-start(bf16[128,4096]{1,0:T(8,128)(2,1)} %param.13), channel_id=1, source_target_pairs={{0,8},{2,10},{4,12},{6,14},{8,16},{10,18},{12,20},{14,22},{16,24},... | collective-permute-start | bytes 3145736 | tf_op jit(solution)/shard_map/ppermute | solution.py:32
  182.8 20.6 %collective-permute-start.40 = (bf16[2,128,1024]{1,2,0:T(8,128)(2,1)S(1)}, bf16[2,128,1024]{1,2,0:T(8,128)(2,1)S(1)}, u32[]{:S(2)}, u32[]{:S(2)}) collective-permute-start(bf16[2,128,1024]{1,2,0:T(8,128)(2,1)S(1)} %collective-permute-done.24), channel_id=1, source_target_pairs={{0,2},{2,0},{4,6},{6,4},{8,10},{10,8},{12,14},{14,12},{16,18},{18,... | collective-permute-start | bytes 1572872 | tf_op jit(solution)/shard_map/ppermute | solution.py:32
  183.5 45.1 %collective-permute-start.49 = (bf16[128,4096]{1,0:T(8,128)(2,1)}, bf16[128,4096]{1,0:T(8,128)(2,1)}, u32[]{:S(2)}, u32[]{:S(2)}) collective-permute-start(bf16[128,4096]{1,0:T(8,128)(2,1)} %param.13), channel_id=1, source_target_pairs={{0,4},{2,6},{4,0},{6,2},{8,12},{10,14},{12,8},{14,10},{16,20},{18,... | collective-permute-start | bytes 3145736 | tf_op jit(solution)/shard_map/ppermute | solution.py:32
  203.3 25.2 %collective-permute-start.47 = (bf16[128,4096]{1,0:T(8,128)(2,1)}, bf16[128,4096]{1,0:T(8,128)(2,1)}, u32[]{:S(2)}, u32[]{:S(2)}) collective-permute-start(bf16[128,4096]{1,0:T(8,128)(2,1)} %collective-permute-done.46), channel_id=1, source_target_pairs={{0,8},{2,10},{4,12},{6,14},{8,16},{10,18},{12,20},{14,22},{16,24},... | collective-permute-start | bytes 3145736 | tf_op jit(solution)/shard_map/ppermute | solution.py:32
  203.3 35.6 %collective-permute-start.50 = (bf16[128,4096]{1,0:T(8,128)(2,1)}, bf16[128,4096]{1,0:T(8,128)(2,1)}, u32[]{:S(2)}, u32[]{:S(2)}) collective-permute-start(bf16[128,4096]{1,0:T(8,128)(2,1)} %collective-permute-done.46), channel_id=1, source_target_pairs={{0,4},{2,6},{4,0},{6,2},{8,12},{10,14},{12,8},{14,10},{16,20},{18,... | collective-permute-start | bytes 3145736 | tf_op jit(solution)/shard_map/ppermute | solution.py:32
  207.4 28.8 %collective-permute-start.53 = (bf16[128,4096]{1,0:T(8,128)(2,1)}, bf16[128,4096]{1,0:T(8,128)(2,1)}, u32[]{:S(2)}, u32[]{:S(2)}) collective-permute-start(bf16[128,4096]{1,0:T(8,128)(2,1)} %param.13), channel_id=1, source_target_pairs={{0,2},{2,0},{4,6},{6,4},{8,10},{10,8},{12,14},{14,12},{16,18},{18,... | collective-permute-start | bytes 3145736 | tf_op jit(solution)/shard_map/ppermute | solution.py:32
  208.7 47.9 %collective-permute-start.54 = (bf16[128,4096]{1,0:T(8,128)(2,1)}, bf16[128,4096]{1,0:T(8,128)(2,1)}, u32[]{:S(2)}, u32[]{:S(2)}) collective-permute-start(bf16[128,4096]{1,0:T(8,128)(2,1)} %collective-permute-done.46), channel_id=1, source_target_pairs={{0,2},{2,0},{4,6},{6,4},{8,10},{10,8},{12,14},{14,12},{16,18},{18,... | collective-permute-start | bytes 3145736 | tf_op jit(solution)/shard_map/ppermute | solution.py:32
  228.5 28.1 %collective-permute-start.48 = (bf16[128,4096]{1,0:T(8,128)(2,1)}, bf16[128,4096]{1,0:T(8,128)(2,1)S(1)}, u32[]{:S(2)}, u32[]{:S(2)}) collective-permute-start(bf16[128,4096]{1,0:T(8,128)(2,1)} %collective-permute-done.47), channel_id=1, source_target_pairs={{0,8},{2,10},{4,12},{6,14},{8,16},{10,18},{12,20},{14,22},{16,24},... | collective-permute-start | bytes 3145736 | tf_op jit(solution)/shard_map/ppermute | solution.py:32
  228.5 46.8 %collective-permute-start.61 = (bf16[128,4096]{1,0:T(8,128)(2,1)S(1)}, bf16[128,4096]{1,0:T(8,128)(2,1)}, u32[]{:S(2)}, u32[]{:S(2)}) collective-permute-start(bf16[128,4096]{1,0:T(8,128)(2,1)S(1)} %copy-done.54), channel_id=1, source_target_pairs={{0,8},{2,10},{4,12},{6,14},{8,16},{10,18},{12,20},{14,22},{16,24},... | collective-permute-start | bytes 3145736 | tf_op jit(solution)/shard_map/ppermute | solution.py:32
  236.3 47.5 %collective-permute-start.51 = (bf16[128,4096]{1,0:T(8,128)(2,1)}, bf16[128,4096]{1,0:T(8,128)(2,1)S(1)}, u32[]{:S(2)}, u32[]{:S(2)}) collective-permute-start(bf16[128,4096]{1,0:T(8,128)(2,1)} %collective-permute-done.47), channel_id=1, source_target_pairs={{0,4},{2,6},{4,0},{6,2},{8,12},{10,14},{12,8},{14,10},{16,20},{18,... | collective-permute-start | bytes 3145736 | tf_op jit(solution)/shard_map/ppermute | solution.py:32
  238.9 47.5 %collective-permute-start.55 = (bf16[128,4096]{1,0:T(8,128)(2,1)}, bf16[128,4096]{1,0:T(8,128)(2,1)S(1)}, u32[]{:S(2)}, u32[]{:S(2)}) collective-permute-start(bf16[128,4096]{1,0:T(8,128)(2,1)} %collective-permute-done.47), channel_id=1, source_target_pairs={{0,2},{2,0},{4,6},{6,4},{8,10},{10,8},{12,14},{14,12},{16,18},{18,... | collective-permute-start | bytes 3145736 | tf_op jit(solution)/shard_map/ppermute | solution.py:32
  256.6 42.5 %collective-permute-start.52 = (bf16[128,4096]{1,0:T(8,128)(2,1)S(1)}, bf16[128,4096]{1,0:T(8,128)(2,1)S(1)}, u32[]{:S(2)}, u32[]{:S(2)}) collective-permute-start(bf16[128,4096]{1,0:T(8,128)(2,1)S(1)} %collective-permute-done.48), channel_id=1, source_target_pairs={{0,4},{2,6},{4,0},{6,2},{8,12},{10,14},{12,8},{14,10},{16,20},{18,... | collective-permute-start | bytes 3145736 | tf_op jit(solution)/shard_map/ppermute | solution.py:32
  256.6 30.5 %collective-permute-start.56 = (bf16[128,4096]{1,0:T(8,128)(2,1)S(1)}, bf16[128,4096]{1,0:T(8,128)(2,1)S(1)}, u32[]{:S(2)}, u32[]{:S(2)}) collective-permute-start(bf16[128,4096]{1,0:T(8,128)(2,1)S(1)} %collective-permute-done.48), channel_id=1, source_target_pairs={{0,2},{2,0},{4,6},{6,4},{8,10},{10,8},{12,14},{14,12},{16,18},{18,... | collective-permute-start | bytes 3145736 | tf_op jit(solution)/shard_map/ppermute | solution.py:32
  275.3 23.8 %collective-permute-start.62 = (bf16[128,4096]{1,0:T(8,128)(2,1)}, bf16[128,4096]{1,0:T(8,128)(2,1)}, u32[]{:S(2)}, u32[]{:S(2)}) collective-permute-start(bf16[128,4096]{1,0:T(8,128)(2,1)} %collective-permute-done.61), channel_id=1, source_target_pairs={{0,8},{2,10},{4,12},{6,14},{8,16},{10,18},{12,20},{14,22},{16,24},... | collective-permute-start | bytes 3145736 | tf_op jit(solution)/shard_map/ppermute | solution.py:32
  283.8 43.8 %collective-permute-start.45 = (bf16[512,2048]{1,0:T(8,128)(2,1)S(1)}, bf16[512,2048]{1,0:T(8,128)(2,1)S(1)}, u32[]{:S(2)}, u32[]{:S(2)}) collective-permute-start(bf16[512,2048]{1,0:T(8,128)(2,1)S(1)} %convolution_convert_fusion.4), channel_id=1, source_target_pairs={{0,1},{1,0},{2,3},{3,2},{4,5},{5,4},{6,7},{7,6},{8,9},{9,8},{10,11... | collective-permute-start | bytes 6291464 | tf_op jit(solution)/shard_map/ppermute | solution.py:191
  286.4 47.7 %collective-permute-start.64 = (bf16[128,4096]{1,0:T(8,128)(2,1)S(1)}, bf16[128,4096]{1,0:T(8,128)(2,1)S(1)}, u32[]{:S(2)}, u32[]{:S(2)}) collective-permute-start(bf16[128,4096]{1,0:T(8,128)(2,1)S(1)} %copy-done.54), channel_id=1, source_target_pairs={{0,4},{2,6},{4,0},{6,2},{8,12},{10,14},{12,8},{14,10},{16,20},{18,... | collective-permute-start | bytes 3145736 | tf_op jit(solution)/shard_map/ppermute | solution.py:32
  287.1 54.6 %collective-permute-start.57 = (bf16[128,4096]{1,0:T(8,128)(2,1)}, bf16[128,4096]{1,0:T(8,128)(2,1)}, u32[]{:S(2)}, u32[]{:S(2)}) collective-permute-start(bf16[128,4096]{1,0:T(8,128)(2,1)} %collective-permute-done.49), channel_id=1, source_target_pairs={{0,2},{2,0},{4,6},{6,4},{8,10},{10,8},{12,14},{14,12},{16,18},{18,... | collective-permute-start | bytes 3145736 | tf_op jit(solution)/shard_map/ppermute | solution.py:32
  299.1 45.0 %collective-permute-start.58 = (bf16[128,4096]{1,0:T(8,128)(2,1)}, bf16[128,4096]{1,0:T(8,128)(2,1)}, u32[]{:S(2)}, u32[]{:S(2)}) collective-permute-start(bf16[128,4096]{1,0:T(8,128)(2,1)} %collective-permute-done.50), channel_id=1, source_target_pairs={{0,2},{2,0},{4,6},{6,4},{8,10},{10,8},{12,14},{14,12},{16,18},{18,... | collective-permute-start | bytes 3145736 | tf_op jit(solution)/shard_map/ppermute | solution.py:32
  299.1 45.5 %collective-permute-start.63 = (bf16[128,4096]{1,0:T(8,128)(2,1)}, bf16[128,4096]{1,0:T(8,128)(2,1)}, u32[]{:S(2)}, u32[]{:S(2)}) collective-permute-start(bf16[128,4096]{1,0:T(8,128)(2,1)} %collective-permute-done.62), channel_id=1, source_target_pairs={{0,8},{2,10},{4,12},{6,14},{8,16},{10,18},{12,20},{14,22},{16,24},... | collective-permute-start | bytes 3145736 | tf_op jit(solution)/shard_map/ppermute | solution.py:32
  327.6 26.4 %collective-permute-start.65 = (bf16[128,4096]{1,0:T(8,128)(2,1)}, bf16[128,4096]{1,0:T(8,128)(2,1)}, u32[]{:S(2)}, u32[]{:S(2)}) collective-permute-start(bf16[128,4096]{1,0:T(8,128)(2,1)} %collective-permute-done.61), channel_id=1, source_target_pairs={{0,4},{2,6},{4,0},{6,2},{8,12},{10,14},{12,8},{14,10},{16,20},{18,... | collective-permute-start | bytes 3145736 | tf_op jit(solution)/shard_map/ppermute | solution.py:32
  334.1 42.4 %collective-permute-start.66 = (bf16[128,4096]{1,0:T(8,128)(2,1)}, bf16[128,4096]{1,0:T(8,128)(2,1)}, u32[]{:S(2)}, u32[]{:S(2)}) collective-permute-start(bf16[128,4096]{1,0:T(8,128)(2,1)} %collective-permute-done.62), channel_id=1, source_target_pairs={{0,4},{2,6},{4,0},{6,2},{8,12},{10,14},{12,8},{14,10},{16,20},{18,... | collective-permute-start | bytes 3145736 | tf_op jit(solution)/shard_map/ppermute | solution.py:32
  354.0 39.8 %collective-permute-start.67 = (bf16[128,4096]{1,0:T(8,128)(2,1)}, bf16[128,4096]{1,0:T(8,128)(2,1)S(1)}, u32[]{:S(2)}, u32[]{:S(2)}) collective-permute-start(bf16[128,4096]{1,0:T(8,128)(2,1)} %collective-permute-done.63), channel_id=1, source_target_pairs={{0,4},{2,6},{4,0},{6,2},{8,12},{10,14},{12,8},{14,10},{16,20},{18,... | collective-permute-start | bytes 3145736 | tf_op jit(solution)/shard_map/ppermute | solution.py:32
  454.5 93.8 %collective-permute-start.76 = (bf16[512,2048]{1,0:T(8,128)(2,1)}, bf16[512,2048]{1,0:T(8,128)(2,1)}, u32[]{:S(2)}, u32[]{:S(2)}) collective-permute-start(bf16[512,2048]{1,0:T(8,128)(2,1)} %convolution_convert_fusion.8), channel_id=1, source_target_pairs={{0,1},{1,0},{2,3},{3,2},{4,5},{5,4},{6,7},{7,6},{8,9},{9,8},{10,11... | collective-permute-start | bytes 6291464 | tf_op jit(solution)/shard_map/ppermute | solution.py:191
  468.9 78.3 %collective-permute-start.77 = (bf16[512,2048]{1,0:T(8,128)(2,1)S(1)}, bf16[512,2048]{1,0:T(8,128)(2,1)S(1)}, u32[]{:S(2)}, u32[]{:S(2)}) collective-permute-start(bf16[512,2048]{1,0:T(8,128)(2,1)S(1)} %convolution_convert_fusion.7), channel_id=1, source_target_pairs={{0,1},{1,0},{2,3},{3,2},{4,5},{5,4},{6,7},{7,6},{8,9},{9,8},{10,11... | collective-permute-start | bytes 6291464 | tf_op jit(solution)/shard_map/ppermute | solution.py:191
  475.0 140.8 %collective-permute-start.84 = (bf16[512,4096]{1,0:T(8,128)(2,1)}, bf16[512,4096]{1,0:T(8,128)(2,1)}, u32[]{:S(2)}, u32[]{:S(2)}) collective-permute-start(bf16[512,4096]{1,0:T(8,128)(2,1)} %convolution_convert_fusion), channel_id=1, source_target_pairs={{0,2},{2,0},{4,6},{6,4},{8,10},{10,8},{12,14},{14,12},{16,18},{18,... | collective-permute-start | bytes 12582920 | tf_op jit(solution)/shard_map/ppermute | solution.py:32
  480.6 152.9 %collective-permute-start.79 = (bf16[512,4096]{1,0:T(8,128)(2,1)}, bf16[512,4096]{1,0:T(8,128)(2,1)}, u32[]{:S(2)}, u32[]{:S(2)}) collective-permute-start(bf16[512,4096]{1,0:T(8,128)(2,1)} %convolution_convert_fusion.2), channel_id=1, source_target_pairs={{0,2},{2,0},{4,6},{6,4},{8,10},{10,8},{12,14},{14,12},{16,18},{18,... | collective-permute-start | bytes 12582920 | tf_op jit(solution)/shard_map/ppermute | solution.py:32
  615.8 59.7 %collective-permute-start.85 = (bf16[512,4096]{1,0:T(8,128)(2,1)}, bf16[512,4096]{1,0:T(8,128)(2,1)}, u32[]{:S(2)}, u32[]{:S(2)}) collective-permute-start(bf16[512,4096]{1,0:T(8,128)(2,1)} %convolution_convert_fusion.1), channel_id=1, source_target_pairs={{0,2},{2,0},{4,6},{6,4},{8,10},{10,8},{12,14},{14,12},{16,18},{18,... | collective-permute-start | bytes 12582920 | tf_op jit(solution)/shard_map/ppermute | solution.py:32
  625.5 26.2 %collective-permute-start.92 = (bf16[128,4096]{1,0:T(8,128)(2,1)}, bf16[128,4096]{1,0:T(8,128)(2,1)S(1)}, u32[]{:S(2)}, u32[]{:S(2)}) collective-permute-start(bf16[128,4096]{1,0:T(8,128)(2,1)} %get-tuple-element.203), channel_id=1, source_target_pairs={{0,4},{2,6},{4,0},{6,2},{8,12},{10,14},{12,8},{14,10},{16,20},{18,... | collective-permute-start | bytes 3145736 | tf_op jit(solution)/shard_map/ppermute | solution.py:32
  628.9 167.6 %collective-permute-start.78 = (bf16[512,2048]{1,0:T(8,128)(2,1)}, bf16[512,2048]{1,0:T(8,128)(2,1)}, u32[]{:S(2)}, u32[]{:S(2)}) collective-permute-start(bf16[512,2048]{1,0:T(8,128)(2,1)} %fusion.23), channel_id=1, source_target_pairs={{0,1},{1,0},{2,3},{3,2},{4,5},{5,4},{6,7},{7,6},{8,9},{9,8},{10,11... | collective-permute-start | bytes 6291464 | tf_op jit(solution)/shard_map/ppermute | solution.py:191
  633.2 40.5 %collective-permute-start.89 = (bf16[128,4096]{1,0:T(8,128)(2,1)}, bf16[128,4096]{1,0:T(8,128)(2,1)S(1)}, u32[]{:S(2)}, u32[]{:S(2)}) collective-permute-start(bf16[128,4096]{1,0:T(8,128)(2,1)} %get-tuple-element.200), channel_id=1, source_target_pairs={{0,4},{2,6},{4,0},{6,2},{8,12},{10,14},{12,8},{14,10},{16,20},{18,... | collective-permute-start | bytes 3145736 | tf_op jit(solution)/shard_map/ppermute | solution.py:32
  633.5 90.5 %collective-permute-start.80 = (bf16[512,4096]{1,0:T(8,128)(2,1)}, bf16[512,4096]{1,0:T(8,128)(2,1)S(1)}, u32[]{:S(2)}, u32[]{:S(2)}) collective-permute-start(bf16[512,4096]{1,0:T(8,128)(2,1)} %convolution_convert_fusion.3), channel_id=1, source_target_pairs={{0,2},{2,0},{4,6},{6,4},{8,10},{10,8},{12,14},{14,12},{16,18},{18,... | collective-permute-start | bytes 12582920 | tf_op jit(solution)/shard_map/ppermute | solution.py:32
  651.9 49.6 %collective-permute-start.95 = (bf16[128,4096]{1,0:T(8,128)(2,1)S(1)}, bf16[128,4096]{1,0:T(8,128)(2,1)S(1)}, u32[]{:S(2)}, u32[]{:S(2)}) collective-permute-start(bf16[128,4096]{1,0:T(8,128)(2,1)S(1)} %add_convert_fusion.12), channel_id=1, source_target_pairs={{0,8},{2,10},{4,12},{6,14},{8,16},{10,18},{12,20},{14,22},{16,24},... | collective-permute-start | bytes 3145736 | tf_op jit(solution)/shard_map/ppermute | solution.py:32
  673.7 26.0 %collective-permute-start.93 = (bf16[128,4096]{1,0:T(8,128)(2,1)S(1)}, bf16[128,4096]{1,0:T(8,128)(2,1)S(1)}, u32[]{:S(2)}, u32[]{:S(2)}) collective-permute-start(bf16[128,4096]{1,0:T(8,128)(2,1)S(1)} %copy-done.70), channel_id=1, source_target_pairs={{0,4},{2,6},{4,0},{6,2},{8,12},{10,14},{12,8},{14,10},{16,20},{18,... | collective-permute-start | bytes 3145736 | tf_op jit(solution)/shard_map/ppermute | solution.py:32
  675.5 46.8 %collective-permute-start.90 = (bf16[128,4096]{1,0:T(8,128)(2,1)S(1)}, bf16[128,4096]{1,0:T(8,128)(2,1)S(1)}, u32[]{:S(2)}, u32[]{:S(2)}) collective-permute-start(bf16[128,4096]{1,0:T(8,128)(2,1)S(1)} %copy-done.69), channel_id=1, source_target_pairs={{0,4},{2,6},{4,0},{6,2},{8,12},{10,14},{12,8},{14,10},{16,20},{18,... | collective-permute-start | bytes 3145736 | tf_op jit(solution)/shard_map/ppermute | solution.py:32
  699.8 44.9 %collective-permute-start.94 = (bf16[128,4096]{1,0:T(8,128)(2,1)S(1)}, bf16[128,4096]{1,0:T(8,128)(2,1)S(1)}, u32[]{:S(2)}, u32[]{:S(2)}) collective-permute-start(bf16[128,4096]{1,0:T(8,128)(2,1)S(1)} %get-tuple-element.205), channel_id=1, source_target_pairs={{0,4},{2,6},{4,0},{6,2},{8,12},{10,14},{12,8},{14,10},{16,20},{18,... | collective-permute-start | bytes 3145736 | tf_op jit(solution)/shard_map/ppermute | solution.py:32
  702.0 43.9 %collective-permute-start.96 = (bf16[128,4096]{1,0:T(8,128)(2,1)S(1)}, bf16[128,4096]{1,0:T(8,128)(2,1)S(1)}, u32[]{:S(2)}, u32[]{:S(2)}) collective-permute-start(bf16[128,4096]{1,0:T(8,128)(2,1)S(1)} %add_convert_fusion.11), channel_id=1, source_target_pairs={{0,8},{2,10},{4,12},{6,14},{8,16},{10,18},{12,20},{14,22},{16,24},... | collective-permute-start | bytes 3145736 | tf_op jit(solution)/shard_map/ppermute | solution.py:32
  722.2 43.9 %collective-permute-start.91 = (bf16[128,4096]{1,0:T(8,128)(2,1)}, bf16[128,4096]{1,0:T(8,128)(2,1)}, u32[]{:S(2)}, u32[]{:S(2)}) collective-permute-start(bf16[128,4096]{1,0:T(8,128)(2,1)} %get-tuple-element.202), channel_id=1, source_target_pairs={{0,4},{2,6},{4,0},{6,2},{8,12},{10,14},{12,8},{14,10},{16,20},{18,... | collective-permute-start | bytes 3145736 | tf_op jit(solution)/shard_map/ppermute | solution.py:32
  724.0 40.9 %collective-permute-start.86 = (bf16[512,1024]{1,0:T(8,128)(2,1)}, bf16[512,1024]{1,0:T(8,128)(2,1)}, u32[]{:S(2)}, u32[]{:S(2)}) collective-permute-start(bf16[512,1024]{1,0:T(8,128)(2,1)} %convolution_convert_fusion.9), channel_id=1, source_target_pairs={{0,2},{2,0},{4,6},{6,4},{8,10},{10,8},{12,14},{14,12},{16,18},{18,... | collective-permute-start | bytes 3145736 | tf_op jit(solution)/shard_map/ppermute | solution.py:32
  745.9 29.0 %collective-permute-start.97 = (bf16[128,4096]{1,0:T(8,128)(2,1)}, bf16[128,4096]{1,0:T(8,128)(2,1)}, u32[]{:S(2)}, u32[]{:S(2)}) collective-permute-start(bf16[128,4096]{1,0:T(8,128)(2,1)} %add_convert_fusion.13), channel_id=1, source_target_pairs={{0,8},{2,10},{4,12},{6,14},{8,16},{10,18},{12,20},{14,22},{16,24},... | collective-permute-start | bytes 3145736 | tf_op jit(solution)/shard_map/ppermute | solution.py:32
  752.1 42.3 %collective-permute-start.98 = (bf16[128,4096]{1,0:T(8,128)(2,1)}, bf16[128,4096]{1,0:T(8,128)(2,1)S(1)}, u32[]{:S(2)}, u32[]{:S(2)}) collective-permute-start(bf16[128,4096]{1,0:T(8,128)(2,1)} %add_convert_fusion.9), channel_id=1, source_target_pairs={{0,8},{2,10},{4,12},{6,14},{8,16},{10,18},{12,20},{14,22},{16,24},... | collective-permute-start | bytes 3145736 | tf_op jit(solution)/shard_map/ppermute | solution.py:32
  764.9 76.7 %collective-permute-start.81 = (bf16[512,1024]{1,0:T(8,128)(2,1)}, bf16[512,1024]{1,0:T(8,128)(2,1)}, u32[]{:S(2)}, u32[]{:S(2)}) collective-permute-start(bf16[512,1024]{1,0:T(8,128)(2,1)} %convolution_convert_fusion.11), channel_id=1, source_target_pairs={{0,2},{2,0},{4,6},{6,4},{8,10},{10,8},{12,14},{14,12},{16,18},{18,... | collective-permute-start | bytes 3145736 | tf_op jit(solution)/shard_map/ppermute | solution.py:32
  766.1 79.7 %collective-permute-start.110 = (bf16[128,4096]{1,0:T(8,128)(2,1)}, bf16[128,4096]{1,0:T(8,128)(2,1)}, u32[]{:S(2)}, u32[]{:S(2)}) collective-permute-start(bf16[128,4096]{1,0:T(8,128)(2,1)} %get-tuple-element.221), channel_id=1, source_target_pairs={{0,4},{2,6},{4,0},{6,2},{8,12},{10,14},{12,8},{14,10},{16,20},{18,... | collective-permute-start | bytes 3145736 | tf_op jit(solution)/shard_map/ppermute | solution.py:32
  775.0 68.9 %collective-permute-start.87 = (bf16[512,1024]{1,0:T(8,128)(2,1)}, bf16[512,1024]{1,0:T(8,128)(2,1)}, u32[]{:S(2)}, u32[]{:S(2)}) collective-permute-start(bf16[512,1024]{1,0:T(8,128)(2,1)} %convolution_convert_fusion.10), channel_id=1, source_target_pairs={{0,2},{2,0},{4,6},{6,4},{8,10},{10,8},{12,14},{14,12},{16,18},{18,... | collective-permute-start | bytes 3145736 | tf_op jit(solution)/shard_map/ppermute | solution.py:32
  794.4 50.0 %collective-permute-start.99 = (bf16[128,4096]{1,0:T(8,128)(2,1)}, bf16[128,4096]{1,0:T(8,128)(2,1)}, u32[]{:S(2)}, u32[]{:S(2)}) collective-permute-start(bf16[128,4096]{1,0:T(8,128)(2,1)} %add_convert_fusion.10), channel_id=1, source_target_pairs={{0,8},{2,10},{4,12},{6,14},{8,16},{10,18},{12,20},{14,22},{16,24},... | collective-permute-start | bytes 3145736 | tf_op jit(solution)/shard_map/ppermute | solution.py:32
  824.7 132.7 %all-to-all-start = ((f32[16,1,1536]{2,1,0:T(1,128)}), f32[16,1,1536]{2,1,0:T(1,128)S(1)}, u32[]{:S(2)}, u32[]{:S(2)}) async-start(f32[16,1,1536]{2,1,0:T(1,128)} %reshape.293), calls=%async_computation | async-start | bytes 196608 | tf_op jit(solution)/shard_map/all_to_all | solution.py:306
  837.6 89.0 %collective-permute-start.106 = (bf16[128,4096]{1,0:T(8,128)(2,1)S(1)}, bf16[128,4096]{1,0:T(8,128)(2,1)S(1)}, u32[]{:S(2)}, u32[]{:S(2)}) collective-permute-start(bf16[128,4096]{1,0:T(8,128)(2,1)S(1)} %copy-done.68), channel_id=1, source_target_pairs={{0,4},{2,6},{4,0},{6,2},{8,12},{10,14},{12,8},{14,10},{16,20},{18,... | collective-permute-start | bytes 3145736 | tf_op jit(solution)/shard_map/ppermute | solution.py:32
  843.9 49.1 %collective-permute-start.88 = (bf16[512,2048]{1,0:T(8,128)(2,1)S(1)}, bf16[512,2048]{1,0:T(8,128)(2,1)S(1)}, u32[]{:S(2)}, u32[]{:S(2)}) collective-permute-start(bf16[512,2048]{1,0:T(8,128)(2,1)S(1)} %copy-done.105), channel_id=1, source_target_pairs={{0,2},{2,0},{4,6},{6,4},{8,10},{10,8},{12,14},{14,12},{16,18},{18,... | collective-permute-start | bytes 6291464 | tf_op jit(solution)/shard_map/ppermute | solution.py:32
  848.2 44.8 %collective-permute-start.115 = (bf16[128,4096]{1,0:T(8,128)(2,1)S(1)}, bf16[128,4096]{1,0:T(8,128)(2,1)S(1)}, u32[]{:S(2)}, u32[]{:S(2)}) collective-permute-start(bf16[128,4096]{1,0:T(8,128)(2,1)S(1)} %add_convert_fusion.6), channel_id=1, source_target_pairs={{0,8},{2,10},{4,12},{6,14},{8,16},{10,18},{12,20},{14,22},{16,24},... | collective-permute-start | bytes 3145736 | tf_op jit(solution)/shard_map/ppermute | solution.py:32
  855.4 27.2 %collective-permute-start.101 = (bf16[128,1024]{1,0:T(8,128)(2,1)S(1)}, bf16[128,1024]{1,0:T(8,128)(2,1)S(1)}, u32[]{:S(2)}, u32[]{:S(2)}) collective-permute-start(bf16[128,1024]{1,0:T(8,128)(2,1)S(1)} %add_convert_fusion.28), channel_id=1, source_target_pairs={{0,8},{2,10},{4,12},{6,14},{8,16},{10,18},{12,20},{14,22},{16,24},... | collective-permute-start | bytes 786440 | tf_op jit(solution)/shard_map/ppermute | solution.py:32
  857.7 63.3 %collective-permute-start.83 = (bf16[512,2048]{1,0:T(8,128)(2,1)S(1)}, bf16[512,2048]{1,0:T(8,128)(2,1)S(1)}, u32[]{:S(2)}, u32[]{:S(2)}) collective-permute-start(bf16[512,2048]{1,0:T(8,128)(2,1)S(1)} %copy-done.104), channel_id=1, source_target_pairs={{0,2},{2,0},{4,6},{6,4},{8,10},{10,8},{12,14},{14,12},{16,18},{18,... | collective-permute-start | bytes 6291464 | tf_op jit(solution)/shard_map/ppermute | solution.py:32
  930.4 37.9 %collective-permute-start.114 = (bf16[128,2048]{1,0:T(8,128)(2,1)S(1)}, bf16[128,2048]{1,0:T(8,128)(2,1)S(1)}, u32[]{:S(2)}, u32[]{:S(2)}) collective-permute-start(bf16[128,2048]{1,0:T(8,128)(2,1)S(1)} %add_convert_fusion.18), channel_id=1, source_target_pairs={{0,8},{2,10},{4,12},{6,14},{8,16},{10,18},{12,20},{14,22},{16,24},... | collective-permute-start | bytes 1572872 | tf_op jit(solution)/shard_map/ppermute | solution.py:32
  935.3 32.9 %collective-permute-start.108 = (bf16[128,2048]{1,0:T(8,128)(2,1)}, bf16[128,2048]{1,0:T(8,128)(2,1)}, u32[]{:S(2)}, u32[]{:S(2)}) collective-permute-start(bf16[128,2048]{1,0:T(8,128)(2,1)} %get-tuple-element.219), channel_id=1, source_target_pairs={{0,4},{2,6},{4,0},{6,2},{8,12},{10,14},{12,8},{14,10},{16,20},{18,... | collective-permute-start | bytes 1572872 | tf_op jit(solution)/shard_map/ppermute | solution.py:32
  941.3 25.8 %collective-permute-start.120 = (bf16[128,1024]{1,0:T(8,128)(2,1)}, bf16[128,1024]{1,0:T(8,128)(2,1)}, u32[]{:S(2)}, u32[]{:S(2)}) collective-permute-start(bf16[128,1024]{1,0:T(8,128)(2,1)} %add_convert_fusion.20), channel_id=1, source_target_pairs={{0,8},{2,10},{4,12},{6,14},{8,16},{10,18},{12,20},{14,22},{16,24},... | collective-permute-start | bytes 786440 | tf_op jit(solution)/shard_map/ppermute | solution.py:32
  (174 other events, 3229.0 us)

commit v2 on v1

v2 whole, which is shorter than its diff:
```python
import jax
import jax.numpy as jnp
from jax import lax
from jax.experimental import pallas as pl
from jax.experimental.pallas import tpu as pltpu
from jax.sharding import PartitionSpec as P

HEAD_DIM = 128
EPS = 1e-06
HIGH = lax.Precision.HIGHEST
F32 = jnp.float32
BF16 = jnp.bfloat16
CORES = 2


def layer_norm(value):
    centre = value - jnp.mean(value, axis=-1, keepdims=True)
    spread = jnp.mean(centre * centre, axis=-1, keepdims=True)
    return centre * lax.rsqrt(spread + EPS)


def modulate(value, shift, scale):
    return layer_norm(value) * (1.0 + scale) + shift


def after(value, *earlier):
    return lax.optimization_barrier((value, *earlier))[0]


def pass_on(in_ref, out_ref):
    out_ref[...] = in_ref[...]


def pace(token, cost):
    return pl.pallas_call(
        pass_on,
        out_shape=jax.ShapeDtypeStruct(token.shape, token.dtype),
        cost_estimate=pl.CostEstimate(
            flops=int(cost * 1.15e9), bytes_accessed=8192, transcendentals=0
        ),
    )(token)


class Phases:
    def __init__(self, dp, mp):
        self.z = 4 if (dp // CORES) % 4 == 0 else 1
        self.x = dp // CORES // self.z
        self.tail, self.results, self.sent, self.last = (), [], [], ()
        self.turn = [(i, (i + 1) % mp) for i in range(mp)]
        self.token = jnp.zeros((8, 128), F32)

    def ring(self, dz, dx, dc):
        index = lambda z, x, c: (z % self.z * self.x + x % self.x) * CORES + c % CORES
        return [
            (index(z, x, c), index(z + dz, x + dx, c + dc))
            for z in range(self.z)
            for x in range(self.x)
            for c in range(CORES)
        ]

    def send(self, value, dz, dx, hold=True):
        value = after(value, *self.tail)
        self.sent.append(value)
        out = lax.ppermute(value, "dp", self.ring(dz, dx, 0))
        if hold:
            self.results.append(out)
        return out

    def send_z(self, value, places):
        return self.send(value, places, 0)

    def send_x(self, value):
        return self.send(value, 0, 1)

    def send_core(self, value):
        return lax.ppermute(value, "dp", self.ring(0, 0, 1))

    def across(self, part):
        out = [lax.optimization_barrier(part)]
        for _ in range(len(self.turn) - 1):
            out.append(lax.ppermute(out[-1], "mp", self.turn))
        return out

    def now(self, value):
        return after(value, *self.tail)

    def begin(self, value):
        return after(value, *self.tail, *self.sent, *self.last)

    def end(self, *values):
        self.last = values

    def close(self, cost=25.0):
        self.token = pace(after(self.token, *self.tail, *self.sent), cost)
        self.tail = (*self.results, *self.last, self.token)
        self.results, self.sent, self.last = [], [], ()

    def gather_x(self, piece):
        pieces = [piece]
        for _ in range(1, self.x):
            pieces.append(self.send_x(pieces[-1]))
        return pieces

    def reduce_x(self, blocks):
        moving = None
        for kx in range(1, self.x):
            value = blocks[kx]
            if moving is not None:
                value = value.astype(F32) + moving.astype(F32)
            moving = self.send_x(value.astype(BF16))
        return moving


def plus(first, *others):
    total = first.astype(F32)
    for other in others:
        if other is not None:
            total = total + other.astype(F32)
    return total


class Grid:
    def __init__(self, phases):
        self.z, self.x, self.phases = phases.z, phases.x, phases
        me = lax.axis_index("dp")
        self.at_z, self.at_x, self.core = (
            me // (self.x * CORES),
            (me // CORES) % self.x,
            me % CORES,
        )

    def to_relative(self):
        return jnp.stack(
            [
                (self.at_z - kz) % self.z * self.x + (self.at_x - kx) % self.x
                for kx in range(self.x)
                for kz in range(self.z)
            ]
        ).astype(jnp.int32)

    def to_absolute(self):
        return jnp.stack(
            [
                (self.at_x - ox) % self.x * self.z + (self.at_z - oz) % self.z
                for oz in range(self.z)
                for ox in range(self.x)
            ]
        ).astype(jnp.int32)

    def by_core(self, first, second, axis):
        return jnp.where(
            self.core == 0,
            jnp.concatenate([first, second], axis=axis),
            jnp.concatenate([second, first], axis=axis),
        )

    def halves(self, value, axis):
        half = value.shape[axis] // 2
        low = lax.slice_in_dim(value, 0, half, axis=axis)
        high = lax.slice_in_dim(value, half, 2 * half, axis=axis)
        return (
            jnp.where(self.core == 0, low, high),
            jnp.where(self.core == 0, high, low),
        )

    def chip_shard(self, shard):
        mine, theirs = self.halves(shard, 1)
        return self.by_core(mine, self.phases.send_core(theirs), 0)

    def own_rows(self, total):
        mine, theirs = self.halves(total, total.ndim - 2)
        return self.by_core(mine, self.phases.send_core(theirs), total.ndim - 1)

    def dots(self, lhs, rhs, kx):
        width = lhs.shape[1] // self.x
        return lax.dot_general(
            lhs[:, kx * width : (kx + 1) * width],
            rhs,
            (((0,), (0,)), ((), ())),
            preferred_element_type=F32,
        ).astype(BF16)


def copy_block(order_ref, in_ref, out_ref):
    out_ref[...] = in_ref[...]


def reorder(value, order):
    count = order.shape[0]
    shape = value.shape
    flat = value.reshape(-1, shape[-1])
    blk = shape[-1] // count
    if blk % 128:
        return jnp.take(flat.reshape(-1, count, blk), order, axis=1).reshape(shape)
    out = pl.pallas_call(
        copy_block,
        grid_spec=pltpu.PrefetchScalarGridSpec(
            num_scalar_prefetch=1,
            grid=(count,),
            in_specs=[pl.BlockSpec((flat.shape[0], blk), lambda j, s: (0, s[j]))],
            out_specs=pl.BlockSpec((flat.shape[0], blk), lambda j, s: (0, j)),
        ),
        out_shape=jax.ShapeDtypeStruct(flat.shape, flat.dtype),
    )(order, flat)
    return out.reshape(shape)


def matmul(lhs, rhs, turned=False):
    return lax.dot_general(
        lhs, rhs, (((1,), (1 if turned else 0,)), ((), ())), preferred_element_type=F32
    )


def make_body(dp, mp):
    def body(tokens, mod_table, w_qkv, w_out_t, w_up, w_down, bins, present, cotangent):
        count, length, width = tokens.shape
        rows = count * length
        ph = Phases(dp, mp)
        grid = Grid(ph)
        relative, absolute = grid.to_relative(), grid.to_absolute()
        turns = list(range(1, grid.x)) + [0]
        join = lambda own, theirs: jnp.concatenate([own, theirs], axis=0)

        def whole(*by_z):
            return jnp.concatenate(
                [by_z[kz][kx] for kx in range(grid.x) for kz in range(grid.z)], axis=0
            )

        def summed(value, weight, between=None):
            part = matmul(ph.begin(value[rows:]), weight, True).astype(BF16)
            ph.end(part)
            theirs = ph.send_core(part)
            if between is not None:
                between()
            part = matmul(ph.begin(value[:rows]), weight, True) + theirs.astype(F32)
            part = part.astype(BF16)
            ph.end(part)
            return ph.across(part)

        def from_both(theirs, value, weight, between=None):
            if between is not None:
                between()
            part = matmul(ph.begin(value[:rows]), weight, True) + theirs.astype(F32)
            part = part.astype(BF16)
            ph.end(part)
            return ph.across(part)

        def dots(lhs, rhs):
            kept = {}
            for kx in turns:
                kept[kx] = grid.dots(ph.begin(lhs), rhs, kx)
                ph.end(kept[kx])
            return kept

        def rows_of(kept, low, high):
            blk = width // grid.x // grid.z
            return {kx: kept[kx][low * blk : high * blk] for kx in kept}

        wide = w_qkv.reshape(3, -1, CORES, w_qkv.shape[2] // CORES).transpose(1, 2, 0, 3)
        s_q = grid.chip_shard(wide.reshape(w_qkv.shape[1], -1))
        z_q, x_q = {1: ph.send_z(s_q, 1)}, {0: ph.gather_x(s_q)}
        s_o = grid.chip_shard(ph.begin(w_out_t))
        ph.end(s_o)
        x_o = jnp.stack(ph.gather_x(s_o))
        table_rows = jnp.arange(mod_table.shape[0])[None, :]
        onehot = (bins[:, None] == table_rows).astype(F32)
        mods = jnp.einsum("cb,btd->ctd", ph.begin(onehot), mod_table, precision=HIGH)
        mods = reorder(mods, relative)
        ph.end(mods)
        ph.close()

        z_q[3] = ph.send_z(s_q, 3)
        x_q[1] = ph.gather_x(z_q[1])
        tokens = reorder(ph.begin(tokens), relative)
        shift1, scale1, gate1 = (mods[:, 0:1], mods[:, 1:2], mods[:, 2:3])
        shift2, scale2, gate2 = (mods[:, 3:4], mods[:, 4:5], mods[:, 5:6])
        mask = present.astype(F32)[:, None, None]
        inputs = tokens.astype(F32)
        normed_own = modulate(inputs, shift1, scale1).astype(BF16).reshape(rows, width)
        ph.end(normed_own)
        ph.close()

        z_q[2] = ph.send_z(z_q[1], 1)
        x_q[3] = ph.gather_x(z_q[3])
        normed_other = ph.send_core(ph.now(normed_own))
        s_u = grid.chip_shard(ph.begin(w_up))
        ph.end(s_u)
        normed = join(normed_own, ph.begin(normed_other))
        ph.end(normed)
        ph.close()

        z_o = {0: x_o, 1: ph.send_z(x_o, 1)}
        x_q[2] = ph.gather_x(z_q[2])
        s_d = grid.chip_shard(ph.begin(w_down))
        ph.end(s_d)
        ph.close()

        z_o[3] = ph.send_z(x_o, 3)
        z_o[2] = ph.send_z(z_o[1], 1)
        x_u = {0: ph.gather_x(s_u)}
        w_a = whole(x_q[0], x_q[1], x_q[2], x_q[3])
        local_width = s_o.shape[1]
        local_heads = local_width // HEAD_DIM
        factor = HEAD_DIM ** (-0.5)
        per_head = lambda value: value.reshape(CORES * count, length, local_heads, HEAD_DIM)
        qkv = matmul(ph.begin(normed), w_a).astype(BF16)
        ph.end(qkv)
        query, keys, values = (per_head(part) for part in jnp.split(ph.begin(qkv), 3, axis=1))
        scores = jnp.einsum("cqhe,ckhe->chqk", query, keys, preferred_element_type=F32) * factor
        top = jnp.max(scores, axis=-1, keepdims=True)
        expo = jnp.exp(scores - top)
        total = jnp.sum(expo, axis=-1, keepdims=True)
        lse = top + jnp.log(total)
        probs_low = (expo / total).astype(BF16)
        ph.end(probs_low)
        ph.close()

        z_u = {1: ph.send_z(s_u, 1)}
        x_d = {0: ph.gather_x(s_d)}
        w_o = jnp.concatenate([z_o[kz][kx] for kx in range(grid.x) for kz in range(grid.z)], axis=0)
        probs_low = ph.begin(probs_low)
        mixed = jnp.einsum("chqk,ckhe->cqhe", probs_low, values, preferred_element_type=F32)
        mixed = mixed.astype(BF16).reshape(CORES * rows, local_width)
        ph.end(mixed)
        att = summed(mixed, w_o)
        ph.close()

        z_u[3] = ph.send_z(s_u, 3)
        x_u[1] = ph.gather_x(z_u[1])
        cotangent = reorder(ph.begin(cotangent), relative)
        grad_dy = cotangent.astype(F32) * mask
        d_mlp_own = (gate2 * grad_dy).astype(BF16).reshape(rows, width)
        ph.end(d_mlp_own)
        ph.close()

        z_u[2] = ph.send_z(z_u[1], 1)
        x_u[3] = ph.gather_x(z_u[3])
        d_mlp = join(d_mlp_own, ph.begin(ph.send_core(ph.now(d_mlp_own))))
        ph.end(d_mlp)
        att[-1] = ph.begin(att[-1])
        att = plus(*att).reshape(count, length, width)
        hidden = inputs + gate1 * att
        second_own = modulate(hidden, shift2, scale2).astype(BF16).reshape(rows, width)
        ph.end(second_own)
        ph.close()

        z_d = {1: ph.send_z(s_d, 1)}
        x_u[2] = ph.gather_x(z_u[2])
        second = join(second_own, ph.begin(ph.send_core(ph.now(second_own))))
        ph.end(second)
        ph.close()

        z_d[3] = ph.send_z(s_d, 3)
        x_d[1] = ph.gather_x(z_d[1])
        w_u = whole(x_u[0], x_u[1], x_u[2], x_u[3])
        up_val = matmul(ph.begin(second), w_u)
        act = jax.nn.gelu(up_val).astype(BF16)
        ph.end(act)
        ph.close()

        z_d[2] = ph.send_z(z_d[1], 1)
        x_d[3] = ph.gather_x(z_d[3])
        down = dots(d_mlp, act)
        half = down[0].shape[1] // 2
        first = jnp.stack([down[kx][:, :half] for kx in range(grid.x)])
        other = {kx: down[kx][:, half:] for kx in down}
        ph.end(first)
        ph.close()

        blk = first.shape[1] // grid.z
        part = lambda stacked, kz: stacked[:, kz * blk : (kz + 1) * blk]
        x_d[2] = ph.gather_x(z_d[2])
        a_2 = ph.send_z(part(first, 2), 3)
        ph.close()

        x_b = {2: ph.reduce_x(rows_of(other, 2, 4))}
        a_3 = ph.send_z(part(first, 3), 1)
        w_d = whole(x_d[0], x_d[1], x_d[2], x_d[3])
        d_act = matmul(ph.begin(d_mlp), w_d)
        _, gelu_pull = jax.vjp(jax.nn.gelu, up_val)
        d_up = gelu_pull(d_act)[0].astype(BF16)
        ph.end(d_up)
        up = {}
        d_second_part = matmul(ph.begin(d_up)[rows:], w_u, True).astype(BF16)
        ph.end(d_second_part)
        ph.close()

        def up_dots(blocks):
            for kx in blocks:
                up[kx] = grid.dots(ph.begin(second), d_up, kx)
                ph.end(up[kx])

        x_b[0] = ph.reduce_x(rows_of(other, 0, 2))
        a_1 = ph.send_z(plus(part(first, 1), ph.now(a_2)).astype(BF16), 3)
        d_second = from_both(ph.send_core(ph.now(d_second_part)), d_up, w_u, lambda: up_dots(turns[:-1]))
        ph.close()

        up_rows = lambda kz: ph.reduce_x(rows_of(up, kz, kz + 1))
        x_up = {2: up_rows(2)}
        b_part = lambda kz: ph.now(x_b[kz // 2 * 2][(kz % 2) * blk : (kz % 2 + 1) * blk])
        b_sum = lambda kz: plus(rows_of(other, kz, kz + 1)[0], b_part(kz))
        b_2 = ph.send_z(b_sum(2).astype(BF16), 3)
        b_3 = ph.send_z(b_sum(3).astype(BF16), 1)
        up_dots(turns[-1:])
        mlp_part = matmul(ph.begin(act)[rows:], w_d, True).astype(BF16)
        ph.end(mlp_part)
        ph.close()

        x_up[3] = up_rows(3)
        up_sum = lambda kz: plus(rows_of(up, kz, kz + 1)[0], ph.now(x_up[kz]))
        u_2 = ph.send_z(up_sum(2).astype(BF16), 3)
        mlp = from_both(ph.send_core(ph.now(mlp_part)), act, w_d)
        d_second[-1] = ph.begin(d_second[-1])
        d_second = plus(*d_second)
        _, norm_pull2 = jax.vjp(modulate, hidden, shift2, scale2)
        d_hidden_n, g_shift2, g_scale2 = norm_pull2(d_second.reshape(count, length, width))
        d_hidden = grad_dy + d_hidden_n
        g_gate1 = jnp.sum(d_hidden * att, axis=1)
        d_att_own = (gate1 * d_hidden).astype(BF16).reshape(rows, width)
        ph.end(d_att_own)
        ph.close()

        x_up[1] = up_rows(1)
        u_3 = ph.send_z(up_sum(3).astype(BF16), 1)
        d_att = join(d_att_own, ph.begin(ph.send_core(ph.now(d_att_own))))
        d_mixed = matmul(d_att, w_o).astype(BF16)
        ph.end(d_mixed)
        d_mixed = per_head(ph.begin(d_mixed))
        again = jnp.einsum("cqhe,ckhe->chqk", query, keys, preferred_element_type=F32) * factor
        probs = jnp.exp(again - lse)
        probs_again = probs.astype(BF16)
        d_probs = jnp.einsum("cqhe,ckhe->chqk", d_mixed, values, preferred_element_type=F32)
        delta = jnp.sum(d_probs * probs, axis=-1, keepdims=True)
        d_scores = (probs * (d_probs - delta)).astype(BF16)
        d_values = jnp.einsum(
            "chqk,cqhe->ckhe", probs_again, d_mixed, preferred_element_type=F32
        ).astype(BF16)
        d_query = (
            jnp.einsum("chqk,ckhe->cqhe", d_scores, keys, preferred_element_type=F32) * factor
        ).astype(BF16)
        d_keys = (
            jnp.einsum("chqk,cqhe->ckhe", d_scores, query, preferred_element_type=F32) * factor
        ).astype(BF16)
        flat = lambda value: value.reshape(CORES * rows, local_width)
        d_qkv = jnp.concatenate([flat(d_query), flat(d_keys), flat(d_values)], axis=1)
        ph.end(d_qkv)
        ph.close()

        x_up[0] = up_rows(0)
        u_1 = ph.send_z((up_sum(1) + ph.now(u_2).astype(F32)).astype(BF16), 3)
        d_normed_part = matmul(ph.begin(d_qkv)[rows:], w_a, True).astype(BF16)
        ph.end(d_normed_part)
        out = {}

        def out_dots():
            out.update(dots(d_att, mixed))

        d_normed = from_both(ph.send_core(d_normed_part), d_qkv, w_a, out_dots)
        proj = dots(normed, d_qkv)
        ph.close()

        x_out = ph.reduce_x(out)
        b_1 = ph.send_z((b_sum(1) + ph.now(b_2).astype(F32)).astype(BF16), 3)
        mlp[-1] = ph.begin(mlp[-1])
        mlp = plus(*mlp).reshape(count, length, width)
        block_out = (mask * (hidden + gate2 * mlp)).astype(BF16)
        block_out = reorder(block_out, absolute)
        g_gate2 = jnp.sum(grad_dy * mlp, axis=1)
        ph.end(block_out, g_gate2)
        ph.close()

        p_rows = lambda kz: ph.reduce_x(rows_of(proj, kz, kz + 1))
        p_sum = lambda kz: plus(rows_of(proj, kz, kz + 1)[0], ph.now(x_p[kz]))
        out_sum = lambda kz: plus(
            rows_of(out, kz, kz + 1)[0], ph.now(x_out[kz * blk : (kz + 1) * blk])
        )
        x_p = {2: p_rows(2)}
        o_2 = ph.send_z(out_sum(2).astype(BF16), 3)
        o_3 = ph.send_z(out_sum(3).astype(BF16), 1)
        up_part = up_sum(0) + ph.now(u_3).astype(F32) + ph.now(u_1).astype(F32)
        up_part = grid.own_rows(ph.begin(up_part))
        ph.end(up_part)
        ph.close(20.0)

        x_p[3] = p_rows(3)
        p_2 = ph.send_z(p_sum(2).astype(BF16), 3)
        d_normed[-1] = ph.begin(d_normed[-1])
        d_normed = plus(*d_normed)
        _, norm_pull1 = jax.vjp(modulate, inputs, shift1, scale1)
        d_input_n, g_shift1, g_scale1 = norm_pull1(d_normed.reshape(count, length, width))
        input_grad = d_hidden + d_input_n
        ph.end(input_grad)
        ph.close(20.0)

        x_p[1] = p_rows(1)
        p_3 = ph.send_z(p_sum(3).astype(BF16), 1)
        input_grad = reorder(ph.begin(input_grad), absolute)
        d_mods = jnp.stack(
            [g_shift1[:, 0], g_scale1[:, 0], g_gate1, g_shift2[:, 0], g_scale2[:, 0], g_gate2],
            axis=1,
        )
        d_mods = reorder(d_mods, absolute)
        bin_row = jnp.broadcast_to(bins.astype(F32)[:, None, None], (count, 1, width))
        d_mods = jnp.concatenate([d_mods, bin_row], axis=1)
        ph.end(input_grad, d_mods)
        ph.close(20.0)

        x_p[0] = p_rows(0)
        p_1 = ph.send_z((p_sum(1) + ph.now(p_2).astype(F32)).astype(BF16), 3)
        d_mods = lax.all_to_all(ph.now(d_mods), "dp", split_axis=2, concat_axis=0, tiled=True)
        d_mods = ph.begin(d_mods)
        onehot_all = (d_mods[:, 6, :1] == table_rows.astype(F32)).astype(F32)
        table_part = jnp.einsum("sb,std->btd", onehot_all, d_mods[:, :6], precision=HIGH)
        ph.end(table_part)
        ph.close(20.0)

        first_sum = plus(part(first, 0), a_3, a_1)
        x_first = ph.reduce_x(first_sum.astype(BF16))
        o_1 = ph.send_z((out_sum(1) + ph.now(o_2).astype(F32)).astype(BF16), 3)
        qkv_part = p_sum(0) + ph.now(p_3).astype(F32) + ph.now(p_1).astype(F32)
        qkv_part = qkv_part.reshape(-1, 3, local_width).transpose(1, 0, 2)
        qkv_part = grid.own_rows(ph.begin(qkv_part))
        ph.end(qkv_part)
        ph.close(15.0)

        down_low = plus(ph.now(first_sum)[0], x_first)
        down_high = b_sum(0) + ph.now(b_3).astype(F32) + ph.now(b_1).astype(F32)
        down_part = grid.own_rows(jnp.concatenate([down_low, down_high], axis=1))
        out_part = grid.own_rows(out_sum(0) + ph.now(o_3).astype(F32) + ph.now(o_1).astype(F32))
        return (block_out, input_grad, table_part, qkv_part, out_part, up_part, down_part)

    return body


def solution(mesh):
    in_specs = (
        P("dp", None, None),
        P(),
        P(None, "dp", "mp"),
        P("dp", "mp"),
        P("dp", "mp"),
        P("dp", "mp"),
        P("dp"),
        P("dp"),
        P("dp", None, None),
    )
    out_specs = (
        P("dp", None, None),
        P("dp", None, None),
        P(None, None, "dp"),
        P(None, "dp", "mp"),
        P("dp", "mp"),
        P("dp", "mp"),
        P("dp", "mp"),
    )
    body = make_body(mesh.shape["dp"], mesh.shape["mp"])
    return jax.shard_map(body, mesh=mesh, in_specs=in_specs, out_specs=out_specs, check_vma=False)
```

time: 1020 us -> 696 us (0.68)
  waiting for transfers between devices: 472 us -> 183 us
  other arithmetic: 76 us -> 114 us
  matrix products: 177 us -> 144 us
  local copies, waits for them, and re-layouts: 131 us -> 103 us
  starting transfers between devices: 77.1 us -> 104 us
  Pallas kernels: 58.5 us -> 36 us
  blocking collectives: 13 us -> 0 us
    ppermute x124 -> x72, waiting for transfers between devices: 472 us -> 175 us  [the longest x52 157 us: send(): out = lax.ppermute(value, 'dp', self.ring(dz, dx, 0))]
    unnamed x312 -> x240, local copies, waits for them, and re-layouts: 93.9 us -> 60.4 us
    dot_general x32 -> x22, matrix products: 166 us -> 134 us  [the longest x12 97.4 us: matmul(): lax.dot_general(lhs, rhs, (((1,), (1 if turned else 0,)), ((), ())), pref...]
    ppermute x124 -> x72, starting transfers between devices: 72.2 us -> 101 us  [the longest x52 93.2 us: send(): out = lax.ppermute(value, 'dp', self.ring(dz, dx, 0))]
    pallas_call x6, Pallas kernels: 58.5 us -> 36 us  [reorder(): pl.pallas_call(copy_block, grid_spec=pltpu.PrefetchScalarGridSpec(num_sca...]
    unnamed x1 -> x0, blocking collectives: 13 us -> none
    convert_element_type x25 -> x20, other arithmetic: 26.8 us -> 37 us  [the longest x1 4.35 us: body(): block_out = (mask * (hidden + gate2 * mlp)).astype(BF16)]
  transfers between devices with their start and end apart: 125 -> 73, of which waited for: 46 -> 31; matrix products, arithmetic and copies ran while one was open for 32% -> 47% of each run, Pallas kernels for 6% -> 5%
where the time goes in v2:
time: 696 us; the launch traced here: 687 us
  waiting for transfers between devices  183 us (26%)
  matrix products  144 us (21%)
  other arithmetic  114 us (16%)
  starting transfers between devices  104 us (15%)
  local copies, waits for them, and re-layouts  103 us (15%)
  Pallas kernels  36 us (5%)
    ppermute x52, waiting for transfers between devices, send(): out = lax.ppermute(value, 'dp', self.ring(dz, dx, 0))  157 us
    dot_general x12, matrix products, matmul(): lax.dot_general(lhs, rhs, (((1,), (1 if turned else 0,)), ((), ())), pref...  97.4 us
    ppermute x52, starting transfers between devices, send(): out = lax.ppermute(value, 'dp', self.ring(dz, dx, 0))  93.2 us
    unnamed x240, local copies, waits for them, and re-layouts  60.4 us
    pallas_call x6, Pallas kernels, reorder(): pl.pallas_call(copy_block, grid_spec=pltpu.PrefetchScalarGridSpec(num_sca...  36 us
    dot_general x8, matrix products, dots(): lax.dot_general(lhs[:, kx * width:(kx + 1) * width], rhs, (((0,), (0,)),...  34.9 us
    reduce_sum x2, other arithmetic, modulate(): return layer_norm(value) * (1.0 + scale) + shift  17.3 us
    ppermute x16, waiting for transfers between devices, send_core(): return lax.ppermute(value, 'dp', self.ring(0, 0, 1))  16.5 us
  transfers between devices with their start and end apart: 73, of which 31 were waited for; matrix products, arithmetic and copies ran while one was open for 47% of the time, Pallas kernels for 5%

profile of v2, /device:TPU:0, one launch (start us, length us, event | category | flops | bytes accessed | tf_op | source)
XLA Modules:
  0.0 687.3 jit_solution(15149552043487410526)
XLA Ops:
  15.5 4.8 shard_map.144
  21.4 13.2 %collective-permute-done.4 = bf16[256,512]{1,0:T(8,128)(2,1)S(1)} collective-permute-done((bf16[256,512]{1,0:T(8,128)(2,1)S(1)}, bf16[256,512]{1,0:T(8,128)(2,1)S(1)}, u32[]{:S(2)}, u32[]{:S(2)}) %collective-permute-start.4) | collective-permute-done | bytes 262176 | tf_op jit(solution)/shard_map/ppermute | solution.py:64
  35.5 3.9 collective-permute-start.5
  40.8 6.3 shard_map.145
  52.6 2.9 fusion.15
  63.7 14.5 %collective-permute-done.9 = bf16[256,1536]{0,1:T(8,128)(2,1)S(1)} collective-permute-done((bf16[256,1536]{0,1:T(8,128)(2,1)}, bf16[256,1536]{0,1:T(8,128)(2,1)S(1)}, u32[]{:S(2)}, u32[]{:S(2)}) %collective-permute-start.9) | collective-permute-done | bytes 786464 | tf_op jit(solution)/shard_map/ppermute | solution.py:64
  88.0 11.6 %collective-permute-done.11 = bf16[2,256,512]{2,1,0:T(8,128)(2,1)} collective-permute-done((bf16[2,256,512]{2,1,0:T(8,128)(2,1)}, bf16[2,256,512]{2,1,0:T(8,128)(2,1)}, u32[]{:S(2)}, u32[]{:S(2)}) %collective-permute-start.11) | collective-permute-done | bytes 524320 | tf_op jit(solution)/shard_map/ppermute | solution.py:64
  103.2 3.5 collective-permute-start.14
  108.7 6.9 %convolution_convert_fusion = bf16[1024,1536]{1,0:T(8,128)(2,1)S(1)} fusion(bf16[1024,2048]{1,0:T(8,128)(2,1)S(1)} %pad_maximum_fusion.1, bf16[2048,1536]{0,1:T(8,128)(2,1)S(1)} %constant_dynamic-update-slice_fusion), kind=kOutput, calls=%fused_computation.78 | convolution fusion | flops 6444023808 | bytes 13631488 | tf_op jit(solution)/shard_map/dot_general | solution.py:209
  138.0 4.2 convolution_convert_fusion.10
  144.0 14.1 %collective-permute-done.19 = bf16[256,2048]{1,0:T(8,128)(2,1)} collective-permute-done((bf16[256,2048]{1,0:T(8,128)(2,1)}, bf16[256,2048]{1,0:T(8,128)(2,1)}, u32[]{:S(2)}, u32[]{:S(2)}) %collective-permute-start.19) | collective-permute-done | bytes 1048608 | tf_op jit(solution)/shard_map/ppermute | solution.py:64
  160.5 4.8 add_convert_fusion.3
  168.0 6.4 shard_map.146
  178.1 8.2 %collective-permute-done.21 = bf16[256,2048]{1,0:T(8,128)(2,1)S(1)} collective-permute-done((bf16[256,2048]{1,0:T(8,128)(2,1)}, bf16[256,2048]{1,0:T(8,128)(2,1)S(1)}, u32[]{:S(2)}, u32[]{:S(2)}) %collective-permute-start.21) | collective-permute-done | bytes 1048608 | tf_op jit(solution)/shard_map/ppermute | solution.py:64
  191.3 16.9 %collective-permute-done.24 = bf16[256,2048]{1,0:T(8,128)(2,1)} collective-permute-done((bf16[256,2048]{1,0:T(8,128)(2,1)}, bf16[256,2048]{1,0:T(8,128)(2,1)}, u32[]{:S(2)}, u32[]{:S(2)}) %collective-permute-start.24) | collective-permute-done | bytes 1048608 | tf_op jit(solution)/shard_map/ppermute | solution.py:64
  218.9 3.0 fusion.85
  228.7 15.7 %collective-permute-done.28 = bf16[256,2048]{1,0:T(8,128)(2,1)} collective-permute-done((bf16[256,2048]{1,0:T(8,128)(2,1)}, bf16[256,2048]{1,0:T(8,128)(2,1)}, u32[]{:S(2)}, u32[]{:S(2)}) %collective-permute-start.28) | collective-permute-done | bytes 1048608 | tf_op jit(solution)/shard_map/ppermute | solution.py:64
  255.1 14.5 %multiply_convert_fusion = (bf16[1024,2048]{1,0:T(8,128)(2,1)S(1)}, f32[1024,2048]{1,0:T(8,128)}) fusion(bf16[1024,2048]{1,0:T(8,128)(2,1)S(1)} %pad_maximum_fusion.3, bf16[2048,2048]{1,0:T(8,128)(2,1)} %constant_dynamic-update-slice_fusion.10), kind=kOutput, calls=%fused_computation.9 | convolution fusion | flops 8608808960 | bytes 25165824 | tf_op jit(solution)/shard_map/dot_general | solution.py:209
  269.8 3.7 collective-permute-done.29
  273.5 19.7 %collective-permute-start.31 = (bf16[256,2048]{1,0:T(8,128)(2,1)S(1)}, bf16[256,2048]{1,0:T(8,128)(2,1)S(1)}, u32[]{:S(2)}, u32[]{:S(2)}) collective-permute-start(bf16[256,2048]{1,0:T(8,128)(2,1)S(1)} %collective-permute-done.27), channel_id=1, source_target_pairs={{0,8},{2,10},{4,12},{6,14},{8,16},{10,18},{12,20},{14,22},{16,24},... | collective-permute-start | bytes 3145736 | tf_op jit(solution)/shard_map/ppermute | solution.py:64
  293.2 4.8 convolution_convert_fusion.6
  298.1 4.8 convolution_convert_fusion.5
  317.2 17.2 %collective-permute-done.33 = bf16[256,2048]{1,0:T(8,128)(2,1)S(1)} collective-permute-done((bf16[256,2048]{1,0:T(8,128)(2,1)S(1)}, bf16[256,2048]{1,0:T(8,128)(2,1)S(1)}, u32[]{:S(2)}, u32[]{:S(2)}) %collective-permute-start.33) | collective-permute-done | bytes 1048608 | tf_op jit(solution)/shard_map/ppermute | solution.py:64
  339.9 18.7 %fusion.6 = bf16[1024,2048]{1,0:T(8,128)(2,1)} fusion(f32[1024,2048]{1,0:T(8,128)} %get-tuple-element.413, bf16[1024,2048]{1,0:T(8,128)(2,1)S(1)} %copy-done.35, bf16[2048,2048]{1,0:T(8,128)(2,1)} %constant_dynamic-update-slice_fusion.18), kind=kOutput, calls=%fused_computation.8 | convolution fusion | flops 8631877632 | bytes 25165824 | tf_op jit(solution)/shard_map/dot_general | solution.py:209
  358.6 9.9 %convolution_convert_fusion.9 = bf16[512,2048]{1,0:T(8,128)(2,1)} fusion(bf16[2048,2048]{1,0:T(8,128)(2,1)} %constant_dynamic-update-slice_fusion.10, bf16[1024,2048]{1,0:T(8,128)(2,1)} %fusion.6), kind=kOutput, calls=%fused_computation.89 | convolution fusion | flops 4296015872 | bytes 12582912 | tf_op jit(solution)/shard_map/dot_general | solution.py:209
  373.3 5.0 convolution_convert_fusion.4
  380.6 5.4 collective-permute-done.38
  389.7 8.5 %add_convert_fusion.2 = bf16[512,2048]{1,0:T(8,128)(2,1)S(1)} fusion(bf16[512,2048]{1,0:T(8,128)(2,1)} %collective-permute-done.39, bf16[512,2048]{1,0:T(8,128)(2,1)S(1)} %slice-done, bf16[2048,2048]{1,0:T(8,128)(2,1)} %constant_dynamic-update-slice_fusion.10), kind=kOutput, calls=%fused_computation.69 | convolution fusion | flops 4298113024 | bytes 14680064 | tf_op jit(solution)/shard_map/dot_general | solution.py:209
  398.6 4.0 collective-permute-start.41
  405.8 7.0 %convolution_convert_fusion.3 = bf16[1024,2048]{1,0:T(8,128)(2,1)S(1)} fusion(bf16[1024,2048]{1,0:T(8,128)(2,1)} %fusion.6, bf16[1024,2048]{1,0:T(8,128)(2,1)S(1)} %pad_maximum_fusion.3), kind=kOutput, calls=%fused_computation.81 | convolution fusion | flops 4297064448 | bytes 10485760 | tf_op jit(solution)/shard_map/dot_general | solution.py:176
  412.8 10.1 %convolution_convert_fusion.8 = bf16[512,2048]{1,0:T(8,128)(2,1)S(1)} fusion(bf16[2048,2048]{1,0:T(8,128)(2,1)} %constant_dynamic-update-slice_fusion.18, bf16[1024,2048]{1,0:T(8,128)(2,1)} %copy-done.43), kind=kOutput, calls=%fused_computation.88 | convolution fusion | flops 4296015872 | bytes 12582912 | tf_op jit(solution)/shard_map/dot_general | solution.py:209
  424.1 4.1 collective-permute-start.46
  428.7 4.2 collective-permute-done.43
  432.9 9.2 %add_convert_fusion.1 = bf16[512,2048]{1,0:T(8,128)(2,1)} fusion(bf16[512,2048]{1,0:T(8,128)(2,1)S(1)} %collective-permute-done.43, bf16[512,2048]{1,0:T(8,128)(2,1)S(1)} %slice.384, bf16[2048,2048]{1,0:T(8,128)(2,1)} %constant_dynamic-update-slice_fusion.18), kind=kOutput, calls=%fused_computation.68 | convolution fusion | flops 4298113024 | bytes 14680064 | tf_op jit(solution)/shard_map/dot_general | solution.py:209
  447.1 6.4 fusion.84
  453.5 3.9 fusion.13
  457.4 3.3 add_convert_fusion.5
  463.2 4.1 collective-permute-done.50
  473.8 4.3 fusion.53
  491.6 2.8 add_convert_fusion.4
  495.1 3.6 collective-permute-start.52
  498.7 3.6 convolution_convert_fusion.7
  506.5 4.6 add_convert_fusion
  511.8 4.9 convolution_convert_fusion.2
  516.8 4.8 convolution_convert_fusion.1
  525.3 3.7 collective-permute-start.56
  530.6 4.4 fusion.19.in_ref
  535.0 6.4 fusion.22
  541.5 6.3 shard_map.147
  547.8 3.4 fusion.89
  565.0 7.1 %collective-permute-done.57 = bf16[256,1536]{1,0:T(8,128)(2,1)S(1)} collective-permute-done((bf16[256,1536]{1,0:T(8,128)(2,1)S(1)}, bf16[256,1536]{1,0:T(8,128)(2,1)S(1)}, u32[]{:S(2)}, u32[]{:S(2)}) %collective-permute-start.57) | collective-permute-done | bytes 786464 | tf_op jit(solution)/shard_map/ppermute | solution.py:64
  574.4 3.4 multiply_reduce_fusion.1
  581.8 5.0 fusion.11
  586.9 10.9 %fusion.23 = (f32[2,2048]{1,0:T(2,128)S(1)}, f32[2,2048]{1,0:T(2,128)S(1)}, f32[2,256,2048]{2,1,0:T(8,128)}) fusion(bf16[512,2048]{1,0:T(8,128)(2,1)} %shard_map.145, f32[2,256]{1,0:T(2,128)S(1)} %copy-done.89, f32[2,256]{1,0:T(2,128)S(1)} %get-tuple-element.402, bf16[512,2048]{1,0:T(8,128)(2,1)} %collective-permute-done.54, ...), kind=kLoop, calls=%fused_computation.55 | loop fusion | flops 29351936 | bytes 25264136 | tf_op jit(solution)/shard_map/transpose(jvp())/reduce_sum | solution.py:23
  598.6 4.8 shard_map.149
  607.8 7.4 %shard_map.148 = f32[512,2048]{1,0:T(8,128)} custom-call(s32[8]{0:T(128)} %stack.87.order_ref, f32[512,2048]{1,0:T(8,128)} %bitcast.242), custom_call_target="tpu_custom_call" | custom-call | tf_op jit(solution)/shard_map/pallas_call | solution.py:195
  615.2 9.7 %collective-permute-done.64 = bf16[256,1536]{1,0:T(8,128)(2,1)} collective-permute-done((bf16[256,1536]{1,0:T(8,128)(2,1)}, bf16[256,1536]{1,0:T(8,128)(2,1)}, u32[]{:S(2)}, u32[]{:S(2)}) %collective-permute-start.64) | collective-permute-done | bytes 786464 | tf_op jit(solution)/shard_map/ppermute | solution.py:64
  624.9 2.8 add_convert_fusion.8
  632.3 5.1 reshape.361
  637.4 3.5 all-to-all-start
  640.9 7.6 %all-to-all-done = f32[16,1,1792]{2,1,0:T(1,128)S(1)} async-done(((f32[16,1,1792]{2,1,0:T(1,128)}), f32[16,1,1792]{2,1,0:T(1,128)S(1)}, u32[]{:S(2)}, u32[]{:S(2)}) %all-to-all-start) | async-done | bytes 114720 | tf_op jit(solution)/shard_map/all_to_all | solution.py:510
  650.0 4.5 reshape.362
  666.2 6.8 collective-permute-done.68
  683.1 3.8 maximum_select_fusion.1
  (496 shorter events, 239.8 us)
Async XLA Ops:
  5.6 7.0 %collective-permute-start.3 = (bf16[128,512]{1,0:T(8,128)(2,1)S(1)}, bf16[128,512]{1,0:T(8,128)(2,1)S(1)}, u32[]{:S(2)}, u32[]{:S(2)}) collective-permute-start(bf16[128,512]{1,0:T(8,128)(2,1)S(1)} %get-tuple-element.394), channel_id=1, source_target_pairs={{0,2},{2,0},{4,6},{6,4},{8,10},{10,8},{12,14},{14,12},{16,18},{18,... | collective-permute-start | bytes 393224 | tf_op jit(solution)/shard_map/ppermute | solution.py:76
  8.3 27.2 %collective-permute-start.2 = (bf16[256,1536]{0,1:T(8,128)(2,1)S(1)}, bf16[256,1536]{0,1:T(8,128)(2,1)}, u32[]{:S(2)}, u32[]{:S(2)}) collective-permute-start(bf16[256,1536]{0,1:T(8,128)(2,1)S(1)} %get-tuple-element.160), channel_id=1, source_target_pairs={{0,4},{2,6},{4,0},{6,2},{8,12},{10,14},{12,8},{14,10},{16,20},{18,... | collective-permute-start | bytes 2359304 | tf_op jit(solution)/shard_map/ppermute | solution.py:64
  11.0 24.5 %collective-permute-start.1 = (bf16[256,1536]{0,1:T(8,128)(2,1)S(1)}, bf16[256,1536]{0,1:T(8,128)(2,1)}, u32[]{:S(2)}, u32[]{:S(2)}) collective-permute-start(bf16[256,1536]{0,1:T(8,128)(2,1)S(1)} %get-tuple-element.160), channel_id=1, source_target_pairs={{0,8},{2,10},{4,12},{6,14},{8,16},{10,18},{12,20},{14,22},{16,24},... | collective-permute-start | bytes 2359304 | tf_op jit(solution)/shard_map/ppermute | solution.py:64
  13.3 21.3 %collective-permute-start.4 = (bf16[256,512]{1,0:T(8,128)(2,1)S(1)}, bf16[256,512]{1,0:T(8,128)(2,1)S(1)}, u32[]{:S(2)}, u32[]{:S(2)}) collective-permute-start(bf16[256,512]{1,0:T(8,128)(2,1)S(1)} %get-tuple-element.343), channel_id=1, source_target_pairs={{0,4},{2,6},{4,0},{6,2},{8,12},{10,14},{12,8},{14,10},{16,20},{18,... | collective-permute-start | bytes 786440 | tf_op jit(solution)/shard_map/ppermute | solution.py:64
  35.5 22.1 %collective-permute-start.5 = (bf16[256,1536]{0,1:T(8,128)(2,1)S(1)}, bf16[256,1536]{0,1:T(8,128)(2,1)}, u32[]{:S(2)}, u32[]{:S(2)}) collective-permute-start(bf16[256,1536]{0,1:T(8,128)(2,1)S(1)} %get-tuple-element.160), channel_id=1, source_target_pairs={{0,24},{2,26},{4,28},{6,30},{8,0},{10,2},{12,4},{14,6},{16,8},{18,... | collective-permute-start | bytes 2359304 | tf_op jit(solution)/shard_map/ppermute | solution.py:64
  39.3 19.0 %collective-permute-start.6 = (bf16[256,1536]{0,1:T(8,128)(2,1)}, bf16[256,1536]{0,1:T(8,128)(2,1)}, u32[]{:S(2)}, u32[]{:S(2)}) collective-permute-start(bf16[256,1536]{0,1:T(8,128)(2,1)} %collective-permute-done.1), channel_id=1, source_target_pairs={{0,4},{2,6},{4,0},{6,2},{8,12},{10,14},{12,8},{14,10},{16,20},{18,... | collective-permute-start | bytes 2359304 | tf_op jit(solution)/shard_map/ppermute | solution.py:64
  58.4 19.8 %collective-permute-start.9 = (bf16[256,1536]{0,1:T(8,128)(2,1)}, bf16[256,1536]{0,1:T(8,128)(2,1)S(1)}, u32[]{:S(2)}, u32[]{:S(2)}) collective-permute-start(bf16[256,1536]{0,1:T(8,128)(2,1)} %collective-permute-done.1), channel_id=1, source_target_pairs={{0,8},{2,10},{4,12},{6,14},{8,16},{10,18},{12,20},{14,22},{16,24},... | collective-permute-start | bytes 2359304 | tf_op jit(solution)/shard_map/ppermute | solution.py:64
  58.4 27.8 %collective-permute-start.10 = (bf16[256,1536]{0,1:T(8,128)(2,1)}, bf16[256,1536]{0,1:T(8,128)(2,1)S(1)}, u32[]{:S(2)}, u32[]{:S(2)}) collective-permute-start(bf16[256,1536]{0,1:T(8,128)(2,1)} %collective-permute-done.5), channel_id=1, source_target_pairs={{0,4},{2,6},{4,0},{6,2},{8,12},{10,14},{12,8},{14,10},{16,20},{18,... | collective-permute-start | bytes 2359304 | tf_op jit(solution)/shard_map/ppermute | solution.py:64
  60.0 25.5 %collective-permute-start.7 = (bf16[512,2048]{1,0:T(8,128)(2,1)S(1)}, bf16[512,2048]{1,0:T(8,128)(2,1)S(1)}, u32[]{:S(2)}, u32[]{:S(2)}) collective-permute-start(bf16[512,2048]{1,0:T(8,128)(2,1)S(1)} %fusion.15), channel_id=1, source_target_pairs={{0,2},{2,0},{4,6},{6,4},{8,10},{10,8},{12,14},{14,12},{16,18},{18,... | collective-permute-start | bytes 6291464 | tf_op jit(solution)/shard_map/ppermute | solution.py:76
  86.2 13.4 %collective-permute-start.11 = (bf16[2,256,512]{2,1,0:T(8,128)(2,1)}, bf16[2,256,512]{2,1,0:T(8,128)(2,1)}, u32[]{:S(2)}, u32[]{:S(2)}) collective-permute-start(bf16[2,256,512]{2,1,0:T(8,128)(2,1)} %pad_maximum_fusion.6), channel_id=1, source_target_pairs={{0,8},{2,10},{4,12},{6,14},{8,16},{10,18},{12,20},{14,22},{16,24},... | collective-permute-start | bytes 1572872 | tf_op jit(solution)/shard_map/ppermute | solution.py:64
  86.3 16.9 %collective-permute-start.12 = (bf16[256,1536]{0,1:T(8,128)(2,1)S(1)}, bf16[256,1536]{0,1:T(8,128)(2,1)S(1)}, u32[]{:S(2)}, u32[]{:S(2)}) collective-permute-start(bf16[256,1536]{0,1:T(8,128)(2,1)S(1)} %collective-permute-done.9), channel_id=1, source_target_pairs={{0,4},{2,6},{4,0},{6,2},{8,12},{10,14},{12,8},{14,10},{16,20},{18,... | collective-permute-start | bytes 2359304 | tf_op jit(solution)/shard_map/ppermute | solution.py:64
  87.9 13.4 %collective-permute-start.13 = (bf16[128,2048]{1,0:T(8,128)(2,1)S(1)}, bf16[128,2048]{1,0:T(8,128)(2,1)S(1)}, u32[]{:S(2)}, u32[]{:S(2)}) collective-permute-start(bf16[128,2048]{1,0:T(8,128)(2,1)S(1)} %get-tuple-element.386), channel_id=1, source_target_pairs={{0,2},{2,0},{4,6},{6,4},{8,10},{10,8},{12,14},{14,12},{16,18},{18,... | collective-permute-start | bytes 1572872 | tf_op jit(solution)/shard_map/ppermute | solution.py:76
  103.2 26.6 %collective-permute-start.14 = (bf16[2,256,512]{2,1,0:T(8,128)(2,1)}, bf16[2,256,512]{2,1,0:T(8,128)(2,1)S(1)}, u32[]{:S(2)}, u32[]{:S(2)}) collective-permute-start(bf16[2,256,512]{2,1,0:T(8,128)(2,1)} %pad_maximum_fusion.6), channel_id=1, source_target_pairs={{0,24},{2,26},{4,28},{6,30},{8,0},{10,2},{12,4},{14,6},{16,8},{18,... | collective-permute-start | bytes 1572872 | tf_op jit(solution)/shard_map/ppermute | solution.py:64
  106.7 21.1 %collective-permute-start.15 = (bf16[2,256,512]{2,1,0:T(8,128)(2,1)}, bf16[2,256,512]{2,1,0:T(8,128)(2,1)}, u32[]{:S(2)}, u32[]{:S(2)}) collective-permute-start(bf16[2,256,512]{2,1,0:T(8,128)(2,1)} %collective-permute-done.11), channel_id=1, source_target_pairs={{0,8},{2,10},{4,12},{6,14},{8,16},{10,18},{12,20},{14,22},{16,24},... | collective-permute-start | bytes 1572872 | tf_op jit(solution)/shard_map/ppermute | solution.py:64
  106.9 28.4 %collective-permute-start.16 = (bf16[256,2048]{1,0:T(8,128)(2,1)}, bf16[256,2048]{1,0:T(8,128)(2,1)}, u32[]{:S(2)}, u32[]{:S(2)}) collective-permute-start(bf16[256,2048]{1,0:T(8,128)(2,1)} %get-tuple-element.186), channel_id=1, source_target_pairs={{0,4},{2,6},{4,0},{6,2},{8,12},{10,14},{12,8},{14,10},{16,20},{18,... | collective-permute-start | bytes 3145736 | tf_op jit(solution)/shard_map/ppermute | solution.py:64
  135.3 22.8 %collective-permute-start.19 = (bf16[256,2048]{1,0:T(8,128)(2,1)}, bf16[256,2048]{1,0:T(8,128)(2,1)}, u32[]{:S(2)}, u32[]{:S(2)}) collective-permute-start(bf16[256,2048]{1,0:T(8,128)(2,1)} %get-tuple-element.186), channel_id=1, source_target_pairs={{0,8},{2,10},{4,12},{6,14},{8,16},{10,18},{12,20},{14,22},{16,24},... | collective-permute-start | bytes 3145736 | tf_op jit(solution)/shard_map/ppermute | solution.py:64
  135.5 29.8 %collective-permute-start.20 = (bf16[256,2048]{1,0:T(8,128)(2,1)}, bf16[256,2048]{1,0:T(8,128)(2,1)}, u32[]{:S(2)}, u32[]{:S(2)}) collective-permute-start(bf16[256,2048]{1,0:T(8,128)(2,1)} %get-tuple-element.201), channel_id=1, source_target_pairs={{0,4},{2,6},{4,0},{6,2},{8,12},{10,14},{12,8},{14,10},{16,20},{18,... | collective-permute-start | bytes 3145736 | tf_op jit(solution)/shard_map/ppermute | solution.py:64
  142.2 18.3 %collective-permute-start.17 = (bf16[512,2048]{1,0:T(8,128)(2,1)}, bf16[512,2048]{1,0:T(8,128)(2,1)}, u32[]{:S(2)}, u32[]{:S(2)}) collective-permute-start(bf16[512,2048]{1,0:T(8,128)(2,1)} %convolution_convert_fusion.10), channel_id=1, source_target_pairs={{0,2},{2,0},{4,6},{6,4},{8,10},{10,8},{12,14},{14,12},{16,18},{18,... | collective-permute-start | bytes 6291464 | tf_op jit(solution)/shard_map/ppermute | solution.py:76
  165.3 20.9 %collective-permute-start.21 = (bf16[256,2048]{1,0:T(8,128)(2,1)}, bf16[256,2048]{1,0:T(8,128)(2,1)S(1)}, u32[]{:S(2)}, u32[]{:S(2)}) collective-permute-start(bf16[256,2048]{1,0:T(8,128)(2,1)} %get-tuple-element.186), channel_id=1, source_target_pairs={{0,24},{2,26},{4,28},{6,30},{8,0},{10,2},{12,4},{14,6},{16,8},{18,... | collective-permute-start | bytes 3145736 | tf_op jit(solution)/shard_map/ppermute | solution.py:64
  167.0 21.5 %collective-permute-start.22 = (bf16[256,2048]{1,0:T(8,128)(2,1)}, bf16[256,2048]{1,0:T(8,128)(2,1)S(1)}, u32[]{:S(2)}, u32[]{:S(2)}) collective-permute-start(bf16[256,2048]{1,0:T(8,128)(2,1)} %collective-permute-done.19), channel_id=1, source_target_pairs={{0,4},{2,6},{4,0},{6,2},{8,12},{10,14},{12,8},{14,10},{16,20},{18,... | collective-permute-start | bytes 3145736 | tf_op jit(solution)/shard_map/ppermute | solution.py:64
  174.4 43.4 %collective-permute-start.18 = (bf16[512,2048]{1,0:T(8,128)(2,1)}, bf16[512,2048]{1,0:T(8,128)(2,1)S(1)}, u32[]{:S(2)}, u32[]{:S(2)}) collective-permute-start(bf16[512,2048]{1,0:T(8,128)(2,1)} %add_convert_fusion.3), channel_id=1, source_target_pairs={{0,1},{1,0},{2,3},{3,2},{4,5},{5,4},{6,7},{7,6},{8,9},{9,8},{10,11... | collective-permute-start | bytes 6291464 | tf_op jit(solution)/shard_map/ppermute | solution.py:81
  189.5 18.7 %collective-permute-start.24 = (bf16[256,2048]{1,0:T(8,128)(2,1)}, bf16[256,2048]{1,0:T(8,128)(2,1)}, u32[]{:S(2)}, u32[]{:S(2)}) collective-permute-start(bf16[256,2048]{1,0:T(8,128)(2,1)} %collective-permute-done.19), channel_id=1, source_target_pairs={{0,8},{2,10},{4,12},{6,14},{8,16},{10,18},{12,20},{14,22},{16,24},... | collective-permute-start | bytes 3145736 | tf_op jit(solution)/shard_map/ppermute | solution.py:64
  190.5 34.5 %collective-permute-start.25 = (bf16[256,2048]{1,0:T(8,128)(2,1)S(1)}, bf16[256,2048]{1,0:T(8,128)(2,1)S(1)}, u32[]{:S(2)}, u32[]{:S(2)}) collective-permute-start(bf16[256,2048]{1,0:T(8,128)(2,1)S(1)} %collective-permute-done.21), channel_id=1, source_target_pairs={{0,4},{2,6},{4,0},{6,2},{8,12},{10,14},{12,8},{14,10},{16,20},{18,... | collective-permute-start | bytes 3145736 | tf_op jit(solution)/shard_map/ppermute | solution.py:64
  191.3 23.8 %collective-permute-start.23 = (bf16[512,2048]{1,0:T(8,128)(2,1)S(1)}, bf16[512,2048]{1,0:T(8,128)(2,1)S(1)}, u32[]{:S(2)}, u32[]{:S(2)}) collective-permute-start(bf16[512,2048]{1,0:T(8,128)(2,1)S(1)} %fusion.16), channel_id=1, source_target_pairs={{0,2},{2,0},{4,6},{6,4},{8,10},{10,8},{12,14},{14,12},{16,18},{18,... | collective-permute-start | bytes 6291464 | tf_op jit(solution)/shard_map/ppermute | solution.py:76
  225.0 22.7 %collective-permute-start.27 = (bf16[256,2048]{1,0:T(8,128)(2,1)}, bf16[256,2048]{1,0:T(8,128)(2,1)S(1)}, u32[]{:S(2)}, u32[]{:S(2)}) collective-permute-start(bf16[256,2048]{1,0:T(8,128)(2,1)} %get-tuple-element.201), channel_id=1, source_target_pairs={{0,8},{2,10},{4,12},{6,14},{8,16},{10,18},{12,20},{14,22},{16,24},... | collective-permute-start | bytes 3145736 | tf_op jit(solution)/shard_map/ppermute | solution.py:64
  226.1 18.3 %collective-permute-start.28 = (bf16[256,2048]{1,0:T(8,128)(2,1)}, bf16[256,2048]{1,0:T(8,128)(2,1)}, u32[]{:S(2)}, u32[]{:S(2)}) collective-permute-start(bf16[256,2048]{1,0:T(8,128)(2,1)} %collective-permute-done.24), channel_id=1, source_target_pairs={{0,4},{2,6},{4,0},{6,2},{8,12},{10,14},{12,8},{14,10},{16,20},{18,... | collective-permute-start | bytes 3145736 | tf_op jit(solution)/shard_map/ppermute | solution.py:64
  227.5 21.3 %collective-permute-start.26 = (bf16[512,2048]{1,0:T(8,128)(2,1)}, bf16[512,2048]{1,0:T(8,128)(2,1)}, u32[]{:S(2)}, u32[]{:S(2)}) collective-permute-start(bf16[512,2048]{1,0:T(8,128)(2,1)} %fusion.21), channel_id=1, source_target_pairs={{0,2},{2,0},{4,6},{6,4},{8,10},{10,8},{12,14},{14,12},{16,18},{18,... | collective-permute-start | bytes 6291464 | tf_op jit(solution)/shard_map/ppermute | solution.py:76
  251.4 22.2 %collective-permute-start.29 = (bf16[256,2048]{1,0:T(8,128)(2,1)}, bf16[256,2048]{1,0:T(8,128)(2,1)S(1)}, u32[]{:S(2)}, u32[]{:S(2)}) collective-permute-start(bf16[256,2048]{1,0:T(8,128)(2,1)} %get-tuple-element.201), channel_id=1, source_target_pairs={{0,24},{2,26},{4,28},{6,30},{8,0},{10,2},{12,4},{14,6},{16,8},{18,... | collective-permute-start | bytes 3145736 | tf_op jit(solution)/shard_map/ppermute | solution.py:64
  253.5 20.0 %collective-permute-start.30 = (bf16[256,2048]{1,0:T(8,128)(2,1)S(1)}, bf16[256,2048]{1,0:T(8,128)(2,1)S(1)}, u32[]{:S(2)}, u32[]{:S(2)}) collective-permute-start(bf16[256,2048]{1,0:T(8,128)(2,1)S(1)} %collective-permute-done.27), channel_id=1, source_target_pairs={{0,4},{2,6},{4,0},{6,2},{8,12},{10,14},{12,8},{14,10},{16,20},{18,... | collective-permute-start | bytes 3145736 | tf_op jit(solution)/shard_map/ppermute | solution.py:64
  273.5 33.8 %collective-permute-start.31 = (bf16[256,2048]{1,0:T(8,128)(2,1)S(1)}, bf16[256,2048]{1,0:T(8,128)(2,1)S(1)}, u32[]{:S(2)}, u32[]{:S(2)}) collective-permute-start(bf16[256,2048]{1,0:T(8,128)(2,1)S(1)} %collective-permute-done.27), channel_id=1, source_target_pairs={{0,8},{2,10},{4,12},{6,14},{8,16},{10,18},{12,20},{14,22},{16,24},... | collective-permute-start | bytes 3145736 | tf_op jit(solution)/shard_map/ppermute | solution.py:64
  293.2 16.3 %collective-permute-start.32 = (bf16[256,2048]{1,0:T(8,128)(2,1)S(1)}, bf16[256,2048]{1,0:T(8,128)(2,1)S(1)}, u32[]{:S(2)}, u32[]{:S(2)}) collective-permute-start(bf16[256,2048]{1,0:T(8,128)(2,1)S(1)} %collective-permute-done.29), channel_id=1, source_target_pairs={{0,4},{2,6},{4,0},{6,2},{8,12},{10,14},{12,8},{14,10},{16,20},{18,... | collective-permute-start | bytes 3145736 | tf_op jit(solution)/shard_map/ppermute | solution.py:64
  309.5 24.9 %collective-permute-start.33 = (bf16[256,2048]{1,0:T(8,128)(2,1)S(1)}, bf16[256,2048]{1,0:T(8,128)(2,1)S(1)}, u32[]{:S(2)}, u32[]{:S(2)}) collective-permute-start(bf16[256,2048]{1,0:T(8,128)(2,1)S(1)} %collective-permute-done.31), channel_id=1, source_target_pairs={{0,4},{2,6},{4,0},{6,2},{8,12},{10,14},{12,8},{14,10},{16,20},{18,... | collective-permute-start | bytes 3145736 | tf_op jit(solution)/shard_map/ppermute | solution.py:64
  310.9 25.0 %collective-permute-start.34 = (bf16[2,256,1024]{2,1,0:T(8,128)(2,1)S(1)}, bf16[2,256,1024]{2,1,0:T(8,128)(2,1)S(1)}, u32[]{:S(2)}, u32[]{:S(2)}) collective-permute-start(bf16[2,256,1024]{2,1,0:T(8,128)(2,1)S(1)} %get-tuple-element.211), channel_id=1, source_target_pairs={{0,24},{2,26},{4,28},{6,30},{8,0},{10,2},{12,4},{14,6},{16,8},{18,... | collective-permute-start | bytes 3145736 | tf_op jit(solution)/shard_map/ppermute | solution.py:64
  335.9 32.6 %collective-permute-start.35 = (bf16[512,1024]{1,0:T(8,128)(2,1)S(1)}, bf16[512,1024]{1,0:T(8,128)(2,1)S(1)}, u32[]{:S(2)}, u32[]{:S(2)}) collective-permute-start(bf16[512,1024]{1,0:T(8,128)(2,1)S(1)} %get-tuple-element.213), channel_id=1, source_target_pairs={{0,4},{2,6},{4,0},{6,2},{8,12},{10,14},{12,8},{14,10},{16,20},{18,... | collective-permute-start | bytes 3145736 | tf_op jit(solution)/shard_map/ppermute | solution.py:64
  337.2 31.3 %collective-permute-start.36 = (bf16[2,256,1024]{2,1,0:T(8,128)(2,1)S(1)}, bf16[2,256,1024]{2,1,0:T(8,128)(2,1)}, u32[]{:S(2)}, u32[]{:S(2)}) collective-permute-start(bf16[2,256,1024]{2,1,0:T(8,128)(2,1)S(1)} %get-tuple-element.214), channel_id=1, source_target_pairs={{0,8},{2,10},{4,12},{6,14},{8,16},{10,18},{12,20},{14,22},{16,24},... | collective-permute-start | bytes 3145736 | tf_op jit(solution)/shard_map/ppermute | solution.py:64
  368.9 19.9 %collective-permute-start.37 = (bf16[512,1024]{1,0:T(8,128)(2,1)}, bf16[512,1024]{1,0:T(8,128)(2,1)S(1)}, u32[]{:S(2)}, u32[]{:S(2)}) collective-permute-start(bf16[512,1024]{1,0:T(8,128)(2,1)} %get-tuple-element.218), channel_id=1, source_target_pairs={{0,4},{2,6},{4,0},{6,2},{8,12},{10,14},{12,8},{14,10},{16,20},{18,... | collective-permute-start | bytes 3145736 | tf_op jit(solution)/shard_map/ppermute | solution.py:64
  371.0 15.0 %collective-permute-start.38 = (bf16[2,256,1024]{2,1,0:T(8,128)(2,1)S(1)}, bf16[2,256,1024]{2,1,0:T(8,128)(2,1)S(1)}, u32[]{:S(2)}, u32[]{:S(2)}) collective-permute-start(bf16[2,256,1024]{2,1,0:T(8,128)(2,1)S(1)} %add_convert_fusion.7), channel_id=1, source_target_pairs={{0,24},{2,26},{4,28},{6,30},{8,0},{10,2},{12,4},{14,6},{16,8},{18,... | collective-permute-start | bytes 3145736 | tf_op jit(solution)/shard_map/ppermute | solution.py:64
  373.3 16.4 %collective-permute-start.39 = (bf16[512,2048]{1,0:T(8,128)(2,1)S(1)}, bf16[512,2048]{1,0:T(8,128)(2,1)}, u32[]{:S(2)}, u32[]{:S(2)}) collective-permute-start(bf16[512,2048]{1,0:T(8,128)(2,1)S(1)} %copy-done.96), channel_id=1, source_target_pairs={{0,2},{2,0},{4,6},{6,4},{8,10},{10,8},{12,14},{14,12},{16,18},{18,... | collective-permute-start | bytes 6291464 | tf_op jit(solution)/shard_map/ppermute | solution.py:76
  398.6 24.3 %collective-permute-start.41 = (bf16[256,1024]{1,0:T(8,128)(2,1)S(1)}, bf16[256,1024]{1,0:T(8,128)(2,1)S(1)}, u32[]{:S(2)}, u32[]{:S(2)}) collective-permute-start(bf16[256,1024]{1,0:T(8,128)(2,1)S(1)} %get-tuple-element.227), channel_id=1, source_target_pairs={{0,24},{2,26},{4,28},{6,30},{8,0},{10,2},{12,4},{14,6},{16,8},{18,... | collective-permute-start | bytes 1572872 | tf_op jit(solution)/shard_map/ppermute | solution.py:64
  402.6 20.3 %collective-permute-start.42 = (bf16[256,1024]{1,0:T(8,128)(2,1)S(1)}, bf16[256,1024]{1,0:T(8,128)(2,1)S(1)}, u32[]{:S(2)}, u32[]{:S(2)}) collective-permute-start(bf16[256,1024]{1,0:T(8,128)(2,1)S(1)} %get-tuple-element.229), channel_id=1, source_target_pairs={{0,8},{2,10},{4,12},{6,14},{8,16},{10,18},{12,20},{14,22},{16,24},... | collective-permute-start | bytes 1572872 | tf_op jit(solution)/shard_map/ppermute | solution.py:64
  402.9 40.3 %collective-permute-start.47 = (bf16[512,2048]{1,0:T(8,128)(2,1)S(1)}, bf16[512,2048]{1,0:T(8,128)(2,1)S(1)}, u32[]{:S(2)}, u32[]{:S(2)}) collective-permute-start(bf16[512,2048]{1,0:T(8,128)(2,1)S(1)} %add_convert_fusion.2), channel_id=1, source_target_pairs={{0,1},{1,0},{2,3},{3,2},{4,5},{5,4},{6,7},{7,6},{8,9},{9,8},{10,11... | collective-permute-start | bytes 6291464 | tf_op jit(solution)/shard_map/ppermute | solution.py:81
  404.3 18.6 %collective-permute-start.40 = (bf16[256,2048]{1,0:T(8,128)(2,1)}, bf16[256,2048]{1,0:T(8,128)(2,1)S(1)}, u32[]{:S(2)}, u32[]{:S(2)}) collective-permute-start(bf16[256,2048]{1,0:T(8,128)(2,1)} %get-tuple-element.225), channel_id=1, source_target_pairs={{0,4},{2,6},{4,0},{6,2},{8,12},{10,14},{12,8},{14,10},{16,20},{18,... | collective-permute-start | bytes 3145736 | tf_op jit(solution)/shard_map/ppermute | solution.py:64
  424.1 33.3 %collective-permute-start.46 = (bf16[256,2048]{1,0:T(8,128)(2,1)S(1)}, bf16[256,2048]{1,0:T(8,128)(2,1)}, u32[]{:S(2)}, u32[]{:S(2)}) collective-permute-start(bf16[256,2048]{1,0:T(8,128)(2,1)S(1)} %add_convert_fusion.6), channel_id=1, source_target_pairs={{0,24},{2,26},{4,28},{6,30},{8,0},{10,2},{12,4},{14,6},{16,8},{18,... | collective-permute-start | bytes 3145736 | tf_op jit(solution)/shard_map/ppermute | solution.py:64
  428.2 29.2 %collective-permute-start.45 = (bf16[256,2048]{1,0:T(8,128)(2,1)}, bf16[256,2048]{1,0:T(8,128)(2,1)S(1)}, u32[]{:S(2)}, u32[]{:S(2)}) collective-permute-start(bf16[256,2048]{1,0:T(8,128)(2,1)} %get-tuple-element.233), channel_id=1, source_target_pairs={{0,4},{2,6},{4,0},{6,2},{8,12},{10,14},{12,8},{14,10},{16,20},{18,... | collective-permute-start | bytes 3145736 | tf_op jit(solution)/shard_map/ppermute | solution.py:64
  445.6 84.9 %collective-permute-start.44 = (bf16[512,2048]{1,0:T(8,128)(2,1)}, bf16[512,2048]{1,0:T(8,128)(2,1)}, u32[]{:S(2)}, u32[]{:S(2)}) collective-permute-start(bf16[512,2048]{1,0:T(8,128)(2,1)} %add_convert_fusion.1), channel_id=1, source_target_pairs={{0,1},{1,0},{2,3},{3,2},{4,5},{5,4},{6,7},{7,6},{8,9},{9,8},{10,11... | collective-permute-start | bytes 6291464 | tf_op jit(solution)/shard_map/ppermute | solution.py:81
  460.8 30.8 %collective-permute-start.49 = (bf16[256,2048]{1,0:T(8,128)(2,1)}, bf16[256,2048]{1,0:T(8,128)(2,1)}, u32[]{:S(2)}, u32[]{:S(2)}) collective-permute-start(bf16[256,2048]{1,0:T(8,128)(2,1)} %add_convert_fusion.5), channel_id=1, source_target_pairs={{0,8},{2,10},{4,12},{6,14},{8,16},{10,18},{12,20},{14,22},{16,24},... | collective-permute-start | bytes 3145736 | tf_op jit(solution)/shard_map/ppermute | solution.py:64
  461.6 30.0 %collective-permute-start.48 = (bf16[256,2048]{1,0:T(8,128)(2,1)}, bf16[256,2048]{1,0:T(8,128)(2,1)}, u32[]{:S(2)}, u32[]{:S(2)}) collective-permute-start(bf16[256,2048]{1,0:T(8,128)(2,1)} %get-tuple-element.240), channel_id=1, source_target_pairs={{0,4},{2,6},{4,0},{6,2},{8,12},{10,14},{12,8},{14,10},{16,20},{18,... | collective-permute-start | bytes 3145736 | tf_op jit(solution)/shard_map/ppermute | solution.py:64
  494.5 27.1 %collective-permute-start.51 = (bf16[256,2048]{1,0:T(8,128)(2,1)S(1)}, bf16[256,2048]{1,0:T(8,128)(2,1)S(1)}, u32[]{:S(2)}, u32[]{:S(2)}) collective-permute-start(bf16[256,2048]{1,0:T(8,128)(2,1)S(1)} %copy-done.52), channel_id=1, source_target_pairs={{0,4},{2,6},{4,0},{6,2},{8,12},{10,14},{12,8},{14,10},{16,20},{18,... | collective-permute-start | bytes 3145736 | tf_op jit(solution)/shard_map/ppermute | solution.py:64
  495.1 26.5 %collective-permute-start.52 = (bf16[256,2048]{1,0:T(8,128)(2,1)S(1)}, bf16[256,2048]{1,0:T(8,128)(2,1)S(1)}, u32[]{:S(2)}, u32[]{:S(2)}) collective-permute-start(bf16[256,2048]{1,0:T(8,128)(2,1)S(1)} %add_convert_fusion.4), channel_id=1, source_target_pairs={{0,24},{2,26},{4,28},{6,30},{8,0},{10,2},{12,4},{14,6},{16,8},{18,... | collective-permute-start | bytes 3145736 | tf_op jit(solution)/shard_map/ppermute | solution.py:64
  511.2 63.2 %collective-permute-start.54 = (bf16[512,2048]{1,0:T(8,128)(2,1)}, bf16[512,2048]{1,0:T(8,128)(2,1)}, u32[]{:S(2)}, u32[]{:S(2)}) collective-permute-start(bf16[512,2048]{1,0:T(8,128)(2,1)} %add_convert_fusion), channel_id=1, source_target_pairs={{0,1},{1,0},{2,3},{3,2},{4,5},{5,4},{6,7},{7,6},{8,9},{9,8},{10,11... | collective-permute-start | bytes 6291464 | tf_op jit(solution)/shard_map/ppermute | solution.py:81
  525.3 25.9 %collective-permute-start.56 = (bf16[256,1024]{1,0:T(8,128)(2,1)}, bf16[256,1024]{1,0:T(8,128)(2,1)S(1)}, u32[]{:S(2)}, u32[]{:S(2)}) collective-permute-start(bf16[256,1024]{1,0:T(8,128)(2,1)} %add_convert_fusion.11), channel_id=1, source_target_pairs={{0,24},{2,26},{4,28},{6,30},{8,0},{10,2},{12,4},{14,6},{16,8},{18,... | collective-permute-start | bytes 1572872 | tf_op jit(solution)/shard_map/ppermute | solution.py:64
  529.0 24.0 %collective-permute-start.55 = (bf16[1024,512]{1,0:T(8,128)(2,1)}, bf16[1024,512]{1,0:T(8,128)(2,1)S(1)}, u32[]{:S(2)}, u32[]{:S(2)}) collective-permute-start(bf16[1024,512]{1,0:T(8,128)(2,1)} %fusion.43), channel_id=1, source_target_pairs={{0,4},{2,6},{4,0},{6,2},{8,12},{10,14},{12,8},{14,10},{16,20},{18,... | collective-permute-start | bytes 3145736 | tf_op jit(solution)/shard_map/ppermute | solution.py:64
  553.2 11.8 %collective-permute-start.58 = (bf16[256,512]{1,0:T(8,128)(2,1)S(1)}, bf16[256,512]{1,0:T(8,128)(2,1)S(1)}, u32[]{:S(2)}, u32[]{:S(2)}) collective-permute-start(bf16[256,512]{1,0:T(8,128)(2,1)S(1)} %get-tuple-element.266), channel_id=1, source_target_pairs={{0,24},{2,26},{4,28},{6,30},{8,0},{10,2},{12,4},{14,6},{16,8},{18,... | collective-permute-start | bytes 786440 | tf_op jit(solution)/shard_map/ppermute | solution.py:64
  553.6 11.4 %collective-permute-start.59 = (bf16[256,512]{1,0:T(8,128)(2,1)S(1)}, bf16[256,512]{1,0:T(8,128)(2,1)S(1)}, u32[]{:S(2)}, u32[]{:S(2)}) collective-permute-start(bf16[256,512]{1,0:T(8,128)(2,1)S(1)} %get-tuple-element.268), channel_id=1, source_target_pairs={{0,8},{2,10},{4,12},{6,14},{8,16},{10,18},{12,20},{14,22},{16,24},... | collective-permute-start | bytes 786440 | tf_op jit(solution)/shard_map/ppermute | solution.py:64
  555.3 16.8 %collective-permute-start.57 = (bf16[256,1536]{1,0:T(8,128)(2,1)S(1)}, bf16[256,1536]{1,0:T(8,128)(2,1)S(1)}, u32[]{:S(2)}, u32[]{:S(2)}) collective-permute-start(bf16[256,1536]{1,0:T(8,128)(2,1)S(1)} %get-tuple-element.264), channel_id=1, source_target_pairs={{0,4},{2,6},{4,0},{6,2},{8,12},{10,14},{12,8},{14,10},{16,20},{18,... | collective-permute-start | bytes 2359304 | tf_op jit(solution)/shard_map/ppermute | solution.py:64
  577.8 26.6 %collective-permute-start.62 = (bf16[256,1536]{1,0:T(8,128)(2,1)}, bf16[256,1536]{1,0:T(8,128)(2,1)}, u32[]{:S(2)}, u32[]{:S(2)}) collective-permute-start(bf16[256,1536]{1,0:T(8,128)(2,1)} %add_convert_fusion.10), channel_id=1, source_target_pairs={{0,24},{2,26},{4,28},{6,30},{8,0},{10,2},{12,4},{14,6},{16,8},{18,... | collective-permute-start | bytes 2359304 | tf_op jit(solution)/shard_map/ppermute | solution.py:64
  580.4 24.1 %collective-permute-start.61 = (bf16[256,1536]{1,0:T(8,128)(2,1)S(1)}, bf16[256,1536]{1,0:T(8,128)(2,1)}, u32[]{:S(2)}, u32[]{:S(2)}) collective-permute-start(bf16[256,1536]{1,0:T(8,128)(2,1)S(1)} %copy-done.54), channel_id=1, source_target_pairs={{0,4},{2,6},{4,0},{6,2},{8,12},{10,14},{12,8},{14,10},{16,20},{18,... | collective-permute-start | bytes 2359304 | tf_op jit(solution)/shard_map/ppermute | solution.py:64
  606.9 18.0 %collective-permute-start.64 = (bf16[256,1536]{1,0:T(8,128)(2,1)}, bf16[256,1536]{1,0:T(8,128)(2,1)}, u32[]{:S(2)}, u32[]{:S(2)}) collective-permute-start(bf16[256,1536]{1,0:T(8,128)(2,1)} %add_convert_fusion.9), channel_id=1, source_target_pairs={{0,8},{2,10},{4,12},{6,14},{8,16},{10,18},{12,20},{14,22},{16,24},... | collective-permute-start | bytes 2359304 | tf_op jit(solution)/shard_map/ppermute | solution.py:64
  607.2 17.7 %collective-permute-start.63 = (bf16[256,1536]{1,0:T(8,128)(2,1)}, bf16[256,1536]{1,0:T(8,128)(2,1)}, u32[]{:S(2)}, u32[]{:S(2)}) collective-permute-start(bf16[256,1536]{1,0:T(8,128)(2,1)} %get-tuple-element.279), channel_id=1, source_target_pairs={{0,4},{2,6},{4,0},{6,2},{8,12},{10,14},{12,8},{14,10},{16,20},{18,... | collective-permute-start | bytes 2359304 | tf_op jit(solution)/shard_map/ppermute | solution.py:64
  627.7 29.8 %collective-permute-start.65 = (bf16[256,1536]{1,0:T(8,128)(2,1)S(1)}, bf16[256,1536]{1,0:T(8,128)(2,1)}, u32[]{:S(2)}, u32[]{:S(2)}) collective-permute-start(bf16[256,1536]{1,0:T(8,128)(2,1)S(1)} %copy-done.53), channel_id=1, source_target_pairs={{0,4},{2,6},{4,0},{6,2},{8,12},{10,14},{12,8},{14,10},{16,20},{18,... | collective-permute-start | bytes 2359304 | tf_op jit(solution)/shard_map/ppermute | solution.py:64
  628.3 29.2 %collective-permute-start.66 = (bf16[256,1536]{1,0:T(8,128)(2,1)}, bf16[256,1536]{1,0:T(8,128)(2,1)}, u32[]{:S(2)}, u32[]{:S(2)}) collective-permute-start(bf16[256,1536]{1,0:T(8,128)(2,1)} %add_convert_fusion.8), channel_id=1, source_target_pairs={{0,24},{2,26},{4,28},{6,30},{8,0},{10,2},{12,4},{14,6},{16,8},{18,... | collective-permute-start | bytes 2359304 | tf_op jit(solution)/shard_map/ppermute | solution.py:64
  637.4 11.2 %all-to-all-start = ((f32[16,1,1792]{2,1,0:T(1,128)}), f32[16,1,1792]{2,1,0:T(1,128)S(1)}, u32[]{:S(2)}, u32[]{:S(2)}) async-start(f32[16,1,1792]{2,1,0:T(1,128)} %reshape.361), calls=%async_computation | async-start | bytes 229376 | tf_op jit(solution)/shard_map/all_to_all | solution.py:510
  658.3 7.9 %collective-permute-start.69 = (bf16[256,512]{1,0:T(8,128)(2,1)}, bf16[256,512]{1,0:T(8,128)(2,1)}, u32[]{:S(2)}, u32[]{:S(2)}) collective-permute-start(bf16[256,512]{1,0:T(8,128)(2,1)} %add_convert_fusion.14), channel_id=1, source_target_pairs={{0,24},{2,26},{4,28},{6,30},{8,0},{10,2},{12,4},{14,6},{16,8},{18,... | collective-permute-start | bytes 786440 | tf_op jit(solution)/shard_map/ppermute | solution.py:64
  658.9 14.1 %collective-permute-start.68 = (bf16[256,1024]{1,0:T(8,128)(2,1)}, bf16[256,1024]{1,0:T(8,128)(2,1)}, u32[]{:S(2)}, u32[]{:S(2)}) collective-permute-start(bf16[256,1024]{1,0:T(8,128)(2,1)} %fusion.66), channel_id=1, source_target_pairs={{0,4},{2,6},{4,0},{6,2},{8,12},{10,14},{12,8},{14,10},{16,20},{18,... | collective-permute-start | bytes 1572872 | tf_op jit(solution)/shard_map/ppermute | solution.py:64
  (111 other events, 1944.6 us)

commit v3 on v2

--- a/solution.py
+++ b/solution.py
@@ -1,3 +1,5 @@
+import functools
+
 import jax
 import jax.numpy as jnp
 from jax import lax
@@ -11,16 +13,8 @@
 F32 = jnp.float32
 BF16 = jnp.bfloat16
 CORES = 2
-
-
-def layer_norm(value):
-    centre = value - jnp.mean(value, axis=-1, keepdims=True)
-    spread = jnp.mean(centre * centre, axis=-1, keepdims=True)
-    return centre * lax.rsqrt(spread + EPS)
-
-
-def modulate(value, shift, scale):
-    return layer_norm(value) * (1.0 + scale) + shift
+TILE = 128
+CHUNK = 16
 
 
 def after(value, *earlier):
@@ -74,6 +68,11 @@
 
     def send_core(self, value):
         return lax.ppermute(value, "dp", self.ring(0, 0, 1))
+
+    def hand_over(self, value):
+        out = self.send_core(value)
+        self.results.append(out)
+        return out
 
     def across(self, part):
         out = [lax.optimization_barrier(part)]
@@ -205,6 +204,236 @@
     return out.reshape(shape)
 
 
+def dot(lhs, rhs, left, right):
+    return lax.dot_general(lhs, rhs, (((left,), (right,)), ((), ())), preferred_element_type=F32)
+
+
+def softmax(query, keys):
+    scores = dot(query, keys, 1, 1) * HEAD_DIM ** (-0.5)
+    expo = jnp.exp(scores - jnp.max(scores, axis=-1, keepdims=True))
+    return expo / jnp.sum(expo, axis=-1, keepdims=True)
+
+
+def head_cols(part, head, heads):
+    return pl.ds((part * heads + head) * HEAD_DIM, HEAD_DIM)
+
+
+def attend_kernel(heads, qkv_ref, mixed_ref):
+    for head in range(heads):
+        query, keys, values = (qkv_ref[:, head_cols(part, head, heads)] for part in range(3))
+        probs = softmax(query, keys).astype(BF16)
+        mixed = dot(probs, values, 1, 0).astype(BF16)
+        mixed_ref[:, head_cols(0, head, heads)] = mixed
+
+
+def attend_back_kernel(heads, qkv_ref, d_mixed_ref, d_qkv_ref):
+    factor = HEAD_DIM ** (-0.5)
+    for head in range(heads):
+        query, keys, values = (qkv_ref[:, head_cols(part, head, heads)] for part in range(3))
+        d_mixed = d_mixed_ref[:, head_cols(0, head, heads)]
+        probs = softmax(query, keys)
+        d_probs = dot(d_mixed, values, 1, 1)
+        d_values = dot(probs.astype(BF16), d_mixed, 0, 0)
+        delta = jnp.sum(d_probs * probs, axis=-1, keepdims=True)
+        d_scores = (probs * (d_probs - delta)).astype(BF16)
+        d_query = dot(d_scores, keys, 1, 0) * factor
+        d_keys = dot(d_scores, query, 0, 0) * factor
+        d_qkv_ref[:, head_cols(0, head, heads)] = d_query.astype(BF16)
+        d_qkv_ref[:, head_cols(1, head, heads)] = d_keys.astype(BF16)
+        d_qkv_ref[:, head_cols(2, head, heads)] = d_values.astype(BF16)
+
+
+def by_image(kernel, length, width, *operands):
+    rows = operands[0].shape[0]
+    block = lambda cols: pl.BlockSpec((length, cols), lambda image: (image, 0))
+    return pl.pallas_call(
+        kernel,
+        grid=(rows // length,),
+        in_specs=[block(operand.shape[1]) for operand in operands],
+        out_specs=block(width),
+        out_shape=jax.ShapeDtypeStruct((rows, width), BF16),
+        compiler_params=pltpu.CompilerParams(vmem_limit_bytes=32 * 1024 * 1024),
+        cost_estimate=pl.CostEstimate(
+            flops=rows * length * width * 8, bytes_accessed=rows * 8192, transcendentals=rows * 1024
+        ),
+    )(*operands)
+
+
+def normal(value):
+    centre = value - jnp.mean(value, axis=-1, keepdims=True)
+    factor = lax.rsqrt(jnp.mean(centre * centre, axis=-1, keepdims=True) + EPS)
+    return centre * factor, factor
+
+
+def normal_back(grad, unit, factor):
+    mean = jnp.mean(grad, axis=-1, keepdims=True)
+    along = jnp.mean(grad * unit, axis=-1, keepdims=True)
+    return factor * (grad - mean - unit * along)
+
+
+class Rows:
+    def __init__(self, blocks, order_ref, width):
+        self.blocks, self.order, self.width = blocks, order_ref, width
+
+    def each(self, count, body):
+        def step(index, carry):
+            body(pl.ds(pl.multiple_of(index * CHUNK, CHUNK), CHUNK))
+            return carry
+
+        lax.fori_loop(0, count // CHUNK, step, 0)
+
+    def places(self):
+        if not self.blocks:
+            return [(slice(0, self.width), slice(0, self.width))]
+        blk = self.width // self.blocks
+        return [
+            (
+                slice(k * blk, (k + 1) * blk),
+                pl.ds(pl.multiple_of(self.order[k] * blk, blk), blk),
+            )
+            for k in range(self.blocks)
+        ]
+
+
+def clear_sums(sums_ref):
+    @pl.when(pl.program_id(1) == 0)
+    def _():
+        sums_ref[...] = jnp.zeros_like(sums_ref)
+
+
+def add_sums(sums_ref, places, *terms):
+    for index, term in enumerate(terms):
+        low, high = term[:8], term[8:]
+        for here, there in places:
+            sums_ref[0, index * 8 : index * 8 + 8, there] += low[:, here] + high[:, here]
+
+
+def first_norm_kernel(blocks, order_ref, present_ref, tokens_ref, mods_ref, kept_ref, normed_ref):
+    rows = Rows(blocks, order_ref, tokens_ref.shape[1])
+    for here, there in rows.places():
+        kept_ref[:, here] = tokens_ref[:, there]
+
+    def body(some):
+        unit, _ = normal(kept_ref[some, :].astype(F32))
+        value = unit * (1.0 + mods_ref[0, 1:2, :]) + mods_ref[0, 0:1, :]
+        normed_ref[some, :] = value.astype(BF16)
+
+    rows.each(tokens_ref.shape[0], body)
+
+
+def cotangent_kernel(blocks, order_ref, present_ref, cotangent_ref, mods_ref, dy_ref, d_mlp_ref):
+    rows = Rows(blocks, order_ref, cotangent_ref.shape[1])
+    mask = present_ref[pl.program_id(0)].astype(F32)
+    for here, there in rows.places():
+        dy = cotangent_ref[:, there].astype(F32) * mask
+        dy_ref[:, here] = dy.astype(BF16)
+        d_mlp_ref[:, here] = (mods_ref[0, 5:6, here] * dy).astype(BF16)
+
+
+def second_norm_kernel(
+    blocks, order_ref, present_ref, tokens_ref, att_a, att_b, mods_ref, hidden_ref, second_ref
+):
+    rows = Rows(blocks, order_ref, tokens_ref.shape[1])
+
+    def body(some):
+        att = att_a[some, :].astype(F32) + att_b[some, :].astype(F32)
+        hidden = tokens_ref[some, :].astype(F32) + mods_ref[0, 2:3, :] * att
+        hidden_ref[some, :] = hidden
+        unit, _ = normal(hidden)
+        value = unit * (1.0 + mods_ref[0, 4:5, :]) + mods_ref[0, 3:4, :]
+        second_ref[some, :] = value.astype(BF16)
+
+    rows.each(tokens_ref.shape[0], body)
+
+
+def second_back_kernel(
+    blocks, order_ref, present_ref, hidden_ref, att_a, att_b, d_a, d_b, dy_ref, mods_ref,
+    d_hidden_ref, d_att_ref, sums_ref,
+):
+    rows = Rows(blocks, order_ref, hidden_ref.shape[1])
+    places = rows.places()
+    clear_sums(sums_ref)
+
+    def body(some):
+        grad = d_a[some, :].astype(F32) + d_b[some, :].astype(F32)
+        unit, factor = normal(hidden_ref[some, :])
+        add_sums(sums_ref, places, grad, grad * unit)
+        d_hidden = normal_back(grad * (1.0 + mods_ref[0, 4:5, :]), unit, factor)
+        d_hidden = dy_ref[some, :].astype(F32) + d_hidden
+        d_hidden_ref[some, :] = d_hidden
+        d_att_ref[some, :] = (mods_ref[0, 2:3, :] * d_hidden).astype(BF16)
+        att = att_a[some, :].astype(F32) + att_b[some, :].astype(F32)
+        add_sums(sums_ref.at[:, 16:24], places, d_hidden * att)
+
+    rows.each(hidden_ref.shape[0], body)
+
+
+def first_back_kernel(
+    blocks, order_ref, present_ref, tokens_ref, d_a, d_b, d_hidden_ref, mods_ref,
+    input_grad_ref, sums_ref,
+):
+    rows = Rows(blocks, order_ref, tokens_ref.shape[1])
+    places = rows.places()
+    clear_sums(sums_ref)
+
+    def body(some):
+        grad = d_a[some, :].astype(F32) + d_b[some, :].astype(F32)
+        unit, factor = normal(tokens_ref[some, :].astype(F32))
+        add_sums(sums_ref, places, grad, grad * unit)
+        value = normal_back(grad * (1.0 + mods_ref[0, 1:2, :]), unit, factor)
+        value = d_hidden_ref[some, :] + value
+        for here, there in places:
+            input_grad_ref[some, there] = value[:, here]
+
+    rows.each(tokens_ref.shape[0], body)
+
+
+def block_out_kernel(
+    blocks, order_ref, present_ref, hidden_ref, mlp_a, mlp_b, dy_ref, mods_ref,
+    block_out_ref, sums_ref,
+):
+    rows = Rows(blocks, order_ref, hidden_ref.shape[1])
+    places = rows.places()
+    mask = present_ref[pl.program_id(0)].astype(F32)
+    clear_sums(sums_ref)
+
+    def body(some):
+        mlp = mlp_a[some, :].astype(F32) + mlp_b[some, :].astype(F32)
+        add_sums(sums_ref, places, dy_ref[some, :].astype(F32) * mlp)
+        value = mask * (hidden_ref[some, :] + mods_ref[0, 5:6, :] * mlp)
+        for here, there in places:
+            block_out_ref[some, there] = value[:, here].astype(BF16)
+
+    rows.each(hidden_ref.shape[0], body)
+
+
+def by_rows(kernel, order, present, operands, mods, kinds, sums=0):
+    images, kinds_of_mods, width = mods.shape
+    tiles = operands[0].shape[0] // images // TILE
+    row = pl.BlockSpec((TILE, width), lambda i, t, *s: (i * tiles + t, 0))
+    whole = lambda count: pl.BlockSpec((1, count, width), lambda i, t, *s: (i, 0, 0))
+    shapes = [jax.ShapeDtypeStruct(operands[0].shape, kind) for kind in kinds]
+    specs = [row] * len(kinds)
+    if sums:
+        shapes.append(jax.ShapeDtypeStruct((images, 8 * sums, width), F32))
+        specs.append(whole(8 * sums))
+    blocks = 0 if width // order.shape[0] % 128 else order.shape[0]
+    return pl.pallas_call(
+        functools.partial(kernel, blocks),
+        grid_spec=pltpu.PrefetchScalarGridSpec(
+            num_scalar_prefetch=2,
+            grid=(images, tiles),
+            in_specs=[row] * len(operands) + [whole(kinds_of_mods)],
+            out_specs=specs,
+        ),
+        out_shape=shapes,
+        compiler_params=pltpu.CompilerParams(vmem_limit_bytes=40 * 1024 * 1024),
+        cost_estimate=pl.CostEstimate(
+            flops=operands[0].size * 6000, bytes_accessed=operands[0].size * 8, transcendentals=0
+        ),
+    )(order, present, *operands, mods)
+
+
 def matmul(lhs, rhs, turned=False):
     return lax.dot_general(
         lhs, rhs, (((1,), (1 if turned else 0,)), ((), ())), preferred_element_type=F32
@@ -219,6 +448,10 @@
         grid = Grid(ph)
         relative, absolute = grid.to_relative(), grid.to_absolute()
         turns = list(range(1, grid.x)) + [0]
+        outside = width // relative.shape[0] % 128
+        turn_in = lambda value: reorder(value, relative) if outside else value
+        turn_out = lambda value: reorder(value, absolute) if outside else value
+        flat = lambda value: value.reshape(rows, width)
         join = lambda own, theirs: jnp.concatenate([own, theirs], axis=0)
 
         def whole(*by_z):
@@ -244,6 +477,9 @@
             part = part.astype(BF16)
             ph.end(part)
             return ph.across(part)
+
+        def two(parts):
+            return parts if len(parts) == 2 else [plus(*parts), jnp.zeros_like(parts[0])]
 
         def dots(lhs, rhs):
             kept = {}
@@ -271,18 +507,15 @@
 
         z_q[3] = ph.send_z(s_q, 3)
         x_q[1] = ph.gather_x(z_q[1])
-        tokens = reorder(ph.begin(tokens), relative)
-        shift1, scale1, gate1 = (mods[:, 0:1], mods[:, 1:2], mods[:, 2:3])
-        shift2, scale2, gate2 = (mods[:, 3:4], mods[:, 4:5], mods[:, 5:6])
-        mask = present.astype(F32)[:, None, None]
-        inputs = tokens.astype(F32)
-        normed_own = modulate(inputs, shift1, scale1).astype(BF16).reshape(rows, width)
+        tokens, normed_own = by_rows(
+            first_norm_kernel, relative, present, [flat(turn_in(ph.begin(tokens)))], mods, [BF16, BF16]
+        )
         ph.end(normed_own)
+        normed_other = ph.hand_over(normed_own)
         ph.close()
 
         z_q[2] = ph.send_z(z_q[1], 1)
         x_q[3] = ph.gather_x(z_q[3])
-        normed_other = ph.send_core(ph.now(normed_own))
         s_u = grid.chip_shard(ph.begin(w_up))
         ph.end(s_u)
         normed = join(normed_own, ph.begin(normed_other))
@@ -301,53 +534,52 @@
         w_a = whole(x_q[0], x_q[1], x_q[2], x_q[3])
         local_width = s_o.shape[1]
         local_heads = local_width // HEAD_DIM
-        factor = HEAD_DIM ** (-0.5)
-        per_head = lambda value: value.reshape(CORES * count, length, local_heads, HEAD_DIM)
         qkv = matmul(ph.begin(normed), w_a).astype(BF16)
         ph.end(qkv)
-        query, keys, values = (per_head(part) for part in jnp.split(ph.begin(qkv), 3, axis=1))
-        scores = jnp.einsum("cqhe,ckhe->chqk", query, keys, preferred_element_type=F32) * factor
-        top = jnp.max(scores, axis=-1, keepdims=True)
-        expo = jnp.exp(scores - top)
-        total = jnp.sum(expo, axis=-1, keepdims=True)
-        lse = top + jnp.log(total)
-        probs_low = (expo / total).astype(BF16)
-        ph.end(probs_low)
+        attend = functools.partial(attend_kernel, local_heads)
+        mixed = by_image(attend, length, local_width, ph.begin(qkv))
+        ph.end(mixed)
         ph.close()
 
         z_u = {1: ph.send_z(s_u, 1)}
         x_d = {0: ph.gather_x(s_d)}
         w_o = jnp.concatenate([z_o[kz][kx] for kx in range(grid.x) for kz in range(grid.z)], axis=0)
-        probs_low = ph.begin(probs_low)
-        mixed = jnp.einsum("chqk,ckhe->cqhe", probs_low, values, preferred_element_type=F32)
-        mixed = mixed.astype(BF16).reshape(CORES * rows, local_width)
-        ph.end(mixed)
-        att = summed(mixed, w_o)
+        from_cotangent = []
+
+        def take_cotangent():
+            from_cotangent.extend(
+                by_rows(
+                    cotangent_kernel, relative, present, [flat(turn_in(ph.begin(cotangent)))], mods,
+                    [BF16, BF16],
+                )
+            )
+            ph.end(from_cotangent[1])
+
+        att = summed(mixed, w_o, take_cotangent)
+        dy, d_mlp_own = from_cotangent
         ph.close()
 
         z_u[3] = ph.send_z(s_u, 3)
         x_u[1] = ph.gather_x(z_u[1])
-        cotangent = reorder(ph.begin(cotangent), relative)
-        grad_dy = cotangent.astype(F32) * mask
-        d_mlp_own = (gate2 * grad_dy).astype(BF16).reshape(rows, width)
-        ph.end(d_mlp_own)
+        d_mlp_other = ph.hand_over(ph.now(d_mlp_own))
         ph.close()
 
         z_u[2] = ph.send_z(z_u[1], 1)
         x_u[3] = ph.gather_x(z_u[3])
-        d_mlp = join(d_mlp_own, ph.begin(ph.send_core(ph.now(d_mlp_own))))
-        ph.end(d_mlp)
         att[-1] = ph.begin(att[-1])
-        att = plus(*att).reshape(count, length, width)
-        hidden = inputs + gate1 * att
-        second_own = modulate(hidden, shift2, scale2).astype(BF16).reshape(rows, width)
+        hidden, second_own = by_rows(
+            second_norm_kernel, relative, present, [tokens, *two(att)], mods, [F32, BF16]
+        )
         ph.end(second_own)
+        second_other = ph.hand_over(second_own)
         ph.close()
 
         z_d = {1: ph.send_z(s_d, 1)}
         x_u[2] = ph.gather_x(z_u[2])
-        second = join(second_own, ph.begin(ph.send_core(ph.now(second_own))))
+        second = join(second_own, ph.begin(second_other))
         ph.end(second)
+        d_mlp = join(d_mlp_own, ph.begin(d_mlp_other))
+        ph.end(d_mlp)
         ph.close()
 
         z_d[3] = ph.send_z(s_d, 3)
@@ -371,18 +603,21 @@
         part = lambda stacked, kz: stacked[:, kz * blk : (kz + 1) * blk]
         x_d[2] = ph.gather_x(z_d[2])
         a_2 = ph.send_z(part(first, 2), 3)
+        up_val = ph.begin(up_val)
+        _, gelu_pull = jax.vjp(jax.nn.gelu, up_val)
+        slope = gelu_pull(jnp.ones_like(up_val))[0]
+        ph.end(slope)
         ph.close()
 
         x_b = {2: ph.reduce_x(rows_of(other, 2, 4))}
         a_3 = ph.send_z(part(first, 3), 1)
         w_d = whole(x_d[0], x_d[1], x_d[2], x_d[3])
-        d_act = matmul(ph.begin(d_mlp), w_d)
-        _, gelu_pull = jax.vjp(jax.nn.gelu, up_val)
-        d_up = gelu_pull(d_act)[0].astype(BF16)
+        d_up = (matmul(ph.begin(d_mlp), w_d) * slope).astype(BF16)
         ph.end(d_up)
         up = {}
         d_second_part = matmul(ph.begin(d_up)[rows:], w_u, True).astype(BF16)
         ph.end(d_second_part)
+        d_second_part = ph.hand_over(d_second_part)
         ph.close()
 
         def up_dots(blocks):
@@ -392,7 +627,8 @@
 
         x_b[0] = ph.reduce_x(rows_of(other, 0, 2))
         a_1 = ph.send_z(plus(part(first, 1), ph.now(a_2)).astype(BF16), 3)
-        d_second = from_both(ph.send_core(ph.now(d_second_part)), d_up, w_u, lambda: up_dots(turns[:-1]))
+        d_second = from_both(d_second_part, d_up, w_u)
+        up_dots(turns[:-1])
         ph.close()
 
         up_rows = lambda kz: ph.reduce_x(rows_of(up, kz, kz + 1))
@@ -404,69 +640,57 @@
         up_dots(turns[-1:])
         mlp_part = matmul(ph.begin(act)[rows:], w_d, True).astype(BF16)
         ph.end(mlp_part)
+        mlp_part = ph.hand_over(mlp_part)
         ph.close()
 
         x_up[3] = up_rows(3)
         up_sum = lambda kz: plus(rows_of(up, kz, kz + 1)[0], ph.now(x_up[kz]))
         u_2 = ph.send_z(up_sum(2).astype(BF16), 3)
-        mlp = from_both(ph.send_core(ph.now(mlp_part)), act, w_d)
+        mlp = from_both(mlp_part, act, w_d)
         d_second[-1] = ph.begin(d_second[-1])
-        d_second = plus(*d_second)
-        _, norm_pull2 = jax.vjp(modulate, hidden, shift2, scale2)
-        d_hidden_n, g_shift2, g_scale2 = norm_pull2(d_second.reshape(count, length, width))
-        d_hidden = grad_dy + d_hidden_n
-        g_gate1 = jnp.sum(d_hidden * att, axis=1)
-        d_att_own = (gate1 * d_hidden).astype(BF16).reshape(rows, width)
+        d_hidden, d_att_own, sums2 = by_rows(
+            second_back_kernel, relative, present, [hidden, *two(att), *two(d_second), dy], mods,
+            [F32, BF16], 3,
+        )
         ph.end(d_att_own)
+        d_att_other = ph.hand_over(d_att_own)
         ph.close()
 
         x_up[1] = up_rows(1)
+        first_sum = plus(part(first, 0), a_3, ph.now(a_1))
+        x_first = ph.reduce_x(first_sum.astype(BF16))
         u_3 = ph.send_z(up_sum(3).astype(BF16), 1)
-        d_att = join(d_att_own, ph.begin(ph.send_core(ph.now(d_att_own))))
+        b_1 = ph.send_z((b_sum(1) + ph.now(b_2).astype(F32)).astype(BF16), 3)
+        d_att = join(d_att_own, ph.begin(d_att_other))
         d_mixed = matmul(d_att, w_o).astype(BF16)
         ph.end(d_mixed)
-        d_mixed = per_head(ph.begin(d_mixed))
-        again = jnp.einsum("cqhe,ckhe->chqk", query, keys, preferred_element_type=F32) * factor
-        probs = jnp.exp(again - lse)
-        probs_again = probs.astype(BF16)
-        d_probs = jnp.einsum("cqhe,ckhe->chqk", d_mixed, values, preferred_element_type=F32)
-        delta = jnp.sum(d_probs * probs, axis=-1, keepdims=True)
-        d_scores = (probs * (d_probs - delta)).astype(BF16)
-        d_values = jnp.einsum(
-            "chqk,cqhe->ckhe", probs_again, d_mixed, preferred_element_type=F32
-        ).astype(BF16)
-        d_query = (
-            jnp.einsum("chqk,ckhe->cqhe", d_scores, keys, preferred_element_type=F32) * factor
-        ).astype(BF16)
-        d_keys = (
-            jnp.einsum("chqk,cqhe->ckhe", d_scores, query, preferred_element_type=F32) * factor
-        ).astype(BF16)
-        flat = lambda value: value.reshape(CORES * rows, local_width)
-        d_qkv = jnp.concatenate([flat(d_query), flat(d_keys), flat(d_values)], axis=1)
+        attend_back = functools.partial(attend_back_kernel, local_heads)
+        d_qkv = by_image(attend_back, length, 3 * local_width, qkv, ph.begin(d_mixed))
         ph.end(d_qkv)
+        d_normed_part = matmul(ph.begin(d_qkv)[rows:], w_a, True).astype(BF16)
+        ph.end(d_normed_part)
+        d_normed_part = ph.hand_over(d_normed_part)
         ph.close()
 
         x_up[0] = up_rows(0)
         u_1 = ph.send_z((up_sum(1) + ph.now(u_2).astype(F32)).astype(BF16), 3)
-        d_normed_part = matmul(ph.begin(d_qkv)[rows:], w_a, True).astype(BF16)
-        ph.end(d_normed_part)
-        out = {}
-
-        def out_dots():
-            out.update(dots(d_att, mixed))
-
-        d_normed = from_both(ph.send_core(d_normed_part), d_qkv, w_a, out_dots)
+        d_normed = from_both(d_normed_part, d_qkv, w_a)
+        mlp[-1] = ph.begin(mlp[-1])
+        ph.end(mlp[-1])
+        out = dots(d_att, mixed)
         proj = dots(normed, d_qkv)
         ph.close()
 
         x_out = ph.reduce_x(out)
-        b_1 = ph.send_z((b_sum(1) + ph.now(b_2).astype(F32)).astype(BF16), 3)
         mlp[-1] = ph.begin(mlp[-1])
-        mlp = plus(*mlp).reshape(count, length, width)
-        block_out = (mask * (hidden + gate2 * mlp)).astype(BF16)
-        block_out = reorder(block_out, absolute)
-        g_gate2 = jnp.sum(grad_dy * mlp, axis=1)
-        ph.end(block_out, g_gate2)
+        block_out, sums3 = by_rows(
+            block_out_kernel, relative, present, [hidden, *two(mlp), dy], mods, [BF16], 1
+        )
+        ph.end(block_out)
+        up_total = up_sum(0) + ph.now(u_3).astype(F32) + ph.now(u_1).astype(F32)
+        up_mine, up_theirs = grid.halves(ph.begin(up_total), 0)
+        ph.end(up_mine)
+        up_theirs = ph.hand_over(up_theirs)
         ph.close()
 
         p_rows = lambda kz: ph.reduce_x(rows_of(proj, kz, kz + 1))
@@ -477,56 +701,59 @@
         x_p = {2: p_rows(2)}
         o_2 = ph.send_z(out_sum(2).astype(BF16), 3)
         o_3 = ph.send_z(out_sum(3).astype(BF16), 1)
-        up_part = up_sum(0) + ph.now(u_3).astype(F32) + ph.now(u_1).astype(F32)
-        up_part = grid.own_rows(ph.begin(up_part))
+        d_normed[-1] = ph.begin(d_normed[-1])
+        input_grad, sums1 = by_rows(
+            first_back_kernel, relative, present, [tokens, *two(d_normed), d_hidden], mods, [F32], 2
+        )
+        ph.end(input_grad)
+        ph.close(20.0)
+
+        x_p[3] = p_rows(3)
+        p_2 = ph.send_z(p_sum(2).astype(BF16), 3)
+        o_1 = ph.send_z((out_sum(1) + ph.now(o_2).astype(F32)).astype(BF16), 3)
+        row_sums = [jnp.sum(v.reshape(count, -1, 8, width), axis=2) for v in (sums1, sums2, sums3)]
+        bin_row = jnp.broadcast_to(bins.astype(F32)[:, None, None], (count, 1, width))
+        d_mods = ph.begin(turn_out(jnp.concatenate(row_sums, axis=1)))
+        d_mods = jnp.concatenate([d_mods, bin_row], axis=1)
+        ph.end(d_mods)
+        down_low = plus(ph.now(first_sum)[0], x_first)
+        down_high = b_sum(0) + ph.now(b_3).astype(F32) + ph.now(b_1).astype(F32)
+        down_total = ph.begin(jnp.concatenate([down_low, down_high], axis=1))
+        down_mine, down_theirs = grid.halves(down_total, 0)
+        ph.end(down_mine, d_mods)
+        down_theirs = ph.hand_over(down_theirs)
+        ph.close(20.0)
+
+        x_p[1] = p_rows(1)
+        p_3 = ph.send_z(p_sum(3).astype(BF16), 1)
+        d_mods = lax.all_to_all(ph.now(d_mods), "dp", split_axis=2, concat_axis=0, tiled=True)
+        ph.results.append(d_mods)
+        up_part = grid.by_core(ph.begin(up_mine), up_theirs, 1)
         ph.end(up_part)
         ph.close(20.0)
 
-        x_p[3] = p_rows(3)
-        p_2 = ph.send_z(p_sum(2).astype(BF16), 3)
-        d_normed[-1] = ph.begin(d_normed[-1])
-        d_normed = plus(*d_normed)
-        _, norm_pull1 = jax.vjp(modulate, inputs, shift1, scale1)
-        d_input_n, g_shift1, g_scale1 = norm_pull1(d_normed.reshape(count, length, width))
-        input_grad = d_hidden + d_input_n
-        ph.end(input_grad)
-        ph.close(20.0)
-
-        x_p[1] = p_rows(1)
-        p_3 = ph.send_z(p_sum(3).astype(BF16), 1)
-        input_grad = reorder(ph.begin(input_grad), absolute)
-        d_mods = jnp.stack(
-            [g_shift1[:, 0], g_scale1[:, 0], g_gate1, g_shift2[:, 0], g_scale2[:, 0], g_gate2],
-            axis=1,
-        )
-        d_mods = reorder(d_mods, absolute)
-        bin_row = jnp.broadcast_to(bins.astype(F32)[:, None, None], (count, 1, width))
-        d_mods = jnp.concatenate([d_mods, bin_row], axis=1)
-        ph.end(input_grad, d_mods)
-        ph.close(20.0)
-
         x_p[0] = p_rows(0)
         p_1 = ph.send_z((p_sum(1) + ph.now(p_2).astype(F32)).astype(BF16), 3)
-        d_mods = lax.all_to_all(ph.now(d_mods), "dp", split_axis=2, concat_axis=0, tiled=True)
         d_mods = ph.begin(d_mods)
+        rows_in_order = jnp.stack([d_mods[:, k] for k in (0, 1, 4, 2, 3, 5)], axis=1)
         onehot_all = (d_mods[:, 6, :1] == table_rows.astype(F32)).astype(F32)
-        table_part = jnp.einsum("sb,std->btd", onehot_all, d_mods[:, :6], precision=HIGH)
+        table_part = jnp.einsum("sb,std->btd", onehot_all, rows_in_order, precision=HIGH)
         ph.end(table_part)
+        down_part = grid.by_core(ph.begin(down_mine), down_theirs, 1)
+        ph.end(down_part)
+        out_total = out_sum(0) + ph.now(o_3).astype(F32) + ph.now(o_1).astype(F32)
+        out_mine, out_theirs = grid.halves(ph.begin(out_total), 0)
+        ph.end(out_mine)
+        out_theirs = ph.hand_over(out_theirs)
         ph.close(20.0)
 
-        first_sum = plus(part(first, 0), a_3, a_1)
-        x_first = ph.reduce_x(first_sum.astype(BF16))
-        o_1 = ph.send_z((out_sum(1) + ph.now(o_2).astype(F32)).astype(BF16), 3)
+        out_part = grid.by_core(out_mine, ph.begin(out_theirs), 1)
         qkv_part = p_sum(0) + ph.now(p_3).astype(F32) + ph.now(p_1).astype(F32)
         qkv_part = qkv_part.reshape(-1, 3, local_width).transpose(1, 0, 2)
-        qkv_part = grid.own_rows(ph.begin(qkv_part))
-        ph.end(qkv_part)
-        ph.close(15.0)
-
-        down_low = plus(ph.now(first_sum)[0], x_first)
-        down_high = b_sum(0) + ph.now(b_3).astype(F32) + ph.now(b_1).astype(F32)
-        down_part = grid.own_rows(jnp.concatenate([down_low, down_high], axis=1))
-        out_part = grid.own_rows(out_sum(0) + ph.now(o_3).astype(F32) + ph.now(o_1).astype(F32))
+        qkv_part = grid.own_rows(qkv_part)
+        block_out, input_grad = (
+            turn_out(value).reshape(count, length, width) for value in (block_out, input_grad)
+        )
         return (block_out, input_grad, table_part, qkv_part, out_part, up_part, down_part)
 
     return body

time: 696 us -> 658 us (0.945)
  other arithmetic: 114 us -> 39 us
  waiting for transfers between devices: 183 us -> 256 us
  local copies, waits for them, and re-layouts: 103 us -> 64 us
  Pallas kernels: 36 us -> 66.1 us
  starting transfers between devices: 104 us -> 84.4 us
  matrix products: 144 us -> 136 us
    pallas_call x0 -> x8, Pallas kernels: none -> 61.3 us  [the longest x6 47.9 us: by_rows(): pl.pallas_call(functools.partial(kernel, blocks), grid_spec=pltpu.Prefetc...]
    ppermute x52, waiting for transfers between devices: 157 us -> 209 us  [send(): out = lax.ppermute(value, 'dp', self.ring(dz, dx, 0))]
    reduce_sum x11 -> x3, other arithmetic: 41.6 us -> 0.25 us  [body(): jnp.sum(v.reshape(count, -1, 8, width), axis=2)]
    pallas_call x6 -> x1, Pallas kernels: 36 us -> 4.78 us  [reorder(): pl.pallas_call(copy_block, grid_spec=pltpu.PrefetchScalarGridSpec(num_sca...]
    ppermute x4, waiting for transfers between devices: 1.03 us -> 28.6 us  [across(): out.append(lax.ppermute(out[-1], 'mp', self.turn))]
    ppermute x52, starting transfers between devices: 93.2 us -> 70.6 us  [send(): out = lax.ppermute(value, 'dp', self.ring(dz, dx, 0))]
    convert_element_type x8 -> x0, other arithmetic: 19 us -> none  [the longest x1 4.35 us: body(): block_out = (mask * (hidden + gate2 * mlp)).astype(BF16)]
    unnamed x240 -> x190, local copies, waits for them, and re-layouts: 60.4 us -> 44.8 us
  transfers between devices with their start and end apart: 73 -> 73, of which waited for: 31 -> 35; matrix products, arithmetic and copies ran while one was open for 47% -> 33% of each run, Pallas kernels for 5% -> 10%
where the time goes in v3:
time: 658 us; the launch traced here: 648 us
  waiting for transfers between devices  256 us (39%)
  matrix products  136 us (21%)
  starting transfers between devices  84.4 us (13%)
  Pallas kernels  66.1 us (10%)
  local copies, waits for them, and re-layouts  64 us (10%)
  other arithmetic  39 us (6%)
    ppermute x52, waiting for transfers between devices, send(): out = lax.ppermute(value, 'dp', self.ring(dz, dx, 0))  209 us
    dot_general x12, matrix products, matmul(): lax.dot_general(lhs, rhs, (((1,), (1 if turned else 0,)), ((), ())), pref...  97.4 us
    ppermute x52, starting transfers between devices, send(): out = lax.ppermute(value, 'dp', self.ring(dz, dx, 0))  70.6 us
    pallas_call x6, Pallas kernels, by_rows(): pl.pallas_call(functools.partial(kernel, blocks), grid_spec=pltpu.Prefetc...  47.9 us
    unnamed x190, local copies, waits for them, and re-layouts  44.8 us
    dot_general x8, matrix products, dots(): lax.dot_general(lhs[:, kx * width:(kx + 1) * width], rhs, (((0,), (0,)),...  36.9 us
    ppermute x4, waiting for transfers between devices, across(): out.append(lax.ppermute(out[-1], 'mp', self.turn))  28.6 us
    pallas_call x2, Pallas kernels, by_image(): pl.pallas_call(kernel, grid=(rows // length,), in_specs=[block(operand.sh...  13.4 us
  transfers between devices with their start and end apart: 73, of which 35 were waited for; matrix products, arithmetic and copies ran while one was open for 33% of the time, Pallas kernels for 10%

profile of v3, /device:TPU:0, one launch (start us, length us, event | category | flops | bytes accessed | tf_op | source)
XLA Modules:
  0.0 647.9 jit_solution(11253446314775528206)
XLA Ops:
  7.8 2.6 collective-permute-start.2
  15.0 4.8 shard_map.144
  20.7 13.4 %collective-permute-done.4 = bf16[256,512]{1,0:T(8,128)(2,1)S(1)} collective-permute-done((bf16[256,512]{1,0:T(8,128)(2,1)S(1)}, bf16[256,512]{1,0:T(8,128)(2,1)S(1)}, u32[]{:S(2)}, u32[]{:S(2)}) %collective-permute-start.4) | collective-permute-done | bytes 262176 | tf_op jit(solution)/shard_map/ppermute | solution.py:58
  34.2 3.9 collective-permute-start.6
  41.2 7.8 %shard_map.145 = (bf16[512,2048]{1,0:T(8,128)(2,1)S(1)}, bf16[512,2048]{1,0:T(8,128)(2,1)S(1)}) custom-call(s32[8]{0:T(128)S(1)} %copy-done.10, s32[2]{0:T(128)S(1)} %copy-done.17, bf16[512,2048]{1,0:T(8,128)(2,1)S(1)} %bitcast.99, f32[2,6,2048]{2,1,0:T(8,128)S(1)} %reshape.117.mods_ref), custom_call_target="tpu_custom_call" | custom-call | flops 6291456000 | bytes 8388608 | tf_op jit(solution)/shard_map/pallas_call | solution.py:421
  49.1 2.9 constant_dynamic-update-slice_fusion.8
  52.2 2.5 collective-permute-done.6
  54.7 2.4 collective-permute-done.7
  62.0 14.8 %collective-permute-done.9 = bf16[256,1536]{0,1:T(8,128)(2,1)S(1)} collective-permute-done((bf16[256,1536]{0,1:T(8,128)(2,1)}, bf16[256,1536]{0,1:T(8,128)(2,1)S(1)}, u32[]{:S(2)}, u32[]{:S(2)}) %collective-permute-start.9) | collective-permute-done | bytes 786464 | tf_op jit(solution)/shard_map/ppermute | solution.py:58
  80.1 9.8 %collective-permute-done.11 = bf16[2,256,512]{2,1,0:T(8,128)(2,1)S(1)} collective-permute-done((bf16[2,256,512]{2,1,0:T(8,128)(2,1)S(1)}, bf16[2,256,512]{2,1,0:T(8,128)(2,1)S(1)}, u32[]{:S(2)}, u32[]{:S(2)}) %collective-permute-start.11) | collective-permute-done | bytes 524320 | tf_op jit(solution)/shard_map/ppermute | solution.py:58
  93.8 3.5 collective-permute-start.14
  99.0 7.0 %convolution_convert_fusion.qkv_ref = bf16[1024,1536]{1,0:T(8,128)(2,1)S(1)} fusion(bf16[1024,2048]{1,0:T(8,128)(2,1)S(1)} %constant_dynamic-update-slice_fusion, bf16[2048,1536]{0,1:T(8,128)(2,1)S(1)} %constant_dynamic-update-slice_fusion.2), kind=kOutput, calls=%fused_computation.31 | convolution fusion | flops 6444023808 | bytes 13631488 | tf_op jit(solution)/shard_map/dot_general | solution.py:438
  106.0 4.5 shard_map.146
  110.7 6.2 collective-permute-done.15
  125.3 16.7 %collective-permute-done.19 = bf16[256,2048]{1,0:T(8,128)(2,1)} collective-permute-done((bf16[256,2048]{1,0:T(8,128)(2,1)S(1)}, bf16[256,2048]{1,0:T(8,128)(2,1)}, u32[]{:S(2)}, u32[]{:S(2)}) %collective-permute-start.19) | collective-permute-done | bytes 1048608 | tf_op jit(solution)/shard_map/ppermute | solution.py:58
  142.0 2.3 constant_dynamic-update-slice_fusion.22
  150.6 17.0 %collective-permute-done.21 = bf16[256,2048]{1,0:T(8,128)(2,1)} collective-permute-done((bf16[256,2048]{1,0:T(8,128)(2,1)S(1)}, bf16[256,2048]{1,0:T(8,128)(2,1)}, u32[]{:S(2)}, u32[]{:S(2)}) %collective-permute-start.21) | collective-permute-done | bytes 1048608 | tf_op jit(solution)/shard_map/ppermute | solution.py:58
  167.7 2.6 collective-permute-done.22
  172.2 25.0 %collective-permute-done.18.att_b = bf16[512,2048]{1,0:T(8,128)(2,1)S(1)} collective-permute-done((bf16[512,2048]{1,0:T(8,128)(2,1)S(1)}, bf16[512,2048]{1,0:T(8,128)(2,1)S(1)}, u32[]{:S(2)}, u32[]{:S(2)}) %collective-permute-start.18) | collective-permute-done | bytes 2097184 | tf_op jit(solution)/shard_map/ppermute | solution.py:80
  197.2 7.9 %shard_map.148 = (f32[512,2048]{1,0:T(8,128)S(1)}, bf16[512,2048]{1,0:T(8,128)(2,1)S(1)}) custom-call(s32[8]{0:T(128)S(1)} %copy-done.10, s32[2]{0:T(128)S(1)} %copy-done.17, bf16[512,2048]{1,0:T(8,128)(2,1)S(1)} %get-tuple-element.176.tokens_ref, bf16[512,2048]{1,0:T(8,128)(2,1)S(1)} %add_convert_fusion.3.att_a, ...), custom_call_target="tpu_custom_call" | custom-call | flops 6291456000 | bytes 8388608 | tf_op jit(solution)/shard_map/pallas_call | solution.py:421
  205.4 3.8 constant_dynamic-update-slice_fusion.21
  214.9 25.6 %collective-permute-done.27 = bf16[256,2048]{1,0:T(8,128)(2,1)} collective-permute-done((bf16[256,2048]{1,0:T(8,128)(2,1)S(1)}, bf16[256,2048]{1,0:T(8,128)(2,1)}, u32[]{:S(2)}, u32[]{:S(2)}) %collective-permute-start.27) | collective-permute-done | bytes 1048608 | tf_op jit(solution)/shard_map/ppermute | solution.py:58
  243.9 2.3 constant_dynamic-update-slice_fusion.16
  246.2 14.5 %fusion.13 = (bf16[1024,2048]{1,0:T(8,128)(2,1)S(1)}, f32[1024,2048]{1,0:T(8,128)}) fusion(bf16[1024,2048]{1,0:T(8,128)(2,1)S(1)} %constant_dynamic-update-slice_fusion.12, bf16[2048,2048]{1,0:T(8,128)(2,1)} %constant_dynamic-update-slice_fusion.16), kind=kOutput, calls=%fused_computation.16 | convolution fusion | flops 8608808960 | bytes 25165824 | tf_op jit(solution)/shard_map/dot_general | solution.py:438
  262.2 2.8 constant_dynamic-update-slice_fusion.30
  267.5 5.0 convolution_convert_fusion.6
  272.5 6.5 convolution_convert_fusion.5
  281.8 8.4 %collective-permute-done.31 = bf16[256,2048]{1,0:T(8,128)(2,1)S(1)} collective-permute-done((bf16[256,2048]{1,0:T(8,128)(2,1)}, bf16[256,2048]{1,0:T(8,128)(2,1)S(1)}, u32[]{:S(2)}, u32[]{:S(2)}) %collective-permute-start.31) | collective-permute-done | bytes 1048608 | tf_op jit(solution)/shard_map/ppermute | solution.py:58
  298.1 14.6 %collective-permute-done.33 = bf16[256,2048]{1,0:T(8,128)(2,1)S(1)} collective-permute-done((bf16[256,2048]{1,0:T(8,128)(2,1)S(1)}, bf16[256,2048]{1,0:T(8,128)(2,1)S(1)}, u32[]{:S(2)}, u32[]{:S(2)}) %collective-permute-start.33) | collective-permute-done | bytes 1048608 | tf_op jit(solution)/shard_map/ppermute | solution.py:58
  317.2 16.4 %multiply_convert_fusion = bf16[1024,2048]{1,0:T(8,128)(2,1)S(1)} fusion(bf16[1024,2048]{1,0:T(8,128)(2,1)S(1)} %copy-done.40, bf16[2048,2048]{1,0:T(8,128)(2,1)} %constant_dynamic-update-slice_fusion.24, f32[1024,2048]{1,0:T(8,128)} %get-tuple-element.227), kind=kOutput, calls=%fused_computation.17 | convolution fusion | flops 8629780480 | bytes 25165824 | tf_op jit(solution)/shard_map/dot_general | solution.py:438
  333.6 10.6 %convolution_convert_fusion.9 = bf16[512,2048]{1,0:T(8,128)(2,1)} fusion(bf16[2048,2048]{1,0:T(8,128)(2,1)} %constant_dynamic-update-slice_fusion.16, bf16[1024,2048]{1,0:T(8,128)(2,1)S(1)} %multiply_convert_fusion), kind=kOutput, calls=%fused_computation.40 | convolution fusion | flops 4296015872 | bytes 12582912 | tf_op jit(solution)/shard_map/dot_general | solution.py:438
  344.4 4.3 collective-permute-done.37
  351.2 4.4 collective-permute-start.39
  355.6 8.5 %add_convert_fusion.2.d_a = bf16[512,2048]{1,0:T(8,128)(2,1)S(1)} fusion(bf16[512,2048]{1,0:T(8,128)(2,1)} %copy-done.75, bf16[512,2048]{1,0:T(8,128)(2,1)S(1)} %slice-done.1, bf16[2048,2048]{1,0:T(8,128)(2,1)} %constant_dynamic-update-slice_fusion.16), kind=kOutput, calls=%fused_computation.29 | convolution fusion | flops 4298113024 | bytes 14680064 | tf_op jit(solution)/shard_map/dot_general | solution.py:438
  365.6 7.4 %convolution_convert_fusion.4 = bf16[1024,2048]{1,0:T(8,128)(2,1)S(1)} fusion(bf16[1024,2048]{1,0:T(8,128)(2,1)} %copy-done.32, bf16[1024,2048]{1,0:T(8,128)(2,1)} %copy-done.43), kind=kOutput, calls=%fused_computation.35 | convolution fusion | flops 4297064448 | bytes 10485760 | tf_op jit(solution)/shard_map/dot_general | solution.py:175
  375.7 2.6 collective-permute-done.39
  379.7 4.3 collective-permute-start.41
  384.7 5.0 convolution_convert_fusion.3
  389.7 11.4 %convolution_convert_fusion.8 = bf16[512,2048]{1,0:T(8,128)(2,1)} fusion(bf16[2048,2048]{1,0:T(8,128)(2,1)} %constant_dynamic-update-slice_fusion.24, bf16[1024,2048]{1,0:T(8,128)(2,1)} %copy-done.38), kind=kOutput, calls=%fused_computation.39 | convolution fusion | flops 4296015872 | bytes 12582912 | tf_op jit(solution)/shard_map/dot_general | solution.py:438
  401.2 5.3 collective-permute-done.42
  410.9 3.8 collective-permute-start.46
  415.3 9.2 %add_convert_fusion.1.mlp_a = bf16[512,2048]{1,0:T(8,128)(2,1)S(1)} fusion(bf16[512,2048]{1,0:T(8,128)(2,1)} %copy-done.74, bf16[512,2048]{1,0:T(8,128)(2,1)} %slice.362, bf16[2048,2048]{1,0:T(8,128)(2,1)} %constant_dynamic-update-slice_fusion.24), kind=kOutput, calls=%fused_computation.28 | convolution fusion | flops 4298113024 | bytes 14680064 | tf_op jit(solution)/shard_map/dot_general | solution.py:438
  424.5 14.1 %shard_map.149 = (f32[512,2048]{1,0:T(8,128)}, bf16[512,2048]{1,0:T(8,128)(2,1)S(1)}, f32[2,24,2048]{2,1,0:T(8,128)S(1)}) custom-call(s32[8]{0:T(128)S(1)} %copy-done.10, s32[2]{0:T(128)S(1)} %copy-done.17, f32[512,2048]{1,0:T(8,128)} %copy-done.18, bf16[512,2048]{1,0:T(8,128)(2,1)S(1)} %copy-done.14, bf16[512,2048]{1,0:T(8,128)(2,1)S(1)} %copy-done.16, ...), custom_call_target="tpu_custom_call" | custom-call | flops 6291456000 | bytes 8388608 | tf_op jit(solution)/shard_map/pallas_call | solution.py:421
  440.5 2.4 collective-permute-done.48
  452.1 2.3 convolution_convert_fusion.11.d_mixed_ref
  454.4 8.9 %shard_map.150 = bf16[1024,1536]{1,0:T(8,128)(2,1)S(1)} custom-call(bf16[1024,1536]{1,0:T(8,128)(2,1)S(1)} %copy-done.5, bf16[1024,512]{1,0:T(8,128)(2,1)S(1)} %convolution_convert_fusion.11.d_mixed_ref), custom_call_target="tpu_custom_call" | custom-call | flops 3221225472 | bytes 8388608 | tf_op jit(solution)/shard_map/pallas_call | solution.py:249
  463.3 7.5 %convolution_convert_fusion.7 = bf16[512,2048]{1,0:T(8,128)(2,1)S(1)} fusion(bf16[2048,1536]{0,1:T(8,128)(2,1)} %copy-done.67, bf16[1024,1536]{1,0:T(8,128)(2,1)S(1)} %shard_map.150), kind=kOutput, calls=%fused_computation.38 | convolution fusion | flops 3222274048 | bytes 9961472 | tf_op jit(solution)/shard_map/dot_general | solution.py:438
  471.0 14.3 %collective-permute-done.52 = bf16[256,1024]{1,0:T(8,128)(2,1)S(1)} collective-permute-done((bf16[256,1024]{1,0:T(8,128)(2,1)}, bf16[256,1024]{1,0:T(8,128)(2,1)S(1)}, u32[]{:S(2)}, u32[]{:S(2)}) %collective-permute-start.52) | collective-permute-done | bytes 524320 | tf_op jit(solution)/shard_map/ppermute | solution.py:58
  488.3 7.4 %add_convert_fusion.d_a = bf16[512,2048]{1,0:T(8,128)(2,1)} fusion(bf16[512,2048]{1,0:T(8,128)(2,1)S(1)} %collective-permute-done.53, bf16[512,1536]{1,0:T(8,128)(2,1)S(1)} %slice-done, bf16[2048,1536]{0,1:T(8,128)(2,1)} %copy-done.67), kind=kOutput, calls=%fused_computation.27 | convolution fusion | flops 3224371200 | bytes 12058624 | tf_op jit(solution)/shard_map/dot_general | solution.py:438
  501.7 3.7 convolution_convert_fusion.2
  507.1 4.9 convolution_convert_fusion.1
  513.4 3.6 shard_map.151
  518.8 16.8 %collective-permute-done.57 = bf16[1024,512]{1,0:T(8,128)(2,1)} collective-permute-done((bf16[1024,512]{1,0:T(8,128)(2,1)}, bf16[1024,512]{1,0:T(8,128)(2,1)}, u32[]{:S(2)}, u32[]{:S(2)}) %collective-permute-start.57) | collective-permute-done | bytes 1048608 | tf_op jit(solution)/shard_map/ppermute | solution.py:58
  538.0 3.2 collective-permute-start.60
  542.8 3.6 collective-permute-done.56.d_b
  550.2 13.2 %shard_map.152 = (f32[512,2048]{1,0:T(8,128)}, f32[2,16,2048]{2,1,0:T(8,128)S(1)}) custom-call(s32[8]{0:T(128)S(1)} %copy-done.10, s32[2]{0:T(128)S(1)} %copy-done.17, bf16[512,2048]{1,0:T(8,128)(2,1)S(1)} %copy-done.22, bf16[512,2048]{1,0:T(8,128)(2,1)} %add_convert_fusion.d_a, bf16[512,2048]{1,0:T(8,128)(2,1)} %collective-permute-done.56.d_b, ...), custom_call_target="tpu_custom_call" | custom-call | flops 6291456000 | bytes 8388608 | tf_op jit(solution)/shard_map/pallas_call | solution.py:421
  564.9 3.2 collective-permute-start.64
  574.9 14.6 %collective-permute-done.63 = bf16[256,1536]{1,0:T(8,128)(2,1)S(1)} collective-permute-done((bf16[256,1536]{1,0:T(8,128)(2,1)S(1)}, bf16[256,1536]{1,0:T(8,128)(2,1)S(1)}, u32[]{:S(2)}, u32[]{:S(2)}) %collective-permute-start.63) | collective-permute-done | bytes 786464 | tf_op jit(solution)/shard_map/ppermute | solution.py:58
  593.6 3.7 reshape.128
  597.4 6.2 all-to-all-start
  603.6 3.1 maximum_select_fusion
  606.7 6.7 %all-to-all-done = f32[16,1,1792]{2,1,0:T(1,128)S(1)} async-done(((f32[16,1,1792]{2,1,0:T(1,128)}), f32[16,1,1792]{2,1,0:T(1,128)S(1)}, u32[]{:S(2)}, u32[]{:S(2)}) %all-to-all-start) | async-done | bytes 114720 | tf_op jit(solution)/shard_map/all_to_all | solution.py:729
  614.9 3.2 reshape.129
  628.5 12.5 %collective-permute-done.68 = bf16[256,1536]{1,0:T(8,128)(2,1)S(1)} collective-permute-done((bf16[256,1536]{1,0:T(8,128)(2,1)}, bf16[256,1536]{1,0:T(8,128)(2,1)S(1)}, u32[]{:S(2)}, u32[]{:S(2)}) %collective-permute-start.68) | collective-permute-done | bytes 786464 | tf_op jit(solution)/shard_map/ppermute | solution.py:58
  (387 shorter events, 152.0 us)
Async XLA Ops:
  7.8 26.4 %collective-permute-start.2 = (bf16[256,1536]{0,1:T(8,128)(2,1)S(1)}, bf16[256,1536]{0,1:T(8,128)(2,1)}, u32[]{:S(2)}, u32[]{:S(2)}) collective-permute-start(bf16[256,1536]{0,1:T(8,128)(2,1)S(1)} %get-tuple-element.173), channel_id=1, source_target_pairs={{0,4},{2,6},{4,0},{6,2},{8,12},{10,14},{12,8},{14,10},{16,20},{18,... | collective-permute-start | bytes 2359304 | tf_op jit(solution)/shard_map/ppermute | solution.py:58
  10.5 23.7 %collective-permute-start.1 = (bf16[256,1536]{0,1:T(8,128)(2,1)S(1)}, bf16[256,1536]{0,1:T(8,128)(2,1)}, u32[]{:S(2)}, u32[]{:S(2)}) collective-permute-start(bf16[256,1536]{0,1:T(8,128)(2,1)S(1)} %get-tuple-element.173), channel_id=1, source_target_pairs={{0,8},{2,10},{4,12},{6,14},{8,16},{10,18},{12,20},{14,22},{16,24},... | collective-permute-start | bytes 2359304 | tf_op jit(solution)/shard_map/ppermute | solution.py:58
  12.8 21.3 %collective-permute-start.4 = (bf16[256,512]{1,0:T(8,128)(2,1)S(1)}, bf16[256,512]{1,0:T(8,128)(2,1)S(1)}, u32[]{:S(2)}, u32[]{:S(2)}) collective-permute-start(bf16[256,512]{1,0:T(8,128)(2,1)S(1)} %get-tuple-element.366), channel_id=1, source_target_pairs={{0,4},{2,6},{4,0},{6,2},{8,12},{10,14},{12,8},{14,10},{16,20},{18,... | collective-permute-start | bytes 786440 | tf_op jit(solution)/shard_map/ppermute | solution.py:58
  34.2 20.4 %collective-permute-start.6 = (bf16[256,1536]{0,1:T(8,128)(2,1)S(1)}, bf16[256,1536]{0,1:T(8,128)(2,1)S(1)}, u32[]{:S(2)}, u32[]{:S(2)}) collective-permute-start(bf16[256,1536]{0,1:T(8,128)(2,1)S(1)} %get-tuple-element.173), channel_id=1, source_target_pairs={{0,24},{2,26},{4,28},{6,30},{8,0},{10,2},{12,4},{14,6},{16,8},{18,... | collective-permute-start | bytes 2359304 | tf_op jit(solution)/shard_map/ppermute | solution.py:58
  38.1 18.9 %collective-permute-start.7 = (bf16[256,1536]{0,1:T(8,128)(2,1)}, bf16[256,1536]{0,1:T(8,128)(2,1)S(1)}, u32[]{:S(2)}, u32[]{:S(2)}) collective-permute-start(bf16[256,1536]{0,1:T(8,128)(2,1)} %collective-permute-done.1), channel_id=1, source_target_pairs={{0,4},{2,6},{4,0},{6,2},{8,12},{10,14},{12,8},{14,10},{16,20},{18,... | collective-permute-start | bytes 2359304 | tf_op jit(solution)/shard_map/ppermute | solution.py:58
  57.1 19.8 %collective-permute-start.9 = (bf16[256,1536]{0,1:T(8,128)(2,1)}, bf16[256,1536]{0,1:T(8,128)(2,1)S(1)}, u32[]{:S(2)}, u32[]{:S(2)}) collective-permute-start(bf16[256,1536]{0,1:T(8,128)(2,1)} %collective-permute-done.1), channel_id=1, source_target_pairs={{0,8},{2,10},{4,12},{6,14},{8,16},{10,18},{12,20},{14,22},{16,24},... | collective-permute-start | bytes 2359304 | tf_op jit(solution)/shard_map/ppermute | solution.py:58
  57.1 19.8 %collective-permute-start.10 = (bf16[256,1536]{0,1:T(8,128)(2,1)S(1)}, bf16[256,1536]{0,1:T(8,128)(2,1)S(1)}, u32[]{:S(2)}, u32[]{:S(2)}) collective-permute-start(bf16[256,1536]{0,1:T(8,128)(2,1)S(1)} %collective-permute-done.6), channel_id=1, source_target_pairs={{0,4},{2,6},{4,0},{6,2},{8,12},{10,14},{12,8},{14,10},{16,20},{18,... | collective-permute-start | bytes 2359304 | tf_op jit(solution)/shard_map/ppermute | solution.py:58
  76.9 13.1 %collective-permute-start.11 = (bf16[2,256,512]{2,1,0:T(8,128)(2,1)S(1)}, bf16[2,256,512]{2,1,0:T(8,128)(2,1)S(1)}, u32[]{:S(2)}, u32[]{:S(2)}) collective-permute-start(bf16[2,256,512]{2,1,0:T(8,128)(2,1)S(1)} %pad_maximum_fusion.2), channel_id=1, source_target_pairs={{0,8},{2,10},{4,12},{6,14},{8,16},{10,18},{12,20},{14,22},{16,24},... | collective-permute-start | bytes 1572872 | tf_op jit(solution)/shard_map/ppermute | solution.py:58
  76.9 16.9 %collective-permute-start.12 = (bf16[256,1536]{0,1:T(8,128)(2,1)S(1)}, bf16[256,1536]{0,1:T(8,128)(2,1)S(1)}, u32[]{:S(2)}, u32[]{:S(2)}) collective-permute-start(bf16[256,1536]{0,1:T(8,128)(2,1)S(1)} %collective-permute-done.9), channel_id=1, source_target_pairs={{0,4},{2,6},{4,0},{6,2},{8,12},{10,14},{12,8},{14,10},{16,20},{18,... | collective-permute-start | bytes 2359304 | tf_op jit(solution)/shard_map/ppermute | solution.py:58
  78.5 12.2 %collective-permute-start.13 = (bf16[128,2048]{1,0:T(8,128)(2,1)S(1)}, bf16[128,2048]{1,0:T(8,128)(2,1)S(1)}, u32[]{:S(2)}, u32[]{:S(2)}) collective-permute-start(bf16[128,2048]{1,0:T(8,128)(2,1)S(1)} %get-tuple-element.401), channel_id=1, source_target_pairs={{0,2},{2,0},{4,6},{6,4},{8,10},{10,8},{12,14},{14,12},{16,18},{18,... | collective-permute-start | bytes 1572872 | tf_op jit(solution)/shard_map/ppermute | solution.py:70
  93.8 23.1 %collective-permute-start.14 = (bf16[2,256,512]{2,1,0:T(8,128)(2,1)S(1)}, bf16[2,256,512]{2,1,0:T(8,128)(2,1)S(1)}, u32[]{:S(2)}, u32[]{:S(2)}) collective-permute-start(bf16[2,256,512]{2,1,0:T(8,128)(2,1)S(1)} %pad_maximum_fusion.2), channel_id=1, source_target_pairs={{0,24},{2,26},{4,28},{6,30},{8,0},{10,2},{12,4},{14,6},{16,8},{18,... | collective-permute-start | bytes 1572872 | tf_op jit(solution)/shard_map/ppermute | solution.py:58
  97.3 19.6 %collective-permute-start.15 = (bf16[2,256,512]{2,1,0:T(8,128)(2,1)S(1)}, bf16[2,256,512]{2,1,0:T(8,128)(2,1)S(1)}, u32[]{:S(2)}, u32[]{:S(2)}) collective-permute-start(bf16[2,256,512]{2,1,0:T(8,128)(2,1)S(1)} %collective-permute-done.11), channel_id=1, source_target_pairs={{0,8},{2,10},{4,12},{6,14},{8,16},{10,18},{12,20},{14,22},{16,24},... | collective-permute-start | bytes 1572872 | tf_op jit(solution)/shard_map/ppermute | solution.py:58
  97.3 21.1 %collective-permute-start.16 = (bf16[256,2048]{1,0:T(8,128)(2,1)S(1)}, bf16[256,2048]{1,0:T(8,128)(2,1)S(1)}, u32[]{:S(2)}, u32[]{:S(2)}) collective-permute-start(bf16[256,2048]{1,0:T(8,128)(2,1)S(1)} %get-tuple-element.201), channel_id=1, source_target_pairs={{0,4},{2,6},{4,0},{6,2},{8,12},{10,14},{12,8},{14,10},{16,20},{18,... | collective-permute-start | bytes 3145736 | tf_op jit(solution)/shard_map/ppermute | solution.py:58
  119.4 22.6 %collective-permute-start.19 = (bf16[256,2048]{1,0:T(8,128)(2,1)S(1)}, bf16[256,2048]{1,0:T(8,128)(2,1)}, u32[]{:S(2)}, u32[]{:S(2)}) collective-permute-start(bf16[256,2048]{1,0:T(8,128)(2,1)S(1)} %get-tuple-element.201), channel_id=1, source_target_pairs={{0,8},{2,10},{4,12},{6,14},{8,16},{10,18},{12,20},{14,22},{16,24},... | collective-permute-start | bytes 3145736 | tf_op jit(solution)/shard_map/ppermute | solution.py:58
  120.6 25.0 %collective-permute-start.20 = (bf16[256,2048]{1,0:T(8,128)(2,1)S(1)}, bf16[256,2048]{1,0:T(8,128)(2,1)S(1)}, u32[]{:S(2)}, u32[]{:S(2)}) collective-permute-start(bf16[256,2048]{1,0:T(8,128)(2,1)S(1)} %get-tuple-element.216), channel_id=1, source_target_pairs={{0,4},{2,6},{4,0},{6,2},{8,12},{10,14},{12,8},{14,10},{16,20},{18,... | collective-permute-start | bytes 3145736 | tf_op jit(solution)/shard_map/ppermute | solution.py:58
  123.4 20.9 %collective-permute-start.17 = (bf16[512,2048]{1,0:T(8,128)(2,1)S(1)}, bf16[512,2048]{1,0:T(8,128)(2,1)S(1)}, u32[]{:S(2)}, u32[]{:S(2)}) collective-permute-start(bf16[512,2048]{1,0:T(8,128)(2,1)S(1)} %convolution_convert_fusion.10), channel_id=1, source_target_pairs={{0,2},{2,0},{4,6},{6,4},{8,10},{10,8},{12,14},{14,12},{16,18},{18,... | collective-permute-start | bytes 6291464 | tf_op jit(solution)/shard_map/ppermute | solution.py:70
  145.6 22.0 %collective-permute-start.21 = (bf16[256,2048]{1,0:T(8,128)(2,1)S(1)}, bf16[256,2048]{1,0:T(8,128)(2,1)}, u32[]{:S(2)}, u32[]{:S(2)}) collective-permute-start(bf16[256,2048]{1,0:T(8,128)(2,1)S(1)} %get-tuple-element.201), channel_id=1, source_target_pairs={{0,24},{2,26},{4,28},{6,30},{8,0},{10,2},{12,4},{14,6},{16,8},{18,... | collective-permute-start | bytes 3145736 | tf_op jit(solution)/shard_map/ppermute | solution.py:58
  147.6 22.7 %collective-permute-start.22 = (bf16[256,2048]{1,0:T(8,128)(2,1)}, bf16[256,2048]{1,0:T(8,128)(2,1)S(1)}, u32[]{:S(2)}, u32[]{:S(2)}) collective-permute-start(bf16[256,2048]{1,0:T(8,128)(2,1)} %collective-permute-done.19), channel_id=1, source_target_pairs={{0,4},{2,6},{4,0},{6,2},{8,12},{10,14},{12,8},{14,10},{16,20},{18,... | collective-permute-start | bytes 3145736 | tf_op jit(solution)/shard_map/ppermute | solution.py:58
  149.1 21.2 %collective-permute-start.23 = (bf16[512,2048]{1,0:T(8,128)(2,1)S(1)}, bf16[512,2048]{1,0:T(8,128)(2,1)S(1)}, u32[]{:S(2)}, u32[]{:S(2)}) collective-permute-start(bf16[512,2048]{1,0:T(8,128)(2,1)S(1)} %get-tuple-element.203), channel_id=1, source_target_pairs={{0,2},{2,0},{4,6},{6,4},{8,10},{10,8},{12,14},{14,12},{16,18},{18,... | collective-permute-start | bytes 6291464 | tf_op jit(solution)/shard_map/ppermute | solution.py:70
  149.1 48.0 %collective-permute-start.18 = (bf16[512,2048]{1,0:T(8,128)(2,1)S(1)}, bf16[512,2048]{1,0:T(8,128)(2,1)S(1)}, u32[]{:S(2)}, u32[]{:S(2)}) collective-permute-start(bf16[512,2048]{1,0:T(8,128)(2,1)S(1)} %add_convert_fusion.3.att_a), channel_id=1, source_target_pairs={{0,1},{1,0},{2,3},{3,2},{4,5},{5,4},{6,7},{7,6},{8,9},{9,8},{10,11... | collective-permute-start | bytes 6291464 | tf_op jit(solution)/shard_map/ppermute | solution.py:80
  170.3 35.1 %collective-permute-start.25 = (bf16[256,2048]{1,0:T(8,128)(2,1)}, bf16[256,2048]{1,0:T(8,128)(2,1)}, u32[]{:S(2)}, u32[]{:S(2)}) collective-permute-start(bf16[256,2048]{1,0:T(8,128)(2,1)} %collective-permute-done.19), channel_id=1, source_target_pairs={{0,8},{2,10},{4,12},{6,14},{8,16},{10,18},{12,20},{14,22},{16,24},... | collective-permute-start | bytes 3145736 | tf_op jit(solution)/shard_map/ppermute | solution.py:58
  170.7 43.1 %collective-permute-start.26 = (bf16[256,2048]{1,0:T(8,128)(2,1)}, bf16[256,2048]{1,0:T(8,128)(2,1)}, u32[]{:S(2)}, u32[]{:S(2)}) collective-permute-start(bf16[256,2048]{1,0:T(8,128)(2,1)} %collective-permute-done.21), channel_id=1, source_target_pairs={{0,4},{2,6},{4,0},{6,2},{8,12},{10,14},{12,8},{14,10},{16,20},{18,... | collective-permute-start | bytes 3145736 | tf_op jit(solution)/shard_map/ppermute | solution.py:58
  205.1 8.6 %collective-permute-start.24 = (bf16[512,2048]{1,0:T(8,128)(2,1)S(1)}, bf16[512,2048]{1,0:T(8,128)(2,1)S(1)}, u32[]{:S(2)}, u32[]{:S(2)}) collective-permute-start(bf16[512,2048]{1,0:T(8,128)(2,1)S(1)} %get-tuple-element.209), channel_id=1, source_target_pairs={{0,2},{2,0},{4,6},{6,4},{8,10},{10,8},{12,14},{14,12},{16,18},{18,... | collective-permute-start | bytes 6291464 | tf_op jit(solution)/shard_map/ppermute | solution.py:70
  213.7 26.7 %collective-permute-start.27 = (bf16[256,2048]{1,0:T(8,128)(2,1)S(1)}, bf16[256,2048]{1,0:T(8,128)(2,1)}, u32[]{:S(2)}, u32[]{:S(2)}) collective-permute-start(bf16[256,2048]{1,0:T(8,128)(2,1)S(1)} %get-tuple-element.216), channel_id=1, source_target_pairs={{0,8},{2,10},{4,12},{6,14},{8,16},{10,18},{12,20},{14,22},{16,24},... | collective-permute-start | bytes 3145736 | tf_op jit(solution)/shard_map/ppermute | solution.py:58
  214.0 26.4 %collective-permute-start.28 = (bf16[256,2048]{1,0:T(8,128)(2,1)}, bf16[256,2048]{1,0:T(8,128)(2,1)S(1)}, u32[]{:S(2)}, u32[]{:S(2)}) collective-permute-start(bf16[256,2048]{1,0:T(8,128)(2,1)} %collective-permute-done.25), channel_id=1, source_target_pairs={{0,4},{2,6},{4,0},{6,2},{8,12},{10,14},{12,8},{14,10},{16,20},{18,... | collective-permute-start | bytes 3145736 | tf_op jit(solution)/shard_map/ppermute | solution.py:58
  240.5 24.6 %collective-permute-start.29 = (bf16[256,2048]{1,0:T(8,128)(2,1)S(1)}, bf16[256,2048]{1,0:T(8,128)(2,1)S(1)}, u32[]{:S(2)}, u32[]{:S(2)}) collective-permute-start(bf16[256,2048]{1,0:T(8,128)(2,1)S(1)} %get-tuple-element.216), channel_id=1, source_target_pairs={{0,24},{2,26},{4,28},{6,30},{8,0},{10,2},{12,4},{14,6},{16,8},{18,... | collective-permute-start | bytes 3145736 | tf_op jit(solution)/shard_map/ppermute | solution.py:58
  242.3 23.5 %collective-permute-start.30 = (bf16[256,2048]{1,0:T(8,128)(2,1)}, bf16[256,2048]{1,0:T(8,128)(2,1)S(1)}, u32[]{:S(2)}, u32[]{:S(2)}) collective-permute-start(bf16[256,2048]{1,0:T(8,128)(2,1)} %collective-permute-done.27), channel_id=1, source_target_pairs={{0,4},{2,6},{4,0},{6,2},{8,12},{10,14},{12,8},{14,10},{16,20},{18,... | collective-permute-start | bytes 3145736 | tf_op jit(solution)/shard_map/ppermute | solution.py:58
  265.8 24.4 %collective-permute-start.31 = (bf16[256,2048]{1,0:T(8,128)(2,1)}, bf16[256,2048]{1,0:T(8,128)(2,1)S(1)}, u32[]{:S(2)}, u32[]{:S(2)}) collective-permute-start(bf16[256,2048]{1,0:T(8,128)(2,1)} %collective-permute-done.27), channel_id=1, source_target_pairs={{0,8},{2,10},{4,12},{6,14},{8,16},{10,18},{12,20},{14,22},{16,24},... | collective-permute-start | bytes 3145736 | tf_op jit(solution)/shard_map/ppermute | solution.py:58
  266.8 23.4 %collective-permute-start.32 = (bf16[256,2048]{1,0:T(8,128)(2,1)S(1)}, bf16[256,2048]{1,0:T(8,128)(2,1)S(1)}, u32[]{:S(2)}, u32[]{:S(2)}) collective-permute-start(bf16[256,2048]{1,0:T(8,128)(2,1)S(1)} %collective-permute-done.29), channel_id=1, source_target_pairs={{0,4},{2,6},{4,0},{6,2},{8,12},{10,14},{12,8},{14,10},{16,20},{18,... | collective-permute-start | bytes 3145736 | tf_op jit(solution)/shard_map/ppermute | solution.py:58
  290.2 22.4 %collective-permute-start.33 = (bf16[256,2048]{1,0:T(8,128)(2,1)S(1)}, bf16[256,2048]{1,0:T(8,128)(2,1)S(1)}, u32[]{:S(2)}, u32[]{:S(2)}) collective-permute-start(bf16[256,2048]{1,0:T(8,128)(2,1)S(1)} %collective-permute-done.31), channel_id=1, source_target_pairs={{0,4},{2,6},{4,0},{6,2},{8,12},{10,14},{12,8},{14,10},{16,20},{18,... | collective-permute-start | bytes 3145736 | tf_op jit(solution)/shard_map/ppermute | solution.py:58
  292.4 21.1 %collective-permute-start.34 = (bf16[2,256,1024]{2,1,0:T(8,128)(2,1)S(1)}, bf16[2,256,1024]{2,1,0:T(8,128)(2,1)S(1)}, u32[]{:S(2)}, u32[]{:S(2)}) collective-permute-start(bf16[2,256,1024]{2,1,0:T(8,128)(2,1)S(1)} %get-tuple-element.226), channel_id=1, source_target_pairs={{0,24},{2,26},{4,28},{6,30},{8,0},{10,2},{12,4},{14,6},{16,8},{18,... | collective-permute-start | bytes 3145736 | tf_op jit(solution)/shard_map/ppermute | solution.py:58
  313.5 30.8 %collective-permute-start.35 = (bf16[512,1024]{1,0:T(8,128)(2,1)}, bf16[512,1024]{1,0:T(8,128)(2,1)S(1)}, u32[]{:S(2)}, u32[]{:S(2)}) collective-permute-start(bf16[512,1024]{1,0:T(8,128)(2,1)} %get-tuple-element.229), channel_id=1, source_target_pairs={{0,4},{2,6},{4,0},{6,2},{8,12},{10,14},{12,8},{14,10},{16,20},{18,... | collective-permute-start | bytes 3145736 | tf_op jit(solution)/shard_map/ppermute | solution.py:58
  314.4 30.0 %collective-permute-start.36 = (bf16[2,256,1024]{2,1,0:T(8,128)(2,1)S(1)}, bf16[2,256,1024]{2,1,0:T(8,128)(2,1)}, u32[]{:S(2)}, u32[]{:S(2)}) collective-permute-start(bf16[2,256,1024]{2,1,0:T(8,128)(2,1)S(1)} %get-tuple-element.230), channel_id=1, source_target_pairs={{0,8},{2,10},{4,12},{6,14},{8,16},{10,18},{12,20},{14,22},{16,24},... | collective-permute-start | bytes 3145736 | tf_op jit(solution)/shard_map/ppermute | solution.py:58
  350.3 25.4 %collective-permute-start.38 = (bf16[512,1024]{1,0:T(8,128)(2,1)}, bf16[512,1024]{1,0:T(8,128)(2,1)S(1)}, u32[]{:S(2)}, u32[]{:S(2)}) collective-permute-start(bf16[512,1024]{1,0:T(8,128)(2,1)} %get-tuple-element.234), channel_id=1, source_target_pairs={{0,4},{2,6},{4,0},{6,2},{8,12},{10,14},{12,8},{14,10},{16,20},{18,... | collective-permute-start | bytes 3145736 | tf_op jit(solution)/shard_map/ppermute | solution.py:58
  351.2 27.2 %collective-permute-start.39 = (bf16[2,256,1024]{2,1,0:T(8,128)(2,1)}, bf16[2,256,1024]{2,1,0:T(8,128)(2,1)}, u32[]{:S(2)}, u32[]{:S(2)}) collective-permute-start(bf16[2,256,1024]{2,1,0:T(8,128)(2,1)} %add_convert_fusion.7), channel_id=1, source_target_pairs={{0,24},{2,26},{4,28},{6,30},{8,0},{10,2},{12,4},{14,6},{16,8},{18,... | collective-permute-start | bytes 3145736 | tf_op jit(solution)/shard_map/ppermute | solution.py:58
  364.1 60.4 %collective-permute-start.47 = (bf16[512,2048]{1,0:T(8,128)(2,1)S(1)}, bf16[512,2048]{1,0:T(8,128)(2,1)S(1)}, u32[]{:S(2)}, u32[]{:S(2)}) collective-permute-start(bf16[512,2048]{1,0:T(8,128)(2,1)S(1)} %add_convert_fusion.2.d_a), channel_id=1, source_target_pairs={{0,1},{1,0},{2,3},{3,2},{4,5},{5,4},{6,7},{7,6},{8,9},{9,8},{10,11... | collective-permute-start | bytes 6291464 | tf_op jit(solution)/shard_map/ppermute | solution.py:80
  379.7 21.5 %collective-permute-start.41 = (bf16[256,1024]{1,0:T(8,128)(2,1)}, bf16[256,1024]{1,0:T(8,128)(2,1)S(1)}, u32[]{:S(2)}, u32[]{:S(2)}) collective-permute-start(bf16[256,1024]{1,0:T(8,128)(2,1)} %get-tuple-element.242), channel_id=1, source_target_pairs={{0,24},{2,26},{4,28},{6,30},{8,0},{10,2},{12,4},{14,6},{16,8},{18,... | collective-permute-start | bytes 1572872 | tf_op jit(solution)/shard_map/ppermute | solution.py:58
  384.0 22.5 %collective-permute-start.42 = (bf16[256,1024]{1,0:T(8,128)(2,1)}, bf16[256,1024]{1,0:T(8,128)(2,1)S(1)}, u32[]{:S(2)}, u32[]{:S(2)}) collective-permute-start(bf16[256,1024]{1,0:T(8,128)(2,1)} %get-tuple-element.244), channel_id=1, source_target_pairs={{0,8},{2,10},{4,12},{6,14},{8,16},{10,18},{12,20},{14,22},{16,24},... | collective-permute-start | bytes 1572872 | tf_op jit(solution)/shard_map/ppermute | solution.py:58
  384.2 24.0 %collective-permute-start.40 = (bf16[256,2048]{1,0:T(8,128)(2,1)}, bf16[256,2048]{1,0:T(8,128)(2,1)S(1)}, u32[]{:S(2)}, u32[]{:S(2)}) collective-permute-start(bf16[256,2048]{1,0:T(8,128)(2,1)} %get-tuple-element.240), channel_id=1, source_target_pairs={{0,4},{2,6},{4,0},{6,2},{8,12},{10,14},{12,8},{14,10},{16,20},{18,... | collective-permute-start | bytes 3145736 | tf_op jit(solution)/shard_map/ppermute | solution.py:58
  410.9 29.5 %collective-permute-start.46 = (bf16[256,2048]{1,0:T(8,128)(2,1)}, bf16[256,2048]{1,0:T(8,128)(2,1)}, u32[]{:S(2)}, u32[]{:S(2)}) collective-permute-start(bf16[256,2048]{1,0:T(8,128)(2,1)} %add_convert_fusion.6), channel_id=1, source_target_pairs={{0,24},{2,26},{4,28},{6,30},{8,0},{10,2},{12,4},{14,6},{16,8},{18,... | collective-permute-start | bytes 3145736 | tf_op jit(solution)/shard_map/ppermute | solution.py:58
  414.8 25.7 %collective-permute-start.45 = (bf16[256,2048]{1,0:T(8,128)(2,1)}, bf16[256,2048]{1,0:T(8,128)(2,1)S(1)}, u32[]{:S(2)}, u32[]{:S(2)}) collective-permute-start(bf16[256,2048]{1,0:T(8,128)(2,1)} %get-tuple-element.248), channel_id=1, source_target_pairs={{0,4},{2,6},{4,0},{6,2},{8,12},{10,14},{12,8},{14,10},{16,20},{18,... | collective-permute-start | bytes 3145736 | tf_op jit(solution)/shard_map/ppermute | solution.py:58
  438.7 57.0 %collective-permute-start.44 = (bf16[512,2048]{1,0:T(8,128)(2,1)S(1)}, bf16[512,2048]{1,0:T(8,128)(2,1)S(1)}, u32[]{:S(2)}, u32[]{:S(2)}) collective-permute-start(bf16[512,2048]{1,0:T(8,128)(2,1)S(1)} %add_convert_fusion.1.mlp_a), channel_id=1, source_target_pairs={{0,1},{1,0},{2,3},{3,2},{4,5},{5,4},{6,7},{7,6},{8,9},{9,8},{10,11... | collective-permute-start | bytes 6291464 | tf_op jit(solution)/shard_map/ppermute | solution.py:80
  447.3 23.5 %collective-permute-start.50 = (bf16[256,1024]{1,0:T(8,128)(2,1)S(1)}, bf16[256,1024]{1,0:T(8,128)(2,1)S(1)}, u32[]{:S(2)}, u32[]{:S(2)}) collective-permute-start(bf16[256,1024]{1,0:T(8,128)(2,1)S(1)} %fusion.37), channel_id=1, source_target_pairs={{0,4},{2,6},{4,0},{6,2},{8,12},{10,14},{12,8},{14,10},{16,20},{18,... | collective-permute-start | bytes 1572872 | tf_op jit(solution)/shard_map/ppermute | solution.py:58
  448.9 36.4 %collective-permute-start.52 = (bf16[256,1024]{1,0:T(8,128)(2,1)}, bf16[256,1024]{1,0:T(8,128)(2,1)S(1)}, u32[]{:S(2)}, u32[]{:S(2)}) collective-permute-start(bf16[256,1024]{1,0:T(8,128)(2,1)} %add_convert_fusion.11), channel_id=1, source_target_pairs={{0,24},{2,26},{4,28},{6,30},{8,0},{10,2},{12,4},{14,6},{16,8},{18,... | collective-permute-start | bytes 1572872 | tf_op jit(solution)/shard_map/ppermute | solution.py:58
  449.4 35.9 %collective-permute-start.51 = (bf16[256,2048]{1,0:T(8,128)(2,1)S(1)}, bf16[256,2048]{1,0:T(8,128)(2,1)S(1)}, u32[]{:S(2)}, u32[]{:S(2)}) collective-permute-start(bf16[256,2048]{1,0:T(8,128)(2,1)S(1)} %add_convert_fusion.5), channel_id=1, source_target_pairs={{0,8},{2,10},{4,12},{6,14},{8,16},{10,18},{12,20},{14,22},{16,24},... | collective-permute-start | bytes 3145736 | tf_op jit(solution)/shard_map/ppermute | solution.py:58
  451.4 33.9 %collective-permute-start.49 = (bf16[256,2048]{1,0:T(8,128)(2,1)S(1)}, bf16[256,2048]{1,0:T(8,128)(2,1)S(1)}, u32[]{:S(2)}, u32[]{:S(2)}) collective-permute-start(bf16[256,2048]{1,0:T(8,128)(2,1)S(1)} %copy-done.54), channel_id=1, source_target_pairs={{0,4},{2,6},{4,0},{6,2},{8,12},{10,14},{12,8},{14,10},{16,20},{18,... | collective-permute-start | bytes 3145736 | tf_op jit(solution)/shard_map/ppermute | solution.py:58
  470.9 14.4 %collective-permute-start.53 = (bf16[512,2048]{1,0:T(8,128)(2,1)S(1)}, bf16[512,2048]{1,0:T(8,128)(2,1)S(1)}, u32[]{:S(2)}, u32[]{:S(2)}) collective-permute-start(bf16[512,2048]{1,0:T(8,128)(2,1)S(1)} %convolution_convert_fusion.7), channel_id=1, source_target_pairs={{0,2},{2,0},{4,6},{6,4},{8,10},{10,8},{12,14},{14,12},{16,18},{18,... | collective-permute-start | bytes 6291464 | tf_op jit(solution)/shard_map/ppermute | solution.py:70
  487.3 24.7 %collective-permute-start.54 = (bf16[256,2048]{1,0:T(8,128)(2,1)S(1)}, bf16[256,2048]{1,0:T(8,128)(2,1)S(1)}, u32[]{:S(2)}, u32[]{:S(2)}) collective-permute-start(bf16[256,2048]{1,0:T(8,128)(2,1)S(1)} %copy-done.53), channel_id=1, source_target_pairs={{0,4},{2,6},{4,0},{6,2},{8,12},{10,14},{12,8},{14,10},{16,20},{18,... | collective-permute-start | bytes 3145736 | tf_op jit(solution)/shard_map/ppermute | solution.py:58
  487.8 24.2 %collective-permute-start.55 = (bf16[256,2048]{1,0:T(8,128)(2,1)S(1)}, bf16[256,2048]{1,0:T(8,128)(2,1)S(1)}, u32[]{:S(2)}, u32[]{:S(2)}) collective-permute-start(bf16[256,2048]{1,0:T(8,128)(2,1)S(1)} %add_convert_fusion.4), channel_id=1, source_target_pairs={{0,24},{2,26},{4,28},{6,30},{8,0},{10,2},{12,4},{14,6},{16,8},{18,... | collective-permute-start | bytes 3145736 | tf_op jit(solution)/shard_map/ppermute | solution.py:58
  500.2 46.3 %collective-permute-start.56 = (bf16[512,2048]{1,0:T(8,128)(2,1)}, bf16[512,2048]{1,0:T(8,128)(2,1)}, u32[]{:S(2)}, u32[]{:S(2)}) collective-permute-start(bf16[512,2048]{1,0:T(8,128)(2,1)} %add_convert_fusion.d_a), channel_id=1, source_target_pairs={{0,1},{1,0},{2,3},{3,2},{4,5},{5,4},{6,7},{7,6},{8,9},{9,8},{10,11... | collective-permute-start | bytes 6291464 | tf_op jit(solution)/shard_map/ppermute | solution.py:80
  512.0 23.6 %collective-permute-start.57 = (bf16[1024,512]{1,0:T(8,128)(2,1)}, bf16[1024,512]{1,0:T(8,128)(2,1)}, u32[]{:S(2)}, u32[]{:S(2)}) collective-permute-start(bf16[1024,512]{1,0:T(8,128)(2,1)} %fusion.27), channel_id=1, source_target_pairs={{0,4},{2,6},{4,0},{6,2},{8,12},{10,14},{12,8},{14,10},{16,20},{18,... | collective-permute-start | bytes 3145736 | tf_op jit(solution)/shard_map/ppermute | solution.py:58
  518.7 18.1 %collective-permute-start.58 = (f32[128,2048]{1,0:T(8,128)}, f32[128,2048]{1,0:T(8,128)}, u32[]{:S(2)}, u32[]{:S(2)}) collective-permute-start(f32[128,2048]{1,0:T(8,128)} %get-tuple-element.386), channel_id=1, source_target_pairs={{0,2},{2,0},{4,6},{6,4},{8,10},{10,8},{12,14},{14,12},{16,18},{18,... | collective-permute-start | bytes 3145736 | tf_op jit(solution)/shard_map/ppermute | solution.py:70
  538.0 25.6 %collective-permute-start.60 = (bf16[256,512]{1,0:T(8,128)(2,1)S(1)}, bf16[256,512]{1,0:T(8,128)(2,1)S(1)}, u32[]{:S(2)}, u32[]{:S(2)}) collective-permute-start(bf16[256,512]{1,0:T(8,128)(2,1)S(1)} %get-tuple-element.289), channel_id=1, source_target_pairs={{0,24},{2,26},{4,28},{6,30},{8,0},{10,2},{12,4},{14,6},{16,8},{18,... | collective-permute-start | bytes 786440 | tf_op jit(solution)/shard_map/ppermute | solution.py:58
  541.3 22.4 %collective-permute-start.61 = (bf16[256,512]{1,0:T(8,128)(2,1)S(1)}, bf16[256,512]{1,0:T(8,128)(2,1)S(1)}, u32[]{:S(2)}, u32[]{:S(2)}) collective-permute-start(bf16[256,512]{1,0:T(8,128)(2,1)S(1)} %get-tuple-element.291), channel_id=1, source_target_pairs={{0,8},{2,10},{4,12},{6,14},{8,16},{10,18},{12,20},{14,22},{16,24},... | collective-permute-start | bytes 786440 | tf_op jit(solution)/shard_map/ppermute | solution.py:58
  541.3 22.4 %collective-permute-start.59 = (bf16[256,1536]{1,0:T(8,128)(2,1)}, bf16[256,1536]{1,0:T(8,128)(2,1)S(1)}, u32[]{:S(2)}, u32[]{:S(2)}) collective-permute-start(bf16[256,1536]{1,0:T(8,128)(2,1)} %get-tuple-element.287), channel_id=1, source_target_pairs={{0,4},{2,6},{4,0},{6,2},{8,12},{10,14},{12,8},{14,10},{16,20},{18,... | collective-permute-start | bytes 2359304 | tf_op jit(solution)/shard_map/ppermute | solution.py:58
  564.9 10.0 %collective-permute-start.64 = (bf16[256,512]{1,0:T(8,128)(2,1)S(1)}, bf16[256,512]{1,0:T(8,128)(2,1)S(1)}, u32[]{:S(2)}, u32[]{:S(2)}) collective-permute-start(bf16[256,512]{1,0:T(8,128)(2,1)S(1)} %add_convert_fusion.14), channel_id=1, source_target_pairs={{0,24},{2,26},{4,28},{6,30},{8,0},{10,2},{12,4},{14,6},{16,8},{18,... | collective-permute-start | bytes 786440 | tf_op jit(solution)/shard_map/ppermute | solution.py:58
  568.3 21.1 %collective-permute-start.63 = (bf16[256,1536]{1,0:T(8,128)(2,1)S(1)}, bf16[256,1536]{1,0:T(8,128)(2,1)S(1)}, u32[]{:S(2)}, u32[]{:S(2)}) collective-permute-start(bf16[256,1536]{1,0:T(8,128)(2,1)S(1)} %add_convert_fusion.10), channel_id=1, source_target_pairs={{0,24},{2,26},{4,28},{6,30},{8,0},{10,2},{12,4},{14,6},{16,8},{18,... | collective-permute-start | bytes 2359304 | tf_op jit(solution)/shard_map/ppermute | solution.py:58
  568.7 20.8 %collective-permute-start.62 = (bf16[256,1536]{1,0:T(8,128)(2,1)S(1)}, bf16[256,1536]{1,0:T(8,128)(2,1)S(1)}, u32[]{:S(2)}, u32[]{:S(2)}) collective-permute-start(bf16[256,1536]{1,0:T(8,128)(2,1)S(1)} %copy-done.55), channel_id=1, source_target_pairs={{0,4},{2,6},{4,0},{6,2},{8,12},{10,14},{12,8},{14,10},{16,20},{18,... | collective-permute-start | bytes 2359304 | tf_op jit(solution)/shard_map/ppermute | solution.py:58
  573.3 16.2 %collective-permute-start.65 = (f32[128,2048]{1,0:T(8,128)S(1)}, f32[128,2048]{1,0:T(8,128)S(1)}, u32[]{:S(2)}, u32[]{:S(2)}) collective-permute-start(f32[128,2048]{1,0:T(8,128)S(1)} %get-tuple-element.384), channel_id=1, source_target_pairs={{0,2},{2,0},{4,6},{6,4},{8,10},{10,8},{12,14},{14,12},{16,18},{18,... | collective-permute-start | bytes 3145736 | tf_op jit(solution)/shard_map/ppermute | solution.py:70
  590.7 28.3 %collective-permute-start.67 = (bf16[256,1536]{1,0:T(8,128)(2,1)}, bf16[256,1536]{1,0:T(8,128)(2,1)}, u32[]{:S(2)}, u32[]{:S(2)}) collective-permute-start(bf16[256,1536]{1,0:T(8,128)(2,1)} %add_convert_fusion.9), channel_id=1, source_target_pairs={{0,8},{2,10},{4,12},{6,14},{8,16},{10,18},{12,20},{14,22},{16,24},... | collective-permute-start | bytes 2359304 | tf_op jit(solution)/shard_map/ppermute | solution.py:58
  591.0 28.0 %collective-permute-start.66 = (bf16[256,1536]{1,0:T(8,128)(2,1)}, bf16[256,1536]{1,0:T(8,128)(2,1)}, u32[]{:S(2)}, u32[]{:S(2)}) collective-permute-start(bf16[256,1536]{1,0:T(8,128)(2,1)} %get-tuple-element.313), channel_id=1, source_target_pairs={{0,4},{2,6},{4,0},{6,2},{8,12},{10,14},{12,8},{14,10},{16,20},{18,... | collective-permute-start | bytes 2359304 | tf_op jit(solution)/shard_map/ppermute | solution.py:58
  597.4 16.1 %all-to-all-start = ((f32[16,1,1792]{2,1,0:T(1,128)}), f32[16,1,1792]{2,1,0:T(1,128)S(1)}, u32[]{:S(2)}, u32[]{:S(2)}) async-start(f32[16,1,1792]{2,1,0:T(1,128)} %reshape.128), calls=%async_computation | async-start | bytes 229376 | tf_op jit(solution)/shard_map/all_to_all | solution.py:729
  621.1 19.8 %collective-permute-start.68 = (bf16[256,1536]{1,0:T(8,128)(2,1)}, bf16[256,1536]{1,0:T(8,128)(2,1)S(1)}, u32[]{:S(2)}, u32[]{:S(2)}) collective-permute-start(bf16[256,1536]{1,0:T(8,128)(2,1)} %get-tuple-element.318), channel_id=1, source_target_pairs={{0,4},{2,6},{4,0},{6,2},{8,12},{10,14},{12,8},{14,10},{16,20},{18,... | collective-permute-start | bytes 2359304 | tf_op jit(solution)/shard_map/ppermute | solution.py:58
  621.9 19.3 %collective-permute-start.69 = (bf16[256,1536]{1,0:T(8,128)(2,1)S(1)}, bf16[256,1536]{1,0:T(8,128)(2,1)S(1)}, u32[]{:S(2)}, u32[]{:S(2)}) collective-permute-start(bf16[256,1536]{1,0:T(8,128)(2,1)S(1)} %add_convert_fusion.8), channel_id=1, source_target_pairs={{0,24},{2,26},{4,28},{6,30},{8,0},{10,2},{12,4},{14,6},{16,8},{18,... | collective-permute-start | bytes 2359304 | tf_op jit(solution)/shard_map/ppermute | solution.py:58
  (90 other events, 1663.8 us)

commit v4 on v3

--- a/solution.py
+++ b/solution.py
@@ -459,17 +459,6 @@
                 [by_z[kz][kx] for kx in range(grid.x) for kz in range(grid.z)], axis=0
             )
 
-        def summed(value, weight, between=None):
-            part = matmul(ph.begin(value[rows:]), weight, True).astype(BF16)
-            ph.end(part)
-            theirs = ph.send_core(part)
-            if between is not None:
-                between()
-            part = matmul(ph.begin(value[:rows]), weight, True) + theirs.astype(F32)
-            part = part.astype(BF16)
-            ph.end(part)
-            return ph.across(part)
-
         def from_both(theirs, value, weight, between=None):
             if between is not None:
                 between()
@@ -539,24 +528,19 @@
         attend = functools.partial(attend_kernel, local_heads)
         mixed = by_image(attend, length, local_width, ph.begin(qkv))
         ph.end(mixed)
+        w_o = jnp.concatenate([z_o[kz][kx] for kx in range(grid.x) for kz in range(grid.z)], axis=0)
+        att_part = matmul(ph.begin(mixed)[rows:], w_o, True).astype(BF16)
+        ph.end(att_part)
+        att_part = ph.hand_over(att_part)
         ph.close()
 
         z_u = {1: ph.send_z(s_u, 1)}
         x_d = {0: ph.gather_x(s_d)}
-        w_o = jnp.concatenate([z_o[kz][kx] for kx in range(grid.x) for kz in range(grid.z)], axis=0)
-        from_cotangent = []
-
-        def take_cotangent():
-            from_cotangent.extend(
-                by_rows(
-                    cotangent_kernel, relative, present, [flat(turn_in(ph.begin(cotangent)))], mods,
-                    [BF16, BF16],
-                )
-            )
-            ph.end(from_cotangent[1])
-
-        att = summed(mixed, w_o, take_cotangent)
-        dy, d_mlp_own = from_cotangent
+        att = from_both(att_part, mixed, w_o)
+        dy, d_mlp_own = by_rows(
+            cotangent_kernel, relative, present, [flat(turn_in(ph.begin(cotangent)))], mods, [BF16, BF16]
+        )
+        ph.end(d_mlp_own)
         ph.close()
 
         z_u[3] = ph.send_z(s_u, 3)
@@ -614,39 +598,44 @@
         w_d = whole(x_d[0], x_d[1], x_d[2], x_d[3])
         d_up = (matmul(ph.begin(d_mlp), w_d) * slope).astype(BF16)
         ph.end(d_up)
-        up = {}
         d_second_part = matmul(ph.begin(d_up)[rows:], w_u, True).astype(BF16)
         ph.end(d_second_part)
         d_second_part = ph.hand_over(d_second_part)
-        ph.close()
+        a_1 = ph.begin(plus(part(first, 1), ph.now(a_2)).astype(BF16))
+        ph.end(a_1)
+        ph.close()
+
+        x_b[0] = ph.reduce_x(rows_of(other, 0, 2))
+        a_1 = ph.send_z(a_1, 3)
+        d_second = from_both(d_second_part, d_up, w_u)
+        up = {}
 
         def up_dots(blocks):
             for kx in blocks:
                 up[kx] = grid.dots(ph.begin(second), d_up, kx)
                 ph.end(up[kx])
 
-        x_b[0] = ph.reduce_x(rows_of(other, 0, 2))
-        a_1 = ph.send_z(plus(part(first, 1), ph.now(a_2)).astype(BF16), 3)
-        d_second = from_both(d_second_part, d_up, w_u)
         up_dots(turns[:-1])
+        b_part = lambda kz: ph.now(x_b[kz // 2 * 2][(kz % 2) * blk : (kz % 2 + 1) * blk])
+        b_sum = lambda kz: plus(rows_of(other, kz, kz + 1)[0], b_part(kz))
+        b_2, b_3 = (ph.begin(b_sum(kz).astype(BF16)) for kz in (2, 3))
+        ph.end(b_2, b_3)
         ph.close()
 
         up_rows = lambda kz: ph.reduce_x(rows_of(up, kz, kz + 1))
         x_up = {2: up_rows(2)}
-        b_part = lambda kz: ph.now(x_b[kz // 2 * 2][(kz % 2) * blk : (kz % 2 + 1) * blk])
-        b_sum = lambda kz: plus(rows_of(other, kz, kz + 1)[0], b_part(kz))
-        b_2 = ph.send_z(b_sum(2).astype(BF16), 3)
-        b_3 = ph.send_z(b_sum(3).astype(BF16), 1)
+        b_2 = ph.send_z(b_2, 3)
+        b_3 = ph.send_z(b_3, 1)
         up_dots(turns[-1:])
-        mlp_part = matmul(ph.begin(act)[rows:], w_d, True).astype(BF16)
-        ph.end(mlp_part)
-        mlp_part = ph.hand_over(mlp_part)
+        first_sum = ph.begin(plus(part(first, 0), ph.now(a_3), ph.now(a_1)))
+        ph.end(first_sum)
         ph.close()
 
         x_up[3] = up_rows(3)
         up_sum = lambda kz: plus(rows_of(up, kz, kz + 1)[0], ph.now(x_up[kz]))
         u_2 = ph.send_z(up_sum(2).astype(BF16), 3)
-        mlp = from_both(mlp_part, act, w_d)
+        b_1 = ph.begin((b_sum(1) + ph.now(b_2).astype(F32)).astype(BF16))
+        ph.end(b_1)
         d_second[-1] = ph.begin(d_second[-1])
         d_hidden, d_att_own, sums2 = by_rows(
             second_back_kernel, relative, present, [hidden, *two(att), *two(d_second), dy], mods,
@@ -657,10 +646,9 @@
         ph.close()
 
         x_up[1] = up_rows(1)
-        first_sum = plus(part(first, 0), a_3, ph.now(a_1))
         x_first = ph.reduce_x(first_sum.astype(BF16))
         u_3 = ph.send_z(up_sum(3).astype(BF16), 1)
-        b_1 = ph.send_z((b_sum(1) + ph.now(b_2).astype(F32)).astype(BF16), 3)
+        b_1 = ph.send_z(b_1, 3)
         d_att = join(d_att_own, ph.begin(d_att_other))
         d_mixed = matmul(d_att, w_o).astype(BF16)
         ph.end(d_mixed)
@@ -675,21 +663,18 @@
         x_up[0] = up_rows(0)
         u_1 = ph.send_z((up_sum(1) + ph.now(u_2).astype(F32)).astype(BF16), 3)
         d_normed = from_both(d_normed_part, d_qkv, w_a)
-        mlp[-1] = ph.begin(mlp[-1])
-        ph.end(mlp[-1])
         out = dots(d_att, mixed)
         proj = dots(normed, d_qkv)
         ph.close()
 
         x_out = ph.reduce_x(out)
-        mlp[-1] = ph.begin(mlp[-1])
-        block_out, sums3 = by_rows(
-            block_out_kernel, relative, present, [hidden, *two(mlp), dy], mods, [BF16], 1
-        )
-        ph.end(block_out)
+        mlp_part = matmul(ph.begin(act)[rows:], w_d, True).astype(BF16)
+        ph.end(mlp_part)
+        mlp_part = ph.send_core(mlp_part)
         up_total = up_sum(0) + ph.now(u_3).astype(F32) + ph.now(u_1).astype(F32)
         up_mine, up_theirs = grid.halves(ph.begin(up_total), 0)
         ph.end(up_mine)
+        mlp = from_both(mlp_part, act, w_d)
         up_theirs = ph.hand_over(up_theirs)
         ph.close()
 
@@ -711,23 +696,26 @@
         x_p[3] = p_rows(3)
         p_2 = ph.send_z(p_sum(2).astype(BF16), 3)
         o_1 = ph.send_z((out_sum(1) + ph.now(o_2).astype(F32)).astype(BF16), 3)
-        row_sums = [jnp.sum(v.reshape(count, -1, 8, width), axis=2) for v in (sums1, sums2, sums3)]
-        bin_row = jnp.broadcast_to(bins.astype(F32)[:, None, None], (count, 1, width))
-        d_mods = ph.begin(turn_out(jnp.concatenate(row_sums, axis=1)))
-        d_mods = jnp.concatenate([d_mods, bin_row], axis=1)
-        ph.end(d_mods)
         down_low = plus(ph.now(first_sum)[0], x_first)
         down_high = b_sum(0) + ph.now(b_3).astype(F32) + ph.now(b_1).astype(F32)
         down_total = ph.begin(jnp.concatenate([down_low, down_high], axis=1))
         down_mine, down_theirs = grid.halves(down_total, 0)
-        ph.end(down_mine, d_mods)
+        ph.end(down_mine)
         down_theirs = ph.hand_over(down_theirs)
         ph.close(20.0)
 
         x_p[1] = p_rows(1)
         p_3 = ph.send_z(p_sum(3).astype(BF16), 1)
-        d_mods = lax.all_to_all(ph.now(d_mods), "dp", split_axis=2, concat_axis=0, tiled=True)
-        ph.results.append(d_mods)
+        mlp[-1] = ph.begin(mlp[-1])
+        block_out, sums3 = by_rows(
+            block_out_kernel, relative, present, [hidden, *two(mlp), dy], mods, [BF16], 1
+        )
+        row_sums = [jnp.sum(v.reshape(count, -1, 8, width), axis=2) for v in (sums1, sums2, sums3)]
+        bin_row = jnp.broadcast_to(bins.astype(F32)[:, None, None], (count, 1, width))
+        d_mods = turn_out(jnp.concatenate(row_sums, axis=1))
+        d_mods = jnp.concatenate([d_mods, bin_row], axis=1)
+        ph.end(d_mods)
+        d_mods = lax.all_to_all(d_mods, "dp", split_axis=2, concat_axis=0, tiled=True)
         up_part = grid.by_core(ph.begin(up_mine), up_theirs, 1)
         ph.end(up_part)
         ph.close(20.0)

time: 658 us -> 635 us (0.965)
  waiting for transfers between devices: 256 us -> 237 us
    ppermute x4, waiting for transfers between devices: 28.6 us -> 0.01 us  [across(): out.append(lax.ppermute(out[-1], 'mp', self.turn))]
    ppermute x52, waiting for transfers between devices: 209 us -> 222 us  [send(): out = lax.ppermute(value, 'dp', self.ring(dz, dx, 0))]
    unnamed x190 -> x178, local copies, waits for them, and re-layouts: 44.8 us -> 40.9 us
  transfers between devices with their start and end apart: 73 -> 73, of which waited for: 35 -> 35; matrix products, arithmetic and copies ran while one was open for 33% -> 35% of each run, Pallas kernels for 10% -> 10%
where the time goes in v4:
time: 635 us; the launch traced here: 625 us
  waiting for transfers between devices  237 us (37%)
  matrix products  133 us (21%)
  starting transfers between devices  84.5 us (13%)
  Pallas kernels  64.6 us (10%)
  local copies, waits for them, and re-layouts  60.1 us (9%)
  other arithmetic  42.8 us (7%)
    ppermute x52, waiting for transfers between devices, send(): out = lax.ppermute(value, 'dp', self.ring(dz, dx, 0))  222 us
    dot_general x12, matrix products, matmul(): lax.dot_general(lhs, rhs, (((1,), (1 if turned else 0,)), ((), ())), pref...  95.9 us
    ppermute x52, starting transfers between devices, send(): out = lax.ppermute(value, 'dp', self.ring(dz, dx, 0))  70.5 us
    pallas_call x6, Pallas kernels, by_rows(): pl.pallas_call(functools.partial(kernel, blocks), grid_spec=pltpu.Prefetc...  46.4 us
    unnamed x178, local copies, waits for them, and re-layouts  40.9 us
    dot_general x8, matrix products, dots(): lax.dot_general(lhs[:, kx * width:(kx + 1) * width], rhs, (((0,), (0,)),...  35.3 us
    pallas_call x2, Pallas kernels, by_image(): pl.pallas_call(kernel, grid=(rows // length,), in_specs=[block(operand.sh...  13.4 us
  transfers between devices with their start and end apart: 73, of which 35 were waited for; matrix products, arithmetic and copies ran while one was open for 35% of the time, Pallas kernels for 10%

profile of v4, /device:TPU:0, one launch (start us, length us, event | category | flops | bytes accessed | tf_op | source)
XLA Modules:
  0.0 624.8 jit_solution(3869232771465557226)
XLA Ops:
  7.8 2.6 collective-permute-start.2
  14.9 4.8 shard_map.144
  20.7 13.4 %collective-permute-done.4 = bf16[256,512]{1,0:T(8,128)(2,1)S(1)} collective-permute-done((bf16[256,512]{1,0:T(8,128)(2,1)S(1)}, bf16[256,512]{1,0:T(8,128)(2,1)S(1)}, u32[]{:S(2)}, u32[]{:S(2)}) %collective-permute-start.4) | collective-permute-done | bytes 262176 | tf_op jit(solution)/shard_map/ppermute | solution.py:58
  34.2 3.9 collective-permute-start.6
  41.2 7.8 %shard_map.145 = (bf16[512,2048]{1,0:T(8,128)(2,1)S(1)}, bf16[512,2048]{1,0:T(8,128)(2,1)S(1)}) custom-call(s32[8]{0:T(128)S(1)} %copy-done.8, s32[2]{0:T(128)S(1)} %copy-done.11, bf16[512,2048]{1,0:T(8,128)(2,1)S(1)} %bitcast.98, f32[2,6,2048]{2,1,0:T(8,128)S(1)} %reshape.117.mods_ref), custom_call_target="tpu_custom_call" | custom-call | flops 6291456000 | bytes 8388608 | tf_op jit(solution)/shard_map/pallas_call | solution.py:421
  49.1 3.0 constant_dynamic-update-slice_fusion.8
  52.2 2.4 collective-permute-done.6
  54.6 2.4 collective-permute-done.7
  62.1 14.7 %collective-permute-done.9 = bf16[256,1536]{0,1:T(8,128)(2,1)S(1)} collective-permute-done((bf16[256,1536]{0,1:T(8,128)(2,1)}, bf16[256,1536]{0,1:T(8,128)(2,1)S(1)}, u32[]{:S(2)}, u32[]{:S(2)}) %collective-permute-start.9) | collective-permute-done | bytes 786464 | tf_op jit(solution)/shard_map/ppermute | solution.py:58
  80.1 9.8 %collective-permute-done.11 = bf16[2,256,512]{2,1,0:T(8,128)(2,1)S(1)} collective-permute-done((bf16[2,256,512]{2,1,0:T(8,128)(2,1)S(1)}, bf16[2,256,512]{2,1,0:T(8,128)(2,1)S(1)}, u32[]{:S(2)}, u32[]{:S(2)}) %collective-permute-start.11) | collective-permute-done | bytes 524320 | tf_op jit(solution)/shard_map/ppermute | solution.py:58
  91.2 2.5 collective-permute-done.12
  93.7 3.5 collective-permute-start.14
  99.0 7.0 %convolution_convert_fusion.qkv_ref = bf16[1024,1536]{1,0:T(8,128)(2,1)S(1)} fusion(bf16[1024,2048]{1,0:T(8,128)(2,1)S(1)} %constant_dynamic-update-slice_fusion, bf16[2048,1536]{0,1:T(8,128)(2,1)S(1)} %constant_dynamic-update-slice_fusion.2), kind=kOutput, calls=%fused_computation.31 | convolution fusion | flops 6444023808 | bytes 13631488 | tf_op jit(solution)/shard_map/dot_general | solution.py:438
  106.0 4.5 shard_map.146
  110.5 6.3 %collective-permute-done.15 = bf16[2,256,512]{2,1,0:T(8,128)(2,1)S(1)} collective-permute-done((bf16[2,256,512]{2,1,0:T(8,128)(2,1)S(1)}, bf16[2,256,512]{2,1,0:T(8,128)(2,1)S(1)}, u32[]{:S(2)}, u32[]{:S(2)}) %collective-permute-start.15) | collective-permute-done | bytes 524320 | tf_op jit(solution)/shard_map/ppermute | solution.py:58
  118.5 4.1 collective-permute-done.17
  131.4 18.2 %collective-permute-done.19 = bf16[256,2048]{1,0:T(8,128)(2,1)} collective-permute-done((bf16[256,2048]{1,0:T(8,128)(2,1)S(1)}, bf16[256,2048]{1,0:T(8,128)(2,1)}, u32[]{:S(2)}, u32[]{:S(2)}) %collective-permute-start.19) | collective-permute-done | bytes 1048608 | tf_op jit(solution)/shard_map/ppermute | solution.py:58
  152.9 2.4 constant_dynamic-update-slice_fusion.22
  155.3 19.0 %collective-permute-done.21 = bf16[256,2048]{1,0:T(8,128)(2,1)} collective-permute-done((bf16[256,2048]{1,0:T(8,128)(2,1)S(1)}, bf16[256,2048]{1,0:T(8,128)(2,1)}, u32[]{:S(2)}, u32[]{:S(2)}) %collective-permute-start.21) | collective-permute-done | bytes 1048608 | tf_op jit(solution)/shard_map/ppermute | solution.py:58
  177.6 7.9 %shard_map.148 = (f32[512,2048]{1,0:T(8,128)S(1)}, bf16[512,2048]{1,0:T(8,128)(2,1)S(1)}) custom-call(s32[8]{0:T(128)S(1)} %copy-done.8, s32[2]{0:T(128)S(1)} %copy-done.11, bf16[512,2048]{1,0:T(8,128)(2,1)S(1)} %get-tuple-element.179.tokens_ref, bf16[512,2048]{1,0:T(8,128)(2,1)S(1)} %add_convert_fusion.3.att_a, ...), custom_call_target="tpu_custom_call" | custom-call | flops 6291456000 | bytes 8388608 | tf_op jit(solution)/shard_map/pallas_call | solution.py:421
  185.9 14.5 %collective-permute-done.25 = bf16[256,2048]{1,0:T(8,128)(2,1)S(1)} collective-permute-done((bf16[256,2048]{1,0:T(8,128)(2,1)}, bf16[256,2048]{1,0:T(8,128)(2,1)S(1)}, u32[]{:S(2)}, u32[]{:S(2)}) %collective-permute-start.25) | collective-permute-done | bytes 1048608 | tf_op jit(solution)/shard_map/ppermute | solution.py:58
  208.2 23.3 %collective-permute-done.27 = bf16[256,2048]{1,0:T(8,128)(2,1)S(1)} collective-permute-done((bf16[256,2048]{1,0:T(8,128)(2,1)S(1)}, bf16[256,2048]{1,0:T(8,128)(2,1)S(1)}, u32[]{:S(2)}, u32[]{:S(2)}) %collective-permute-start.27) | collective-permute-done | bytes 1048608 | tf_op jit(solution)/shard_map/ppermute | solution.py:58
  238.4 15.6 %fusion.13 = (bf16[1024,2048]{1,0:T(8,128)(2,1)S(1)}, f32[1024,2048]{1,0:T(8,128)}) fusion(bf16[1024,2048]{1,0:T(8,128)(2,1)} %copy-done.38, bf16[2048,2048]{1,0:T(8,128)(2,1)} %constant_dynamic-update-slice_fusion.16), kind=kOutput, calls=%fused_computation.16 | convolution fusion | flops 8608808960 | bytes 25165824 | tf_op jit(solution)/shard_map/dot_general | solution.py:438
  257.7 4.9 convolution_convert_fusion.6
  262.7 5.0 convolution_convert_fusion.5
  271.0 9.8 %collective-permute-done.31 = bf16[256,2048]{1,0:T(8,128)(2,1)} collective-permute-done((bf16[256,2048]{1,0:T(8,128)(2,1)S(1)}, bf16[256,2048]{1,0:T(8,128)(2,1)}, u32[]{:S(2)}, u32[]{:S(2)}) %collective-permute-start.31) | collective-permute-done | bytes 1048608 | tf_op jit(solution)/shard_map/ppermute | solution.py:58
  283.9 2.3 constant_dynamic-update-slice_fusion.29
  289.5 12.2 %collective-permute-done.33 = bf16[256,2048]{1,0:T(8,128)(2,1)S(1)} collective-permute-done((bf16[256,2048]{1,0:T(8,128)(2,1)}, bf16[256,2048]{1,0:T(8,128)(2,1)S(1)}, u32[]{:S(2)}, u32[]{:S(2)}) %collective-permute-start.33) | collective-permute-done | bytes 1048608 | tf_op jit(solution)/shard_map/ppermute | solution.py:58
  307.3 18.1 %multiply_convert_fusion = bf16[1024,2048]{1,0:T(8,128)(2,1)} fusion(bf16[1024,2048]{1,0:T(8,128)(2,1)S(1)} %copy-done.35, bf16[2048,2048]{1,0:T(8,128)(2,1)} %constant_dynamic-update-slice_fusion.24, f32[1024,2048]{1,0:T(8,128)} %get-tuple-element.230), kind=kOutput, calls=%fused_computation.17 | convolution fusion | flops 8629780480 | bytes 25165824 | tf_op jit(solution)/shard_map/dot_general | solution.py:438
  325.4 10.0 %convolution_convert_fusion.9 = bf16[512,2048]{1,0:T(8,128)(2,1)} fusion(bf16[2048,2048]{1,0:T(8,128)(2,1)} %constant_dynamic-update-slice_fusion.16, bf16[1024,2048]{1,0:T(8,128)(2,1)} %multiply_convert_fusion), kind=kOutput, calls=%fused_computation.40 | convolution fusion | flops 4296015872 | bytes 12582912 | tf_op jit(solution)/shard_map/dot_general | solution.py:438
  341.0 4.2 collective-permute-start.39
  345.2 8.5 %add_convert_fusion.2.d_a = bf16[512,2048]{1,0:T(8,128)(2,1)S(1)} fusion(bf16[512,2048]{1,0:T(8,128)(2,1)} %copy-done.69, bf16[512,2048]{1,0:T(8,128)(2,1)S(1)} %slice-done.1, bf16[2048,2048]{1,0:T(8,128)(2,1)} %constant_dynamic-update-slice_fusion.16), kind=kOutput, calls=%fused_computation.29 | convolution fusion | flops 4298113024 | bytes 14680064 | tf_op jit(solution)/shard_map/dot_general | solution.py:438
  355.3 7.4 %convolution_convert_fusion.4 = bf16[1024,2048]{1,0:T(8,128)(2,1)S(1)} fusion(bf16[1024,2048]{1,0:T(8,128)(2,1)} %multiply_convert_fusion, bf16[1024,2048]{1,0:T(8,128)(2,1)} %copy-done.38), kind=kOutput, calls=%fused_computation.35 | convolution fusion | flops 4297064448 | bytes 10485760 | tf_op jit(solution)/shard_map/dot_general | solution.py:175
  362.7 2.6 add_convert_fusion.12
  368.3 4.3 collective-permute-start.41
  373.2 5.0 convolution_convert_fusion.3
  378.1 3.6 convert_add_fusion.1
  382.7 2.5 collective-permute-done.41
  385.2 10.1 %collective-permute-done.42 = bf16[256,1024]{1,0:T(8,128)(2,1)S(1)} collective-permute-done((bf16[256,1024]{1,0:T(8,128)(2,1)}, bf16[256,1024]{1,0:T(8,128)(2,1)S(1)}, u32[]{:S(2)}, u32[]{:S(2)}) %collective-permute-start.42) | collective-permute-done | bytes 524320 | tf_op jit(solution)/shard_map/ppermute | solution.py:58
  397.2 3.8 collective-permute-start.44
  402.9 14.1 %shard_map.149 = (f32[512,2048]{1,0:T(8,128)}, bf16[512,2048]{1,0:T(8,128)(2,1)S(1)}, f32[2,24,2048]{2,1,0:T(8,128)S(1)}) custom-call(s32[8]{0:T(128)S(1)} %copy-done.8, s32[2]{0:T(128)S(1)} %copy-done.11, f32[512,2048]{1,0:T(8,128)} %copy-done.12, bf16[512,2048]{1,0:T(8,128)(2,1)S(1)} %add_convert_fusion.3.att_a, ...), custom_call_target="tpu_custom_call" | custom-call | flops 6291456000 | bytes 8388608 | tf_op jit(solution)/shard_map/pallas_call | solution.py:421
  418.1 3.3 collective-permute-done.44
  430.9 8.9 %shard_map.150 = bf16[1024,1536]{1,0:T(8,128)(2,1)S(1)} custom-call(bf16[1024,1536]{1,0:T(8,128)(2,1)S(1)} %copy-done.3, bf16[1024,512]{1,0:T(8,128)(2,1)S(1)} %convolution_convert_fusion.11.d_mixed_ref), custom_call_target="tpu_custom_call" | custom-call | flops 3221225472 | bytes 8388608 | tf_op jit(solution)/shard_map/pallas_call | solution.py:249
  439.8 7.5 %convolution_convert_fusion.8 = bf16[512,2048]{1,0:T(8,128)(2,1)S(1)} fusion(bf16[2048,1536]{0,1:T(8,128)(2,1)} %copy-done.63, bf16[1024,1536]{1,0:T(8,128)(2,1)S(1)} %shard_map.150), kind=kOutput, calls=%fused_computation.39 | convolution fusion | flops 3222274048 | bytes 9961472 | tf_op jit(solution)/shard_map/dot_general | solution.py:438
  447.5 11.4 %collective-permute-done.50 = bf16[256,1024]{1,0:T(8,128)(2,1)S(1)} collective-permute-done((bf16[256,1024]{1,0:T(8,128)(2,1)S(1)}, bf16[256,1024]{1,0:T(8,128)(2,1)S(1)}, u32[]{:S(2)}, u32[]{:S(2)}) %collective-permute-start.50) | collective-permute-done | bytes 524320 | tf_op jit(solution)/shard_map/ppermute | solution.py:58
  461.9 6.4 %add_convert_fusion.1.d_a = bf16[512,2048]{1,0:T(8,128)(2,1)S(1)} fusion(bf16[512,2048]{1,0:T(8,128)(2,1)S(1)} %collective-permute-done.51, bf16[512,1536]{1,0:T(8,128)(2,1)S(1)} %slice-done, bf16[2048,1536]{0,1:T(8,128)(2,1)} %copy-done.63), kind=kOutput, calls=%fused_computation.28 | convolution fusion | flops 3224371200 | bytes 12058624 | tf_op jit(solution)/shard_map/dot_general | solution.py:438
  474.4 3.7 convolution_convert_fusion.2
  479.8 4.8 convolution_convert_fusion.1
  485.3 9.1 %convolution_convert_fusion.7 = bf16[512,2048]{1,0:T(8,128)(2,1)} fusion(bf16[2048,2048]{1,0:T(8,128)(2,1)} %constant_dynamic-update-slice_fusion.24, bf16[1024,2048]{1,0:T(8,128)(2,1)S(1)} %copy-done.32), kind=kOutput, calls=%fused_computation.38 | convolution fusion | flops 4296015872 | bytes 12582912 | tf_op jit(solution)/shard_map/dot_general | solution.py:438
  497.9 9.9 %collective-permute-done.56 = bf16[1024,512]{1,0:T(8,128)(2,1)} collective-permute-done((bf16[1024,512]{1,0:T(8,128)(2,1)}, bf16[1024,512]{1,0:T(8,128)(2,1)}, u32[]{:S(2)}, u32[]{:S(2)}) %collective-permute-start.56) | collective-permute-done | bytes 1048608 | tf_op jit(solution)/shard_map/ppermute | solution.py:58
  509.1 8.9 %add_convert_fusion.mlp_a = bf16[512,2048]{1,0:T(8,128)(2,1)S(1)} fusion(bf16[512,2048]{1,0:T(8,128)(2,1)} %collective-permute-done.54, bf16[512,2048]{1,0:T(8,128)(2,1)S(1)} %copy-done.23, bf16[2048,2048]{1,0:T(8,128)(2,1)} %constant_dynamic-update-slice_fusion.24), kind=kOutput, calls=%fused_computation.27 | convolution fusion | flops 4298113024 | bytes 14680064 | tf_op jit(solution)/shard_map/dot_general | solution.py:438
  519.6 3.2 collective-permute-start.59
  525.1 11.7 %shard_map.151 = (f32[512,2048]{1,0:T(8,128)}, f32[2,16,2048]{2,1,0:T(8,128)S(1)}) custom-call(s32[8]{0:T(128)S(1)} %copy-done.8, s32[2]{0:T(128)S(1)} %copy-done.11, bf16[512,2048]{1,0:T(8,128)(2,1)S(1)} %copy-done.16, bf16[512,2048]{1,0:T(8,128)(2,1)S(1)} %add_convert_fusion.1.d_a, bf16[512,2048]{1,0:T(8,128)(2,1)S(1)} %collective-permute-done.61.d_b, ...), custom_call_target="tpu_custom_call" | custom-call | flops 6291456000 | bytes 8388608 | tf_op jit(solution)/shard_map/pallas_call | solution.py:421
  536.9 4.0 collective-permute-done.58
  542.0 3.6 collective-permute-start.64
  552.3 12.4 %collective-permute-done.63 = bf16[256,1536]{1,0:T(8,128)(2,1)S(1)} collective-permute-done((bf16[256,1536]{1,0:T(8,128)(2,1)S(1)}, bf16[256,1536]{1,0:T(8,128)(2,1)S(1)}, u32[]{:S(2)}, u32[]{:S(2)}) %collective-permute-start.63) | collective-permute-done | bytes 786464 | tf_op jit(solution)/shard_map/ppermute | solution.py:58
  564.8 2.8 add_convert_fusion.9
  568.9 3.6 shard_map.152
  573.8 3.7 reshape.128
  577.6 5.7 all-to-all-start
  583.3 3.1 maximum_select_fusion
  586.5 4.5 all-to-all-done
  592.4 3.2 reshape.129
  605.5 12.1 %collective-permute-done.68 = bf16[256,1536]{1,0:T(8,128)(2,1)S(1)} collective-permute-done((bf16[256,1536]{1,0:T(8,128)(2,1)}, bf16[256,1536]{1,0:T(8,128)(2,1)S(1)}, u32[]{:S(2)}, u32[]{:S(2)}) %collective-permute-start.68) | collective-permute-done | bytes 786464 | tf_op jit(solution)/shard_map/ppermute | solution.py:58
  (374 shorter events, 152.6 us)
Async XLA Ops:
  7.8 26.4 %collective-permute-start.2 = (bf16[256,1536]{0,1:T(8,128)(2,1)S(1)}, bf16[256,1536]{0,1:T(8,128)(2,1)}, u32[]{:S(2)}, u32[]{:S(2)}) collective-permute-start(bf16[256,1536]{0,1:T(8,128)(2,1)S(1)} %get-tuple-element.176), channel_id=1, source_target_pairs={{0,4},{2,6},{4,0},{6,2},{8,12},{10,14},{12,8},{14,10},{16,20},{18,... | collective-permute-start | bytes 2359304 | tf_op jit(solution)/shard_map/ppermute | solution.py:58
  10.4 23.7 %collective-permute-start.1 = (bf16[256,1536]{0,1:T(8,128)(2,1)S(1)}, bf16[256,1536]{0,1:T(8,128)(2,1)}, u32[]{:S(2)}, u32[]{:S(2)}) collective-permute-start(bf16[256,1536]{0,1:T(8,128)(2,1)S(1)} %get-tuple-element.176), channel_id=1, source_target_pairs={{0,8},{2,10},{4,12},{6,14},{8,16},{10,18},{12,20},{14,22},{16,24},... | collective-permute-start | bytes 2359304 | tf_op jit(solution)/shard_map/ppermute | solution.py:58
  12.8 21.3 %collective-permute-start.4 = (bf16[256,512]{1,0:T(8,128)(2,1)S(1)}, bf16[256,512]{1,0:T(8,128)(2,1)S(1)}, u32[]{:S(2)}, u32[]{:S(2)}) collective-permute-start(bf16[256,512]{1,0:T(8,128)(2,1)S(1)} %get-tuple-element.374), channel_id=1, source_target_pairs={{0,4},{2,6},{4,0},{6,2},{8,12},{10,14},{12,8},{14,10},{16,20},{18,... | collective-permute-start | bytes 786440 | tf_op jit(solution)/shard_map/ppermute | solution.py:58
  34.2 20.4 %collective-permute-start.6 = (bf16[256,1536]{0,1:T(8,128)(2,1)S(1)}, bf16[256,1536]{0,1:T(8,128)(2,1)S(1)}, u32[]{:S(2)}, u32[]{:S(2)}) collective-permute-start(bf16[256,1536]{0,1:T(8,128)(2,1)S(1)} %get-tuple-element.176), channel_id=1, source_target_pairs={{0,24},{2,26},{4,28},{6,30},{8,0},{10,2},{12,4},{14,6},{16,8},{18,... | collective-permute-start | bytes 2359304 | tf_op jit(solution)/shard_map/ppermute | solution.py:58
  38.1 18.9 %collective-permute-start.7 = (bf16[256,1536]{0,1:T(8,128)(2,1)}, bf16[256,1536]{0,1:T(8,128)(2,1)S(1)}, u32[]{:S(2)}, u32[]{:S(2)}) collective-permute-start(bf16[256,1536]{0,1:T(8,128)(2,1)} %collective-permute-done.1), channel_id=1, source_target_pairs={{0,4},{2,6},{4,0},{6,2},{8,12},{10,14},{12,8},{14,10},{16,20},{18,... | collective-permute-start | bytes 2359304 | tf_op jit(solution)/shard_map/ppermute | solution.py:58
  57.0 19.8 %collective-permute-start.9 = (bf16[256,1536]{0,1:T(8,128)(2,1)}, bf16[256,1536]{0,1:T(8,128)(2,1)S(1)}, u32[]{:S(2)}, u32[]{:S(2)}) collective-permute-start(bf16[256,1536]{0,1:T(8,128)(2,1)} %collective-permute-done.1), channel_id=1, source_target_pairs={{0,8},{2,10},{4,12},{6,14},{8,16},{10,18},{12,20},{14,22},{16,24},... | collective-permute-start | bytes 2359304 | tf_op jit(solution)/shard_map/ppermute | solution.py:58
  57.0 19.8 %collective-permute-start.10 = (bf16[256,1536]{0,1:T(8,128)(2,1)S(1)}, bf16[256,1536]{0,1:T(8,128)(2,1)S(1)}, u32[]{:S(2)}, u32[]{:S(2)}) collective-permute-start(bf16[256,1536]{0,1:T(8,128)(2,1)S(1)} %collective-permute-done.6), channel_id=1, source_target_pairs={{0,4},{2,6},{4,0},{6,2},{8,12},{10,14},{12,8},{14,10},{16,20},{18,... | collective-permute-start | bytes 2359304 | tf_op jit(solution)/shard_map/ppermute | solution.py:58
  76.8 13.1 %collective-permute-start.11 = (bf16[2,256,512]{2,1,0:T(8,128)(2,1)S(1)}, bf16[2,256,512]{2,1,0:T(8,128)(2,1)S(1)}, u32[]{:S(2)}, u32[]{:S(2)}) collective-permute-start(bf16[2,256,512]{2,1,0:T(8,128)(2,1)S(1)} %pad_maximum_fusion.2), channel_id=1, source_target_pairs={{0,8},{2,10},{4,12},{6,14},{8,16},{10,18},{12,20},{14,22},{16,24},... | collective-permute-start | bytes 1572872 | tf_op jit(solution)/shard_map/ppermute | solution.py:58
  76.8 16.9 %collective-permute-start.12 = (bf16[256,1536]{0,1:T(8,128)(2,1)S(1)}, bf16[256,1536]{0,1:T(8,128)(2,1)S(1)}, u32[]{:S(2)}, u32[]{:S(2)}) collective-permute-start(bf16[256,1536]{0,1:T(8,128)(2,1)S(1)} %collective-permute-done.9), channel_id=1, source_target_pairs={{0,4},{2,6},{4,0},{6,2},{8,12},{10,14},{12,8},{14,10},{16,20},{18,... | collective-permute-start | bytes 2359304 | tf_op jit(solution)/shard_map/ppermute | solution.py:58
  78.4 11.5 %collective-permute-start.13 = (bf16[128,2048]{1,0:T(8,128)(2,1)S(1)}, bf16[128,2048]{1,0:T(8,128)(2,1)S(1)}, u32[]{:S(2)}, u32[]{:S(2)}) collective-permute-start(bf16[128,2048]{1,0:T(8,128)(2,1)S(1)} %get-tuple-element.405), channel_id=1, source_target_pairs={{0,2},{2,0},{4,6},{6,4},{8,10},{10,8},{12,14},{14,12},{16,18},{18,... | collective-permute-start | bytes 1572872 | tf_op jit(solution)/shard_map/ppermute | solution.py:70
  93.7 23.1 %collective-permute-start.14 = (bf16[2,256,512]{2,1,0:T(8,128)(2,1)S(1)}, bf16[2,256,512]{2,1,0:T(8,128)(2,1)S(1)}, u32[]{:S(2)}, u32[]{:S(2)}) collective-permute-start(bf16[2,256,512]{2,1,0:T(8,128)(2,1)S(1)} %pad_maximum_fusion.2), channel_id=1, source_target_pairs={{0,24},{2,26},{4,28},{6,30},{8,0},{10,2},{12,4},{14,6},{16,8},{18,... | collective-permute-start | bytes 1572872 | tf_op jit(solution)/shard_map/ppermute | solution.py:58
  97.3 19.6 %collective-permute-start.15 = (bf16[2,256,512]{2,1,0:T(8,128)(2,1)S(1)}, bf16[2,256,512]{2,1,0:T(8,128)(2,1)S(1)}, u32[]{:S(2)}, u32[]{:S(2)}) collective-permute-start(bf16[2,256,512]{2,1,0:T(8,128)(2,1)S(1)} %collective-permute-done.11), channel_id=1, source_target_pairs={{0,8},{2,10},{4,12},{6,14},{8,16},{10,18},{12,20},{14,22},{16,24},... | collective-permute-start | bytes 1572872 | tf_op jit(solution)/shard_map/ppermute | solution.py:58
  97.3 21.2 %collective-permute-start.16 = (bf16[256,2048]{1,0:T(8,128)(2,1)S(1)}, bf16[256,2048]{1,0:T(8,128)(2,1)S(1)}, u32[]{:S(2)}, u32[]{:S(2)}) collective-permute-start(bf16[256,2048]{1,0:T(8,128)(2,1)S(1)} %get-tuple-element.204), channel_id=1, source_target_pairs={{0,4},{2,6},{4,0},{6,2},{8,12},{10,14},{12,8},{14,10},{16,20},{18,... | collective-permute-start | bytes 3145736 | tf_op jit(solution)/shard_map/ppermute | solution.py:58
  122.5 27.1 %collective-permute-start.19 = (bf16[256,2048]{1,0:T(8,128)(2,1)S(1)}, bf16[256,2048]{1,0:T(8,128)(2,1)}, u32[]{:S(2)}, u32[]{:S(2)}) collective-permute-start(bf16[256,2048]{1,0:T(8,128)(2,1)S(1)} %get-tuple-element.204), channel_id=1, source_target_pairs={{0,8},{2,10},{4,12},{6,14},{8,16},{10,18},{12,20},{14,22},{16,24},... | collective-permute-start | bytes 3145736 | tf_op jit(solution)/shard_map/ppermute | solution.py:58
  124.3 25.3 %collective-permute-start.20 = (bf16[256,2048]{1,0:T(8,128)(2,1)S(1)}, bf16[256,2048]{1,0:T(8,128)(2,1)S(1)}, u32[]{:S(2)}, u32[]{:S(2)}) collective-permute-start(bf16[256,2048]{1,0:T(8,128)(2,1)S(1)} %get-tuple-element.219), channel_id=1, source_target_pairs={{0,4},{2,6},{4,0},{6,2},{8,12},{10,14},{12,8},{14,10},{16,20},{18,... | collective-permute-start | bytes 3145736 | tf_op jit(solution)/shard_map/ppermute | solution.py:58
  127.1 50.5 %collective-permute-start.18 = (bf16[512,2048]{1,0:T(8,128)(2,1)S(1)}, bf16[512,2048]{1,0:T(8,128)(2,1)S(1)}, u32[]{:S(2)}, u32[]{:S(2)}) collective-permute-start(bf16[512,2048]{1,0:T(8,128)(2,1)S(1)} %add_convert_fusion.3.att_a), channel_id=1, source_target_pairs={{0,1},{1,0},{2,3},{3,2},{4,5},{5,4},{6,7},{7,6},{8,9},{9,8},{10,11... | collective-permute-start | bytes 6291464 | tf_op jit(solution)/shard_map/ppermute | solution.py:80
  149.6 24.6 %collective-permute-start.21 = (bf16[256,2048]{1,0:T(8,128)(2,1)S(1)}, bf16[256,2048]{1,0:T(8,128)(2,1)}, u32[]{:S(2)}, u32[]{:S(2)}) collective-permute-start(bf16[256,2048]{1,0:T(8,128)(2,1)S(1)} %get-tuple-element.204), channel_id=1, source_target_pairs={{0,24},{2,26},{4,28},{6,30},{8,0},{10,2},{12,4},{14,6},{16,8},{18,... | collective-permute-start | bytes 3145736 | tf_op jit(solution)/shard_map/ppermute | solution.py:58
  151.4 24.0 %collective-permute-start.22 = (bf16[256,2048]{1,0:T(8,128)(2,1)}, bf16[256,2048]{1,0:T(8,128)(2,1)S(1)}, u32[]{:S(2)}, u32[]{:S(2)}) collective-permute-start(bf16[256,2048]{1,0:T(8,128)(2,1)} %collective-permute-done.19), channel_id=1, source_target_pairs={{0,4},{2,6},{4,0},{6,2},{8,12},{10,14},{12,8},{14,10},{16,20},{18,... | collective-permute-start | bytes 3145736 | tf_op jit(solution)/shard_map/ppermute | solution.py:58
  152.9 22.5 %collective-permute-start.23 = (bf16[512,2048]{1,0:T(8,128)(2,1)S(1)}, bf16[512,2048]{1,0:T(8,128)(2,1)S(1)}, u32[]{:S(2)}, u32[]{:S(2)}) collective-permute-start(bf16[512,2048]{1,0:T(8,128)(2,1)S(1)} %get-tuple-element.206), channel_id=1, source_target_pairs={{0,2},{2,0},{4,6},{6,4},{8,10},{10,8},{12,14},{14,12},{16,18},{18,... | collective-permute-start | bytes 6291464 | tf_op jit(solution)/shard_map/ppermute | solution.py:70
  175.4 25.0 %collective-permute-start.25 = (bf16[256,2048]{1,0:T(8,128)(2,1)}, bf16[256,2048]{1,0:T(8,128)(2,1)S(1)}, u32[]{:S(2)}, u32[]{:S(2)}) collective-permute-start(bf16[256,2048]{1,0:T(8,128)(2,1)} %collective-permute-done.19), channel_id=1, source_target_pairs={{0,8},{2,10},{4,12},{6,14},{8,16},{10,18},{12,20},{14,22},{16,24},... | collective-permute-start | bytes 3145736 | tf_op jit(solution)/shard_map/ppermute | solution.py:58
  176.1 30.1 %collective-permute-start.26 = (bf16[256,2048]{1,0:T(8,128)(2,1)}, bf16[256,2048]{1,0:T(8,128)(2,1)}, u32[]{:S(2)}, u32[]{:S(2)}) collective-permute-start(bf16[256,2048]{1,0:T(8,128)(2,1)} %collective-permute-done.21), channel_id=1, source_target_pairs={{0,4},{2,6},{4,0},{6,2},{8,12},{10,14},{12,8},{14,10},{16,20},{18,... | collective-permute-start | bytes 3145736 | tf_op jit(solution)/shard_map/ppermute | solution.py:58
  185.5 20.7 %collective-permute-start.24 = (bf16[512,2048]{1,0:T(8,128)(2,1)S(1)}, bf16[512,2048]{1,0:T(8,128)(2,1)S(1)}, u32[]{:S(2)}, u32[]{:S(2)}) collective-permute-start(bf16[512,2048]{1,0:T(8,128)(2,1)S(1)} %get-tuple-element.212), channel_id=1, source_target_pairs={{0,2},{2,0},{4,6},{6,4},{8,10},{10,8},{12,14},{14,12},{16,18},{18,... | collective-permute-start | bytes 6291464 | tf_op jit(solution)/shard_map/ppermute | solution.py:70
  206.2 25.2 %collective-permute-start.27 = (bf16[256,2048]{1,0:T(8,128)(2,1)S(1)}, bf16[256,2048]{1,0:T(8,128)(2,1)S(1)}, u32[]{:S(2)}, u32[]{:S(2)}) collective-permute-start(bf16[256,2048]{1,0:T(8,128)(2,1)S(1)} %get-tuple-element.219), channel_id=1, source_target_pairs={{0,8},{2,10},{4,12},{6,14},{8,16},{10,18},{12,20},{14,22},{16,24},... | collective-permute-start | bytes 3145736 | tf_op jit(solution)/shard_map/ppermute | solution.py:58
  206.2 25.2 %collective-permute-start.28 = (bf16[256,2048]{1,0:T(8,128)(2,1)}, bf16[256,2048]{1,0:T(8,128)(2,1)S(1)}, u32[]{:S(2)}, u32[]{:S(2)}) collective-permute-start(bf16[256,2048]{1,0:T(8,128)(2,1)} %copy-done.42), channel_id=1, source_target_pairs={{0,4},{2,6},{4,0},{6,2},{8,12},{10,14},{12,8},{14,10},{16,20},{18,... | collective-permute-start | bytes 3145736 | tf_op jit(solution)/shard_map/ppermute | solution.py:58
  231.5 25.6 %collective-permute-start.29 = (bf16[256,2048]{1,0:T(8,128)(2,1)S(1)}, bf16[256,2048]{1,0:T(8,128)(2,1)S(1)}, u32[]{:S(2)}, u32[]{:S(2)}) collective-permute-start(bf16[256,2048]{1,0:T(8,128)(2,1)S(1)} %get-tuple-element.219), channel_id=1, source_target_pairs={{0,24},{2,26},{4,28},{6,30},{8,0},{10,2},{12,4},{14,6},{16,8},{18,... | collective-permute-start | bytes 3145736 | tf_op jit(solution)/shard_map/ppermute | solution.py:58
  233.6 23.5 %collective-permute-start.30 = (bf16[256,2048]{1,0:T(8,128)(2,1)S(1)}, bf16[256,2048]{1,0:T(8,128)(2,1)S(1)}, u32[]{:S(2)}, u32[]{:S(2)}) collective-permute-start(bf16[256,2048]{1,0:T(8,128)(2,1)S(1)} %collective-permute-done.27), channel_id=1, source_target_pairs={{0,4},{2,6},{4,0},{6,2},{8,12},{10,14},{12,8},{14,10},{16,20},{18,... | collective-permute-start | bytes 3145736 | tf_op jit(solution)/shard_map/ppermute | solution.py:58
  257.1 23.7 %collective-permute-start.31 = (bf16[256,2048]{1,0:T(8,128)(2,1)S(1)}, bf16[256,2048]{1,0:T(8,128)(2,1)}, u32[]{:S(2)}, u32[]{:S(2)}) collective-permute-start(bf16[256,2048]{1,0:T(8,128)(2,1)S(1)} %collective-permute-done.27), channel_id=1, source_target_pairs={{0,8},{2,10},{4,12},{6,14},{8,16},{10,18},{12,20},{14,22},{16,24},... | collective-permute-start | bytes 3145736 | tf_op jit(solution)/shard_map/ppermute | solution.py:58
  257.1 23.7 %collective-permute-start.32 = (bf16[256,2048]{1,0:T(8,128)(2,1)S(1)}, bf16[256,2048]{1,0:T(8,128)(2,1)S(1)}, u32[]{:S(2)}, u32[]{:S(2)}) collective-permute-start(bf16[256,2048]{1,0:T(8,128)(2,1)S(1)} %collective-permute-done.29), channel_id=1, source_target_pairs={{0,4},{2,6},{4,0},{6,2},{8,12},{10,14},{12,8},{14,10},{16,20},{18,... | collective-permute-start | bytes 3145736 | tf_op jit(solution)/shard_map/ppermute | solution.py:58
  280.8 20.8 %collective-permute-start.33 = (bf16[256,2048]{1,0:T(8,128)(2,1)}, bf16[256,2048]{1,0:T(8,128)(2,1)S(1)}, u32[]{:S(2)}, u32[]{:S(2)}) collective-permute-start(bf16[256,2048]{1,0:T(8,128)(2,1)} %collective-permute-done.31), channel_id=1, source_target_pairs={{0,4},{2,6},{4,0},{6,2},{8,12},{10,14},{12,8},{14,10},{16,20},{18,... | collective-permute-start | bytes 3145736 | tf_op jit(solution)/shard_map/ppermute | solution.py:58
  281.6 20.4 %collective-permute-start.34 = (bf16[2,256,1024]{2,1,0:T(8,128)(2,1)S(1)}, bf16[2,256,1024]{2,1,0:T(8,128)(2,1)S(1)}, u32[]{:S(2)}, u32[]{:S(2)}) collective-permute-start(bf16[2,256,1024]{2,1,0:T(8,128)(2,1)S(1)} %get-tuple-element.229), channel_id=1, source_target_pairs={{0,24},{2,26},{4,28},{6,30},{8,0},{10,2},{12,4},{14,6},{16,8},{18,... | collective-permute-start | bytes 3145736 | tf_op jit(solution)/shard_map/ppermute | solution.py:58
  302.9 35.0 %collective-permute-start.35 = (bf16[512,1024]{1,0:T(8,128)(2,1)S(1)}, bf16[512,1024]{1,0:T(8,128)(2,1)S(1)}, u32[]{:S(2)}, u32[]{:S(2)}) collective-permute-start(bf16[512,1024]{1,0:T(8,128)(2,1)S(1)} %get-tuple-element.232), channel_id=1, source_target_pairs={{0,4},{2,6},{4,0},{6,2},{8,12},{10,14},{12,8},{14,10},{16,20},{18,... | collective-permute-start | bytes 3145736 | tf_op jit(solution)/shard_map/ppermute | solution.py:58
  305.0 33.0 %collective-permute-start.36 = (bf16[2,256,1024]{2,1,0:T(8,128)(2,1)S(1)}, bf16[2,256,1024]{2,1,0:T(8,128)(2,1)}, u32[]{:S(2)}, u32[]{:S(2)}) collective-permute-start(bf16[2,256,1024]{2,1,0:T(8,128)(2,1)S(1)} %get-tuple-element.233), channel_id=1, source_target_pairs={{0,8},{2,10},{4,12},{6,14},{8,16},{10,18},{12,20},{14,22},{16,24},... | collective-permute-start | bytes 3145736 | tf_op jit(solution)/shard_map/ppermute | solution.py:58
  339.7 27.8 %collective-permute-start.38 = (bf16[512,1024]{1,0:T(8,128)(2,1)}, bf16[512,1024]{1,0:T(8,128)(2,1)S(1)}, u32[]{:S(2)}, u32[]{:S(2)}) collective-permute-start(bf16[512,1024]{1,0:T(8,128)(2,1)} %get-tuple-element.239), channel_id=1, source_target_pairs={{0,4},{2,6},{4,0},{6,2},{8,12},{10,14},{12,8},{14,10},{16,20},{18,... | collective-permute-start | bytes 3145736 | tf_op jit(solution)/shard_map/ppermute | solution.py:58
  341.0 27.2 %collective-permute-start.39 = (bf16[2,256,1024]{2,1,0:T(8,128)(2,1)}, bf16[2,256,1024]{2,1,0:T(8,128)(2,1)}, u32[]{:S(2)}, u32[]{:S(2)}) collective-permute-start(bf16[2,256,1024]{2,1,0:T(8,128)(2,1)} %add_convert_fusion.7), channel_id=1, source_target_pairs={{0,24},{2,26},{4,28},{6,30},{8,0},{10,2},{12,4},{14,6},{16,8},{18,... | collective-permute-start | bytes 3145736 | tf_op jit(solution)/shard_map/ppermute | solution.py:58
  353.7 49.1 %collective-permute-start.45 = (bf16[512,2048]{1,0:T(8,128)(2,1)S(1)}, bf16[512,2048]{1,0:T(8,128)(2,1)S(1)}, u32[]{:S(2)}, u32[]{:S(2)}) collective-permute-start(bf16[512,2048]{1,0:T(8,128)(2,1)S(1)} %add_convert_fusion.2.d_a), channel_id=1, source_target_pairs={{0,1},{1,0},{2,3},{3,2},{4,5},{5,4},{6,7},{7,6},{8,9},{9,8},{10,11... | collective-permute-start | bytes 6291464 | tf_op jit(solution)/shard_map/ppermute | solution.py:80
  368.3 17.0 %collective-permute-start.41 = (bf16[256,1024]{1,0:T(8,128)(2,1)}, bf16[256,1024]{1,0:T(8,128)(2,1)S(1)}, u32[]{:S(2)}, u32[]{:S(2)}) collective-permute-start(bf16[256,1024]{1,0:T(8,128)(2,1)} %get-tuple-element.249), channel_id=1, source_target_pairs={{0,24},{2,26},{4,28},{6,30},{8,0},{10,2},{12,4},{14,6},{16,8},{18,... | collective-permute-start | bytes 1572872 | tf_op jit(solution)/shard_map/ppermute | solution.py:58
  372.5 22.8 %collective-permute-start.42 = (bf16[256,1024]{1,0:T(8,128)(2,1)}, bf16[256,1024]{1,0:T(8,128)(2,1)S(1)}, u32[]{:S(2)}, u32[]{:S(2)}) collective-permute-start(bf16[256,1024]{1,0:T(8,128)(2,1)} %get-tuple-element.250), channel_id=1, source_target_pairs={{0,8},{2,10},{4,12},{6,14},{8,16},{10,18},{12,20},{14,22},{16,24},... | collective-permute-start | bytes 1572872 | tf_op jit(solution)/shard_map/ppermute | solution.py:58
  372.5 24.3 %collective-permute-start.40 = (bf16[256,2048]{1,0:T(8,128)(2,1)}, bf16[256,2048]{1,0:T(8,128)(2,1)S(1)}, u32[]{:S(2)}, u32[]{:S(2)}) collective-permute-start(bf16[256,2048]{1,0:T(8,128)(2,1)} %get-tuple-element.248), channel_id=1, source_target_pairs={{0,4},{2,6},{4,0},{6,2},{8,12},{10,14},{12,8},{14,10},{16,20},{18,... | collective-permute-start | bytes 3145736 | tf_op jit(solution)/shard_map/ppermute | solution.py:58
  397.2 24.2 %collective-permute-start.44 = (bf16[256,2048]{1,0:T(8,128)(2,1)S(1)}, bf16[256,2048]{1,0:T(8,128)(2,1)S(1)}, u32[]{:S(2)}, u32[]{:S(2)}) collective-permute-start(bf16[256,2048]{1,0:T(8,128)(2,1)S(1)} %add_convert_fusion.6), channel_id=1, source_target_pairs={{0,24},{2,26},{4,28},{6,30},{8,0},{10,2},{12,4},{14,6},{16,8},{18,... | collective-permute-start | bytes 3145736 | tf_op jit(solution)/shard_map/ppermute | solution.py:58
  401.0 22.6 %collective-permute-start.43 = (bf16[256,2048]{1,0:T(8,128)(2,1)S(1)}, bf16[256,2048]{1,0:T(8,128)(2,1)S(1)}, u32[]{:S(2)}, u32[]{:S(2)}) collective-permute-start(bf16[256,2048]{1,0:T(8,128)(2,1)S(1)} %copy-done.50), channel_id=1, source_target_pairs={{0,4},{2,6},{4,0},{6,2},{8,12},{10,14},{12,8},{14,10},{16,20},{18,... | collective-permute-start | bytes 3145736 | tf_op jit(solution)/shard_map/ppermute | solution.py:58
  423.6 23.8 %collective-permute-start.48 = (bf16[256,1024]{1,0:T(8,128)(2,1)S(1)}, bf16[256,1024]{1,0:T(8,128)(2,1)S(1)}, u32[]{:S(2)}, u32[]{:S(2)}) collective-permute-start(bf16[256,1024]{1,0:T(8,128)(2,1)S(1)} %fusion.37), channel_id=1, source_target_pairs={{0,4},{2,6},{4,0},{6,2},{8,12},{10,14},{12,8},{14,10},{16,20},{18,... | collective-permute-start | bytes 1572872 | tf_op jit(solution)/shard_map/ppermute | solution.py:58
  424.0 34.9 %collective-permute-start.50 = (bf16[256,1024]{1,0:T(8,128)(2,1)S(1)}, bf16[256,1024]{1,0:T(8,128)(2,1)S(1)}, u32[]{:S(2)}, u32[]{:S(2)}) collective-permute-start(bf16[256,1024]{1,0:T(8,128)(2,1)S(1)} %add_convert_fusion.11), channel_id=1, source_target_pairs={{0,24},{2,26},{4,28},{6,30},{8,0},{10,2},{12,4},{14,6},{16,8},{18,... | collective-permute-start | bytes 1572872 | tf_op jit(solution)/shard_map/ppermute | solution.py:58
  426.5 32.4 %collective-permute-start.49 = (bf16[256,2048]{1,0:T(8,128)(2,1)S(1)}, bf16[256,2048]{1,0:T(8,128)(2,1)S(1)}, u32[]{:S(2)}, u32[]{:S(2)}) collective-permute-start(bf16[256,2048]{1,0:T(8,128)(2,1)S(1)} %add_convert_fusion.5), channel_id=1, source_target_pairs={{0,8},{2,10},{4,12},{6,14},{8,16},{10,18},{12,20},{14,22},{16,24},... | collective-permute-start | bytes 3145736 | tf_op jit(solution)/shard_map/ppermute | solution.py:58
  426.6 32.3 %collective-permute-start.47 = (bf16[256,2048]{1,0:T(8,128)(2,1)S(1)}, bf16[256,2048]{1,0:T(8,128)(2,1)S(1)}, u32[]{:S(2)}, u32[]{:S(2)}) collective-permute-start(bf16[256,2048]{1,0:T(8,128)(2,1)S(1)} %copy-done.49), channel_id=1, source_target_pairs={{0,4},{2,6},{4,0},{6,2},{8,12},{10,14},{12,8},{14,10},{16,20},{18,... | collective-permute-start | bytes 3145736 | tf_op jit(solution)/shard_map/ppermute | solution.py:58
  447.3 11.6 %collective-permute-start.51 = (bf16[512,2048]{1,0:T(8,128)(2,1)S(1)}, bf16[512,2048]{1,0:T(8,128)(2,1)S(1)}, u32[]{:S(2)}, u32[]{:S(2)}) collective-permute-start(bf16[512,2048]{1,0:T(8,128)(2,1)S(1)} %convolution_convert_fusion.8), channel_id=1, source_target_pairs={{0,2},{2,0},{4,6},{6,4},{8,10},{10,8},{12,14},{14,12},{16,18},{18,... | collective-permute-start | bytes 6291464 | tf_op jit(solution)/shard_map/ppermute | solution.py:70
  459.7 24.9 %collective-permute-start.52 = (bf16[256,2048]{1,0:T(8,128)(2,1)S(1)}, bf16[256,2048]{1,0:T(8,128)(2,1)S(1)}, u32[]{:S(2)}, u32[]{:S(2)}) collective-permute-start(bf16[256,2048]{1,0:T(8,128)(2,1)S(1)} %copy-done.48), channel_id=1, source_target_pairs={{0,4},{2,6},{4,0},{6,2},{8,12},{10,14},{12,8},{14,10},{16,20},{18,... | collective-permute-start | bytes 3145736 | tf_op jit(solution)/shard_map/ppermute | solution.py:58
  460.2 24.4 %collective-permute-start.53 = (bf16[256,2048]{1,0:T(8,128)(2,1)S(1)}, bf16[256,2048]{1,0:T(8,128)(2,1)S(1)}, u32[]{:S(2)}, u32[]{:S(2)}) collective-permute-start(bf16[256,2048]{1,0:T(8,128)(2,1)S(1)} %add_convert_fusion.4), channel_id=1, source_target_pairs={{0,24},{2,26},{4,28},{6,30},{8,0},{10,2},{12,4},{14,6},{16,8},{18,... | collective-permute-start | bytes 3145736 | tf_op jit(solution)/shard_map/ppermute | solution.py:58
  472.9 52.2 %collective-permute-start.61 = (bf16[512,2048]{1,0:T(8,128)(2,1)S(1)}, bf16[512,2048]{1,0:T(8,128)(2,1)S(1)}, u32[]{:S(2)}, u32[]{:S(2)}) collective-permute-start(bf16[512,2048]{1,0:T(8,128)(2,1)S(1)} %add_convert_fusion.1.d_a), channel_id=1, source_target_pairs={{0,1},{1,0},{2,3},{3,2},{4,5},{5,4},{6,7},{7,6},{8,9},{9,8},{10,11... | collective-permute-start | bytes 6291464 | tf_op jit(solution)/shard_map/ppermute | solution.py:80
  484.6 23.2 %collective-permute-start.56 = (bf16[1024,512]{1,0:T(8,128)(2,1)}, bf16[1024,512]{1,0:T(8,128)(2,1)}, u32[]{:S(2)}, u32[]{:S(2)}) collective-permute-start(bf16[1024,512]{1,0:T(8,128)(2,1)} %fusion.27), channel_id=1, source_target_pairs={{0,4},{2,6},{4,0},{6,2},{8,12},{10,14},{12,8},{14,10},{16,20},{18,... | collective-permute-start | bytes 3145736 | tf_op jit(solution)/shard_map/ppermute | solution.py:58
  494.4 14.7 %collective-permute-start.54 = (bf16[512,2048]{1,0:T(8,128)(2,1)}, bf16[512,2048]{1,0:T(8,128)(2,1)}, u32[]{:S(2)}, u32[]{:S(2)}) collective-permute-start(bf16[512,2048]{1,0:T(8,128)(2,1)} %convolution_convert_fusion.7), channel_id=1, source_target_pairs={{0,2},{2,0},{4,6},{6,4},{8,10},{10,8},{12,14},{14,12},{16,18},{18,... | collective-permute-start | bytes 6291464 | tf_op jit(solution)/shard_map/ppermute | solution.py:70
  497.4 20.6 %collective-permute-start.57 = (f32[128,2048]{1,0:T(8,128)}, f32[128,2048]{1,0:T(8,128)S(1)}, u32[]{:S(2)}, u32[]{:S(2)}) collective-permute-start(f32[128,2048]{1,0:T(8,128)} %get-tuple-element.391), channel_id=1, source_target_pairs={{0,2},{2,0},{4,6},{6,4},{8,10},{10,8},{12,14},{14,12},{16,18},{18,... | collective-permute-start | bytes 3145736 | tf_op jit(solution)/shard_map/ppermute | solution.py:70
  519.6 17.4 %collective-permute-start.59 = (bf16[256,512]{1,0:T(8,128)(2,1)S(1)}, bf16[256,512]{1,0:T(8,128)(2,1)S(1)}, u32[]{:S(2)}, u32[]{:S(2)}) collective-permute-start(bf16[256,512]{1,0:T(8,128)(2,1)S(1)} %get-tuple-element.295), channel_id=1, source_target_pairs={{0,24},{2,26},{4,28},{6,30},{8,0},{10,2},{12,4},{14,6},{16,8},{18,... | collective-permute-start | bytes 786440 | tf_op jit(solution)/shard_map/ppermute | solution.py:58
  522.7 14.2 %collective-permute-start.60 = (bf16[256,512]{1,0:T(8,128)(2,1)S(1)}, bf16[256,512]{1,0:T(8,128)(2,1)S(1)}, u32[]{:S(2)}, u32[]{:S(2)}) collective-permute-start(bf16[256,512]{1,0:T(8,128)(2,1)S(1)} %get-tuple-element.297), channel_id=1, source_target_pairs={{0,8},{2,10},{4,12},{6,14},{8,16},{10,18},{12,20},{14,22},{16,24},... | collective-permute-start | bytes 786440 | tf_op jit(solution)/shard_map/ppermute | solution.py:58
  522.7 46.1 %collective-permute-start.55 = (bf16[512,2048]{1,0:T(8,128)(2,1)S(1)}, bf16[512,2048]{1,0:T(8,128)(2,1)S(1)}, u32[]{:S(2)}, u32[]{:S(2)}) collective-permute-start(bf16[512,2048]{1,0:T(8,128)(2,1)S(1)} %add_convert_fusion.mlp_a), channel_id=1, source_target_pairs={{0,1},{1,0},{2,3},{3,2},{4,5},{5,4},{6,7},{7,6},{8,9},{9,8},{10,11... | collective-permute-start | bytes 6291464 | tf_op jit(solution)/shard_map/ppermute | solution.py:80
  524.3 16.7 %collective-permute-start.58 = (bf16[256,1536]{1,0:T(8,128)(2,1)}, bf16[256,1536]{1,0:T(8,128)(2,1)S(1)}, u32[]{:S(2)}, u32[]{:S(2)}) collective-permute-start(bf16[256,1536]{1,0:T(8,128)(2,1)} %get-tuple-element.293), channel_id=1, source_target_pairs={{0,4},{2,6},{4,0},{6,2},{8,12},{10,14},{12,8},{14,10},{16,20},{18,... | collective-permute-start | bytes 2359304 | tf_op jit(solution)/shard_map/ppermute | solution.py:58
  542.0 10.4 %collective-permute-start.64 = (bf16[256,512]{1,0:T(8,128)(2,1)S(1)}, bf16[256,512]{1,0:T(8,128)(2,1)S(1)}, u32[]{:S(2)}, u32[]{:S(2)}) collective-permute-start(bf16[256,512]{1,0:T(8,128)(2,1)S(1)} %add_convert_fusion.14), channel_id=1, source_target_pairs={{0,24},{2,26},{4,28},{6,30},{8,0},{10,2},{12,4},{14,6},{16,8},{18,... | collective-permute-start | bytes 786440 | tf_op jit(solution)/shard_map/ppermute | solution.py:58
  546.9 17.8 %collective-permute-start.63 = (bf16[256,1536]{1,0:T(8,128)(2,1)S(1)}, bf16[256,1536]{1,0:T(8,128)(2,1)S(1)}, u32[]{:S(2)}, u32[]{:S(2)}) collective-permute-start(bf16[256,1536]{1,0:T(8,128)(2,1)S(1)} %add_convert_fusion.10), channel_id=1, source_target_pairs={{0,24},{2,26},{4,28},{6,30},{8,0},{10,2},{12,4},{14,6},{16,8},{18,... | collective-permute-start | bytes 2359304 | tf_op jit(solution)/shard_map/ppermute | solution.py:58
  547.0 17.8 %collective-permute-start.62 = (bf16[256,1536]{1,0:T(8,128)(2,1)}, bf16[256,1536]{1,0:T(8,128)(2,1)S(1)}, u32[]{:S(2)}, u32[]{:S(2)}) collective-permute-start(bf16[256,1536]{1,0:T(8,128)(2,1)} %get-tuple-element.302), channel_id=1, source_target_pairs={{0,4},{2,6},{4,0},{6,2},{8,12},{10,14},{12,8},{14,10},{16,20},{18,... | collective-permute-start | bytes 2359304 | tf_op jit(solution)/shard_map/ppermute | solution.py:58
  550.9 13.8 %collective-permute-start.65 = (f32[128,2048]{1,0:T(8,128)S(1)}, f32[128,2048]{1,0:T(8,128)S(1)}, u32[]{:S(2)}, u32[]{:S(2)}) collective-permute-start(f32[128,2048]{1,0:T(8,128)S(1)} %get-tuple-element.390), channel_id=1, source_target_pairs={{0,2},{2,0},{4,6},{6,4},{8,10},{10,8},{12,14},{14,12},{16,18},{18,... | collective-permute-start | bytes 3145736 | tf_op jit(solution)/shard_map/ppermute | solution.py:70
  567.6 28.9 %collective-permute-start.67 = (bf16[256,1536]{1,0:T(8,128)(2,1)}, bf16[256,1536]{1,0:T(8,128)(2,1)}, u32[]{:S(2)}, u32[]{:S(2)}) collective-permute-start(bf16[256,1536]{1,0:T(8,128)(2,1)} %add_convert_fusion.9), channel_id=1, source_target_pairs={{0,8},{2,10},{4,12},{6,14},{8,16},{10,18},{12,20},{14,22},{16,24},... | collective-permute-start | bytes 2359304 | tf_op jit(solution)/shard_map/ppermute | solution.py:58
  567.6 28.9 %collective-permute-start.66 = (bf16[256,1536]{1,0:T(8,128)(2,1)}, bf16[256,1536]{1,0:T(8,128)(2,1)}, u32[]{:S(2)}, u32[]{:S(2)}) collective-permute-start(bf16[256,1536]{1,0:T(8,128)(2,1)} %get-tuple-element.314), channel_id=1, source_target_pairs={{0,4},{2,6},{4,0},{6,2},{8,12},{10,14},{12,8},{14,10},{16,20},{18,... | collective-permute-start | bytes 2359304 | tf_op jit(solution)/shard_map/ppermute | solution.py:58
  577.6 13.4 %all-to-all-start = ((f32[16,1,1792]{2,1,0:T(1,128)}), f32[16,1,1792]{2,1,0:T(1,128)S(1)}, u32[]{:S(2)}, u32[]{:S(2)}) async-start(f32[16,1,1792]{2,1,0:T(1,128)} %reshape.128), calls=%async_computation | async-start | bytes 229376 | tf_op jit(solution)/shard_map/all_to_all | solution.py:718
  598.5 19.1 %collective-permute-start.68 = (bf16[256,1536]{1,0:T(8,128)(2,1)}, bf16[256,1536]{1,0:T(8,128)(2,1)S(1)}, u32[]{:S(2)}, u32[]{:S(2)}) collective-permute-start(bf16[256,1536]{1,0:T(8,128)(2,1)} %get-tuple-element.324), channel_id=1, source_target_pairs={{0,4},{2,6},{4,0},{6,2},{8,12},{10,14},{12,8},{14,10},{16,20},{18,... | collective-permute-start | bytes 2359304 | tf_op jit(solution)/shard_map/ppermute | solution.py:58
  598.6 19.2 %collective-permute-start.69 = (bf16[256,1536]{1,0:T(8,128)(2,1)S(1)}, bf16[256,1536]{1,0:T(8,128)(2,1)S(1)}, u32[]{:S(2)}, u32[]{:S(2)}) collective-permute-start(bf16[256,1536]{1,0:T(8,128)(2,1)S(1)} %add_convert_fusion.8), channel_id=1, source_target_pairs={{0,24},{2,26},{4,28},{6,30},{8,0},{10,2},{12,4},{14,6},{16,8},{18,... | collective-permute-start | bytes 2359304 | tf_op jit(solution)/shard_map/ppermute | solution.py:58
  (84 other events, 1139.4 us)

commit v5 on v4

--- a/solution.py
+++ b/solution.py
@@ -581,22 +581,43 @@
         first = jnp.stack([down[kx][:, :half] for kx in range(grid.x)])
         other = {kx: down[kx][:, half:] for kx in down}
         ph.end(first)
+        up_val = ph.begin(up_val)
+        _, gelu_pull = jax.vjp(jax.nn.gelu, up_val)
+        slope = gelu_pull(jnp.ones_like(up_val))[0]
+        ph.end(slope)
         ph.close()
 
         blk = first.shape[1] // grid.z
         part = lambda stacked, kz: stacked[:, kz * blk : (kz + 1) * blk]
         x_d[2] = ph.gather_x(z_d[2])
         a_2 = ph.send_z(part(first, 2), 3)
-        up_val = ph.begin(up_val)
-        _, gelu_pull = jax.vjp(jax.nn.gelu, up_val)
-        slope = gelu_pull(jnp.ones_like(up_val))[0]
-        ph.end(slope)
+        step = width // (grid.x * grid.z)
+        feature_blocks = lambda value, some: jnp.concatenate(
+            [
+                value[:, (kx * grid.z + kz) * step : (kx * grid.z + kz + 1) * step]
+                for kx in range(grid.x)
+                for kz in some
+            ],
+            axis=1,
+        )
+        some_of = lambda by_z, some: jnp.concatenate(
+            [by_z[kz][kx] for kx in range(grid.x) for kz in some], axis=0
+        )
+        there = [kz for kz in range(grid.z) if kz != 2]
+        late = feature_blocks(d_mlp, [2])
+        w_d = [some_of(x_d, there)]
+        d_act = [
+            matmul(ph.begin(feature_blocks(d_mlp[half_rows], there)), w_d[0])
+            for half_rows in (slice(0, rows), slice(rows, None))
+        ]
+        ph.end(*d_act, late)
         ph.close()
 
         x_b = {2: ph.reduce_x(rows_of(other, 2, 4))}
         a_3 = ph.send_z(part(first, 3), 1)
-        w_d = whole(x_d[0], x_d[1], x_d[2], x_d[3])
-        d_up = (matmul(ph.begin(d_mlp), w_d) * slope).astype(BF16)
+        w_d.append(some_of(x_d, [2]))
+        d_act = jnp.concatenate(d_act, axis=0) + matmul(ph.begin(late), w_d[1])
+        d_up = (d_act * slope).astype(BF16)
         ph.end(d_up)
         d_second_part = matmul(ph.begin(d_up)[rows:], w_u, True).astype(BF16)
         ph.end(d_second_part)
@@ -668,13 +689,13 @@
         ph.close()
 
         x_out = ph.reduce_x(out)
-        mlp_part = matmul(ph.begin(act)[rows:], w_d, True).astype(BF16)
+        down_of = lambda value: jnp.concatenate([matmul(value, w, True) for w in w_d], axis=1)
+        mlp_part = down_of(ph.begin(act)[rows:]).astype(BF16)
         ph.end(mlp_part)
-        mlp_part = ph.send_core(mlp_part)
+        mlp_part = ph.hand_over(mlp_part)
         up_total = up_sum(0) + ph.now(u_3).astype(F32) + ph.now(u_1).astype(F32)
         up_mine, up_theirs = grid.halves(ph.begin(up_total), 0)
         ph.end(up_mine)
-        mlp = from_both(mlp_part, act, w_d)
         up_theirs = ph.hand_over(up_theirs)
         ph.close()
 
@@ -686,56 +707,68 @@
         x_p = {2: p_rows(2)}
         o_2 = ph.send_z(out_sum(2).astype(BF16), 3)
         o_3 = ph.send_z(out_sum(3).astype(BF16), 1)
+        mlp = (down_of(ph.begin(act)[:rows]) + mlp_part.astype(F32)).astype(BF16)
+        ph.end(mlp)
+        mlp = ph.across(mlp)
         d_normed[-1] = ph.begin(d_normed[-1])
         input_grad, sums1 = by_rows(
             first_back_kernel, relative, present, [tokens, *two(d_normed), d_hidden], mods, [F32], 2
         )
         ph.end(input_grad)
+        up_part = grid.by_core(ph.begin(up_mine), up_theirs, 1)
+        ph.end(up_part)
         ph.close(20.0)
 
         x_p[3] = p_rows(3)
         p_2 = ph.send_z(p_sum(2).astype(BF16), 3)
         o_1 = ph.send_z((out_sum(1) + ph.now(o_2).astype(F32)).astype(BF16), 3)
+        row_sums = [jnp.sum(v.reshape(count, -1, 8, width), axis=2) for v in (sums1, sums2)]
+        row_sums = ph.begin(jnp.concatenate(row_sums, axis=1))
         down_low = plus(ph.now(first_sum)[0], x_first)
         down_high = b_sum(0) + ph.now(b_3).astype(F32) + ph.now(b_1).astype(F32)
-        down_total = ph.begin(jnp.concatenate([down_low, down_high], axis=1))
-        down_mine, down_theirs = grid.halves(down_total, 0)
-        ph.end(down_mine)
+        down_total = jnp.concatenate([down_low, down_high], axis=1)
+        down_mine, down_theirs = grid.halves(ph.begin(down_total), 0)
+        ph.end(down_mine, row_sums)
         down_theirs = ph.hand_over(down_theirs)
         ph.close(20.0)
 
         x_p[1] = p_rows(1)
         p_3 = ph.send_z(p_sum(3).astype(BF16), 1)
+        down_part = grid.by_core(ph.begin(down_mine), down_theirs, 1)
+        ph.end(down_part)
         mlp[-1] = ph.begin(mlp[-1])
+        places = [(kx, kz) for some in (there, [2]) for kx in range(grid.x) for kz in some]
+        in_order = [places.index((kx, kz)) for kx in range(grid.x) for kz in range(grid.z)]
+        mlp = [
+            jnp.concatenate([v[:, k * step : (k + 1) * step] for k in in_order], axis=1) for v in mlp
+        ]
         block_out, sums3 = by_rows(
             block_out_kernel, relative, present, [hidden, *two(mlp), dy], mods, [BF16], 1
         )
-        row_sums = [jnp.sum(v.reshape(count, -1, 8, width), axis=2) for v in (sums1, sums2, sums3)]
-        bin_row = jnp.broadcast_to(bins.astype(F32)[:, None, None], (count, 1, width))
-        d_mods = turn_out(jnp.concatenate(row_sums, axis=1))
-        d_mods = jnp.concatenate([d_mods, bin_row], axis=1)
-        ph.end(d_mods)
-        d_mods = lax.all_to_all(d_mods, "dp", split_axis=2, concat_axis=0, tiled=True)
-        up_part = grid.by_core(ph.begin(up_mine), up_theirs, 1)
-        ph.end(up_part)
+        ph.end(block_out)
         ph.close(20.0)
 
         x_p[0] = p_rows(0)
         p_1 = ph.send_z((p_sum(1) + ph.now(p_2).astype(F32)).astype(BF16), 3)
+        sums3 = jnp.sum(sums3.reshape(count, -1, 8, width), axis=2)
+        bin_row = jnp.broadcast_to(bins.astype(F32)[:, None, None], (count, 1, width))
+        d_mods = turn_out(jnp.concatenate([row_sums, sums3], axis=1))
+        d_mods = jnp.concatenate([d_mods, bin_row], axis=1)
+        d_mods = d_mods.reshape(-1, dp, width // dp).transpose(1, 0, 2)
         d_mods = ph.begin(d_mods)
-        rows_in_order = jnp.stack([d_mods[:, k] for k in (0, 1, 4, 2, 3, 5)], axis=1)
-        onehot_all = (d_mods[:, 6, :1] == table_rows.astype(F32)).astype(F32)
-        table_part = jnp.einsum("sb,std->btd", onehot_all, rows_in_order, precision=HIGH)
-        ph.end(table_part)
-        down_part = grid.by_core(ph.begin(down_mine), down_theirs, 1)
-        ph.end(down_part)
+        ph.end(d_mods)
+        d_mods = lax.all_to_all(d_mods, "dp", split_axis=0, concat_axis=0, tiled=True)
         out_total = out_sum(0) + ph.now(o_3).astype(F32) + ph.now(o_1).astype(F32)
         out_mine, out_theirs = grid.halves(ph.begin(out_total), 0)
         ph.end(out_mine)
         out_theirs = ph.hand_over(out_theirs)
         ph.close(20.0)
 
-        out_part = grid.by_core(out_mine, ph.begin(out_theirs), 1)
+        d_mods = ph.now(d_mods).reshape(dp * count, -1, width // dp)
+        rows_in_order = jnp.stack([d_mods[:, k] for k in (0, 1, 4, 2, 3, 5)], axis=1)
+        onehot_all = (d_mods[:, 6, :1] == table_rows.astype(F32)).astype(F32)
+        table_part = jnp.einsum("sb,std->btd", onehot_all, rows_in_order, precision=HIGH)
+        out_part = grid.by_core(out_mine, ph.now(out_theirs), 1)
         qkv_part = p_sum(0) + ph.now(p_3).astype(F32) + ph.now(p_1).astype(F32)
         qkv_part = qkv_part.reshape(-1, 3, local_width).transpose(1, 0, 2)
         qkv_part = grid.own_rows(qkv_part)

time: 635 us -> 613 us (0.965)
  waiting for transfers between devices: 237 us -> 217 us
  matrix products: 133 us -> 144 us
  local copies, waits for them, and re-layouts: 60.1 us -> 53.2 us
    ppermute x52, waiting for transfers between devices: 222 us -> 206 us  [send(): out = lax.ppermute(value, 'dp', self.ring(dz, dx, 0))]
    unnamed x178 -> x187, local copies, waits for them, and re-layouts: 40.9 us -> 34.1 us
    dot_general x12 -> x16, matrix products: 95.9 us -> 102 us  [matmul(): lax.dot_general(lhs, rhs, (((1,), (1 if turned else 0,)), ((), ())), pref...]
  transfers between devices with their start and end apart: 73 -> 73, of which waited for: 35 -> 35; matrix products, arithmetic and copies ran while one was open for 35% -> 36% of each run, Pallas kernels for 10% -> 11%
where the time goes in v5:
time: 613 us; the launch traced here: 604 us
  waiting for transfers between devices  217 us (35%)
  matrix products  144 us (23%)
  starting transfers between devices  84 us (14%)
  Pallas kernels  64.6 us (11%)
  local copies, waits for them, and re-layouts  53.2 us (9%)
  other arithmetic  38.5 us (6%)
    ppermute x52, waiting for transfers between devices, send(): out = lax.ppermute(value, 'dp', self.ring(dz, dx, 0))  206 us
    dot_general x16, matrix products, matmul(): lax.dot_general(lhs, rhs, (((1,), (1 if turned else 0,)), ((), ())), pref...  102 us
    ppermute x52, starting transfers between devices, send(): out = lax.ppermute(value, 'dp', self.ring(dz, dx, 0))  71.3 us
    pallas_call x6, Pallas kernels, by_rows(): pl.pallas_call(functools.partial(kernel, blocks), grid_spec=pltpu.Prefetc...  46.4 us
    dot_general x8, matrix products, dots(): lax.dot_general(lhs[:, kx * width:(kx + 1) * width], rhs, (((0,), (0,)),...  39.9 us
    unnamed x187, local copies, waits for them, and re-layouts  34.1 us
    pallas_call x2, Pallas kernels, by_image(): pl.pallas_call(kernel, grid=(rows // length,), in_specs=[block(operand.sh...  13.4 us
  transfers between devices with their start and end apart: 73, of which 35 were waited for; matrix products, arithmetic and copies ran while one was open for 36% of the time, Pallas kernels for 11%

profile of v5, /device:TPU:0, one launch (start us, length us, event | category | flops | bytes accessed | tf_op | source)
XLA Modules:
  0.0 604.3 jit_solution(8659469932210889389)
XLA Ops:
  7.7 2.6 collective-permute-start.2
  14.9 4.8 shard_map.144
  21.7 12.3 %collective-permute-done.4 = bf16[256,512]{1,0:T(8,128)(2,1)S(1)} collective-permute-done((bf16[256,512]{1,0:T(8,128)(2,1)}, bf16[256,512]{1,0:T(8,128)(2,1)S(1)}, u32[]{:S(2)}, u32[]{:S(2)}) %collective-permute-start.4) | collective-permute-done | bytes 262176 | tf_op jit(solution)/shard_map/ppermute | solution.py:58
  34.1 3.9 collective-permute-start.6
  41.1 7.8 %shard_map.145 = (bf16[512,2048]{1,0:T(8,128)(2,1)S(1)}, bf16[512,2048]{1,0:T(8,128)(2,1)S(1)}) custom-call(s32[8]{0:T(128)S(1)} %copy-done.8, s32[2]{0:T(128)S(1)} %copy-done.11, bf16[512,2048]{1,0:T(8,128)(2,1)S(1)} %bitcast.101, f32[2,6,2048]{2,1,0:T(8,128)S(1)} %reshape.123.mods_ref), custom_call_target="tpu_custom_call" | custom-call | flops 6291456000 | bytes 8388608 | tf_op jit(solution)/shard_map/pallas_call | solution.py:421
  49.0 3.0 constant_dynamic-update-slice_fusion.8
  52.1 2.4 collective-permute-done.6
  54.5 2.4 collective-permute-done.7
  61.9 14.9 %collective-permute-done.9 = bf16[256,1536]{0,1:T(8,128)(2,1)S(1)} collective-permute-done((bf16[256,1536]{0,1:T(8,128)(2,1)}, bf16[256,1536]{0,1:T(8,128)(2,1)S(1)}, u32[]{:S(2)}, u32[]{:S(2)}) %collective-permute-start.9) | collective-permute-done | bytes 786464 | tf_op jit(solution)/shard_map/ppermute | solution.py:58
  78.9 10.9 %collective-permute-done.11 = bf16[2,256,512]{2,1,0:T(8,128)(2,1)S(1)} collective-permute-done((bf16[2,256,512]{2,1,0:T(8,128)(2,1)S(1)}, bf16[2,256,512]{2,1,0:T(8,128)(2,1)S(1)}, u32[]{:S(2)}, u32[]{:S(2)}) %collective-permute-start.11) | collective-permute-done | bytes 524320 | tf_op jit(solution)/shard_map/ppermute | solution.py:58
  91.2 2.4 collective-permute-done.12
  93.7 3.5 collective-permute-start.14
  98.9 7.0 %convolution_convert_fusion.qkv_ref = bf16[1024,1536]{1,0:T(8,128)(2,1)S(1)} fusion(bf16[1024,2048]{1,0:T(8,128)(2,1)S(1)} %constant_dynamic-update-slice_fusion, bf16[2048,1536]{0,1:T(8,128)(2,1)S(1)} %constant_dynamic-update-slice_fusion.2), kind=kOutput, calls=%fused_computation.34 | convolution fusion | flops 6444023808 | bytes 13631488 | tf_op jit(solution)/shard_map/dot_general | solution.py:438
  105.9 4.5 shard_map.146
  110.5 6.3 %collective-permute-done.15 = bf16[2,256,512]{2,1,0:T(8,128)(2,1)S(1)} collective-permute-done((bf16[2,256,512]{2,1,0:T(8,128)(2,1)S(1)}, bf16[2,256,512]{2,1,0:T(8,128)(2,1)S(1)}, u32[]{:S(2)}, u32[]{:S(2)}) %collective-permute-start.15) | collective-permute-done | bytes 524320 | tf_op jit(solution)/shard_map/ppermute | solution.py:58
  118.4 4.1 collective-permute-done.17
  131.8 17.9 %collective-permute-done.19 = bf16[256,2048]{1,0:T(8,128)(2,1)} collective-permute-done((bf16[256,2048]{1,0:T(8,128)(2,1)S(1)}, bf16[256,2048]{1,0:T(8,128)(2,1)}, u32[]{:S(2)}, u32[]{:S(2)}) %collective-permute-start.19) | collective-permute-done | bytes 1048608 | tf_op jit(solution)/shard_map/ppermute | solution.py:58
  152.8 2.4 constant_dynamic-update-slice_fusion.22
  155.3 18.9 %collective-permute-done.21 = bf16[256,2048]{1,0:T(8,128)(2,1)} collective-permute-done((bf16[256,2048]{1,0:T(8,128)(2,1)S(1)}, bf16[256,2048]{1,0:T(8,128)(2,1)}, u32[]{:S(2)}, u32[]{:S(2)}) %collective-permute-start.21) | collective-permute-done | bytes 1048608 | tf_op jit(solution)/shard_map/ppermute | solution.py:58
  177.6 7.9 %shard_map.148 = (f32[512,2048]{1,0:T(8,128)S(1)}, bf16[512,2048]{1,0:T(8,128)(2,1)S(1)}) custom-call(s32[8]{0:T(128)S(1)} %copy-done.8, s32[2]{0:T(128)S(1)} %copy-done.11, bf16[512,2048]{1,0:T(8,128)(2,1)S(1)} %get-tuple-element.183.tokens_ref, bf16[512,2048]{1,0:T(8,128)(2,1)S(1)} %add_convert_fusion.2.att_a, ...), custom_call_target="tpu_custom_call" | custom-call | flops 6291456000 | bytes 8388608 | tf_op jit(solution)/shard_map/pallas_call | solution.py:421
  185.7 14.7 %collective-permute-done.25 = bf16[256,2048]{1,0:T(8,128)(2,1)} collective-permute-done((bf16[256,2048]{1,0:T(8,128)(2,1)}, bf16[256,2048]{1,0:T(8,128)(2,1)}, u32[]{:S(2)}, u32[]{:S(2)}) %collective-permute-start.25) | collective-permute-done | bytes 1048608 | tf_op jit(solution)/shard_map/ppermute | solution.py:58
  202.8 2.4 constant_dynamic-update-slice_fusion.20
  212.2 20.4 %collective-permute-done.27 = bf16[256,2048]{1,0:T(8,128)(2,1)S(1)} collective-permute-done((bf16[256,2048]{1,0:T(8,128)(2,1)S(1)}, bf16[256,2048]{1,0:T(8,128)(2,1)S(1)}, u32[]{:S(2)}, u32[]{:S(2)}) %collective-permute-start.27) | collective-permute-done | bytes 1048608 | tf_op jit(solution)/shard_map/ppermute | solution.py:58
  239.6 15.1 %fusion.13 = (bf16[1024,2048]{1,0:T(8,128)(2,1)}, f32[1024,2048]{1,0:T(8,128)}) fusion(bf16[1024,2048]{1,0:T(8,128)(2,1)S(1)} %constant_dynamic-update-slice_fusion.12, bf16[2048,2048]{1,0:T(8,128)(2,1)} %constant_dynamic-update-slice_fusion.16), kind=kOutput, calls=%fused_computation.16 | convolution fusion | flops 8608808960 | bytes 25165824 | tf_op jit(solution)/shard_map/dot_general | solution.py:438
  256.6 7.0 %convolution_convert_fusion.6 = bf16[1024,2048]{1,0:T(8,128)(2,1)S(1)} fusion(bf16[1024,2048]{1,0:T(8,128)(2,1)} %get-tuple-element.303, bf16[1024,2048]{1,0:T(8,128)(2,1)S(1)} %constant_dynamic-update-slice_fusion.14), kind=kOutput, calls=%fused_computation.40 | convolution fusion | flops 4297064448 | bytes 10485760 | tf_op jit(solution)/shard_map/dot_general | solution.py:175
  264.8 7.0 %convolution_convert_fusion.5 = bf16[1024,2048]{1,0:T(8,128)(2,1)S(1)} fusion(bf16[1024,2048]{1,0:T(8,128)(2,1)} %get-tuple-element.303, bf16[1024,2048]{1,0:T(8,128)(2,1)S(1)} %constant_dynamic-update-slice_fusion.14), kind=kOutput, calls=%fused_computation.39 | convolution fusion | flops 4297064448 | bytes 10485760 | tf_op jit(solution)/shard_map/dot_general | solution.py:175
  279.9 2.6 collective-permute-start.34
  283.5 7.9 %fusion.81 = f32[512,2048]{1,0:T(8,128)} fusion(bf16[512,1536]{1,0:T(8,128)(2,1)S(1)} %pad_maximum_fusion.3, bf16[1536,2048]{1,0:T(8,128)(2,1)} %constant_dynamic-update-slice_fusion.24), kind=kOutput, calls=%fused_computation.214 | convolution fusion | flops 3221225472 | bytes 12058624 | tf_op jit(solution)/shard_map/dot_general | solution.py:438
  292.5 5.1 fusion.82
  297.6 4.0 collective-permute-done.33
  304.6 12.7 %fusion.15 = bf16[1024,2048]{1,0:T(8,128)(2,1)} fusion(f32[512,2048]{1,0:T(8,128)} %fusion.82, f32[512,2048]{1,0:T(8,128)} %fusion.81, f32[1024,2048]{1,0:T(8,128)} %get-tuple-element.231, bf16[1024,512]{1,0:T(8,128)(2,1)S(1)} %pad_maximum_fusion.5, bf16[512,2048]{1,0:T(8,128)(2,1)} %constant_dynamic-update-slice_fusion.30), kind=kOutput, calls=%fused_computation.19 | convolution fusion | flops 2191523840 | bytes 24117248 | tf_op jit(solution)/shard_map/dot_general | solution.py:438
  317.3 9.9 %convolution_convert_fusion.9 = bf16[512,2048]{1,0:T(8,128)(2,1)} fusion(bf16[2048,2048]{1,0:T(8,128)(2,1)} %constant_dynamic-update-slice_fusion.16, bf16[1024,2048]{1,0:T(8,128)(2,1)} %fusion.15), kind=kOutput, calls=%fused_computation.43 | convolution fusion | flops 4296015872 | bytes 12582912 | tf_op jit(solution)/shard_map/dot_general | solution.py:438
  328.7 2.9 collective-permute-done.37
  332.9 4.2 collective-permute-start.40
  337.1 8.5 %add_convert_fusion.1.d_a = bf16[512,2048]{1,0:T(8,128)(2,1)S(1)} fusion(bf16[512,2048]{1,0:T(8,128)(2,1)} %copy-done.66, bf16[512,2048]{1,0:T(8,128)(2,1)S(1)} %slice-done.4, bf16[2048,2048]{1,0:T(8,128)(2,1)} %constant_dynamic-update-slice_fusion.16), kind=kOutput, calls=%fused_computation.32 | convolution fusion | flops 4298113024 | bytes 14680064 | tf_op jit(solution)/shard_map/dot_general | solution.py:438
  347.2 7.4 %convolution_convert_fusion.4 = bf16[1024,2048]{1,0:T(8,128)(2,1)S(1)} fusion(bf16[1024,2048]{1,0:T(8,128)(2,1)} %fusion.15, bf16[1024,2048]{1,0:T(8,128)(2,1)} %copy-done.32), kind=kOutput, calls=%fused_computation.38 | convolution fusion | flops 4297064448 | bytes 10485760 | tf_op jit(solution)/shard_map/dot_general | solution.py:175
  360.1 4.3 collective-permute-start.42
  364.9 6.5 %convolution_convert_fusion.3 = bf16[1024,2048]{1,0:T(8,128)(2,1)S(1)} fusion(bf16[1024,2048]{1,0:T(8,128)(2,1)S(1)} %copy-done.25, bf16[1024,2048]{1,0:T(8,128)(2,1)} %copy-done.32), kind=kOutput, calls=%fused_computation.37 | convolution fusion | flops 4297064448 | bytes 10485760 | tf_op jit(solution)/shard_map/dot_general | solution.py:175
  371.4 2.6 convert_add_fusion.1
  376.8 10.2 %collective-permute-done.43 = bf16[256,1024]{1,0:T(8,128)(2,1)S(1)} collective-permute-done((bf16[256,1024]{1,0:T(8,128)(2,1)S(1)}, bf16[256,1024]{1,0:T(8,128)(2,1)S(1)}, u32[]{:S(2)}, u32[]{:S(2)}) %collective-permute-start.43) | collective-permute-done | bytes 524320 | tf_op jit(solution)/shard_map/ppermute | solution.py:58
  388.9 3.8 collective-permute-start.46
  395.3 14.2 %shard_map.149 = (f32[512,2048]{1,0:T(8,128)}, bf16[512,2048]{1,0:T(8,128)(2,1)S(1)}, f32[2,24,2048]{2,1,0:T(8,128)S(1)}) custom-call(s32[8]{0:T(128)S(1)} %copy-done.8, s32[2]{0:T(128)S(1)} %copy-done.11, f32[512,2048]{1,0:T(8,128)} %copy-done.12, bf16[512,2048]{1,0:T(8,128)(2,1)S(1)} %add_convert_fusion.2.att_a, ...), custom_call_target="tpu_custom_call" | custom-call | flops 6291456000 | bytes 8388608 | tf_op jit(solution)/shard_map/pallas_call | solution.py:421
  409.7 3.4 collective-permute-done.46
  413.1 2.4 collective-permute-done.45
  422.5 8.9 %shard_map.150 = bf16[1024,1536]{1,0:T(8,128)(2,1)S(1)} custom-call(bf16[1024,1536]{1,0:T(8,128)(2,1)S(1)} %copy-done.3, bf16[1024,512]{1,0:T(8,128)(2,1)S(1)} %convolution_convert_fusion.11.d_mixed_ref), custom_call_target="tpu_custom_call" | custom-call | flops 3221225472 | bytes 8388608 | tf_op jit(solution)/shard_map/pallas_call | solution.py:249
  431.4 7.5 %convolution_convert_fusion.8 = bf16[512,2048]{1,0:T(8,128)(2,1)S(1)} fusion(bf16[2048,1536]{0,1:T(8,128)(2,1)} %copy-done.60, bf16[1024,1536]{1,0:T(8,128)(2,1)S(1)} %shard_map.150), kind=kOutput, calls=%fused_computation.42 | convolution fusion | flops 3222274048 | bytes 9961472 | tf_op jit(solution)/shard_map/dot_general | solution.py:438
  439.1 12.6 %collective-permute-done.50 = bf16[256,1024]{1,0:T(8,128)(2,1)S(1)} collective-permute-done((bf16[256,1024]{1,0:T(8,128)(2,1)}, bf16[256,1024]{1,0:T(8,128)(2,1)S(1)}, u32[]{:S(2)}, u32[]{:S(2)}) %collective-permute-start.50) | collective-permute-done | bytes 524320 | tf_op jit(solution)/shard_map/ppermute | solution.py:58
  453.7 6.5 %add_convert_fusion.d_a = bf16[512,2048]{1,0:T(8,128)(2,1)S(1)} fusion(bf16[512,2048]{1,0:T(8,128)(2,1)S(1)} %collective-permute-done.51, bf16[512,1536]{1,0:T(8,128)(2,1)S(1)} %slice-done, bf16[2048,1536]{0,1:T(8,128)(2,1)} %copy-done.60), kind=kOutput, calls=%fused_computation.31 | convolution fusion | flops 3224371200 | bytes 12058624 | tf_op jit(solution)/shard_map/dot_general | solution.py:438
  465.6 3.7 convolution_convert_fusion.2
  471.0 4.8 convolution_convert_fusion.1
  477.0 2.9 fusion.42
  479.9 6.2 %convolution_convert_fusion.7 = bf16[512,1536]{1,0:T(8,128)(2,1)S(1)} fusion(bf16[1536,2048]{1,0:T(8,128)(2,1)} %constant_dynamic-update-slice_fusion.24, bf16[1024,2048]{1,0:T(8,128)(2,1)S(1)} %copy-done.68), kind=kOutput, calls=%fused_computation.41 | convolution fusion | flops 3222011904 | bytes 9961472 | tf_op jit(solution)/shard_map/dot_general | solution.py:438
  487.9 11.2 %collective-permute-done.54 = bf16[1024,512]{1,0:T(8,128)(2,1)S(1)} collective-permute-done((bf16[1024,512]{1,0:T(8,128)(2,1)}, bf16[1024,512]{1,0:T(8,128)(2,1)S(1)}, u32[]{:S(2)}, u32[]{:S(2)}) %collective-permute-start.54) | collective-permute-done | bytes 1048608 | tf_op jit(solution)/shard_map/ppermute | solution.py:58
  500.3 3.9 collective-permute-start.59
  505.5 2.9 fusion.28
  508.5 5.2 fusion.30
  516.5 11.7 %shard_map.151 = (f32[512,2048]{1,0:T(8,128)}, f32[2,16,2048]{2,1,0:T(8,128)S(1)}) custom-call(s32[8]{0:T(128)S(1)} %copy-done.8, s32[2]{0:T(128)S(1)} %copy-done.11, bf16[512,2048]{1,0:T(8,128)(2,1)S(1)} %copy-done.16, bf16[512,2048]{1,0:T(8,128)(2,1)S(1)} %add_convert_fusion.d_a, bf16[512,2048]{1,0:T(8,128)(2,1)S(1)} %collective-permute-done.61.d_b, ...), custom_call_target="tpu_custom_call" | custom-call | flops 6291456000 | bytes 8388608 | tf_op jit(solution)/shard_map/pallas_call | solution.py:421
  531.6 3.9 collective-permute-start.64
  542.2 14.3 %collective-permute-done.63 = bf16[256,1536]{1,0:T(8,128)(2,1)S(1)} collective-permute-done((bf16[256,1536]{1,0:T(8,128)(2,1)S(1)}, bf16[256,1536]{1,0:T(8,128)(2,1)S(1)}, u32[]{:S(2)}, u32[]{:S(2)}) %collective-permute-start.63) | collective-permute-done | bytes 786464 | tf_op jit(solution)/shard_map/ppermute | solution.py:58
  565.2 3.6 shard_map.152
  569.1 6.3 %collective-permute-done.67 = bf16[256,1536]{1,0:T(8,128)(2,1)} collective-permute-done((bf16[256,1536]{1,0:T(8,128)(2,1)}, bf16[256,1536]{1,0:T(8,128)(2,1)}, u32[]{:S(2)}, u32[]{:S(2)}) %collective-permute-start.67) | collective-permute-done | bytes 786464 | tf_op jit(solution)/shard_map/ppermute | solution.py:58
  575.4 2.8 add_convert_fusion.7
  582.4 4.2 all-to-all-start
  586.6 6.5 %collective-permute-done.68 = bf16[256,1536]{1,0:T(8,128)(2,1)} collective-permute-done((bf16[256,1536]{1,0:T(8,128)(2,1)S(1)}, bf16[256,1536]{1,0:T(8,128)(2,1)}, u32[]{:S(2)}, u32[]{:S(2)}) %collective-permute-start.68) | collective-permute-done | bytes 786464 | tf_op jit(solution)/shard_map/ppermute | solution.py:58
  (404 shorter events, 152.9 us)
Async XLA Ops:
  7.7 26.4 %collective-permute-start.2 = (bf16[256,1536]{0,1:T(8,128)(2,1)S(1)}, bf16[256,1536]{0,1:T(8,128)(2,1)S(1)}, u32[]{:S(2)}, u32[]{:S(2)}) collective-permute-start(bf16[256,1536]{0,1:T(8,128)(2,1)S(1)} %get-tuple-element.180), channel_id=1, source_target_pairs={{0,4},{2,6},{4,0},{6,2},{8,12},{10,14},{12,8},{14,10},{16,20},{18,... | collective-permute-start | bytes 2359304 | tf_op jit(solution)/shard_map/ppermute | solution.py:58
  10.4 23.7 %collective-permute-start.1 = (bf16[256,1536]{0,1:T(8,128)(2,1)S(1)}, bf16[256,1536]{0,1:T(8,128)(2,1)}, u32[]{:S(2)}, u32[]{:S(2)}) collective-permute-start(bf16[256,1536]{0,1:T(8,128)(2,1)S(1)} %get-tuple-element.180), channel_id=1, source_target_pairs={{0,8},{2,10},{4,12},{6,14},{8,16},{10,18},{12,20},{14,22},{16,24},... | collective-permute-start | bytes 2359304 | tf_op jit(solution)/shard_map/ppermute | solution.py:58
  12.8 21.2 %collective-permute-start.4 = (bf16[256,512]{1,0:T(8,128)(2,1)}, bf16[256,512]{1,0:T(8,128)(2,1)S(1)}, u32[]{:S(2)}, u32[]{:S(2)}) collective-permute-start(bf16[256,512]{1,0:T(8,128)(2,1)} %get-tuple-element.375), channel_id=1, source_target_pairs={{0,4},{2,6},{4,0},{6,2},{8,12},{10,14},{12,8},{14,10},{16,20},{18,... | collective-permute-start | bytes 786440 | tf_op jit(solution)/shard_map/ppermute | solution.py:58
  34.1 20.4 %collective-permute-start.6 = (bf16[256,1536]{0,1:T(8,128)(2,1)S(1)}, bf16[256,1536]{0,1:T(8,128)(2,1)S(1)}, u32[]{:S(2)}, u32[]{:S(2)}) collective-permute-start(bf16[256,1536]{0,1:T(8,128)(2,1)S(1)} %get-tuple-element.180), channel_id=1, source_target_pairs={{0,24},{2,26},{4,28},{6,30},{8,0},{10,2},{12,4},{14,6},{16,8},{18,... | collective-permute-start | bytes 2359304 | tf_op jit(solution)/shard_map/ppermute | solution.py:58
  38.0 18.9 %collective-permute-start.7 = (bf16[256,1536]{0,1:T(8,128)(2,1)}, bf16[256,1536]{0,1:T(8,128)(2,1)S(1)}, u32[]{:S(2)}, u32[]{:S(2)}) collective-permute-start(bf16[256,1536]{0,1:T(8,128)(2,1)} %collective-permute-done.1), channel_id=1, source_target_pairs={{0,4},{2,6},{4,0},{6,2},{8,12},{10,14},{12,8},{14,10},{16,20},{18,... | collective-permute-start | bytes 2359304 | tf_op jit(solution)/shard_map/ppermute | solution.py:58
  57.0 19.8 %collective-permute-start.9 = (bf16[256,1536]{0,1:T(8,128)(2,1)}, bf16[256,1536]{0,1:T(8,128)(2,1)S(1)}, u32[]{:S(2)}, u32[]{:S(2)}) collective-permute-start(bf16[256,1536]{0,1:T(8,128)(2,1)} %collective-permute-done.1), channel_id=1, source_target_pairs={{0,8},{2,10},{4,12},{6,14},{8,16},{10,18},{12,20},{14,22},{16,24},... | collective-permute-start | bytes 2359304 | tf_op jit(solution)/shard_map/ppermute | solution.py:58
  57.0 19.8 %collective-permute-start.10 = (bf16[256,1536]{0,1:T(8,128)(2,1)S(1)}, bf16[256,1536]{0,1:T(8,128)(2,1)S(1)}, u32[]{:S(2)}, u32[]{:S(2)}) collective-permute-start(bf16[256,1536]{0,1:T(8,128)(2,1)S(1)} %collective-permute-done.6), channel_id=1, source_target_pairs={{0,4},{2,6},{4,0},{6,2},{8,12},{10,14},{12,8},{14,10},{16,20},{18,... | collective-permute-start | bytes 2359304 | tf_op jit(solution)/shard_map/ppermute | solution.py:58
  76.8 13.1 %collective-permute-start.11 = (bf16[2,256,512]{2,1,0:T(8,128)(2,1)S(1)}, bf16[2,256,512]{2,1,0:T(8,128)(2,1)S(1)}, u32[]{:S(2)}, u32[]{:S(2)}) collective-permute-start(bf16[2,256,512]{2,1,0:T(8,128)(2,1)S(1)} %pad_maximum_fusion.6), channel_id=1, source_target_pairs={{0,8},{2,10},{4,12},{6,14},{8,16},{10,18},{12,20},{14,22},{16,24},... | collective-permute-start | bytes 1572872 | tf_op jit(solution)/shard_map/ppermute | solution.py:58
  76.8 16.9 %collective-permute-start.12 = (bf16[256,1536]{0,1:T(8,128)(2,1)S(1)}, bf16[256,1536]{0,1:T(8,128)(2,1)S(1)}, u32[]{:S(2)}, u32[]{:S(2)}) collective-permute-start(bf16[256,1536]{0,1:T(8,128)(2,1)S(1)} %collective-permute-done.9), channel_id=1, source_target_pairs={{0,4},{2,6},{4,0},{6,2},{8,12},{10,14},{12,8},{14,10},{16,20},{18,... | collective-permute-start | bytes 2359304 | tf_op jit(solution)/shard_map/ppermute | solution.py:58
  78.4 11.5 %collective-permute-start.13 = (bf16[128,2048]{1,0:T(8,128)(2,1)S(1)}, bf16[128,2048]{1,0:T(8,128)(2,1)S(1)}, u32[]{:S(2)}, u32[]{:S(2)}) collective-permute-start(bf16[128,2048]{1,0:T(8,128)(2,1)S(1)} %get-tuple-element.408), channel_id=1, source_target_pairs={{0,2},{2,0},{4,6},{6,4},{8,10},{10,8},{12,14},{14,12},{16,18},{18,... | collective-permute-start | bytes 1572872 | tf_op jit(solution)/shard_map/ppermute | solution.py:70
  93.7 23.1 %collective-permute-start.14 = (bf16[2,256,512]{2,1,0:T(8,128)(2,1)S(1)}, bf16[2,256,512]{2,1,0:T(8,128)(2,1)S(1)}, u32[]{:S(2)}, u32[]{:S(2)}) collective-permute-start(bf16[2,256,512]{2,1,0:T(8,128)(2,1)S(1)} %pad_maximum_fusion.6), channel_id=1, source_target_pairs={{0,24},{2,26},{4,28},{6,30},{8,0},{10,2},{12,4},{14,6},{16,8},{18,... | collective-permute-start | bytes 1572872 | tf_op jit(solution)/shard_map/ppermute | solution.py:58
  97.2 19.6 %collective-permute-start.15 = (bf16[2,256,512]{2,1,0:T(8,128)(2,1)S(1)}, bf16[2,256,512]{2,1,0:T(8,128)(2,1)S(1)}, u32[]{:S(2)}, u32[]{:S(2)}) collective-permute-start(bf16[2,256,512]{2,1,0:T(8,128)(2,1)S(1)} %collective-permute-done.11), channel_id=1, source_target_pairs={{0,8},{2,10},{4,12},{6,14},{8,16},{10,18},{12,20},{14,22},{16,24},... | collective-permute-start | bytes 1572872 | tf_op jit(solution)/shard_map/ppermute | solution.py:58
  97.2 21.2 %collective-permute-start.16 = (bf16[256,2048]{1,0:T(8,128)(2,1)S(1)}, bf16[256,2048]{1,0:T(8,128)(2,1)S(1)}, u32[]{:S(2)}, u32[]{:S(2)}) collective-permute-start(bf16[256,2048]{1,0:T(8,128)(2,1)S(1)} %get-tuple-element.208), channel_id=1, source_target_pairs={{0,4},{2,6},{4,0},{6,2},{8,12},{10,14},{12,8},{14,10},{16,20},{18,... | collective-permute-start | bytes 3145736 | tf_op jit(solution)/shard_map/ppermute | solution.py:58
  122.5 27.3 %collective-permute-start.19 = (bf16[256,2048]{1,0:T(8,128)(2,1)S(1)}, bf16[256,2048]{1,0:T(8,128)(2,1)}, u32[]{:S(2)}, u32[]{:S(2)}) collective-permute-start(bf16[256,2048]{1,0:T(8,128)(2,1)S(1)} %get-tuple-element.208), channel_id=1, source_target_pairs={{0,8},{2,10},{4,12},{6,14},{8,16},{10,18},{12,20},{14,22},{16,24},... | collective-permute-start | bytes 3145736 | tf_op jit(solution)/shard_map/ppermute | solution.py:58
  124.4 25.3 %collective-permute-start.20 = (bf16[256,2048]{1,0:T(8,128)(2,1)S(1)}, bf16[256,2048]{1,0:T(8,128)(2,1)S(1)}, u32[]{:S(2)}, u32[]{:S(2)}) collective-permute-start(bf16[256,2048]{1,0:T(8,128)(2,1)S(1)} %get-tuple-element.223), channel_id=1, source_target_pairs={{0,4},{2,6},{4,0},{6,2},{8,12},{10,14},{12,8},{14,10},{16,20},{18,... | collective-permute-start | bytes 3145736 | tf_op jit(solution)/shard_map/ppermute | solution.py:58
  128.7 48.9 %collective-permute-start.18 = (bf16[512,2048]{1,0:T(8,128)(2,1)S(1)}, bf16[512,2048]{1,0:T(8,128)(2,1)S(1)}, u32[]{:S(2)}, u32[]{:S(2)}) collective-permute-start(bf16[512,2048]{1,0:T(8,128)(2,1)S(1)} %add_convert_fusion.2.att_a), channel_id=1, source_target_pairs={{0,1},{1,0},{2,3},{3,2},{4,5},{5,4},{6,7},{7,6},{8,9},{9,8},{10,11... | collective-permute-start | bytes 6291464 | tf_op jit(solution)/shard_map/ppermute | solution.py:80
  149.7 24.5 %collective-permute-start.21 = (bf16[256,2048]{1,0:T(8,128)(2,1)S(1)}, bf16[256,2048]{1,0:T(8,128)(2,1)}, u32[]{:S(2)}, u32[]{:S(2)}) collective-permute-start(bf16[256,2048]{1,0:T(8,128)(2,1)S(1)} %get-tuple-element.208), channel_id=1, source_target_pairs={{0,24},{2,26},{4,28},{6,30},{8,0},{10,2},{12,4},{14,6},{16,8},{18,... | collective-permute-start | bytes 3145736 | tf_op jit(solution)/shard_map/ppermute | solution.py:58
  151.4 24.0 %collective-permute-start.22 = (bf16[256,2048]{1,0:T(8,128)(2,1)}, bf16[256,2048]{1,0:T(8,128)(2,1)S(1)}, u32[]{:S(2)}, u32[]{:S(2)}) collective-permute-start(bf16[256,2048]{1,0:T(8,128)(2,1)} %collective-permute-done.19), channel_id=1, source_target_pairs={{0,4},{2,6},{4,0},{6,2},{8,12},{10,14},{12,8},{14,10},{16,20},{18,... | collective-permute-start | bytes 3145736 | tf_op jit(solution)/shard_map/ppermute | solution.py:58
  152.8 22.5 %collective-permute-start.23 = (bf16[512,2048]{1,0:T(8,128)(2,1)S(1)}, bf16[512,2048]{1,0:T(8,128)(2,1)S(1)}, u32[]{:S(2)}, u32[]{:S(2)}) collective-permute-start(bf16[512,2048]{1,0:T(8,128)(2,1)S(1)} %get-tuple-element.210), channel_id=1, source_target_pairs={{0,2},{2,0},{4,6},{6,4},{8,10},{10,8},{12,14},{14,12},{16,18},{18,... | collective-permute-start | bytes 6291464 | tf_op jit(solution)/shard_map/ppermute | solution.py:70
  175.3 25.1 %collective-permute-start.25 = (bf16[256,2048]{1,0:T(8,128)(2,1)}, bf16[256,2048]{1,0:T(8,128)(2,1)}, u32[]{:S(2)}, u32[]{:S(2)}) collective-permute-start(bf16[256,2048]{1,0:T(8,128)(2,1)} %collective-permute-done.19), channel_id=1, source_target_pairs={{0,8},{2,10},{4,12},{6,14},{8,16},{10,18},{12,20},{14,22},{16,24},... | collective-permute-start | bytes 3145736 | tf_op jit(solution)/shard_map/ppermute | solution.py:58
  176.1 31.2 %collective-permute-start.26 = (bf16[256,2048]{1,0:T(8,128)(2,1)}, bf16[256,2048]{1,0:T(8,128)(2,1)}, u32[]{:S(2)}, u32[]{:S(2)}) collective-permute-start(bf16[256,2048]{1,0:T(8,128)(2,1)} %collective-permute-done.21), channel_id=1, source_target_pairs={{0,4},{2,6},{4,0},{6,2},{8,12},{10,14},{12,8},{14,10},{16,20},{18,... | collective-permute-start | bytes 3145736 | tf_op jit(solution)/shard_map/ppermute | solution.py:58
  185.5 21.8 %collective-permute-start.24 = (bf16[512,2048]{1,0:T(8,128)(2,1)S(1)}, bf16[512,2048]{1,0:T(8,128)(2,1)S(1)}, u32[]{:S(2)}, u32[]{:S(2)}) collective-permute-start(bf16[512,2048]{1,0:T(8,128)(2,1)S(1)} %get-tuple-element.216), channel_id=1, source_target_pairs={{0,2},{2,0},{4,6},{6,4},{8,10},{10,8},{12,14},{14,12},{16,18},{18,... | collective-permute-start | bytes 6291464 | tf_op jit(solution)/shard_map/ppermute | solution.py:70
  207.3 25.3 %collective-permute-start.27 = (bf16[256,2048]{1,0:T(8,128)(2,1)S(1)}, bf16[256,2048]{1,0:T(8,128)(2,1)S(1)}, u32[]{:S(2)}, u32[]{:S(2)}) collective-permute-start(bf16[256,2048]{1,0:T(8,128)(2,1)S(1)} %copy-done.34), channel_id=1, source_target_pairs={{0,8},{2,10},{4,12},{6,14},{8,16},{10,18},{12,20},{14,22},{16,24},... | collective-permute-start | bytes 3145736 | tf_op jit(solution)/shard_map/ppermute | solution.py:58
  207.4 25.2 %collective-permute-start.28 = (bf16[256,2048]{1,0:T(8,128)(2,1)}, bf16[256,2048]{1,0:T(8,128)(2,1)S(1)}, u32[]{:S(2)}, u32[]{:S(2)}) collective-permute-start(bf16[256,2048]{1,0:T(8,128)(2,1)} %collective-permute-done.25), channel_id=1, source_target_pairs={{0,4},{2,6},{4,0},{6,2},{8,12},{10,14},{12,8},{14,10},{16,20},{18,... | collective-permute-start | bytes 3145736 | tf_op jit(solution)/shard_map/ppermute | solution.py:58
  232.6 23.2 %collective-permute-start.29 = (bf16[256,2048]{1,0:T(8,128)(2,1)S(1)}, bf16[256,2048]{1,0:T(8,128)(2,1)S(1)}, u32[]{:S(2)}, u32[]{:S(2)}) collective-permute-start(bf16[256,2048]{1,0:T(8,128)(2,1)S(1)} %copy-done.34), channel_id=1, source_target_pairs={{0,24},{2,26},{4,28},{6,30},{8,0},{10,2},{12,4},{14,6},{16,8},{18,... | collective-permute-start | bytes 3145736 | tf_op jit(solution)/shard_map/ppermute | solution.py:58
  234.7 21.1 %collective-permute-start.30 = (bf16[256,2048]{1,0:T(8,128)(2,1)S(1)}, bf16[256,2048]{1,0:T(8,128)(2,1)S(1)}, u32[]{:S(2)}, u32[]{:S(2)}) collective-permute-start(bf16[256,2048]{1,0:T(8,128)(2,1)S(1)} %collective-permute-done.27), channel_id=1, source_target_pairs={{0,4},{2,6},{4,0},{6,2},{8,12},{10,14},{12,8},{14,10},{16,20},{18,... | collective-permute-start | bytes 3145736 | tf_op jit(solution)/shard_map/ppermute | solution.py:58
  255.8 21.4 %collective-permute-start.31 = (bf16[256,2048]{1,0:T(8,128)(2,1)S(1)}, bf16[256,2048]{1,0:T(8,128)(2,1)S(1)}, u32[]{:S(2)}, u32[]{:S(2)}) collective-permute-start(bf16[256,2048]{1,0:T(8,128)(2,1)S(1)} %collective-permute-done.27), channel_id=1, source_target_pairs={{0,8},{2,10},{4,12},{6,14},{8,16},{10,18},{12,20},{14,22},{16,24},... | collective-permute-start | bytes 3145736 | tf_op jit(solution)/shard_map/ppermute | solution.py:58
  256.0 22.3 %collective-permute-start.32 = (bf16[256,2048]{1,0:T(8,128)(2,1)S(1)}, bf16[256,2048]{1,0:T(8,128)(2,1)S(1)}, u32[]{:S(2)}, u32[]{:S(2)}) collective-permute-start(bf16[256,2048]{1,0:T(8,128)(2,1)S(1)} %collective-permute-done.29), channel_id=1, source_target_pairs={{0,4},{2,6},{4,0},{6,2},{8,12},{10,14},{12,8},{14,10},{16,20},{18,... | collective-permute-start | bytes 3145736 | tf_op jit(solution)/shard_map/ppermute | solution.py:58
  278.3 23.3 %collective-permute-start.33 = (bf16[256,2048]{1,0:T(8,128)(2,1)S(1)}, bf16[256,2048]{1,0:T(8,128)(2,1)S(1)}, u32[]{:S(2)}, u32[]{:S(2)}) collective-permute-start(bf16[256,2048]{1,0:T(8,128)(2,1)S(1)} %collective-permute-done.31), channel_id=1, source_target_pairs={{0,4},{2,6},{4,0},{6,2},{8,12},{10,14},{12,8},{14,10},{16,20},{18,... | collective-permute-start | bytes 3145736 | tf_op jit(solution)/shard_map/ppermute | solution.py:58
  279.9 21.7 %collective-permute-start.34 = (bf16[2,256,1024]{2,1,0:T(8,128)(2,1)S(1)}, bf16[2,256,1024]{2,1,0:T(8,128)(2,1)S(1)}, u32[]{:S(2)}, u32[]{:S(2)}) collective-permute-start(bf16[2,256,1024]{2,1,0:T(8,128)(2,1)S(1)} %get-tuple-element.234), channel_id=1, source_target_pairs={{0,24},{2,26},{4,28},{6,30},{8,0},{10,2},{12,4},{14,6},{16,8},{18,... | collective-permute-start | bytes 3145736 | tf_op jit(solution)/shard_map/ppermute | solution.py:58
  301.6 27.0 %collective-permute-start.35 = (bf16[512,1024]{1,0:T(8,128)(2,1)S(1)}, bf16[512,1024]{1,0:T(8,128)(2,1)S(1)}, u32[]{:S(2)}, u32[]{:S(2)}) collective-permute-start(bf16[512,1024]{1,0:T(8,128)(2,1)S(1)} %get-tuple-element.238), channel_id=1, source_target_pairs={{0,4},{2,6},{4,0},{6,2},{8,12},{10,14},{12,8},{14,10},{16,20},{18,... | collective-permute-start | bytes 3145736 | tf_op jit(solution)/shard_map/ppermute | solution.py:58
  303.2 25.4 %collective-permute-start.36 = (bf16[2,256,1024]{2,1,0:T(8,128)(2,1)S(1)}, bf16[2,256,1024]{2,1,0:T(8,128)(2,1)S(1)}, u32[]{:S(2)}, u32[]{:S(2)}) collective-permute-start(bf16[2,256,1024]{2,1,0:T(8,128)(2,1)S(1)} %get-tuple-element.239), channel_id=1, source_target_pairs={{0,8},{2,10},{4,12},{6,14},{8,16},{10,18},{12,20},{14,22},{16,24},... | collective-permute-start | bytes 3145736 | tf_op jit(solution)/shard_map/ppermute | solution.py:58
  331.5 26.5 %collective-permute-start.39 = (bf16[512,1024]{1,0:T(8,128)(2,1)}, bf16[512,1024]{1,0:T(8,128)(2,1)S(1)}, u32[]{:S(2)}, u32[]{:S(2)}) collective-permute-start(bf16[512,1024]{1,0:T(8,128)(2,1)} %get-tuple-element.245), channel_id=1, source_target_pairs={{0,4},{2,6},{4,0},{6,2},{8,12},{10,14},{12,8},{14,10},{16,20},{18,... | collective-permute-start | bytes 3145736 | tf_op jit(solution)/shard_map/ppermute | solution.py:58
  332.9 27.3 %collective-permute-start.40 = (bf16[2,256,1024]{2,1,0:T(8,128)(2,1)}, bf16[2,256,1024]{2,1,0:T(8,128)(2,1)}, u32[]{:S(2)}, u32[]{:S(2)}) collective-permute-start(bf16[2,256,1024]{2,1,0:T(8,128)(2,1)} %add_convert_fusion.6), channel_id=1, source_target_pairs={{0,24},{2,26},{4,28},{6,30},{8,0},{10,2},{12,4},{14,6},{16,8},{18,... | collective-permute-start | bytes 3145736 | tf_op jit(solution)/shard_map/ppermute | solution.py:58
  345.6 49.7 %collective-permute-start.38 = (bf16[512,2048]{1,0:T(8,128)(2,1)S(1)}, bf16[512,2048]{1,0:T(8,128)(2,1)S(1)}, u32[]{:S(2)}, u32[]{:S(2)}) collective-permute-start(bf16[512,2048]{1,0:T(8,128)(2,1)S(1)} %add_convert_fusion.1.d_a), channel_id=1, source_target_pairs={{0,1},{1,0},{2,3},{3,2},{4,5},{5,4},{6,7},{7,6},{8,9},{9,8},{10,11... | collective-permute-start | bytes 6291464 | tf_op jit(solution)/shard_map/ppermute | solution.py:80
  360.1 16.7 %collective-permute-start.42 = (bf16[256,1024]{1,0:T(8,128)(2,1)S(1)}, bf16[256,1024]{1,0:T(8,128)(2,1)S(1)}, u32[]{:S(2)}, u32[]{:S(2)}) collective-permute-start(bf16[256,1024]{1,0:T(8,128)(2,1)S(1)} %get-tuple-element.255), channel_id=1, source_target_pairs={{0,24},{2,26},{4,28},{6,30},{8,0},{10,2},{12,4},{14,6},{16,8},{18,... | collective-permute-start | bytes 1572872 | tf_op jit(solution)/shard_map/ppermute | solution.py:58
  364.4 22.6 %collective-permute-start.43 = (bf16[256,1024]{1,0:T(8,128)(2,1)S(1)}, bf16[256,1024]{1,0:T(8,128)(2,1)S(1)}, u32[]{:S(2)}, u32[]{:S(2)}) collective-permute-start(bf16[256,1024]{1,0:T(8,128)(2,1)S(1)} %get-tuple-element.256), channel_id=1, source_target_pairs={{0,8},{2,10},{4,12},{6,14},{8,16},{10,18},{12,20},{14,22},{16,24},... | collective-permute-start | bytes 1572872 | tf_op jit(solution)/shard_map/ppermute | solution.py:58
  364.4 24.1 %collective-permute-start.41 = (bf16[256,2048]{1,0:T(8,128)(2,1)S(1)}, bf16[256,2048]{1,0:T(8,128)(2,1)S(1)}, u32[]{:S(2)}, u32[]{:S(2)}) collective-permute-start(bf16[256,2048]{1,0:T(8,128)(2,1)S(1)} %get-tuple-element.254), channel_id=1, source_target_pairs={{0,4},{2,6},{4,0},{6,2},{8,12},{10,14},{12,8},{14,10},{16,20},{18,... | collective-permute-start | bytes 3145736 | tf_op jit(solution)/shard_map/ppermute | solution.py:58
  388.9 24.2 %collective-permute-start.46 = (bf16[256,2048]{1,0:T(8,128)(2,1)S(1)}, bf16[256,2048]{1,0:T(8,128)(2,1)S(1)}, u32[]{:S(2)}, u32[]{:S(2)}) collective-permute-start(bf16[256,2048]{1,0:T(8,128)(2,1)S(1)} %add_convert_fusion.5), channel_id=1, source_target_pairs={{0,24},{2,26},{4,28},{6,30},{8,0},{10,2},{12,4},{14,6},{16,8},{18,... | collective-permute-start | bytes 3145736 | tf_op jit(solution)/shard_map/ppermute | solution.py:58
  392.7 22.8 %collective-permute-start.45 = (bf16[256,2048]{1,0:T(8,128)(2,1)}, bf16[256,2048]{1,0:T(8,128)(2,1)S(1)}, u32[]{:S(2)}, u32[]{:S(2)}) collective-permute-start(bf16[256,2048]{1,0:T(8,128)(2,1)} %get-tuple-element.262), channel_id=1, source_target_pairs={{0,4},{2,6},{4,0},{6,2},{8,12},{10,14},{12,8},{14,10},{16,20},{18,... | collective-permute-start | bytes 3145736 | tf_op jit(solution)/shard_map/ppermute | solution.py:58
  415.5 23.6 %collective-permute-start.48 = (bf16[256,1024]{1,0:T(8,128)(2,1)}, bf16[256,1024]{1,0:T(8,128)(2,1)S(1)}, u32[]{:S(2)}, u32[]{:S(2)}) collective-permute-start(bf16[256,1024]{1,0:T(8,128)(2,1)} %fusion.49), channel_id=1, source_target_pairs={{0,4},{2,6},{4,0},{6,2},{8,12},{10,14},{12,8},{14,10},{16,20},{18,... | collective-permute-start | bytes 1572872 | tf_op jit(solution)/shard_map/ppermute | solution.py:58
  415.8 35.9 %collective-permute-start.50 = (bf16[256,1024]{1,0:T(8,128)(2,1)}, bf16[256,1024]{1,0:T(8,128)(2,1)S(1)}, u32[]{:S(2)}, u32[]{:S(2)}) collective-permute-start(bf16[256,1024]{1,0:T(8,128)(2,1)} %add_convert_fusion.10), channel_id=1, source_target_pairs={{0,24},{2,26},{4,28},{6,30},{8,0},{10,2},{12,4},{14,6},{16,8},{18,... | collective-permute-start | bytes 1572872 | tf_op jit(solution)/shard_map/ppermute | solution.py:58
  418.0 33.7 %collective-permute-start.49 = (bf16[256,2048]{1,0:T(8,128)(2,1)S(1)}, bf16[256,2048]{1,0:T(8,128)(2,1)S(1)}, u32[]{:S(2)}, u32[]{:S(2)}) collective-permute-start(bf16[256,2048]{1,0:T(8,128)(2,1)S(1)} %add_convert_fusion.4), channel_id=1, source_target_pairs={{0,8},{2,10},{4,12},{6,14},{8,16},{10,18},{12,20},{14,22},{16,24},... | collective-permute-start | bytes 3145736 | tf_op jit(solution)/shard_map/ppermute | solution.py:58
  418.3 33.4 %collective-permute-start.47 = (bf16[256,2048]{1,0:T(8,128)(2,1)S(1)}, bf16[256,2048]{1,0:T(8,128)(2,1)S(1)}, u32[]{:S(2)}, u32[]{:S(2)}) collective-permute-start(bf16[256,2048]{1,0:T(8,128)(2,1)S(1)} %copy-done.42), channel_id=1, source_target_pairs={{0,4},{2,6},{4,0},{6,2},{8,12},{10,14},{12,8},{14,10},{16,20},{18,... | collective-permute-start | bytes 3145736 | tf_op jit(solution)/shard_map/ppermute | solution.py:58
  439.0 12.7 %collective-permute-start.51 = (bf16[512,2048]{1,0:T(8,128)(2,1)S(1)}, bf16[512,2048]{1,0:T(8,128)(2,1)S(1)}, u32[]{:S(2)}, u32[]{:S(2)}) collective-permute-start(bf16[512,2048]{1,0:T(8,128)(2,1)S(1)} %convolution_convert_fusion.8), channel_id=1, source_target_pairs={{0,2},{2,0},{4,6},{6,4},{8,10},{10,8},{12,14},{14,12},{16,18},{18,... | collective-permute-start | bytes 6291464 | tf_op jit(solution)/shard_map/ppermute | solution.py:70
  452.3 23.6 %collective-permute-start.52 = (bf16[256,2048]{1,0:T(8,128)(2,1)S(1)}, bf16[256,2048]{1,0:T(8,128)(2,1)S(1)}, u32[]{:S(2)}, u32[]{:S(2)}) collective-permute-start(bf16[256,2048]{1,0:T(8,128)(2,1)S(1)} %copy-done.41), channel_id=1, source_target_pairs={{0,4},{2,6},{4,0},{6,2},{8,12},{10,14},{12,8},{14,10},{16,20},{18,... | collective-permute-start | bytes 3145736 | tf_op jit(solution)/shard_map/ppermute | solution.py:58
  452.6 23.7 %collective-permute-start.53 = (bf16[256,2048]{1,0:T(8,128)(2,1)S(1)}, bf16[256,2048]{1,0:T(8,128)(2,1)S(1)}, u32[]{:S(2)}, u32[]{:S(2)}) collective-permute-start(bf16[256,2048]{1,0:T(8,128)(2,1)S(1)} %add_convert_fusion.3), channel_id=1, source_target_pairs={{0,24},{2,26},{4,28},{6,30},{8,0},{10,2},{12,4},{14,6},{16,8},{18,... | collective-permute-start | bytes 3145736 | tf_op jit(solution)/shard_map/ppermute | solution.py:58
  463.8 52.4 %collective-permute-start.61 = (bf16[512,2048]{1,0:T(8,128)(2,1)S(1)}, bf16[512,2048]{1,0:T(8,128)(2,1)S(1)}, u32[]{:S(2)}, u32[]{:S(2)}) collective-permute-start(bf16[512,2048]{1,0:T(8,128)(2,1)S(1)} %add_convert_fusion.d_a), channel_id=1, source_target_pairs={{0,1},{1,0},{2,3},{3,2},{4,5},{5,4},{6,7},{7,6},{8,9},{9,8},{10,11... | collective-permute-start | bytes 6291464 | tf_op jit(solution)/shard_map/ppermute | solution.py:80
  476.3 22.8 %collective-permute-start.54 = (bf16[1024,512]{1,0:T(8,128)(2,1)}, bf16[1024,512]{1,0:T(8,128)(2,1)S(1)}, u32[]{:S(2)}, u32[]{:S(2)}) collective-permute-start(bf16[1024,512]{1,0:T(8,128)(2,1)} %fusion.36), channel_id=1, source_target_pairs={{0,4},{2,6},{4,0},{6,2},{8,12},{10,14},{12,8},{14,10},{16,20},{18,... | collective-permute-start | bytes 3145736 | tf_op jit(solution)/shard_map/ppermute | solution.py:58
  486.4 12.7 %collective-permute-start.55 = (bf16[512,2048]{1,0:T(8,128)(2,1)S(1)}, bf16[512,2048]{1,0:T(8,128)(2,1)S(1)}, u32[]{:S(2)}, u32[]{:S(2)}) collective-permute-start(bf16[512,2048]{1,0:T(8,128)(2,1)S(1)} %pad_maximum_fusion.1), channel_id=1, source_target_pairs={{0,2},{2,0},{4,6},{6,4},{8,10},{10,8},{12,14},{14,12},{16,18},{18,... | collective-permute-start | bytes 6291464 | tf_op jit(solution)/shard_map/ppermute | solution.py:70
  487.3 11.8 %collective-permute-start.56 = (f32[128,2048]{1,0:T(8,128)S(1)}, f32[128,2048]{1,0:T(8,128)S(1)}, u32[]{:S(2)}, u32[]{:S(2)}) collective-permute-start(f32[128,2048]{1,0:T(8,128)S(1)} %get-tuple-element.395), channel_id=1, source_target_pairs={{0,2},{2,0},{4,6},{6,4},{8,10},{10,8},{12,14},{14,12},{16,18},{18,... | collective-permute-start | bytes 3145736 | tf_op jit(solution)/shard_map/ppermute | solution.py:70
  500.3 30.0 %collective-permute-start.59 = (bf16[256,512]{1,0:T(8,128)(2,1)}, bf16[256,512]{1,0:T(8,128)(2,1)}, u32[]{:S(2)}, u32[]{:S(2)}) collective-permute-start(bf16[256,512]{1,0:T(8,128)(2,1)} %get-tuple-element.300), channel_id=1, source_target_pairs={{0,24},{2,26},{4,28},{6,30},{8,0},{10,2},{12,4},{14,6},{16,8},{18,... | collective-permute-start | bytes 786440 | tf_op jit(solution)/shard_map/ppermute | solution.py:58
  504.2 26.1 %collective-permute-start.60 = (bf16[256,512]{1,0:T(8,128)(2,1)}, bf16[256,512]{1,0:T(8,128)(2,1)}, u32[]{:S(2)}, u32[]{:S(2)}) collective-permute-start(bf16[256,512]{1,0:T(8,128)(2,1)} %get-tuple-element.302), channel_id=1, source_target_pairs={{0,8},{2,10},{4,12},{6,14},{8,16},{10,18},{12,20},{14,22},{16,24},... | collective-permute-start | bytes 786440 | tf_op jit(solution)/shard_map/ppermute | solution.py:58
  504.2 26.1 %collective-permute-start.58 = (bf16[256,1536]{1,0:T(8,128)(2,1)}, bf16[256,1536]{1,0:T(8,128)(2,1)}, u32[]{:S(2)}, u32[]{:S(2)}) collective-permute-start(bf16[256,1536]{1,0:T(8,128)(2,1)} %get-tuple-element.298), channel_id=1, source_target_pairs={{0,4},{2,6},{4,0},{6,2},{8,12},{10,14},{12,8},{14,10},{16,20},{18,... | collective-permute-start | bytes 2359304 | tf_op jit(solution)/shard_map/ppermute | solution.py:58
  514.5 45.4 %collective-permute-start.57 = (bf16[512,2048]{1,0:T(8,128)(2,1)S(1)}, bf16[512,2048]{1,0:T(8,128)(2,1)}, u32[]{:S(2)}, u32[]{:S(2)}) collective-permute-start(bf16[512,2048]{1,0:T(8,128)(2,1)S(1)} %fusion.16), channel_id=1, source_target_pairs={{0,1},{1,0},{2,3},{3,2},{4,5},{5,4},{6,7},{7,6},{8,9},{9,8},{10,11... | collective-permute-start | bytes 6291464 | tf_op jit(solution)/shard_map/ppermute | solution.py:80
  531.6 10.6 %collective-permute-start.64 = (bf16[256,512]{1,0:T(8,128)(2,1)S(1)}, bf16[256,512]{1,0:T(8,128)(2,1)S(1)}, u32[]{:S(2)}, u32[]{:S(2)}) collective-permute-start(bf16[256,512]{1,0:T(8,128)(2,1)S(1)} %add_convert_fusion.13), channel_id=1, source_target_pairs={{0,24},{2,26},{4,28},{6,30},{8,0},{10,2},{12,4},{14,6},{16,8},{18,... | collective-permute-start | bytes 786440 | tf_op jit(solution)/shard_map/ppermute | solution.py:58
  536.8 19.8 %collective-permute-start.63 = (bf16[256,1536]{1,0:T(8,128)(2,1)S(1)}, bf16[256,1536]{1,0:T(8,128)(2,1)S(1)}, u32[]{:S(2)}, u32[]{:S(2)}) collective-permute-start(bf16[256,1536]{1,0:T(8,128)(2,1)S(1)} %add_convert_fusion.9), channel_id=1, source_target_pairs={{0,24},{2,26},{4,28},{6,30},{8,0},{10,2},{12,4},{14,6},{16,8},{18,... | collective-permute-start | bytes 2359304 | tf_op jit(solution)/shard_map/ppermute | solution.py:58
  537.1 19.5 %collective-permute-start.62 = (bf16[256,1536]{1,0:T(8,128)(2,1)S(1)}, bf16[256,1536]{1,0:T(8,128)(2,1)S(1)}, u32[]{:S(2)}, u32[]{:S(2)}) collective-permute-start(bf16[256,1536]{1,0:T(8,128)(2,1)S(1)} %copy-done.46), channel_id=1, source_target_pairs={{0,4},{2,6},{4,0},{6,2},{8,12},{10,14},{12,8},{14,10},{16,20},{18,... | collective-permute-start | bytes 2359304 | tf_op jit(solution)/shard_map/ppermute | solution.py:58
  539.8 16.8 %collective-permute-start.65 = (f32[128,2048]{1,0:T(8,128)S(1)}, f32[128,2048]{1,0:T(8,128)S(1)}, u32[]{:S(2)}, u32[]{:S(2)}) collective-permute-start(f32[128,2048]{1,0:T(8,128)S(1)} %get-tuple-element.393), channel_id=1, source_target_pairs={{0,2},{2,0},{4,6},{6,4},{8,10},{10,8},{12,14},{14,12},{16,18},{18,... | collective-permute-start | bytes 3145736 | tf_op jit(solution)/shard_map/ppermute | solution.py:70
  557.7 17.7 %collective-permute-start.67 = (bf16[256,1536]{1,0:T(8,128)(2,1)}, bf16[256,1536]{1,0:T(8,128)(2,1)}, u32[]{:S(2)}, u32[]{:S(2)}) collective-permute-start(bf16[256,1536]{1,0:T(8,128)(2,1)} %add_convert_fusion.8), channel_id=1, source_target_pairs={{0,8},{2,10},{4,12},{6,14},{8,16},{10,18},{12,20},{14,22},{16,24},... | collective-permute-start | bytes 2359304 | tf_op jit(solution)/shard_map/ppermute | solution.py:58
  557.7 17.7 %collective-permute-start.66 = (bf16[256,1536]{1,0:T(8,128)(2,1)}, bf16[256,1536]{1,0:T(8,128)(2,1)}, u32[]{:S(2)}, u32[]{:S(2)}) collective-permute-start(bf16[256,1536]{1,0:T(8,128)(2,1)} %get-tuple-element.324), channel_id=1, source_target_pairs={{0,4},{2,6},{4,0},{6,2},{8,12},{10,14},{12,8},{14,10},{16,20},{18,... | collective-permute-start | bytes 2359304 | tf_op jit(solution)/shard_map/ppermute | solution.py:58
  578.2 14.9 %collective-permute-start.68 = (bf16[256,1536]{1,0:T(8,128)(2,1)S(1)}, bf16[256,1536]{1,0:T(8,128)(2,1)}, u32[]{:S(2)}, u32[]{:S(2)}) collective-permute-start(bf16[256,1536]{1,0:T(8,128)(2,1)S(1)} %copy-done.45), channel_id=1, source_target_pairs={{0,4},{2,6},{4,0},{6,2},{8,12},{10,14},{12,8},{14,10},{16,20},{18,... | collective-permute-start | bytes 2359304 | tf_op jit(solution)/shard_map/ppermute | solution.py:58
  578.7 15.7 %collective-permute-start.69 = (bf16[256,1536]{1,0:T(8,128)(2,1)}, bf16[256,1536]{1,0:T(8,128)(2,1)}, u32[]{:S(2)}, u32[]{:S(2)}) collective-permute-start(bf16[256,1536]{1,0:T(8,128)(2,1)} %add_convert_fusion.7), channel_id=1, source_target_pairs={{0,24},{2,26},{4,28},{6,30},{8,0},{10,2},{12,4},{14,6},{16,8},{18,... | collective-permute-start | bytes 2359304 | tf_op jit(solution)/shard_map/ppermute | solution.py:58
  582.4 15.8 %all-to-all-start = ((f32[16,14,128]{2,1,0:T(8,128)}), f32[16,14,128]{2,1,0:T(8,128)S(1)}, u32[]{:S(2)}, u32[]{:S(2)}) async-start(f32[16,14,128]{2,1,0:T(8,128)} %copy.47), calls=%async_computation | async-start | bytes 262144 | tf_op jit(solution)/shard_map/all_to_all | solution.py:760
  (88 other events, 995.0 us)

commit v6 on v5

--- a/solution.py
+++ b/solution.py
@@ -15,6 +15,7 @@
 CORES = 2
 TILE = 128
 CHUNK = 16
+UNROLL = 8
 
 
 def after(value, *earlier):
@@ -280,7 +281,7 @@
             body(pl.ds(pl.multiple_of(index * CHUNK, CHUNK), CHUNK))
             return carry
 
-        lax.fori_loop(0, count // CHUNK, step, 0)
+        lax.fori_loop(0, count // CHUNK, step, 0, unroll=UNROLL)
 
     def places(self):
         if not self.blocks:
@@ -559,6 +560,7 @@
         ph.close()
 
         z_d = {1: ph.send_z(s_d, 1)}
+        x_u = {kz: [ph.now(piece) for piece in x_u[kz]] for kz in x_u}
         x_u[2] = ph.gather_x(z_u[2])
         second = join(second_own, ph.begin(second_other))
         ph.end(second)
@@ -715,12 +717,12 @@
             first_back_kernel, relative, present, [tokens, *two(d_normed), d_hidden], mods, [F32], 2
         )
         ph.end(input_grad)
+        ph.close(20.0)
+
+        x_p[3] = p_rows(3)
+        p_2 = ph.send_z(p_sum(2).astype(BF16), 3)
         up_part = grid.by_core(ph.begin(up_mine), up_theirs, 1)
         ph.end(up_part)
-        ph.close(20.0)
-
-        x_p[3] = p_rows(3)
-        p_2 = ph.send_z(p_sum(2).astype(BF16), 3)
         o_1 = ph.send_z((out_sum(1) + ph.now(o_2).astype(F32)).astype(BF16), 3)
         row_sums = [jnp.sum(v.reshape(count, -1, 8, width), axis=2) for v in (sums1, sums2)]
         row_sums = ph.begin(jnp.concatenate(row_sums, axis=1))

time: 613 us -> 605 us (0.987)
  Pallas kernels: 64.6 us -> 45.7 us
  starting transfers between devices: 84 us -> 96.3 us
    pallas_call x6, Pallas kernels: 46.4 us -> 27.5 us  [by_rows(): pl.pallas_call(functools.partial(kernel, blocks), grid_spec=pltpu.Prefetc...]
    ppermute x52, starting transfers between devices: 71.3 us -> 84.3 us  [send(): out = lax.ppermute(value, 'dp', self.ring(dz, dx, 0))]
    unnamed x187 -> x184, local copies, waits for them, and re-layouts: 34.1 us -> 32.4 us
  transfers between devices with their start and end apart: 73 -> 73, of which waited for: 35 -> 35; matrix products, arithmetic and copies ran while one was open for 36% -> 36% of each run, Pallas kernels for 11% -> 8%
where the time goes in v6:
time: 605 us; the launch traced here: 597 us
  waiting for transfers between devices  221 us (37%)
  matrix products  143 us (24%)
  starting transfers between devices  96.3 us (16%)
  local copies, waits for them, and re-layouts  47.9 us (8%)
  Pallas kernels  45.7 us (8%)
  other arithmetic  39.9 us (7%)
    ppermute x52, waiting for transfers between devices, send(): out = lax.ppermute(value, 'dp', self.ring(dz, dx, 0))  206 us
    dot_general x16, matrix products, matmul(): lax.dot_general(lhs, rhs, (((1,), (1 if turned else 0,)), ((), ())), pref...  101 us
    ppermute x52, starting transfers between devices, send(): out = lax.ppermute(value, 'dp', self.ring(dz, dx, 0))  84.3 us
    dot_general x8, matrix products, dots(): lax.dot_general(lhs[:, kx * width:(kx + 1) * width], rhs, (((0,), (0,)),...  39.9 us
    unnamed x184, local copies, waits for them, and re-layouts  32.4 us
    pallas_call x6, Pallas kernels, by_rows(): pl.pallas_call(functools.partial(kernel, blocks), grid_spec=pltpu.Prefetc...  27.5 us
    pallas_call x2, Pallas kernels, by_image(): pl.pallas_call(kernel, grid=(rows // length,), in_specs=[block(operand.sh...  13.4 us
  transfers between devices with their start and end apart: 73, of which 35 were waited for; matrix products, arithmetic and copies ran while one was open for 36% of the time, Pallas kernels for 8%

profile of v6, /device:TPU:0, one launch (start us, length us, event | category | flops | bytes accessed | tf_op | source)
XLA Modules:
  0.0 596.5 jit_solution(13860084422245524975)
XLA Ops:
  7.7 2.6 collective-permute-start.2
  14.9 4.8 shard_map.144
  21.6 12.3 %collective-permute-done.4 = bf16[256,512]{1,0:T(8,128)(2,1)S(1)} collective-permute-done((bf16[256,512]{1,0:T(8,128)(2,1)}, bf16[256,512]{1,0:T(8,128)(2,1)S(1)}, u32[]{:S(2)}, u32[]{:S(2)}) %collective-permute-start.4) | collective-permute-done | bytes 262176 | tf_op jit(solution)/shard_map/ppermute | solution.py:59
  34.1 3.9 collective-permute-start.6
  41.0 2.4 shard_map.145
  43.6 3.0 constant_dynamic-update-slice_fusion.8
  46.7 7.8 %collective-permute-done.6 = bf16[256,1536]{0,1:T(8,128)(2,1)S(1)} collective-permute-done((bf16[256,1536]{0,1:T(8,128)(2,1)S(1)}, bf16[256,1536]{0,1:T(8,128)(2,1)S(1)}, u32[]{:S(2)}, u32[]{:S(2)}) %collective-permute-start.6) | collective-permute-done | bytes 786464 | tf_op jit(solution)/shard_map/ppermute | solution.py:59
  54.5 2.4 collective-permute-done.7
  60.9 15.8 %collective-permute-done.9 = bf16[256,1536]{0,1:T(8,128)(2,1)S(1)} collective-permute-done((bf16[256,1536]{0,1:T(8,128)(2,1)}, bf16[256,1536]{0,1:T(8,128)(2,1)S(1)}, u32[]{:S(2)}, u32[]{:S(2)}) %collective-permute-start.9) | collective-permute-done | bytes 786464 | tf_op jit(solution)/shard_map/ppermute | solution.py:59
  78.8 10.9 %collective-permute-done.11 = bf16[2,256,512]{2,1,0:T(8,128)(2,1)S(1)} collective-permute-done((bf16[2,256,512]{2,1,0:T(8,128)(2,1)S(1)}, bf16[2,256,512]{2,1,0:T(8,128)(2,1)S(1)}, u32[]{:S(2)}, u32[]{:S(2)}) %collective-permute-start.11) | collective-permute-done | bytes 524320 | tf_op jit(solution)/shard_map/ppermute | solution.py:59
  91.0 2.5 collective-permute-done.12
  93.6 3.5 collective-permute-start.14
  98.9 7.0 %convolution_convert_fusion.qkv_ref = bf16[1024,1536]{1,0:T(8,128)(2,1)S(1)} fusion(bf16[1024,2048]{1,0:T(8,128)(2,1)S(1)} %constant_dynamic-update-slice_fusion, bf16[2048,1536]{0,1:T(8,128)(2,1)S(1)} %constant_dynamic-update-slice_fusion.2), kind=kOutput, calls=%fused_computation.34 | convolution fusion | flops 6444023808 | bytes 13631488 | tf_op jit(solution)/shard_map/dot_general | solution.py:439
  105.8 4.5 shard_map.146
  110.4 6.3 %collective-permute-done.15 = bf16[2,256,512]{2,1,0:T(8,128)(2,1)S(1)} collective-permute-done((bf16[2,256,512]{2,1,0:T(8,128)(2,1)S(1)}, bf16[2,256,512]{2,1,0:T(8,128)(2,1)S(1)}, u32[]{:S(2)}, u32[]{:S(2)}) %collective-permute-start.15) | collective-permute-done | bytes 524320 | tf_op jit(solution)/shard_map/ppermute | solution.py:59
  118.3 4.1 collective-permute-done.17
  131.8 17.9 %collective-permute-done.19 = bf16[256,2048]{1,0:T(8,128)(2,1)} collective-permute-done((bf16[256,2048]{1,0:T(8,128)(2,1)S(1)}, bf16[256,2048]{1,0:T(8,128)(2,1)}, u32[]{:S(2)}, u32[]{:S(2)}) %collective-permute-start.19) | collective-permute-done | bytes 1048608 | tf_op jit(solution)/shard_map/ppermute | solution.py:59
  152.8 21.3 %collective-permute-done.21 = bf16[256,2048]{1,0:T(8,128)(2,1)} collective-permute-done((bf16[256,2048]{1,0:T(8,128)(2,1)S(1)}, bf16[256,2048]{1,0:T(8,128)(2,1)}, u32[]{:S(2)}, u32[]{:S(2)}) %collective-permute-start.21) | collective-permute-done | bytes 1048608 | tf_op jit(solution)/shard_map/ppermute | solution.py:59
  177.5 3.0 shard_map.148
  180.9 19.5 %collective-permute-done.25 = bf16[256,2048]{1,0:T(8,128)(2,1)} collective-permute-done((bf16[256,2048]{1,0:T(8,128)(2,1)}, bf16[256,2048]{1,0:T(8,128)(2,1)}, u32[]{:S(2)}, u32[]{:S(2)}) %collective-permute-start.25) | collective-permute-done | bytes 1048608 | tf_op jit(solution)/shard_map/ppermute | solution.py:59
  210.1 2.5 constant_dynamic-update-slice_fusion.20
  214.8 10.9 %collective-permute-done.27 = bf16[256,2048]{1,0:T(8,128)(2,1)S(1)} collective-permute-done((bf16[256,2048]{1,0:T(8,128)(2,1)S(1)}, bf16[256,2048]{1,0:T(8,128)(2,1)S(1)}, u32[]{:S(2)}, u32[]{:S(2)}) %collective-permute-start.27) | collective-permute-done | bytes 1048608 | tf_op jit(solution)/shard_map/ppermute | solution.py:59
  232.7 15.3 %fusion.13 = (bf16[1024,2048]{1,0:T(8,128)(2,1)}, f32[1024,2048]{1,0:T(8,128)}) fusion(bf16[1024,2048]{1,0:T(8,128)(2,1)S(1)} %copy-done.30, bf16[2048,2048]{1,0:T(8,128)(2,1)} %constant_dynamic-update-slice_fusion.16), kind=kOutput, calls=%fused_computation.16 | convolution fusion | flops 8608808960 | bytes 25165824 | tf_op jit(solution)/shard_map/dot_general | solution.py:439
  249.9 7.0 %convolution_convert_fusion.6 = bf16[1024,2048]{1,0:T(8,128)(2,1)S(1)} fusion(bf16[1024,2048]{1,0:T(8,128)(2,1)} %get-tuple-element.315, bf16[1024,2048]{1,0:T(8,128)(2,1)S(1)} %constant_dynamic-update-slice_fusion.14), kind=kOutput, calls=%fused_computation.40 | convolution fusion | flops 4297064448 | bytes 10485760 | tf_op jit(solution)/shard_map/dot_general | solution.py:176
  258.4 7.0 %convolution_convert_fusion.5 = bf16[1024,2048]{1,0:T(8,128)(2,1)S(1)} fusion(bf16[1024,2048]{1,0:T(8,128)(2,1)} %get-tuple-element.315, bf16[1024,2048]{1,0:T(8,128)(2,1)S(1)} %constant_dynamic-update-slice_fusion.14), kind=kOutput, calls=%fused_computation.39 | convolution fusion | flops 4297064448 | bytes 10485760 | tf_op jit(solution)/shard_map/dot_general | solution.py:176
  273.3 3.7 collective-permute-start.34
  278.1 7.9 %fusion.81 = f32[512,2048]{1,0:T(8,128)} fusion(bf16[512,1536]{1,0:T(8,128)(2,1)S(1)} %pad_maximum_fusion.3, bf16[1536,2048]{1,0:T(8,128)(2,1)} %constant_dynamic-update-slice_fusion.24), kind=kOutput, calls=%fused_computation.214 | convolution fusion | flops 3221225472 | bytes 12058624 | tf_op jit(solution)/shard_map/dot_general | solution.py:439
  286.0 5.0 fusion.82
  291.1 3.8 collective-permute-done.33
  295.2 10.3 %collective-permute-start.35 = (bf16[512,1024]{1,0:T(8,128)(2,1)}, bf16[512,1024]{1,0:T(8,128)(2,1)S(1)}, u32[]{:S(2)}, u32[]{:S(2)}) collective-permute-start(bf16[512,1024]{1,0:T(8,128)(2,1)} %get-tuple-element.250), channel_id=1, source_target_pairs={{0,4},{2,6},{4,0},{6,2},{8,12},{10,14},{12,8},{14,10},{16,20},{18,... | collective-permute-start | bytes 3145736 | tf_op jit(solution)/shard_map/ppermute | solution.py:59
  307.1 11.5 %fusion.15 = bf16[1024,2048]{1,0:T(8,128)(2,1)} fusion(f32[512,2048]{1,0:T(8,128)} %fusion.82, f32[512,2048]{1,0:T(8,128)} %fusion.81, f32[1024,2048]{1,0:T(8,128)} %get-tuple-element.243, bf16[1024,512]{1,0:T(8,128)(2,1)S(1)} %pad_maximum_fusion.5, bf16[512,2048]{1,0:T(8,128)(2,1)S(1)} %constant_dynamic-update-slice_fusion.30), kind=kOutput, calls=%fused_computation.19 | convolution fusion | flops 2191523840 | bytes 24117248 | tf_op jit(solution)/shard_map/dot_general | solution.py:439
  318.6 9.9 %convolution_convert_fusion.9 = bf16[512,2048]{1,0:T(8,128)(2,1)} fusion(bf16[2048,2048]{1,0:T(8,128)(2,1)} %constant_dynamic-update-slice_fusion.16, bf16[1024,2048]{1,0:T(8,128)(2,1)} %fusion.15), kind=kOutput, calls=%fused_computation.43 | convolution fusion | flops 4296015872 | bytes 12582912 | tf_op jit(solution)/shard_map/dot_general | solution.py:439
  330.0 2.8 collective-permute-done.37
  332.8 4.3 collective-permute-start.40
  337.1 8.2 %add_convert_fusion.1.d_a = bf16[512,2048]{1,0:T(8,128)(2,1)S(1)} fusion(bf16[512,2048]{1,0:T(8,128)(2,1)S(1)} %collective-permute-done.37, bf16[512,2048]{1,0:T(8,128)(2,1)S(1)} %slice-done.4, bf16[2048,2048]{1,0:T(8,128)(2,1)} %constant_dynamic-update-slice_fusion.16), kind=kOutput, calls=%fused_computation.32 | convolution fusion | flops 4298113024 | bytes 14680064 | tf_op jit(solution)/shard_map/dot_general | solution.py:439
  346.8 7.4 %convolution_convert_fusion.4 = bf16[1024,2048]{1,0:T(8,128)(2,1)S(1)} fusion(bf16[1024,2048]{1,0:T(8,128)(2,1)} %fusion.15, bf16[1024,2048]{1,0:T(8,128)(2,1)} %copy-done.29), kind=kOutput, calls=%fused_computation.38 | convolution fusion | flops 4297064448 | bytes 10485760 | tf_op jit(solution)/shard_map/dot_general | solution.py:176
  360.1 4.3 collective-permute-start.42
  366.1 6.5 %convolution_convert_fusion.3 = bf16[1024,2048]{1,0:T(8,128)(2,1)S(1)} fusion(bf16[1024,2048]{1,0:T(8,128)(2,1)S(1)} %copy-done.24, bf16[1024,2048]{1,0:T(8,128)(2,1)} %copy-done.29), kind=kOutput, calls=%fused_computation.37 | convolution fusion | flops 4297064448 | bytes 10485760 | tf_op jit(solution)/shard_map/dot_general | solution.py:176
  372.6 2.6 convert_add_fusion.1
  376.8 10.2 %collective-permute-done.43 = bf16[256,1024]{1,0:T(8,128)(2,1)S(1)} collective-permute-done((bf16[256,1024]{1,0:T(8,128)(2,1)S(1)}, bf16[256,1024]{1,0:T(8,128)(2,1)S(1)}, u32[]{:S(2)}, u32[]{:S(2)}) %collective-permute-start.43) | collective-permute-done | bytes 524320 | tf_op jit(solution)/shard_map/ppermute | solution.py:59
  388.9 3.8 collective-permute-start.46
  396.4 10.4 %shard_map.149 = (f32[512,2048]{1,0:T(8,128)}, bf16[512,2048]{1,0:T(8,128)(2,1)S(1)}, f32[2,24,2048]{2,1,0:T(8,128)S(1)}) custom-call(s32[8]{0:T(128)S(1)} %copy-done.8, s32[2]{0:T(128)S(1)} %copy-done.11, f32[512,2048]{1,0:T(8,128)} %copy-done.12, bf16[512,2048]{1,0:T(8,128)(2,1)S(1)} %add_convert_fusion.2.att_a, ...), custom_call_target="tpu_custom_call" | custom-call | flops 6291456000 | bytes 8388608 | tf_op jit(solution)/shard_map/pallas_call | solution.py:422
  407.0 6.0 %collective-permute-done.46 = bf16[256,2048]{1,0:T(8,128)(2,1)S(1)} collective-permute-done((bf16[256,2048]{1,0:T(8,128)(2,1)S(1)}, bf16[256,2048]{1,0:T(8,128)(2,1)S(1)}, u32[]{:S(2)}, u32[]{:S(2)}) %collective-permute-start.46) | collective-permute-done | bytes 1048608 | tf_op jit(solution)/shard_map/ppermute | solution.py:59
  413.0 2.9 collective-permute-done.45
  423.0 8.9 %shard_map.150 = bf16[1024,1536]{1,0:T(8,128)(2,1)S(1)} custom-call(bf16[1024,1536]{1,0:T(8,128)(2,1)S(1)} %copy-done.3, bf16[1024,512]{1,0:T(8,128)(2,1)S(1)} %convolution_convert_fusion.11.d_mixed_ref), custom_call_target="tpu_custom_call" | custom-call | flops 3221225472 | bytes 8388608 | tf_op jit(solution)/shard_map/pallas_call | solution.py:250
  431.9 7.5 %convolution_convert_fusion.8 = bf16[512,2048]{1,0:T(8,128)(2,1)S(1)} fusion(bf16[2048,1536]{0,1:T(8,128)(2,1)} %copy-done.64, bf16[1024,1536]{1,0:T(8,128)(2,1)S(1)} %shard_map.150), kind=kOutput, calls=%fused_computation.42 | convolution fusion | flops 3222274048 | bytes 9961472 | tf_op jit(solution)/shard_map/dot_general | solution.py:439
  439.6 10.0 %collective-permute-done.49 = bf16[256,2048]{1,0:T(8,128)(2,1)S(1)} collective-permute-done((bf16[256,2048]{1,0:T(8,128)(2,1)S(1)}, bf16[256,2048]{1,0:T(8,128)(2,1)S(1)}, u32[]{:S(2)}, u32[]{:S(2)}) %collective-permute-start.49) | collective-permute-done | bytes 1048608 | tf_op jit(solution)/shard_map/ppermute | solution.py:59
  453.6 6.5 %add_convert_fusion.d_a = bf16[512,2048]{1,0:T(8,128)(2,1)S(1)} fusion(bf16[512,2048]{1,0:T(8,128)(2,1)S(1)} %collective-permute-done.51, bf16[512,1536]{1,0:T(8,128)(2,1)S(1)} %slice-done, bf16[2048,1536]{0,1:T(8,128)(2,1)} %copy-done.64), kind=kOutput, calls=%fused_computation.31 | convolution fusion | flops 3224371200 | bytes 12058624 | tf_op jit(solution)/shard_map/dot_general | solution.py:439
  465.9 3.7 convolution_convert_fusion.2
  471.4 4.8 convolution_convert_fusion.1
  477.0 2.9 fusion.42
  479.9 6.9 %convolution_convert_fusion.7 = bf16[512,1536]{1,0:T(8,128)(2,1)S(1)} fusion(bf16[1536,2048]{1,0:T(8,128)(2,1)} %constant_dynamic-update-slice_fusion.24, bf16[1024,2048]{1,0:T(8,128)(2,1)} %get-tuple-element.315), kind=kOutput, calls=%fused_computation.41 | convolution fusion | flops 3222011904 | bytes 9961472 | tf_op jit(solution)/shard_map/dot_general | solution.py:439
  488.6 10.7 %collective-permute-done.54 = bf16[1024,512]{1,0:T(8,128)(2,1)S(1)} collective-permute-done((bf16[1024,512]{1,0:T(8,128)(2,1)}, bf16[1024,512]{1,0:T(8,128)(2,1)S(1)}, u32[]{:S(2)}, u32[]{:S(2)}) %collective-permute-start.54) | collective-permute-done | bytes 1048608 | tf_op jit(solution)/shard_map/ppermute | solution.py:59
  504.8 6.3 %fusion.30 = f32[512,1536]{1,0:T(8,128)S(1)} fusion(bf16[1536,2048]{1,0:T(8,128)(2,1)} %constant_dynamic-update-slice_fusion.24, bf16[1024,2048]{1,0:T(8,128)(2,1)} %get-tuple-element.315), kind=kOutput, calls=%fused_computation.70 | convolution fusion | flops 3221225472 | bytes 11534336 | tf_op jit(solution)/shard_map/dot_general | solution.py:439
  514.1 7.0 %shard_map.151 = (f32[512,2048]{1,0:T(8,128)}, f32[2,16,2048]{2,1,0:T(8,128)S(1)}) custom-call(s32[8]{0:T(128)S(1)} %copy-done.8, s32[2]{0:T(128)S(1)} %copy-done.11, bf16[512,2048]{1,0:T(8,128)(2,1)S(1)} %copy-done.16, bf16[512,2048]{1,0:T(8,128)(2,1)S(1)} %add_convert_fusion.d_a, bf16[512,2048]{1,0:T(8,128)(2,1)S(1)} %collective-permute-done.61.d_b, ...), custom_call_target="tpu_custom_call" | custom-call | flops 6291456000 | bytes 8388608 | tf_op jit(solution)/shard_map/pallas_call | solution.py:422
  522.7 3.6 collective-permute-start.64
  533.0 12.2 %collective-permute-done.63 = bf16[256,1536]{1,0:T(8,128)(2,1)S(1)} collective-permute-done((bf16[256,1536]{1,0:T(8,128)(2,1)S(1)}, bf16[256,1536]{1,0:T(8,128)(2,1)S(1)}, u32[]{:S(2)}, u32[]{:S(2)}) %collective-permute-start.63) | collective-permute-done | bytes 786464 | tf_op jit(solution)/shard_map/ppermute | solution.py:59
  545.2 2.5 add_convert_fusion.8
  550.5 4.9 collective-permute-done.57
  555.7 3.4 shard_map.152
  559.4 6.4 %collective-permute-done.67 = bf16[256,1536]{1,0:T(8,128)(2,1)S(1)} collective-permute-done((bf16[256,1536]{1,0:T(8,128)(2,1)}, bf16[256,1536]{1,0:T(8,128)(2,1)S(1)}, u32[]{:S(2)}, u32[]{:S(2)}) %collective-permute-start.67) | collective-permute-done | bytes 786464 | tf_op jit(solution)/shard_map/ppermute | solution.py:59
  565.8 3.1 add_convert_fusion.7
  573.4 3.5 all-to-all-start
  576.9 7.6 %collective-permute-done.68 = bf16[256,1536]{1,0:T(8,128)(2,1)S(1)} collective-permute-done((bf16[256,1536]{1,0:T(8,128)(2,1)S(1)}, bf16[256,1536]{1,0:T(8,128)(2,1)S(1)}, u32[]{:S(2)}, u32[]{:S(2)}) %collective-permute-start.68) | collective-permute-done | bytes 786464 | tf_op jit(solution)/shard_map/ppermute | solution.py:59
  (399 shorter events, 151.9 us)
Async XLA Ops:
  7.7 26.4 %collective-permute-start.2 = (bf16[256,1536]{0,1:T(8,128)(2,1)S(1)}, bf16[256,1536]{0,1:T(8,128)(2,1)S(1)}, u32[]{:S(2)}, u32[]{:S(2)}) collective-permute-start(bf16[256,1536]{0,1:T(8,128)(2,1)S(1)} %get-tuple-element.186), channel_id=1, source_target_pairs={{0,4},{2,6},{4,0},{6,2},{8,12},{10,14},{12,8},{14,10},{16,20},{18,... | collective-permute-start | bytes 2359304 | tf_op jit(solution)/shard_map/ppermute | solution.py:59
  10.3 23.7 %collective-permute-start.1 = (bf16[256,1536]{0,1:T(8,128)(2,1)S(1)}, bf16[256,1536]{0,1:T(8,128)(2,1)}, u32[]{:S(2)}, u32[]{:S(2)}) collective-permute-start(bf16[256,1536]{0,1:T(8,128)(2,1)S(1)} %get-tuple-element.186), channel_id=1, source_target_pairs={{0,8},{2,10},{4,12},{6,14},{8,16},{10,18},{12,20},{14,22},{16,24},... | collective-permute-start | bytes 2359304 | tf_op jit(solution)/shard_map/ppermute | solution.py:59
  12.7 21.2 %collective-permute-start.4 = (bf16[256,512]{1,0:T(8,128)(2,1)}, bf16[256,512]{1,0:T(8,128)(2,1)S(1)}, u32[]{:S(2)}, u32[]{:S(2)}) collective-permute-start(bf16[256,512]{1,0:T(8,128)(2,1)} %get-tuple-element.385), channel_id=1, source_target_pairs={{0,4},{2,6},{4,0},{6,2},{8,12},{10,14},{12,8},{14,10},{16,20},{18,... | collective-permute-start | bytes 786440 | tf_op jit(solution)/shard_map/ppermute | solution.py:59
  34.1 20.4 %collective-permute-start.6 = (bf16[256,1536]{0,1:T(8,128)(2,1)S(1)}, bf16[256,1536]{0,1:T(8,128)(2,1)S(1)}, u32[]{:S(2)}, u32[]{:S(2)}) collective-permute-start(bf16[256,1536]{0,1:T(8,128)(2,1)S(1)} %get-tuple-element.186), channel_id=1, source_target_pairs={{0,24},{2,26},{4,28},{6,30},{8,0},{10,2},{12,4},{14,6},{16,8},{18,... | collective-permute-start | bytes 2359304 | tf_op jit(solution)/shard_map/ppermute | solution.py:59
  38.0 18.9 %collective-permute-start.7 = (bf16[256,1536]{0,1:T(8,128)(2,1)}, bf16[256,1536]{0,1:T(8,128)(2,1)S(1)}, u32[]{:S(2)}, u32[]{:S(2)}) collective-permute-start(bf16[256,1536]{0,1:T(8,128)(2,1)} %collective-permute-done.1), channel_id=1, source_target_pairs={{0,4},{2,6},{4,0},{6,2},{8,12},{10,14},{12,8},{14,10},{16,20},{18,... | collective-permute-start | bytes 2359304 | tf_op jit(solution)/shard_map/ppermute | solution.py:59
  43.5 13.4 %collective-permute-start.5 = (bf16[512,2048]{1,0:T(8,128)(2,1)S(1)}, bf16[512,2048]{1,0:T(8,128)(2,1)S(1)}, u32[]{:S(2)}, u32[]{:S(2)}) collective-permute-start(bf16[512,2048]{1,0:T(8,128)(2,1)S(1)} %get-tuple-element.190), channel_id=1, source_target_pairs={{0,2},{2,0},{4,6},{6,4},{8,10},{10,8},{12,14},{14,12},{16,18},{18,... | collective-permute-start | bytes 6291464 | tf_op jit(solution)/shard_map/ppermute | solution.py:71
  56.9 19.8 %collective-permute-start.9 = (bf16[256,1536]{0,1:T(8,128)(2,1)}, bf16[256,1536]{0,1:T(8,128)(2,1)S(1)}, u32[]{:S(2)}, u32[]{:S(2)}) collective-permute-start(bf16[256,1536]{0,1:T(8,128)(2,1)} %collective-permute-done.1), channel_id=1, source_target_pairs={{0,8},{2,10},{4,12},{6,14},{8,16},{10,18},{12,20},{14,22},{16,24},... | collective-permute-start | bytes 2359304 | tf_op jit(solution)/shard_map/ppermute | solution.py:59
  56.9 19.8 %collective-permute-start.10 = (bf16[256,1536]{0,1:T(8,128)(2,1)S(1)}, bf16[256,1536]{0,1:T(8,128)(2,1)S(1)}, u32[]{:S(2)}, u32[]{:S(2)}) collective-permute-start(bf16[256,1536]{0,1:T(8,128)(2,1)S(1)} %collective-permute-done.6), channel_id=1, source_target_pairs={{0,4},{2,6},{4,0},{6,2},{8,12},{10,14},{12,8},{14,10},{16,20},{18,... | collective-permute-start | bytes 2359304 | tf_op jit(solution)/shard_map/ppermute | solution.py:59
  76.7 13.1 %collective-permute-start.11 = (bf16[2,256,512]{2,1,0:T(8,128)(2,1)S(1)}, bf16[2,256,512]{2,1,0:T(8,128)(2,1)S(1)}, u32[]{:S(2)}, u32[]{:S(2)}) collective-permute-start(bf16[2,256,512]{2,1,0:T(8,128)(2,1)S(1)} %pad_maximum_fusion.6), channel_id=1, source_target_pairs={{0,8},{2,10},{4,12},{6,14},{8,16},{10,18},{12,20},{14,22},{16,24},... | collective-permute-start | bytes 1572872 | tf_op jit(solution)/shard_map/ppermute | solution.py:59
  76.7 16.9 %collective-permute-start.12 = (bf16[256,1536]{0,1:T(8,128)(2,1)S(1)}, bf16[256,1536]{0,1:T(8,128)(2,1)S(1)}, u32[]{:S(2)}, u32[]{:S(2)}) collective-permute-start(bf16[256,1536]{0,1:T(8,128)(2,1)S(1)} %collective-permute-done.9), channel_id=1, source_target_pairs={{0,4},{2,6},{4,0},{6,2},{8,12},{10,14},{12,8},{14,10},{16,20},{18,... | collective-permute-start | bytes 2359304 | tf_op jit(solution)/shard_map/ppermute | solution.py:59
  78.3 11.5 %collective-permute-start.13 = (bf16[128,2048]{1,0:T(8,128)(2,1)S(1)}, bf16[128,2048]{1,0:T(8,128)(2,1)S(1)}, u32[]{:S(2)}, u32[]{:S(2)}) collective-permute-start(bf16[128,2048]{1,0:T(8,128)(2,1)S(1)} %get-tuple-element.418), channel_id=1, source_target_pairs={{0,2},{2,0},{4,6},{6,4},{8,10},{10,8},{12,14},{14,12},{16,18},{18,... | collective-permute-start | bytes 1572872 | tf_op jit(solution)/shard_map/ppermute | solution.py:71
  93.6 23.1 %collective-permute-start.14 = (bf16[2,256,512]{2,1,0:T(8,128)(2,1)S(1)}, bf16[2,256,512]{2,1,0:T(8,128)(2,1)S(1)}, u32[]{:S(2)}, u32[]{:S(2)}) collective-permute-start(bf16[2,256,512]{2,1,0:T(8,128)(2,1)S(1)} %pad_maximum_fusion.6), channel_id=1, source_target_pairs={{0,24},{2,26},{4,28},{6,30},{8,0},{10,2},{12,4},{14,6},{16,8},{18,... | collective-permute-start | bytes 1572872 | tf_op jit(solution)/shard_map/ppermute | solution.py:59
  97.1 19.6 %collective-permute-start.15 = (bf16[2,256,512]{2,1,0:T(8,128)(2,1)S(1)}, bf16[2,256,512]{2,1,0:T(8,128)(2,1)S(1)}, u32[]{:S(2)}, u32[]{:S(2)}) collective-permute-start(bf16[2,256,512]{2,1,0:T(8,128)(2,1)S(1)} %collective-permute-done.11), channel_id=1, source_target_pairs={{0,8},{2,10},{4,12},{6,14},{8,16},{10,18},{12,20},{14,22},{16,24},... | collective-permute-start | bytes 1572872 | tf_op jit(solution)/shard_map/ppermute | solution.py:59
  97.1 21.2 %collective-permute-start.16 = (bf16[256,2048]{1,0:T(8,128)(2,1)S(1)}, bf16[256,2048]{1,0:T(8,128)(2,1)S(1)}, u32[]{:S(2)}, u32[]{:S(2)}) collective-permute-start(bf16[256,2048]{1,0:T(8,128)(2,1)S(1)} %maximum_select_fusion.3), channel_id=1, source_target_pairs={{0,4},{2,6},{4,0},{6,2},{8,12},{10,14},{12,8},{14,10},{16,20},{18,... | collective-permute-start | bytes 3145736 | tf_op jit(solution)/shard_map/ppermute | solution.py:59
  122.4 27.3 %collective-permute-start.19 = (bf16[256,2048]{1,0:T(8,128)(2,1)S(1)}, bf16[256,2048]{1,0:T(8,128)(2,1)}, u32[]{:S(2)}, u32[]{:S(2)}) collective-permute-start(bf16[256,2048]{1,0:T(8,128)(2,1)S(1)} %maximum_select_fusion.3), channel_id=1, source_target_pairs={{0,8},{2,10},{4,12},{6,14},{8,16},{10,18},{12,20},{14,22},{16,24},... | collective-permute-start | bytes 3145736 | tf_op jit(solution)/shard_map/ppermute | solution.py:59
  124.3 25.3 %collective-permute-start.20 = (bf16[256,2048]{1,0:T(8,128)(2,1)S(1)}, bf16[256,2048]{1,0:T(8,128)(2,1)S(1)}, u32[]{:S(2)}, u32[]{:S(2)}) collective-permute-start(bf16[256,2048]{1,0:T(8,128)(2,1)S(1)} %get-tuple-element.229), channel_id=1, source_target_pairs={{0,4},{2,6},{4,0},{6,2},{8,12},{10,14},{12,8},{14,10},{16,20},{18,... | collective-permute-start | bytes 3145736 | tf_op jit(solution)/shard_map/ppermute | solution.py:59
  128.6 48.9 %collective-permute-start.18 = (bf16[512,2048]{1,0:T(8,128)(2,1)S(1)}, bf16[512,2048]{1,0:T(8,128)(2,1)S(1)}, u32[]{:S(2)}, u32[]{:S(2)}) collective-permute-start(bf16[512,2048]{1,0:T(8,128)(2,1)S(1)} %add_convert_fusion.2.att_a), channel_id=1, source_target_pairs={{0,1},{1,0},{2,3},{3,2},{4,5},{5,4},{6,7},{7,6},{8,9},{9,8},{10,11... | collective-permute-start | bytes 6291464 | tf_op jit(solution)/shard_map/ppermute | solution.py:81
  149.7 24.5 %collective-permute-start.21 = (bf16[256,2048]{1,0:T(8,128)(2,1)S(1)}, bf16[256,2048]{1,0:T(8,128)(2,1)}, u32[]{:S(2)}, u32[]{:S(2)}) collective-permute-start(bf16[256,2048]{1,0:T(8,128)(2,1)S(1)} %maximum_select_fusion.3), channel_id=1, source_target_pairs={{0,24},{2,26},{4,28},{6,30},{8,0},{10,2},{12,4},{14,6},{16,8},{18,... | collective-permute-start | bytes 3145736 | tf_op jit(solution)/shard_map/ppermute | solution.py:59
  151.3 24.0 %collective-permute-start.22 = (bf16[256,2048]{1,0:T(8,128)(2,1)}, bf16[256,2048]{1,0:T(8,128)(2,1)S(1)}, u32[]{:S(2)}, u32[]{:S(2)}) collective-permute-start(bf16[256,2048]{1,0:T(8,128)(2,1)} %collective-permute-done.19), channel_id=1, source_target_pairs={{0,4},{2,6},{4,0},{6,2},{8,12},{10,14},{12,8},{14,10},{16,20},{18,... | collective-permute-start | bytes 3145736 | tf_op jit(solution)/shard_map/ppermute | solution.py:59
  152.8 22.5 %collective-permute-start.23 = (bf16[512,2048]{1,0:T(8,128)(2,1)S(1)}, bf16[512,2048]{1,0:T(8,128)(2,1)S(1)}, u32[]{:S(2)}, u32[]{:S(2)}) collective-permute-start(bf16[512,2048]{1,0:T(8,128)(2,1)S(1)} %get-tuple-element.216), channel_id=1, source_target_pairs={{0,2},{2,0},{4,6},{6,4},{8,10},{10,8},{12,14},{14,12},{16,18},{18,... | collective-permute-start | bytes 6291464 | tf_op jit(solution)/shard_map/ppermute | solution.py:71
  175.3 25.1 %collective-permute-start.25 = (bf16[256,2048]{1,0:T(8,128)(2,1)}, bf16[256,2048]{1,0:T(8,128)(2,1)}, u32[]{:S(2)}, u32[]{:S(2)}) collective-permute-start(bf16[256,2048]{1,0:T(8,128)(2,1)} %collective-permute-done.19), channel_id=1, source_target_pairs={{0,8},{2,10},{4,12},{6,14},{8,16},{10,18},{12,20},{14,22},{16,24},... | collective-permute-start | bytes 3145736 | tf_op jit(solution)/shard_map/ppermute | solution.py:59
  176.0 24.4 %collective-permute-start.26 = (bf16[256,2048]{1,0:T(8,128)(2,1)}, bf16[256,2048]{1,0:T(8,128)(2,1)}, u32[]{:S(2)}, u32[]{:S(2)}) collective-permute-start(bf16[256,2048]{1,0:T(8,128)(2,1)} %collective-permute-done.21), channel_id=1, source_target_pairs={{0,4},{2,6},{4,0},{6,2},{8,12},{10,14},{12,8},{14,10},{16,20},{18,... | collective-permute-start | bytes 3145736 | tf_op jit(solution)/shard_map/ppermute | solution.py:59
  180.5 19.9 %collective-permute-start.24 = (bf16[512,2048]{1,0:T(8,128)(2,1)S(1)}, bf16[512,2048]{1,0:T(8,128)(2,1)S(1)}, u32[]{:S(2)}, u32[]{:S(2)}) collective-permute-start(bf16[512,2048]{1,0:T(8,128)(2,1)S(1)} %get-tuple-element.222), channel_id=1, source_target_pairs={{0,2},{2,0},{4,6},{6,4},{8,10},{10,8},{12,14},{14,12},{16,18},{18,... | collective-permute-start | bytes 6291464 | tf_op jit(solution)/shard_map/ppermute | solution.py:71
  200.4 25.3 %collective-permute-start.27 = (bf16[256,2048]{1,0:T(8,128)(2,1)S(1)}, bf16[256,2048]{1,0:T(8,128)(2,1)S(1)}, u32[]{:S(2)}, u32[]{:S(2)}) collective-permute-start(bf16[256,2048]{1,0:T(8,128)(2,1)S(1)} %copy-done.33), channel_id=1, source_target_pairs={{0,8},{2,10},{4,12},{6,14},{8,16},{10,18},{12,20},{14,22},{16,24},... | collective-permute-start | bytes 3145736 | tf_op jit(solution)/shard_map/ppermute | solution.py:59
  200.5 25.2 %collective-permute-start.28 = (bf16[256,2048]{1,0:T(8,128)(2,1)}, bf16[256,2048]{1,0:T(8,128)(2,1)S(1)}, u32[]{:S(2)}, u32[]{:S(2)}) collective-permute-start(bf16[256,2048]{1,0:T(8,128)(2,1)} %collective-permute-done.25), channel_id=1, source_target_pairs={{0,4},{2,6},{4,0},{6,2},{8,12},{10,14},{12,8},{14,10},{16,20},{18,... | collective-permute-start | bytes 3145736 | tf_op jit(solution)/shard_map/ppermute | solution.py:59
  225.7 23.3 %collective-permute-start.29 = (bf16[256,2048]{1,0:T(8,128)(2,1)S(1)}, bf16[256,2048]{1,0:T(8,128)(2,1)S(1)}, u32[]{:S(2)}, u32[]{:S(2)}) collective-permute-start(bf16[256,2048]{1,0:T(8,128)(2,1)S(1)} %copy-done.33), channel_id=1, source_target_pairs={{0,24},{2,26},{4,28},{6,30},{8,0},{10,2},{12,4},{14,6},{16,8},{18,... | collective-permute-start | bytes 3145736 | tf_op jit(solution)/shard_map/ppermute | solution.py:59
  227.8 21.2 %collective-permute-start.30 = (bf16[256,2048]{1,0:T(8,128)(2,1)S(1)}, bf16[256,2048]{1,0:T(8,128)(2,1)S(1)}, u32[]{:S(2)}, u32[]{:S(2)}) collective-permute-start(bf16[256,2048]{1,0:T(8,128)(2,1)S(1)} %collective-permute-done.27), channel_id=1, source_target_pairs={{0,4},{2,6},{4,0},{6,2},{8,12},{10,14},{12,8},{14,10},{16,20},{18,... | collective-permute-start | bytes 3145736 | tf_op jit(solution)/shard_map/ppermute | solution.py:59
  249.0 22.7 %collective-permute-start.31 = (bf16[256,2048]{1,0:T(8,128)(2,1)S(1)}, bf16[256,2048]{1,0:T(8,128)(2,1)S(1)}, u32[]{:S(2)}, u32[]{:S(2)}) collective-permute-start(bf16[256,2048]{1,0:T(8,128)(2,1)S(1)} %collective-permute-done.27), channel_id=1, source_target_pairs={{0,8},{2,10},{4,12},{6,14},{8,16},{10,18},{12,20},{14,22},{16,24},... | collective-permute-start | bytes 3145736 | tf_op jit(solution)/shard_map/ppermute | solution.py:59
  249.3 22.5 %collective-permute-start.32 = (bf16[256,2048]{1,0:T(8,128)(2,1)S(1)}, bf16[256,2048]{1,0:T(8,128)(2,1)S(1)}, u32[]{:S(2)}, u32[]{:S(2)}) collective-permute-start(bf16[256,2048]{1,0:T(8,128)(2,1)S(1)} %collective-permute-done.29), channel_id=1, source_target_pairs={{0,4},{2,6},{4,0},{6,2},{8,12},{10,14},{12,8},{14,10},{16,20},{18,... | collective-permute-start | bytes 3145736 | tf_op jit(solution)/shard_map/ppermute | solution.py:59
  271.8 23.1 %collective-permute-start.33 = (bf16[256,2048]{1,0:T(8,128)(2,1)S(1)}, bf16[256,2048]{1,0:T(8,128)(2,1)S(1)}, u32[]{:S(2)}, u32[]{:S(2)}) collective-permute-start(bf16[256,2048]{1,0:T(8,128)(2,1)S(1)} %collective-permute-done.31), channel_id=1, source_target_pairs={{0,4},{2,6},{4,0},{6,2},{8,12},{10,14},{12,8},{14,10},{16,20},{18,... | collective-permute-start | bytes 3145736 | tf_op jit(solution)/shard_map/ppermute | solution.py:59
  273.3 21.9 %collective-permute-start.34 = (bf16[2,256,1024]{2,1,0:T(8,128)(2,1)S(1)}, bf16[2,256,1024]{2,1,0:T(8,128)(2,1)S(1)}, u32[]{:S(2)}, u32[]{:S(2)}) collective-permute-start(bf16[2,256,1024]{2,1,0:T(8,128)(2,1)S(1)} %get-tuple-element.246), channel_id=1, source_target_pairs={{0,24},{2,26},{4,28},{6,30},{8,0},{10,2},{12,4},{14,6},{16,8},{18,... | collective-permute-start | bytes 3145736 | tf_op jit(solution)/shard_map/ppermute | solution.py:59
  295.2 34.7 %collective-permute-start.35 = (bf16[512,1024]{1,0:T(8,128)(2,1)}, bf16[512,1024]{1,0:T(8,128)(2,1)S(1)}, u32[]{:S(2)}, u32[]{:S(2)}) collective-permute-start(bf16[512,1024]{1,0:T(8,128)(2,1)} %get-tuple-element.250), channel_id=1, source_target_pairs={{0,4},{2,6},{4,0},{6,2},{8,12},{10,14},{12,8},{14,10},{16,20},{18,... | collective-permute-start | bytes 3145736 | tf_op jit(solution)/shard_map/ppermute | solution.py:59
  305.4 24.5 %collective-permute-start.36 = (bf16[2,256,1024]{2,1,0:T(8,128)(2,1)}, bf16[2,256,1024]{2,1,0:T(8,128)(2,1)S(1)}, u32[]{:S(2)}, u32[]{:S(2)}) collective-permute-start(bf16[2,256,1024]{2,1,0:T(8,128)(2,1)} %get-tuple-element.251), channel_id=1, source_target_pairs={{0,8},{2,10},{4,12},{6,14},{8,16},{10,18},{12,20},{14,22},{16,24},... | collective-permute-start | bytes 3145736 | tf_op jit(solution)/shard_map/ppermute | solution.py:59
  332.8 25.4 %collective-permute-start.39 = (bf16[512,1024]{1,0:T(8,128)(2,1)}, bf16[512,1024]{1,0:T(8,128)(2,1)S(1)}, u32[]{:S(2)}, u32[]{:S(2)}) collective-permute-start(bf16[512,1024]{1,0:T(8,128)(2,1)} %get-tuple-element.257), channel_id=1, source_target_pairs={{0,4},{2,6},{4,0},{6,2},{8,12},{10,14},{12,8},{14,10},{16,20},{18,... | collective-permute-start | bytes 3145736 | tf_op jit(solution)/shard_map/ppermute | solution.py:59
  332.8 27.3 %collective-permute-start.40 = (bf16[2,256,1024]{2,1,0:T(8,128)(2,1)}, bf16[2,256,1024]{2,1,0:T(8,128)(2,1)}, u32[]{:S(2)}, u32[]{:S(2)}) collective-permute-start(bf16[2,256,1024]{2,1,0:T(8,128)(2,1)} %add_convert_fusion.6), channel_id=1, source_target_pairs={{0,24},{2,26},{4,28},{6,30},{8,0},{10,2},{12,4},{14,6},{16,8},{18,... | collective-permute-start | bytes 3145736 | tf_op jit(solution)/shard_map/ppermute | solution.py:59
  345.2 51.1 %collective-permute-start.38 = (bf16[512,2048]{1,0:T(8,128)(2,1)S(1)}, bf16[512,2048]{1,0:T(8,128)(2,1)S(1)}, u32[]{:S(2)}, u32[]{:S(2)}) collective-permute-start(bf16[512,2048]{1,0:T(8,128)(2,1)S(1)} %add_convert_fusion.1.d_a), channel_id=1, source_target_pairs={{0,1},{1,0},{2,3},{3,2},{4,5},{5,4},{6,7},{7,6},{8,9},{9,8},{10,11... | collective-permute-start | bytes 6291464 | tf_op jit(solution)/shard_map/ppermute | solution.py:81
  360.1 16.7 %collective-permute-start.42 = (bf16[256,1024]{1,0:T(8,128)(2,1)S(1)}, bf16[256,1024]{1,0:T(8,128)(2,1)S(1)}, u32[]{:S(2)}, u32[]{:S(2)}) collective-permute-start(bf16[256,1024]{1,0:T(8,128)(2,1)S(1)} %get-tuple-element.267), channel_id=1, source_target_pairs={{0,24},{2,26},{4,28},{6,30},{8,0},{10,2},{12,4},{14,6},{16,8},{18,... | collective-permute-start | bytes 1572872 | tf_op jit(solution)/shard_map/ppermute | solution.py:59
  364.4 22.6 %collective-permute-start.43 = (bf16[256,1024]{1,0:T(8,128)(2,1)S(1)}, bf16[256,1024]{1,0:T(8,128)(2,1)S(1)}, u32[]{:S(2)}, u32[]{:S(2)}) collective-permute-start(bf16[256,1024]{1,0:T(8,128)(2,1)S(1)} %get-tuple-element.268), channel_id=1, source_target_pairs={{0,8},{2,10},{4,12},{6,14},{8,16},{10,18},{12,20},{14,22},{16,24},... | collective-permute-start | bytes 1572872 | tf_op jit(solution)/shard_map/ppermute | solution.py:59
  364.4 24.1 %collective-permute-start.41 = (bf16[256,2048]{1,0:T(8,128)(2,1)S(1)}, bf16[256,2048]{1,0:T(8,128)(2,1)S(1)}, u32[]{:S(2)}, u32[]{:S(2)}) collective-permute-start(bf16[256,2048]{1,0:T(8,128)(2,1)S(1)} %get-tuple-element.266), channel_id=1, source_target_pairs={{0,4},{2,6},{4,0},{6,2},{8,12},{10,14},{12,8},{14,10},{16,20},{18,... | collective-permute-start | bytes 3145736 | tf_op jit(solution)/shard_map/ppermute | solution.py:59
  388.9 24.2 %collective-permute-start.46 = (bf16[256,2048]{1,0:T(8,128)(2,1)S(1)}, bf16[256,2048]{1,0:T(8,128)(2,1)S(1)}, u32[]{:S(2)}, u32[]{:S(2)}) collective-permute-start(bf16[256,2048]{1,0:T(8,128)(2,1)S(1)} %add_convert_fusion.5), channel_id=1, source_target_pairs={{0,24},{2,26},{4,28},{6,30},{8,0},{10,2},{12,4},{14,6},{16,8},{18,... | collective-permute-start | bytes 3145736 | tf_op jit(solution)/shard_map/ppermute | solution.py:59
  392.6 23.3 %collective-permute-start.45 = (bf16[256,2048]{1,0:T(8,128)(2,1)}, bf16[256,2048]{1,0:T(8,128)(2,1)S(1)}, u32[]{:S(2)}, u32[]{:S(2)}) collective-permute-start(bf16[256,2048]{1,0:T(8,128)(2,1)} %get-tuple-element.274), channel_id=1, source_target_pairs={{0,4},{2,6},{4,0},{6,2},{8,12},{10,14},{12,8},{14,10},{16,20},{18,... | collective-permute-start | bytes 3145736 | tf_op jit(solution)/shard_map/ppermute | solution.py:59
  416.0 23.6 %collective-permute-start.48 = (bf16[256,1024]{1,0:T(8,128)(2,1)}, bf16[256,1024]{1,0:T(8,128)(2,1)S(1)}, u32[]{:S(2)}, u32[]{:S(2)}) collective-permute-start(bf16[256,1024]{1,0:T(8,128)(2,1)} %fusion.49), channel_id=1, source_target_pairs={{0,4},{2,6},{4,0},{6,2},{8,12},{10,14},{12,8},{14,10},{16,20},{18,... | collective-permute-start | bytes 1572872 | tf_op jit(solution)/shard_map/ppermute | solution.py:59
  417.4 22.1 %collective-permute-start.50 = (bf16[256,1024]{1,0:T(8,128)(2,1)}, bf16[256,1024]{1,0:T(8,128)(2,1)S(1)}, u32[]{:S(2)}, u32[]{:S(2)}) collective-permute-start(bf16[256,1024]{1,0:T(8,128)(2,1)} %add_convert_fusion.10), channel_id=1, source_target_pairs={{0,24},{2,26},{4,28},{6,30},{8,0},{10,2},{12,4},{14,6},{16,8},{18,... | collective-permute-start | bytes 1572872 | tf_op jit(solution)/shard_map/ppermute | solution.py:59
  418.9 30.7 %collective-permute-start.49 = (bf16[256,2048]{1,0:T(8,128)(2,1)S(1)}, bf16[256,2048]{1,0:T(8,128)(2,1)S(1)}, u32[]{:S(2)}, u32[]{:S(2)}) collective-permute-start(bf16[256,2048]{1,0:T(8,128)(2,1)S(1)} %add_convert_fusion.4), channel_id=1, source_target_pairs={{0,8},{2,10},{4,12},{6,14},{8,16},{10,18},{12,20},{14,22},{16,24},... | collective-permute-start | bytes 3145736 | tf_op jit(solution)/shard_map/ppermute | solution.py:59
  419.9 29.9 %collective-permute-start.47 = (bf16[256,2048]{1,0:T(8,128)(2,1)S(1)}, bf16[256,2048]{1,0:T(8,128)(2,1)S(1)}, u32[]{:S(2)}, u32[]{:S(2)}) collective-permute-start(bf16[256,2048]{1,0:T(8,128)(2,1)S(1)} %copy-done.41), channel_id=1, source_target_pairs={{0,4},{2,6},{4,0},{6,2},{8,12},{10,14},{12,8},{14,10},{16,20},{18,... | collective-permute-start | bytes 3145736 | tf_op jit(solution)/shard_map/ppermute | solution.py:59
  439.4 10.3 %collective-permute-start.51 = (bf16[512,2048]{1,0:T(8,128)(2,1)S(1)}, bf16[512,2048]{1,0:T(8,128)(2,1)S(1)}, u32[]{:S(2)}, u32[]{:S(2)}) collective-permute-start(bf16[512,2048]{1,0:T(8,128)(2,1)S(1)} %convolution_convert_fusion.8), channel_id=1, source_target_pairs={{0,2},{2,0},{4,6},{6,4},{8,10},{10,8},{12,14},{14,12},{16,18},{18,... | collective-permute-start | bytes 6291464 | tf_op jit(solution)/shard_map/ppermute | solution.py:71
  450.3 25.9 %collective-permute-start.52 = (bf16[256,2048]{1,0:T(8,128)(2,1)S(1)}, bf16[256,2048]{1,0:T(8,128)(2,1)S(1)}, u32[]{:S(2)}, u32[]{:S(2)}) collective-permute-start(bf16[256,2048]{1,0:T(8,128)(2,1)S(1)} %copy-done.40), channel_id=1, source_target_pairs={{0,4},{2,6},{4,0},{6,2},{8,12},{10,14},{12,8},{14,10},{16,20},{18,... | collective-permute-start | bytes 3145736 | tf_op jit(solution)/shard_map/ppermute | solution.py:59
  451.4 24.8 %collective-permute-start.53 = (bf16[256,2048]{1,0:T(8,128)(2,1)S(1)}, bf16[256,2048]{1,0:T(8,128)(2,1)S(1)}, u32[]{:S(2)}, u32[]{:S(2)}) collective-permute-start(bf16[256,2048]{1,0:T(8,128)(2,1)S(1)} %add_convert_fusion.3), channel_id=1, source_target_pairs={{0,24},{2,26},{4,28},{6,30},{8,0},{10,2},{12,4},{14,6},{16,8},{18,... | collective-permute-start | bytes 3145736 | tf_op jit(solution)/shard_map/ppermute | solution.py:59
  463.7 49.8 %collective-permute-start.61 = (bf16[512,2048]{1,0:T(8,128)(2,1)S(1)}, bf16[512,2048]{1,0:T(8,128)(2,1)S(1)}, u32[]{:S(2)}, u32[]{:S(2)}) collective-permute-start(bf16[512,2048]{1,0:T(8,128)(2,1)S(1)} %add_convert_fusion.d_a), channel_id=1, source_target_pairs={{0,1},{1,0},{2,3},{3,2},{4,5},{5,4},{6,7},{7,6},{8,9},{9,8},{10,11... | collective-permute-start | bytes 6291464 | tf_op jit(solution)/shard_map/ppermute | solution.py:81
  476.2 23.1 %collective-permute-start.54 = (bf16[1024,512]{1,0:T(8,128)(2,1)}, bf16[1024,512]{1,0:T(8,128)(2,1)S(1)}, u32[]{:S(2)}, u32[]{:S(2)}) collective-permute-start(bf16[1024,512]{1,0:T(8,128)(2,1)} %fusion.36), channel_id=1, source_target_pairs={{0,4},{2,6},{4,0},{6,2},{8,12},{10,14},{12,8},{14,10},{16,20},{18,... | collective-permute-start | bytes 3145736 | tf_op jit(solution)/shard_map/ppermute | solution.py:59
  487.1 12.2 %collective-permute-start.55 = (bf16[512,2048]{1,0:T(8,128)(2,1)S(1)}, bf16[512,2048]{1,0:T(8,128)(2,1)S(1)}, u32[]{:S(2)}, u32[]{:S(2)}) collective-permute-start(bf16[512,2048]{1,0:T(8,128)(2,1)S(1)} %pad_maximum_fusion.1), channel_id=1, source_target_pairs={{0,2},{2,0},{4,6},{6,4},{8,10},{10,8},{12,14},{14,12},{16,18},{18,... | collective-permute-start | bytes 6291464 | tf_op jit(solution)/shard_map/ppermute | solution.py:71
  488.0 11.3 %collective-permute-start.56 = (f32[128,2048]{1,0:T(8,128)S(1)}, f32[128,2048]{1,0:T(8,128)S(1)}, u32[]{:S(2)}, u32[]{:S(2)}) collective-permute-start(f32[128,2048]{1,0:T(8,128)S(1)} %get-tuple-element.405), channel_id=1, source_target_pairs={{0,2},{2,0},{4,6},{6,4},{8,10},{10,8},{12,14},{14,12},{16,18},{18,... | collective-permute-start | bytes 3145736 | tf_op jit(solution)/shard_map/ppermute | solution.py:71
  500.3 21.1 %collective-permute-start.59 = (bf16[256,512]{1,0:T(8,128)(2,1)}, bf16[256,512]{1,0:T(8,128)(2,1)}, u32[]{:S(2)}, u32[]{:S(2)}) collective-permute-start(bf16[256,512]{1,0:T(8,128)(2,1)} %get-tuple-element.312), channel_id=1, source_target_pairs={{0,24},{2,26},{4,28},{6,30},{8,0},{10,2},{12,4},{14,6},{16,8},{18,... | collective-permute-start | bytes 786440 | tf_op jit(solution)/shard_map/ppermute | solution.py:59
  502.2 19.1 %collective-permute-start.60 = (bf16[256,512]{1,0:T(8,128)(2,1)}, bf16[256,512]{1,0:T(8,128)(2,1)}, u32[]{:S(2)}, u32[]{:S(2)}) collective-permute-start(bf16[256,512]{1,0:T(8,128)(2,1)} %get-tuple-element.314), channel_id=1, source_target_pairs={{0,8},{2,10},{4,12},{6,14},{8,16},{10,18},{12,20},{14,22},{16,24},... | collective-permute-start | bytes 786440 | tf_op jit(solution)/shard_map/ppermute | solution.py:59
  502.5 18.8 %collective-permute-start.58 = (bf16[256,1536]{1,0:T(8,128)(2,1)}, bf16[256,1536]{1,0:T(8,128)(2,1)}, u32[]{:S(2)}, u32[]{:S(2)}) collective-permute-start(bf16[256,1536]{1,0:T(8,128)(2,1)} %get-tuple-element.310), channel_id=1, source_target_pairs={{0,4},{2,6},{4,0},{6,2},{8,12},{10,14},{12,8},{14,10},{16,20},{18,... | collective-permute-start | bytes 2359304 | tf_op jit(solution)/shard_map/ppermute | solution.py:59
  511.8 43.6 %collective-permute-start.57 = (bf16[512,2048]{1,0:T(8,128)(2,1)S(1)}, bf16[512,2048]{1,0:T(8,128)(2,1)S(1)}, u32[]{:S(2)}, u32[]{:S(2)}) collective-permute-start(bf16[512,2048]{1,0:T(8,128)(2,1)S(1)} %fusion.16), channel_id=1, source_target_pairs={{0,1},{1,0},{2,3},{3,2},{4,5},{5,4},{6,7},{7,6},{8,9},{9,8},{10,11... | collective-permute-start | bytes 6291464 | tf_op jit(solution)/shard_map/ppermute | solution.py:81
  527.8 17.4 %collective-permute-start.63 = (bf16[256,1536]{1,0:T(8,128)(2,1)S(1)}, bf16[256,1536]{1,0:T(8,128)(2,1)S(1)}, u32[]{:S(2)}, u32[]{:S(2)}) collective-permute-start(bf16[256,1536]{1,0:T(8,128)(2,1)S(1)} %add_convert_fusion.9), channel_id=1, source_target_pairs={{0,24},{2,26},{4,28},{6,30},{8,0},{10,2},{12,4},{14,6},{16,8},{18,... | collective-permute-start | bytes 2359304 | tf_op jit(solution)/shard_map/ppermute | solution.py:59
  527.9 17.3 %collective-permute-start.62 = (bf16[256,1536]{1,0:T(8,128)(2,1)S(1)}, bf16[256,1536]{1,0:T(8,128)(2,1)S(1)}, u32[]{:S(2)}, u32[]{:S(2)}) collective-permute-start(bf16[256,1536]{1,0:T(8,128)(2,1)S(1)} %copy-done.46), channel_id=1, source_target_pairs={{0,4},{2,6},{4,0},{6,2},{8,12},{10,14},{12,8},{14,10},{16,20},{18,... | collective-permute-start | bytes 2359304 | tf_op jit(solution)/shard_map/ppermute | solution.py:59
  532.8 12.5 %collective-permute-start.65 = (f32[128,2048]{1,0:T(8,128)S(1)}, f32[128,2048]{1,0:T(8,128)S(1)}, u32[]{:S(2)}, u32[]{:S(2)}) collective-permute-start(f32[128,2048]{1,0:T(8,128)S(1)} %get-tuple-element.403), channel_id=1, source_target_pairs={{0,2},{2,0},{4,6},{6,4},{8,10},{10,8},{12,14},{14,12},{16,18},{18,... | collective-permute-start | bytes 3145736 | tf_op jit(solution)/shard_map/ppermute | solution.py:71
  547.7 18.0 %collective-permute-start.67 = (bf16[256,1536]{1,0:T(8,128)(2,1)}, bf16[256,1536]{1,0:T(8,128)(2,1)S(1)}, u32[]{:S(2)}, u32[]{:S(2)}) collective-permute-start(bf16[256,1536]{1,0:T(8,128)(2,1)} %add_convert_fusion.8), channel_id=1, source_target_pairs={{0,8},{2,10},{4,12},{6,14},{8,16},{10,18},{12,20},{14,22},{16,24},... | collective-permute-start | bytes 2359304 | tf_op jit(solution)/shard_map/ppermute | solution.py:59
  547.7 18.0 %collective-permute-start.66 = (bf16[256,1536]{1,0:T(8,128)(2,1)S(1)}, bf16[256,1536]{1,0:T(8,128)(2,1)}, u32[]{:S(2)}, u32[]{:S(2)}) collective-permute-start(bf16[256,1536]{1,0:T(8,128)(2,1)S(1)} %copy-done.45), channel_id=1, source_target_pairs={{0,4},{2,6},{4,0},{6,2},{8,12},{10,14},{12,8},{14,10},{16,20},{18,... | collective-permute-start | bytes 2359304 | tf_op jit(solution)/shard_map/ppermute | solution.py:59
  568.8 15.7 %collective-permute-start.68 = (bf16[256,1536]{1,0:T(8,128)(2,1)S(1)}, bf16[256,1536]{1,0:T(8,128)(2,1)S(1)}, u32[]{:S(2)}, u32[]{:S(2)}) collective-permute-start(bf16[256,1536]{1,0:T(8,128)(2,1)S(1)} %copy-done.44), channel_id=1, source_target_pairs={{0,4},{2,6},{4,0},{6,2},{8,12},{10,14},{12,8},{14,10},{16,20},{18,... | collective-permute-start | bytes 2359304 | tf_op jit(solution)/shard_map/ppermute | solution.py:59
  570.0 16.9 %collective-permute-start.69 = (bf16[256,1536]{1,0:T(8,128)(2,1)}, bf16[256,1536]{1,0:T(8,128)(2,1)}, u32[]{:S(2)}, u32[]{:S(2)}) collective-permute-start(bf16[256,1536]{1,0:T(8,128)(2,1)} %add_convert_fusion.7), channel_id=1, source_target_pairs={{0,24},{2,26},{4,28},{6,30},{8,0},{10,2},{12,4},{14,6},{16,8},{18,... | collective-permute-start | bytes 2359304 | tf_op jit(solution)/shard_map/ppermute | solution.py:59
  573.4 17.0 %all-to-all-start = ((f32[16,14,128]{2,1,0:T(8,128)}), f32[16,14,128]{2,1,0:T(8,128)S(1)}, u32[]{:S(2)}, u32[]{:S(2)}) async-start(f32[16,14,128]{2,1,0:T(8,128)} %copy.47), calls=%async_computation | async-start | bytes 262144 | tf_op jit(solution)/shard_map/all_to_all | solution.py:762
  (86 other events, 1019.3 us)

commit v7 on v6

--- a/solution.py
+++ b/solution.py
@@ -592,7 +592,7 @@
         blk = first.shape[1] // grid.z
         part = lambda stacked, kz: stacked[:, kz * blk : (kz + 1) * blk]
         x_d[2] = ph.gather_x(z_d[2])
-        a_2 = ph.send_z(part(first, 2), 3)
+        a_2 = ph.send(part(first, 2), 3, 0, hold=False)
         step = width // (grid.x * grid.z)
         feature_blocks = lambda value, some: jnp.concatenate(
             [
@@ -617,6 +617,7 @@
 
         x_b = {2: ph.reduce_x(rows_of(other, 2, 4))}
         a_3 = ph.send_z(part(first, 3), 1)
+        ph.results.append(a_2)
         w_d.append(some_of(x_d, [2]))
         d_act = jnp.concatenate(d_act, axis=0) + matmul(ph.begin(late), w_d[1])
         d_up = (d_act * slope).astype(BF16)

time: 605 us -> 598 us (0.988)
  starting transfers between devices: 96.3 us -> 86.8 us
    ppermute x52, starting transfers between devices: 84.3 us -> 74.7 us  [send(): out = lax.ppermute(value, 'dp', self.ring(dz, dx, 0))]
    unnamed x184 -> x186, local copies, waits for them, and re-layouts: 32.4 us -> 32.5 us
  transfers between devices with their start and end apart: 73 -> 73, of which waited for: 35 -> 32; matrix products, arithmetic and copies ran while one was open for 36% -> 37% of each run, Pallas kernels for 8% -> 8%
where the time goes in v7:
time: 598 us; the launch traced here: 589 us
  waiting for transfers between devices  221 us (37%)
  matrix products  143 us (24%)
  starting transfers between devices  86.8 us (15%)
  local copies, waits for them, and re-layouts  48 us (8%)
  Pallas kernels  45.7 us (8%)
  other arithmetic  41.6 us (7%)
    ppermute x52, waiting for transfers between devices, send(): out = lax.ppermute(value, 'dp', self.ring(dz, dx, 0))  208 us
    dot_general x16, matrix products, matmul(): lax.dot_general(lhs, rhs, (((1,), (1 if turned else 0,)), ((), ())), pref...  101 us
    ppermute x52, starting transfers between devices, send(): out = lax.ppermute(value, 'dp', self.ring(dz, dx, 0))  74.7 us
    dot_general x8, matrix products, dots(): lax.dot_general(lhs[:, kx * width:(kx + 1) * width], rhs, (((0,), (0,)),...  39.9 us
    unnamed x186, local copies, waits for them, and re-layouts  32.5 us
    pallas_call x6, Pallas kernels, by_rows(): pl.pallas_call(functools.partial(kernel, blocks), grid_spec=pltpu.Prefetc...  27.5 us
    pallas_call x2, Pallas kernels, by_image(): pl.pallas_call(kernel, grid=(rows // length,), in_specs=[block(operand.sh...  13.4 us
  transfers between devices with their start and end apart: 73, of which 32 were waited for; matrix products, arithmetic and copies ran while one was open for 37% of the time, Pallas kernels for 8%

profile of v7, /device:TPU:0, one launch (start us, length us, event | category | flops | bytes accessed | tf_op | source)
XLA Modules:
  0.0 589.1 jit_solution(15617761802026531622)
XLA Ops:
  7.7 2.6 collective-permute-start.2
  14.9 4.8 shard_map.144
  21.7 12.3 %collective-permute-done.4 = bf16[256,512]{1,0:T(8,128)(2,1)S(1)} collective-permute-done((bf16[256,512]{1,0:T(8,128)(2,1)}, bf16[256,512]{1,0:T(8,128)(2,1)S(1)}, u32[]{:S(2)}, u32[]{:S(2)}) %collective-permute-start.4) | collective-permute-done | bytes 262176 | tf_op jit(solution)/shard_map/ppermute | solution.py:59
  34.1 3.9 collective-permute-start.6
  41.1 2.4 shard_map.145
  43.6 2.9 constant_dynamic-update-slice_fusion.8
  46.7 7.8 %collective-permute-done.6 = bf16[256,1536]{0,1:T(8,128)(2,1)S(1)} collective-permute-done((bf16[256,1536]{0,1:T(8,128)(2,1)S(1)}, bf16[256,1536]{0,1:T(8,128)(2,1)S(1)}, u32[]{:S(2)}, u32[]{:S(2)}) %collective-permute-start.6) | collective-permute-done | bytes 786464 | tf_op jit(solution)/shard_map/ppermute | solution.py:59
  54.5 2.4 collective-permute-done.7
  60.9 15.8 %collective-permute-done.9 = bf16[256,1536]{0,1:T(8,128)(2,1)S(1)} collective-permute-done((bf16[256,1536]{0,1:T(8,128)(2,1)}, bf16[256,1536]{0,1:T(8,128)(2,1)S(1)}, u32[]{:S(2)}, u32[]{:S(2)}) %collective-permute-start.9) | collective-permute-done | bytes 786464 | tf_op jit(solution)/shard_map/ppermute | solution.py:59
  78.8 10.9 %collective-permute-done.11 = bf16[2,256,512]{2,1,0:T(8,128)(2,1)S(1)} collective-permute-done((bf16[2,256,512]{2,1,0:T(8,128)(2,1)S(1)}, bf16[2,256,512]{2,1,0:T(8,128)(2,1)S(1)}, u32[]{:S(2)}, u32[]{:S(2)}) %collective-permute-start.11) | collective-permute-done | bytes 524320 | tf_op jit(solution)/shard_map/ppermute | solution.py:59
  91.1 2.5 collective-permute-done.12
  93.6 3.5 collective-permute-start.14
  98.9 7.0 %convolution_convert_fusion.qkv_ref = bf16[1024,1536]{1,0:T(8,128)(2,1)S(1)} fusion(bf16[1024,2048]{1,0:T(8,128)(2,1)S(1)} %constant_dynamic-update-slice_fusion, bf16[2048,1536]{0,1:T(8,128)(2,1)S(1)} %constant_dynamic-update-slice_fusion.2), kind=kOutput, calls=%fused_computation.34 | convolution fusion | flops 6444023808 | bytes 13631488 | tf_op jit(solution)/shard_map/dot_general | solution.py:439
  105.9 4.5 shard_map.146
  110.4 6.3 %collective-permute-done.15 = bf16[2,256,512]{2,1,0:T(8,128)(2,1)S(1)} collective-permute-done((bf16[2,256,512]{2,1,0:T(8,128)(2,1)S(1)}, bf16[2,256,512]{2,1,0:T(8,128)(2,1)S(1)}, u32[]{:S(2)}, u32[]{:S(2)}) %collective-permute-start.15) | collective-permute-done | bytes 524320 | tf_op jit(solution)/shard_map/ppermute | solution.py:59
  118.4 4.1 collective-permute-done.17
  131.8 17.9 %collective-permute-done.19 = bf16[256,2048]{1,0:T(8,128)(2,1)} collective-permute-done((bf16[256,2048]{1,0:T(8,128)(2,1)S(1)}, bf16[256,2048]{1,0:T(8,128)(2,1)}, u32[]{:S(2)}, u32[]{:S(2)}) %collective-permute-start.19) | collective-permute-done | bytes 1048608 | tf_op jit(solution)/shard_map/ppermute | solution.py:59
  152.8 21.3 %collective-permute-done.21 = bf16[256,2048]{1,0:T(8,128)(2,1)} collective-permute-done((bf16[256,2048]{1,0:T(8,128)(2,1)S(1)}, bf16[256,2048]{1,0:T(8,128)(2,1)}, u32[]{:S(2)}, u32[]{:S(2)}) %collective-permute-start.21) | collective-permute-done | bytes 1048608 | tf_op jit(solution)/shard_map/ppermute | solution.py:59
  177.6 3.0 shard_map.148
  180.9 19.5 %collective-permute-done.25 = bf16[256,2048]{1,0:T(8,128)(2,1)} collective-permute-done((bf16[256,2048]{1,0:T(8,128)(2,1)}, bf16[256,2048]{1,0:T(8,128)(2,1)}, u32[]{:S(2)}, u32[]{:S(2)}) %collective-permute-start.25) | collective-permute-done | bytes 1048608 | tf_op jit(solution)/shard_map/ppermute | solution.py:59
  210.1 2.5 constant_dynamic-update-slice_fusion.20
  214.9 10.9 %collective-permute-done.27 = bf16[256,2048]{1,0:T(8,128)(2,1)S(1)} collective-permute-done((bf16[256,2048]{1,0:T(8,128)(2,1)S(1)}, bf16[256,2048]{1,0:T(8,128)(2,1)S(1)}, u32[]{:S(2)}, u32[]{:S(2)}) %collective-permute-start.27) | collective-permute-done | bytes 1048608 | tf_op jit(solution)/shard_map/ppermute | solution.py:59
  232.7 15.3 %fusion.13 = (bf16[1024,2048]{1,0:T(8,128)(2,1)}, f32[1024,2048]{1,0:T(8,128)}) fusion(bf16[1024,2048]{1,0:T(8,128)(2,1)S(1)} %copy-done.30, bf16[2048,2048]{1,0:T(8,128)(2,1)} %constant_dynamic-update-slice_fusion.16), kind=kOutput, calls=%fused_computation.16 | convolution fusion | flops 8608808960 | bytes 25165824 | tf_op jit(solution)/shard_map/dot_general | solution.py:439
  249.9 7.0 %convolution_convert_fusion.6 = bf16[1024,2048]{1,0:T(8,128)(2,1)S(1)} fusion(bf16[1024,2048]{1,0:T(8,128)(2,1)} %get-tuple-element.315, bf16[1024,2048]{1,0:T(8,128)(2,1)S(1)} %constant_dynamic-update-slice_fusion.14), kind=kOutput, calls=%fused_computation.40 | convolution fusion | flops 4297064448 | bytes 10485760 | tf_op jit(solution)/shard_map/dot_general | solution.py:176
  258.4 7.0 %convolution_convert_fusion.5 = bf16[1024,2048]{1,0:T(8,128)(2,1)S(1)} fusion(bf16[1024,2048]{1,0:T(8,128)(2,1)} %get-tuple-element.315, bf16[1024,2048]{1,0:T(8,128)(2,1)S(1)} %constant_dynamic-update-slice_fusion.14), kind=kOutput, calls=%fused_computation.39 | convolution fusion | flops 4297064448 | bytes 10485760 | tf_op jit(solution)/shard_map/dot_general | solution.py:176
  273.7 3.7 collective-permute-start.36
  278.5 7.9 %fusion.81 = f32[512,2048]{1,0:T(8,128)} fusion(bf16[512,1536]{1,0:T(8,128)(2,1)S(1)} %pad_maximum_fusion.3, bf16[1536,2048]{1,0:T(8,128)(2,1)} %constant_dynamic-update-slice_fusion.24), kind=kOutput, calls=%fused_computation.214 | convolution fusion | flops 3221225472 | bytes 12058624 | tf_op jit(solution)/shard_map/dot_general | solution.py:439
  286.5 5.1 fusion.82
  291.6 3.6 collective-permute-done.33
  297.7 11.5 %fusion.15 = bf16[1024,2048]{1,0:T(8,128)(2,1)} fusion(f32[512,2048]{1,0:T(8,128)} %fusion.82, f32[512,2048]{1,0:T(8,128)} %fusion.81, f32[1024,2048]{1,0:T(8,128)} %get-tuple-element.243, bf16[1024,512]{1,0:T(8,128)(2,1)S(1)} %pad_maximum_fusion.5, bf16[512,2048]{1,0:T(8,128)(2,1)S(1)} %constant_dynamic-update-slice_fusion.30), kind=kOutput, calls=%fused_computation.19 | convolution fusion | flops 2191523840 | bytes 24117248 | tf_op jit(solution)/shard_map/dot_general | solution.py:439
  309.1 9.9 %convolution_convert_fusion.9 = bf16[512,2048]{1,0:T(8,128)(2,1)} fusion(bf16[2048,2048]{1,0:T(8,128)(2,1)} %constant_dynamic-update-slice_fusion.16, bf16[1024,2048]{1,0:T(8,128)(2,1)} %fusion.15), kind=kOutput, calls=%fused_computation.43 | convolution fusion | flops 4296015872 | bytes 12582912 | tf_op jit(solution)/shard_map/dot_general | solution.py:439
  319.0 2.8 add_convert_fusion.6
  324.7 4.9 collective-permute-start.40
  329.6 8.5 %add_convert_fusion.1.d_a = bf16[512,2048]{1,0:T(8,128)(2,1)S(1)} fusion(bf16[512,2048]{1,0:T(8,128)(2,1)} %copy-done.70, bf16[512,2048]{1,0:T(8,128)(2,1)S(1)} %slice-done.4, bf16[2048,2048]{1,0:T(8,128)(2,1)} %constant_dynamic-update-slice_fusion.16), kind=kOutput, calls=%fused_computation.32 | convolution fusion | flops 4298113024 | bytes 14680064 | tf_op jit(solution)/shard_map/dot_general | solution.py:439
  339.6 7.4 %convolution_convert_fusion.4 = bf16[1024,2048]{1,0:T(8,128)(2,1)S(1)} fusion(bf16[1024,2048]{1,0:T(8,128)(2,1)} %fusion.15, bf16[1024,2048]{1,0:T(8,128)(2,1)} %copy-done.29), kind=kOutput, calls=%fused_computation.38 | convolution fusion | flops 4297064448 | bytes 10485760 | tf_op jit(solution)/shard_map/dot_general | solution.py:176
  352.6 4.3 collective-permute-start.42
  357.5 6.5 %convolution_convert_fusion.3 = bf16[1024,2048]{1,0:T(8,128)(2,1)S(1)} fusion(bf16[1024,2048]{1,0:T(8,128)(2,1)S(1)} %copy-done.24, bf16[1024,2048]{1,0:T(8,128)(2,1)} %copy-done.29), kind=kOutput, calls=%fused_computation.37 | convolution fusion | flops 4297064448 | bytes 10485760 | tf_op jit(solution)/shard_map/dot_general | solution.py:176
  364.0 2.6 convert_add_fusion.1
  369.3 10.2 %collective-permute-done.43 = bf16[256,1024]{1,0:T(8,128)(2,1)S(1)} collective-permute-done((bf16[256,1024]{1,0:T(8,128)(2,1)S(1)}, bf16[256,1024]{1,0:T(8,128)(2,1)S(1)}, u32[]{:S(2)}, u32[]{:S(2)}) %collective-permute-start.43) | collective-permute-done | bytes 524320 | tf_op jit(solution)/shard_map/ppermute | solution.py:59
  381.4 3.8 collective-permute-start.46
  387.9 10.4 %shard_map.149 = (f32[512,2048]{1,0:T(8,128)}, bf16[512,2048]{1,0:T(8,128)(2,1)S(1)}, f32[2,24,2048]{2,1,0:T(8,128)S(1)}) custom-call(s32[8]{0:T(128)S(1)} %copy-done.8, s32[2]{0:T(128)S(1)} %copy-done.11, f32[512,2048]{1,0:T(8,128)} %copy-done.12, bf16[512,2048]{1,0:T(8,128)(2,1)S(1)} %add_convert_fusion.2.att_a, ...), custom_call_target="tpu_custom_call" | custom-call | flops 6291456000 | bytes 8388608 | tf_op jit(solution)/shard_map/pallas_call | solution.py:422
  398.6 7.0 %collective-permute-done.46 = bf16[256,2048]{1,0:T(8,128)(2,1)S(1)} collective-permute-done((bf16[256,2048]{1,0:T(8,128)(2,1)S(1)}, bf16[256,2048]{1,0:T(8,128)(2,1)S(1)}, u32[]{:S(2)}, u32[]{:S(2)}) %collective-permute-start.46) | collective-permute-done | bytes 1048608 | tf_op jit(solution)/shard_map/ppermute | solution.py:59
  405.6 2.9 collective-permute-done.45
  415.5 8.9 %shard_map.150 = bf16[1024,1536]{1,0:T(8,128)(2,1)S(1)} custom-call(bf16[1024,1536]{1,0:T(8,128)(2,1)S(1)} %copy-done.3, bf16[1024,512]{1,0:T(8,128)(2,1)S(1)} %convolution_convert_fusion.11.d_mixed_ref), custom_call_target="tpu_custom_call" | custom-call | flops 3221225472 | bytes 8388608 | tf_op jit(solution)/shard_map/pallas_call | solution.py:250
  424.4 7.5 %convolution_convert_fusion.8 = bf16[512,2048]{1,0:T(8,128)(2,1)S(1)} fusion(bf16[2048,1536]{0,1:T(8,128)(2,1)} %copy-done.64, bf16[1024,1536]{1,0:T(8,128)(2,1)S(1)} %shard_map.150), kind=kOutput, calls=%fused_computation.42 | convolution fusion | flops 3222274048 | bytes 9961472 | tf_op jit(solution)/shard_map/dot_general | solution.py:439
  432.1 9.6 %collective-permute-done.49 = bf16[256,2048]{1,0:T(8,128)(2,1)S(1)} collective-permute-done((bf16[256,2048]{1,0:T(8,128)(2,1)S(1)}, bf16[256,2048]{1,0:T(8,128)(2,1)S(1)}, u32[]{:S(2)}, u32[]{:S(2)}) %collective-permute-start.49) | collective-permute-done | bytes 1048608 | tf_op jit(solution)/shard_map/ppermute | solution.py:59
  446.2 6.5 %add_convert_fusion.d_a = bf16[512,2048]{1,0:T(8,128)(2,1)S(1)} fusion(bf16[512,2048]{1,0:T(8,128)(2,1)S(1)} %collective-permute-done.51, bf16[512,1536]{1,0:T(8,128)(2,1)S(1)} %slice-done, bf16[2048,1536]{0,1:T(8,128)(2,1)} %copy-done.64), kind=kOutput, calls=%fused_computation.31 | convolution fusion | flops 3224371200 | bytes 12058624 | tf_op jit(solution)/shard_map/dot_general | solution.py:439
  458.5 3.7 convolution_convert_fusion.2
  463.9 4.8 convolution_convert_fusion.1
  469.1 2.9 fusion.42
  472.0 6.9 %convolution_convert_fusion.7 = bf16[512,1536]{1,0:T(8,128)(2,1)S(1)} fusion(bf16[1536,2048]{1,0:T(8,128)(2,1)} %constant_dynamic-update-slice_fusion.24, bf16[1024,2048]{1,0:T(8,128)(2,1)} %get-tuple-element.315), kind=kOutput, calls=%fused_computation.41 | convolution fusion | flops 3222011904 | bytes 9961472 | tf_op jit(solution)/shard_map/dot_general | solution.py:439
  480.7 11.2 %collective-permute-done.54 = bf16[1024,512]{1,0:T(8,128)(2,1)S(1)} collective-permute-done((bf16[1024,512]{1,0:T(8,128)(2,1)}, bf16[1024,512]{1,0:T(8,128)(2,1)S(1)}, u32[]{:S(2)}, u32[]{:S(2)}) %collective-permute-start.54) | collective-permute-done | bytes 1048608 | tf_op jit(solution)/shard_map/ppermute | solution.py:59
  496.9 6.3 %fusion.30 = f32[512,1536]{1,0:T(8,128)S(1)} fusion(bf16[1536,2048]{1,0:T(8,128)(2,1)} %constant_dynamic-update-slice_fusion.24, bf16[1024,2048]{1,0:T(8,128)(2,1)} %get-tuple-element.315), kind=kOutput, calls=%fused_computation.70 | convolution fusion | flops 3221225472 | bytes 11534336 | tf_op jit(solution)/shard_map/dot_general | solution.py:439
  506.2 7.0 %shard_map.151 = (f32[512,2048]{1,0:T(8,128)}, f32[2,16,2048]{2,1,0:T(8,128)S(1)}) custom-call(s32[8]{0:T(128)S(1)} %copy-done.8, s32[2]{0:T(128)S(1)} %copy-done.11, bf16[512,2048]{1,0:T(8,128)(2,1)S(1)} %copy-done.16, bf16[512,2048]{1,0:T(8,128)(2,1)S(1)} %add_convert_fusion.d_a, bf16[512,2048]{1,0:T(8,128)(2,1)S(1)} %collective-permute-done.61.d_b, ...), custom_call_target="tpu_custom_call" | custom-call | flops 6291456000 | bytes 8388608 | tf_op jit(solution)/shard_map/pallas_call | solution.py:422
  514.8 3.6 collective-permute-start.64
  525.4 12.0 %collective-permute-done.63 = bf16[256,1536]{1,0:T(8,128)(2,1)S(1)} collective-permute-done((bf16[256,1536]{1,0:T(8,128)(2,1)S(1)}, bf16[256,1536]{1,0:T(8,128)(2,1)S(1)}, u32[]{:S(2)}, u32[]{:S(2)}) %collective-permute-start.63) | collective-permute-done | bytes 786464 | tf_op jit(solution)/shard_map/ppermute | solution.py:59
  537.4 2.5 add_convert_fusion.8
  543.1 4.4 collective-permute-done.57
  547.9 3.4 shard_map.152
  551.5 6.5 %collective-permute-done.67 = bf16[256,1536]{1,0:T(8,128)(2,1)S(1)} collective-permute-done((bf16[256,1536]{1,0:T(8,128)(2,1)}, bf16[256,1536]{1,0:T(8,128)(2,1)S(1)}, u32[]{:S(2)}, u32[]{:S(2)}) %collective-permute-start.67) | collective-permute-done | bytes 786464 | tf_op jit(solution)/shard_map/ppermute | solution.py:59
  558.0 3.1 add_convert_fusion.7
  566.0 3.5 all-to-all-start
  569.5 7.3 %collective-permute-done.68 = bf16[256,1536]{1,0:T(8,128)(2,1)S(1)} collective-permute-done((bf16[256,1536]{1,0:T(8,128)(2,1)S(1)}, bf16[256,1536]{1,0:T(8,128)(2,1)S(1)}, u32[]{:S(2)}, u32[]{:S(2)}) %collective-permute-start.68) | collective-permute-done | bytes 786464 | tf_op jit(solution)/shard_map/ppermute | solution.py:59
  576.9 2.7 collective-permute-done.69
  (401 shorter events, 151.1 us)
Async XLA Ops:
  7.7 26.4 %collective-permute-start.2 = (bf16[256,1536]{0,1:T(8,128)(2,1)S(1)}, bf16[256,1536]{0,1:T(8,128)(2,1)S(1)}, u32[]{:S(2)}, u32[]{:S(2)}) collective-permute-start(bf16[256,1536]{0,1:T(8,128)(2,1)S(1)} %get-tuple-element.186), channel_id=1, source_target_pairs={{0,4},{2,6},{4,0},{6,2},{8,12},{10,14},{12,8},{14,10},{16,20},{18,... | collective-permute-start | bytes 2359304 | tf_op jit(solution)/shard_map/ppermute | solution.py:59
  10.3 23.7 %collective-permute-start.1 = (bf16[256,1536]{0,1:T(8,128)(2,1)S(1)}, bf16[256,1536]{0,1:T(8,128)(2,1)}, u32[]{:S(2)}, u32[]{:S(2)}) collective-permute-start(bf16[256,1536]{0,1:T(8,128)(2,1)S(1)} %get-tuple-element.186), channel_id=1, source_target_pairs={{0,8},{2,10},{4,12},{6,14},{8,16},{10,18},{12,20},{14,22},{16,24},... | collective-permute-start | bytes 2359304 | tf_op jit(solution)/shard_map/ppermute | solution.py:59
  12.8 21.2 %collective-permute-start.4 = (bf16[256,512]{1,0:T(8,128)(2,1)}, bf16[256,512]{1,0:T(8,128)(2,1)S(1)}, u32[]{:S(2)}, u32[]{:S(2)}) collective-permute-start(bf16[256,512]{1,0:T(8,128)(2,1)} %get-tuple-element.385), channel_id=1, source_target_pairs={{0,4},{2,6},{4,0},{6,2},{8,12},{10,14},{12,8},{14,10},{16,20},{18,... | collective-permute-start | bytes 786440 | tf_op jit(solution)/shard_map/ppermute | solution.py:59
  34.1 20.4 %collective-permute-start.6 = (bf16[256,1536]{0,1:T(8,128)(2,1)S(1)}, bf16[256,1536]{0,1:T(8,128)(2,1)S(1)}, u32[]{:S(2)}, u32[]{:S(2)}) collective-permute-start(bf16[256,1536]{0,1:T(8,128)(2,1)S(1)} %get-tuple-element.186), channel_id=1, source_target_pairs={{0,24},{2,26},{4,28},{6,30},{8,0},{10,2},{12,4},{14,6},{16,8},{18,... | collective-permute-start | bytes 2359304 | tf_op jit(solution)/shard_map/ppermute | solution.py:59
  38.0 18.9 %collective-permute-start.7 = (bf16[256,1536]{0,1:T(8,128)(2,1)}, bf16[256,1536]{0,1:T(8,128)(2,1)S(1)}, u32[]{:S(2)}, u32[]{:S(2)}) collective-permute-start(bf16[256,1536]{0,1:T(8,128)(2,1)} %collective-permute-done.1), channel_id=1, source_target_pairs={{0,4},{2,6},{4,0},{6,2},{8,12},{10,14},{12,8},{14,10},{16,20},{18,... | collective-permute-start | bytes 2359304 | tf_op jit(solution)/shard_map/ppermute | solution.py:59
  43.5 13.4 %collective-permute-start.5 = (bf16[512,2048]{1,0:T(8,128)(2,1)S(1)}, bf16[512,2048]{1,0:T(8,128)(2,1)S(1)}, u32[]{:S(2)}, u32[]{:S(2)}) collective-permute-start(bf16[512,2048]{1,0:T(8,128)(2,1)S(1)} %get-tuple-element.190), channel_id=1, source_target_pairs={{0,2},{2,0},{4,6},{6,4},{8,10},{10,8},{12,14},{14,12},{16,18},{18,... | collective-permute-start | bytes 6291464 | tf_op jit(solution)/shard_map/ppermute | solution.py:71
  56.9 19.8 %collective-permute-start.9 = (bf16[256,1536]{0,1:T(8,128)(2,1)}, bf16[256,1536]{0,1:T(8,128)(2,1)S(1)}, u32[]{:S(2)}, u32[]{:S(2)}) collective-permute-start(bf16[256,1536]{0,1:T(8,128)(2,1)} %collective-permute-done.1), channel_id=1, source_target_pairs={{0,8},{2,10},{4,12},{6,14},{8,16},{10,18},{12,20},{14,22},{16,24},... | collective-permute-start | bytes 2359304 | tf_op jit(solution)/shard_map/ppermute | solution.py:59
  56.9 19.8 %collective-permute-start.10 = (bf16[256,1536]{0,1:T(8,128)(2,1)S(1)}, bf16[256,1536]{0,1:T(8,128)(2,1)S(1)}, u32[]{:S(2)}, u32[]{:S(2)}) collective-permute-start(bf16[256,1536]{0,1:T(8,128)(2,1)S(1)} %collective-permute-done.6), channel_id=1, source_target_pairs={{0,4},{2,6},{4,0},{6,2},{8,12},{10,14},{12,8},{14,10},{16,20},{18,... | collective-permute-start | bytes 2359304 | tf_op jit(solution)/shard_map/ppermute | solution.py:59
  76.7 13.1 %collective-permute-start.11 = (bf16[2,256,512]{2,1,0:T(8,128)(2,1)S(1)}, bf16[2,256,512]{2,1,0:T(8,128)(2,1)S(1)}, u32[]{:S(2)}, u32[]{:S(2)}) collective-permute-start(bf16[2,256,512]{2,1,0:T(8,128)(2,1)S(1)} %pad_maximum_fusion.6), channel_id=1, source_target_pairs={{0,8},{2,10},{4,12},{6,14},{8,16},{10,18},{12,20},{14,22},{16,24},... | collective-permute-start | bytes 1572872 | tf_op jit(solution)/shard_map/ppermute | solution.py:59
  76.7 16.9 %collective-permute-start.12 = (bf16[256,1536]{0,1:T(8,128)(2,1)S(1)}, bf16[256,1536]{0,1:T(8,128)(2,1)S(1)}, u32[]{:S(2)}, u32[]{:S(2)}) collective-permute-start(bf16[256,1536]{0,1:T(8,128)(2,1)S(1)} %collective-permute-done.9), channel_id=1, source_target_pairs={{0,4},{2,6},{4,0},{6,2},{8,12},{10,14},{12,8},{14,10},{16,20},{18,... | collective-permute-start | bytes 2359304 | tf_op jit(solution)/shard_map/ppermute | solution.py:59
  78.3 11.5 %collective-permute-start.13 = (bf16[128,2048]{1,0:T(8,128)(2,1)S(1)}, bf16[128,2048]{1,0:T(8,128)(2,1)S(1)}, u32[]{:S(2)}, u32[]{:S(2)}) collective-permute-start(bf16[128,2048]{1,0:T(8,128)(2,1)S(1)} %get-tuple-element.418), channel_id=1, source_target_pairs={{0,2},{2,0},{4,6},{6,4},{8,10},{10,8},{12,14},{14,12},{16,18},{18,... | collective-permute-start | bytes 1572872 | tf_op jit(solution)/shard_map/ppermute | solution.py:71
  93.6 23.1 %collective-permute-start.14 = (bf16[2,256,512]{2,1,0:T(8,128)(2,1)S(1)}, bf16[2,256,512]{2,1,0:T(8,128)(2,1)S(1)}, u32[]{:S(2)}, u32[]{:S(2)}) collective-permute-start(bf16[2,256,512]{2,1,0:T(8,128)(2,1)S(1)} %pad_maximum_fusion.6), channel_id=1, source_target_pairs={{0,24},{2,26},{4,28},{6,30},{8,0},{10,2},{12,4},{14,6},{16,8},{18,... | collective-permute-start | bytes 1572872 | tf_op jit(solution)/shard_map/ppermute | solution.py:59
  97.2 19.6 %collective-permute-start.15 = (bf16[2,256,512]{2,1,0:T(8,128)(2,1)S(1)}, bf16[2,256,512]{2,1,0:T(8,128)(2,1)S(1)}, u32[]{:S(2)}, u32[]{:S(2)}) collective-permute-start(bf16[2,256,512]{2,1,0:T(8,128)(2,1)S(1)} %collective-permute-done.11), channel_id=1, source_target_pairs={{0,8},{2,10},{4,12},{6,14},{8,16},{10,18},{12,20},{14,22},{16,24},... | collective-permute-start | bytes 1572872 | tf_op jit(solution)/shard_map/ppermute | solution.py:59
  97.2 21.2 %collective-permute-start.16 = (bf16[256,2048]{1,0:T(8,128)(2,1)S(1)}, bf16[256,2048]{1,0:T(8,128)(2,1)S(1)}, u32[]{:S(2)}, u32[]{:S(2)}) collective-permute-start(bf16[256,2048]{1,0:T(8,128)(2,1)S(1)} %maximum_select_fusion.3), channel_id=1, source_target_pairs={{0,4},{2,6},{4,0},{6,2},{8,12},{10,14},{12,8},{14,10},{16,20},{18,... | collective-permute-start | bytes 3145736 | tf_op jit(solution)/shard_map/ppermute | solution.py:59
  122.4 27.3 %collective-permute-start.19 = (bf16[256,2048]{1,0:T(8,128)(2,1)S(1)}, bf16[256,2048]{1,0:T(8,128)(2,1)}, u32[]{:S(2)}, u32[]{:S(2)}) collective-permute-start(bf16[256,2048]{1,0:T(8,128)(2,1)S(1)} %maximum_select_fusion.3), channel_id=1, source_target_pairs={{0,8},{2,10},{4,12},{6,14},{8,16},{10,18},{12,20},{14,22},{16,24},... | collective-permute-start | bytes 3145736 | tf_op jit(solution)/shard_map/ppermute | solution.py:59
  124.4 25.3 %collective-permute-start.20 = (bf16[256,2048]{1,0:T(8,128)(2,1)S(1)}, bf16[256,2048]{1,0:T(8,128)(2,1)S(1)}, u32[]{:S(2)}, u32[]{:S(2)}) collective-permute-start(bf16[256,2048]{1,0:T(8,128)(2,1)S(1)} %get-tuple-element.229), channel_id=1, source_target_pairs={{0,4},{2,6},{4,0},{6,2},{8,12},{10,14},{12,8},{14,10},{16,20},{18,... | collective-permute-start | bytes 3145736 | tf_op jit(solution)/shard_map/ppermute | solution.py:59
  128.6 48.9 %collective-permute-start.18 = (bf16[512,2048]{1,0:T(8,128)(2,1)S(1)}, bf16[512,2048]{1,0:T(8,128)(2,1)S(1)}, u32[]{:S(2)}, u32[]{:S(2)}) collective-permute-start(bf16[512,2048]{1,0:T(8,128)(2,1)S(1)} %add_convert_fusion.2.att_a), channel_id=1, source_target_pairs={{0,1},{1,0},{2,3},{3,2},{4,5},{5,4},{6,7},{7,6},{8,9},{9,8},{10,11... | collective-permute-start | bytes 6291464 | tf_op jit(solution)/shard_map/ppermute | solution.py:81
  149.7 24.5 %collective-permute-start.21 = (bf16[256,2048]{1,0:T(8,128)(2,1)S(1)}, bf16[256,2048]{1,0:T(8,128)(2,1)}, u32[]{:S(2)}, u32[]{:S(2)}) collective-permute-start(bf16[256,2048]{1,0:T(8,128)(2,1)S(1)} %maximum_select_fusion.3), channel_id=1, source_target_pairs={{0,24},{2,26},{4,28},{6,30},{8,0},{10,2},{12,4},{14,6},{16,8},{18,... | collective-permute-start | bytes 3145736 | tf_op jit(solution)/shard_map/ppermute | solution.py:59
  151.3 24.0 %collective-permute-start.22 = (bf16[256,2048]{1,0:T(8,128)(2,1)}, bf16[256,2048]{1,0:T(8,128)(2,1)S(1)}, u32[]{:S(2)}, u32[]{:S(2)}) collective-permute-start(bf16[256,2048]{1,0:T(8,128)(2,1)} %collective-permute-done.19), channel_id=1, source_target_pairs={{0,4},{2,6},{4,0},{6,2},{8,12},{10,14},{12,8},{14,10},{16,20},{18,... | collective-permute-start | bytes 3145736 | tf_op jit(solution)/shard_map/ppermute | solution.py:59
  152.8 22.5 %collective-permute-start.23 = (bf16[512,2048]{1,0:T(8,128)(2,1)S(1)}, bf16[512,2048]{1,0:T(8,128)(2,1)S(1)}, u32[]{:S(2)}, u32[]{:S(2)}) collective-permute-start(bf16[512,2048]{1,0:T(8,128)(2,1)S(1)} %get-tuple-element.216), channel_id=1, source_target_pairs={{0,2},{2,0},{4,6},{6,4},{8,10},{10,8},{12,14},{14,12},{16,18},{18,... | collective-permute-start | bytes 6291464 | tf_op jit(solution)/shard_map/ppermute | solution.py:71
  175.3 25.1 %collective-permute-start.25 = (bf16[256,2048]{1,0:T(8,128)(2,1)}, bf16[256,2048]{1,0:T(8,128)(2,1)}, u32[]{:S(2)}, u32[]{:S(2)}) collective-permute-start(bf16[256,2048]{1,0:T(8,128)(2,1)} %collective-permute-done.19), channel_id=1, source_target_pairs={{0,8},{2,10},{4,12},{6,14},{8,16},{10,18},{12,20},{14,22},{16,24},... | collective-permute-start | bytes 3145736 | tf_op jit(solution)/shard_map/ppermute | solution.py:59
  176.1 24.4 %collective-permute-start.26 = (bf16[256,2048]{1,0:T(8,128)(2,1)}, bf16[256,2048]{1,0:T(8,128)(2,1)}, u32[]{:S(2)}, u32[]{:S(2)}) collective-permute-start(bf16[256,2048]{1,0:T(8,128)(2,1)} %collective-permute-done.21), channel_id=1, source_target_pairs={{0,4},{2,6},{4,0},{6,2},{8,12},{10,14},{12,8},{14,10},{16,20},{18,... | collective-permute-start | bytes 3145736 | tf_op jit(solution)/shard_map/ppermute | solution.py:59
  180.6 19.9 %collective-permute-start.24 = (bf16[512,2048]{1,0:T(8,128)(2,1)S(1)}, bf16[512,2048]{1,0:T(8,128)(2,1)S(1)}, u32[]{:S(2)}, u32[]{:S(2)}) collective-permute-start(bf16[512,2048]{1,0:T(8,128)(2,1)S(1)} %get-tuple-element.222), channel_id=1, source_target_pairs={{0,2},{2,0},{4,6},{6,4},{8,10},{10,8},{12,14},{14,12},{16,18},{18,... | collective-permute-start | bytes 6291464 | tf_op jit(solution)/shard_map/ppermute | solution.py:71
  200.4 25.3 %collective-permute-start.27 = (bf16[256,2048]{1,0:T(8,128)(2,1)S(1)}, bf16[256,2048]{1,0:T(8,128)(2,1)S(1)}, u32[]{:S(2)}, u32[]{:S(2)}) collective-permute-start(bf16[256,2048]{1,0:T(8,128)(2,1)S(1)} %copy-done.33), channel_id=1, source_target_pairs={{0,8},{2,10},{4,12},{6,14},{8,16},{10,18},{12,20},{14,22},{16,24},... | collective-permute-start | bytes 3145736 | tf_op jit(solution)/shard_map/ppermute | solution.py:59
  200.5 25.2 %collective-permute-start.28 = (bf16[256,2048]{1,0:T(8,128)(2,1)}, bf16[256,2048]{1,0:T(8,128)(2,1)S(1)}, u32[]{:S(2)}, u32[]{:S(2)}) collective-permute-start(bf16[256,2048]{1,0:T(8,128)(2,1)} %collective-permute-done.25), channel_id=1, source_target_pairs={{0,4},{2,6},{4,0},{6,2},{8,12},{10,14},{12,8},{14,10},{16,20},{18,... | collective-permute-start | bytes 3145736 | tf_op jit(solution)/shard_map/ppermute | solution.py:59
  225.7 23.4 %collective-permute-start.29 = (bf16[256,2048]{1,0:T(8,128)(2,1)S(1)}, bf16[256,2048]{1,0:T(8,128)(2,1)S(1)}, u32[]{:S(2)}, u32[]{:S(2)}) collective-permute-start(bf16[256,2048]{1,0:T(8,128)(2,1)S(1)} %copy-done.33), channel_id=1, source_target_pairs={{0,24},{2,26},{4,28},{6,30},{8,0},{10,2},{12,4},{14,6},{16,8},{18,... | collective-permute-start | bytes 3145736 | tf_op jit(solution)/shard_map/ppermute | solution.py:59
  227.8 21.3 %collective-permute-start.30 = (bf16[256,2048]{1,0:T(8,128)(2,1)S(1)}, bf16[256,2048]{1,0:T(8,128)(2,1)S(1)}, u32[]{:S(2)}, u32[]{:S(2)}) collective-permute-start(bf16[256,2048]{1,0:T(8,128)(2,1)S(1)} %collective-permute-done.27), channel_id=1, source_target_pairs={{0,4},{2,6},{4,0},{6,2},{8,12},{10,14},{12,8},{14,10},{16,20},{18,... | collective-permute-start | bytes 3145736 | tf_op jit(solution)/shard_map/ppermute | solution.py:59
  249.1 23.1 %collective-permute-start.31 = (bf16[256,2048]{1,0:T(8,128)(2,1)S(1)}, bf16[256,2048]{1,0:T(8,128)(2,1)S(1)}, u32[]{:S(2)}, u32[]{:S(2)}) collective-permute-start(bf16[256,2048]{1,0:T(8,128)(2,1)S(1)} %collective-permute-done.27), channel_id=1, source_target_pairs={{0,8},{2,10},{4,12},{6,14},{8,16},{10,18},{12,20},{14,22},{16,24},... | collective-permute-start | bytes 3145736 | tf_op jit(solution)/shard_map/ppermute | solution.py:59
  249.3 22.9 %collective-permute-start.32 = (bf16[256,2048]{1,0:T(8,128)(2,1)S(1)}, bf16[256,2048]{1,0:T(8,128)(2,1)S(1)}, u32[]{:S(2)}, u32[]{:S(2)}) collective-permute-start(bf16[256,2048]{1,0:T(8,128)(2,1)S(1)} %collective-permute-done.29), channel_id=1, source_target_pairs={{0,4},{2,6},{4,0},{6,2},{8,12},{10,14},{12,8},{14,10},{16,20},{18,... | collective-permute-start | bytes 3145736 | tf_op jit(solution)/shard_map/ppermute | solution.py:59
  272.2 23.0 %collective-permute-start.33 = (bf16[256,2048]{1,0:T(8,128)(2,1)S(1)}, bf16[256,2048]{1,0:T(8,128)(2,1)S(1)}, u32[]{:S(2)}, u32[]{:S(2)}) collective-permute-start(bf16[256,2048]{1,0:T(8,128)(2,1)S(1)} %collective-permute-done.31), channel_id=1, source_target_pairs={{0,4},{2,6},{4,0},{6,2},{8,12},{10,14},{12,8},{14,10},{16,20},{18,... | collective-permute-start | bytes 3145736 | tf_op jit(solution)/shard_map/ppermute | solution.py:59
  273.7 45.3 %collective-permute-start.36 = (bf16[2,256,1024]{2,1,0:T(8,128)(2,1)}, bf16[2,256,1024]{2,1,0:T(8,128)(2,1)}, u32[]{:S(2)}, u32[]{:S(2)}) collective-permute-start(bf16[2,256,1024]{2,1,0:T(8,128)(2,1)} %get-tuple-element.246), channel_id=1, source_target_pairs={{0,24},{2,26},{4,28},{6,30},{8,0},{10,2},{12,4},{14,6},{16,8},{18,... | collective-permute-start | bytes 3145736 | tf_op jit(solution)/shard_map/ppermute | solution.py:59
  295.2 26.6 %collective-permute-start.34 = (bf16[512,1024]{1,0:T(8,128)(2,1)}, bf16[512,1024]{1,0:T(8,128)(2,1)S(1)}, u32[]{:S(2)}, u32[]{:S(2)}) collective-permute-start(bf16[512,1024]{1,0:T(8,128)(2,1)} %get-tuple-element.250), channel_id=1, source_target_pairs={{0,4},{2,6},{4,0},{6,2},{8,12},{10,14},{12,8},{14,10},{16,20},{18,... | collective-permute-start | bytes 3145736 | tf_op jit(solution)/shard_map/ppermute | solution.py:59
  296.0 25.8 %collective-permute-start.35 = (bf16[2,256,1024]{2,1,0:T(8,128)(2,1)}, bf16[2,256,1024]{2,1,0:T(8,128)(2,1)S(1)}, u32[]{:S(2)}, u32[]{:S(2)}) collective-permute-start(bf16[2,256,1024]{2,1,0:T(8,128)(2,1)} %get-tuple-element.251), channel_id=1, source_target_pairs={{0,8},{2,10},{4,12},{6,14},{8,16},{10,18},{12,20},{14,22},{16,24},... | collective-permute-start | bytes 3145736 | tf_op jit(solution)/shard_map/ppermute | solution.py:59
  323.4 27.1 %collective-permute-start.39 = (bf16[512,1024]{1,0:T(8,128)(2,1)}, bf16[512,1024]{1,0:T(8,128)(2,1)S(1)}, u32[]{:S(2)}, u32[]{:S(2)}) collective-permute-start(bf16[512,1024]{1,0:T(8,128)(2,1)} %get-tuple-element.257), channel_id=1, source_target_pairs={{0,4},{2,6},{4,0},{6,2},{8,12},{10,14},{12,8},{14,10},{16,20},{18,... | collective-permute-start | bytes 3145736 | tf_op jit(solution)/shard_map/ppermute | solution.py:59
  324.7 27.9 %collective-permute-start.40 = (bf16[2,256,1024]{2,1,0:T(8,128)(2,1)}, bf16[2,256,1024]{2,1,0:T(8,128)(2,1)}, u32[]{:S(2)}, u32[]{:S(2)}) collective-permute-start(bf16[2,256,1024]{2,1,0:T(8,128)(2,1)} %add_convert_fusion.6), channel_id=1, source_target_pairs={{0,24},{2,26},{4,28},{6,30},{8,0},{10,2},{12,4},{14,6},{16,8},{18,... | collective-permute-start | bytes 3145736 | tf_op jit(solution)/shard_map/ppermute | solution.py:59
  338.1 49.9 %collective-permute-start.38 = (bf16[512,2048]{1,0:T(8,128)(2,1)S(1)}, bf16[512,2048]{1,0:T(8,128)(2,1)S(1)}, u32[]{:S(2)}, u32[]{:S(2)}) collective-permute-start(bf16[512,2048]{1,0:T(8,128)(2,1)S(1)} %add_convert_fusion.1.d_a), channel_id=1, source_target_pairs={{0,1},{1,0},{2,3},{3,2},{4,5},{5,4},{6,7},{7,6},{8,9},{9,8},{10,11... | collective-permute-start | bytes 6291464 | tf_op jit(solution)/shard_map/ppermute | solution.py:81
  352.6 16.7 %collective-permute-start.42 = (bf16[256,1024]{1,0:T(8,128)(2,1)S(1)}, bf16[256,1024]{1,0:T(8,128)(2,1)S(1)}, u32[]{:S(2)}, u32[]{:S(2)}) collective-permute-start(bf16[256,1024]{1,0:T(8,128)(2,1)S(1)} %get-tuple-element.267), channel_id=1, source_target_pairs={{0,24},{2,26},{4,28},{6,30},{8,0},{10,2},{12,4},{14,6},{16,8},{18,... | collective-permute-start | bytes 1572872 | tf_op jit(solution)/shard_map/ppermute | solution.py:59
  356.9 22.6 %collective-permute-start.43 = (bf16[256,1024]{1,0:T(8,128)(2,1)S(1)}, bf16[256,1024]{1,0:T(8,128)(2,1)S(1)}, u32[]{:S(2)}, u32[]{:S(2)}) collective-permute-start(bf16[256,1024]{1,0:T(8,128)(2,1)S(1)} %get-tuple-element.268), channel_id=1, source_target_pairs={{0,8},{2,10},{4,12},{6,14},{8,16},{10,18},{12,20},{14,22},{16,24},... | collective-permute-start | bytes 1572872 | tf_op jit(solution)/shard_map/ppermute | solution.py:59
  356.9 24.1 %collective-permute-start.41 = (bf16[256,2048]{1,0:T(8,128)(2,1)S(1)}, bf16[256,2048]{1,0:T(8,128)(2,1)S(1)}, u32[]{:S(2)}, u32[]{:S(2)}) collective-permute-start(bf16[256,2048]{1,0:T(8,128)(2,1)S(1)} %get-tuple-element.266), channel_id=1, source_target_pairs={{0,4},{2,6},{4,0},{6,2},{8,12},{10,14},{12,8},{14,10},{16,20},{18,... | collective-permute-start | bytes 3145736 | tf_op jit(solution)/shard_map/ppermute | solution.py:59
  381.4 24.2 %collective-permute-start.46 = (bf16[256,2048]{1,0:T(8,128)(2,1)S(1)}, bf16[256,2048]{1,0:T(8,128)(2,1)S(1)}, u32[]{:S(2)}, u32[]{:S(2)}) collective-permute-start(bf16[256,2048]{1,0:T(8,128)(2,1)S(1)} %add_convert_fusion.5), channel_id=1, source_target_pairs={{0,24},{2,26},{4,28},{6,30},{8,0},{10,2},{12,4},{14,6},{16,8},{18,... | collective-permute-start | bytes 3145736 | tf_op jit(solution)/shard_map/ppermute | solution.py:59
  385.2 23.3 %collective-permute-start.45 = (bf16[256,2048]{1,0:T(8,128)(2,1)}, bf16[256,2048]{1,0:T(8,128)(2,1)S(1)}, u32[]{:S(2)}, u32[]{:S(2)}) collective-permute-start(bf16[256,2048]{1,0:T(8,128)(2,1)} %get-tuple-element.274), channel_id=1, source_target_pairs={{0,4},{2,6},{4,0},{6,2},{8,12},{10,14},{12,8},{14,10},{16,20},{18,... | collective-permute-start | bytes 3145736 | tf_op jit(solution)/shard_map/ppermute | solution.py:59
  408.5 23.6 %collective-permute-start.48 = (bf16[256,1024]{1,0:T(8,128)(2,1)}, bf16[256,1024]{1,0:T(8,128)(2,1)S(1)}, u32[]{:S(2)}, u32[]{:S(2)}) collective-permute-start(bf16[256,1024]{1,0:T(8,128)(2,1)} %fusion.49), channel_id=1, source_target_pairs={{0,4},{2,6},{4,0},{6,2},{8,12},{10,14},{12,8},{14,10},{16,20},{18,... | collective-permute-start | bytes 1572872 | tf_op jit(solution)/shard_map/ppermute | solution.py:59
  408.9 23.2 %collective-permute-start.50 = (bf16[256,1024]{1,0:T(8,128)(2,1)}, bf16[256,1024]{1,0:T(8,128)(2,1)S(1)}, u32[]{:S(2)}, u32[]{:S(2)}) collective-permute-start(bf16[256,1024]{1,0:T(8,128)(2,1)} %add_convert_fusion.10), channel_id=1, source_target_pairs={{0,24},{2,26},{4,28},{6,30},{8,0},{10,2},{12,4},{14,6},{16,8},{18,... | collective-permute-start | bytes 1572872 | tf_op jit(solution)/shard_map/ppermute | solution.py:59
  410.7 31.0 %collective-permute-start.49 = (bf16[256,2048]{1,0:T(8,128)(2,1)S(1)}, bf16[256,2048]{1,0:T(8,128)(2,1)S(1)}, u32[]{:S(2)}, u32[]{:S(2)}) collective-permute-start(bf16[256,2048]{1,0:T(8,128)(2,1)S(1)} %add_convert_fusion.4), channel_id=1, source_target_pairs={{0,8},{2,10},{4,12},{6,14},{8,16},{10,18},{12,20},{14,22},{16,24},... | collective-permute-start | bytes 3145736 | tf_op jit(solution)/shard_map/ppermute | solution.py:59
  411.3 31.1 %collective-permute-start.47 = (bf16[256,2048]{1,0:T(8,128)(2,1)S(1)}, bf16[256,2048]{1,0:T(8,128)(2,1)S(1)}, u32[]{:S(2)}, u32[]{:S(2)}) collective-permute-start(bf16[256,2048]{1,0:T(8,128)(2,1)S(1)} %copy-done.41), channel_id=1, source_target_pairs={{0,4},{2,6},{4,0},{6,2},{8,12},{10,14},{12,8},{14,10},{16,20},{18,... | collective-permute-start | bytes 3145736 | tf_op jit(solution)/shard_map/ppermute | solution.py:59
  443.0 25.8 %collective-permute-start.52 = (bf16[256,2048]{1,0:T(8,128)(2,1)S(1)}, bf16[256,2048]{1,0:T(8,128)(2,1)S(1)}, u32[]{:S(2)}, u32[]{:S(2)}) collective-permute-start(bf16[256,2048]{1,0:T(8,128)(2,1)S(1)} %copy-done.40), channel_id=1, source_target_pairs={{0,4},{2,6},{4,0},{6,2},{8,12},{10,14},{12,8},{14,10},{16,20},{18,... | collective-permute-start | bytes 3145736 | tf_op jit(solution)/shard_map/ppermute | solution.py:59
  444.0 24.7 %collective-permute-start.53 = (bf16[256,2048]{1,0:T(8,128)(2,1)S(1)}, bf16[256,2048]{1,0:T(8,128)(2,1)S(1)}, u32[]{:S(2)}, u32[]{:S(2)}) collective-permute-start(bf16[256,2048]{1,0:T(8,128)(2,1)S(1)} %add_convert_fusion.3), channel_id=1, source_target_pairs={{0,24},{2,26},{4,28},{6,30},{8,0},{10,2},{12,4},{14,6},{16,8},{18,... | collective-permute-start | bytes 3145736 | tf_op jit(solution)/shard_map/ppermute | solution.py:59
  456.2 49.3 %collective-permute-start.61 = (bf16[512,2048]{1,0:T(8,128)(2,1)S(1)}, bf16[512,2048]{1,0:T(8,128)(2,1)S(1)}, u32[]{:S(2)}, u32[]{:S(2)}) collective-permute-start(bf16[512,2048]{1,0:T(8,128)(2,1)S(1)} %add_convert_fusion.d_a), channel_id=1, source_target_pairs={{0,1},{1,0},{2,3},{3,2},{4,5},{5,4},{6,7},{7,6},{8,9},{9,8},{10,11... | collective-permute-start | bytes 6291464 | tf_op jit(solution)/shard_map/ppermute | solution.py:81
  468.8 23.1 %collective-permute-start.54 = (bf16[1024,512]{1,0:T(8,128)(2,1)}, bf16[1024,512]{1,0:T(8,128)(2,1)S(1)}, u32[]{:S(2)}, u32[]{:S(2)}) collective-permute-start(bf16[1024,512]{1,0:T(8,128)(2,1)} %fusion.36), channel_id=1, source_target_pairs={{0,4},{2,6},{4,0},{6,2},{8,12},{10,14},{12,8},{14,10},{16,20},{18,... | collective-permute-start | bytes 3145736 | tf_op jit(solution)/shard_map/ppermute | solution.py:59
  479.2 12.7 %collective-permute-start.55 = (bf16[512,2048]{1,0:T(8,128)(2,1)S(1)}, bf16[512,2048]{1,0:T(8,128)(2,1)S(1)}, u32[]{:S(2)}, u32[]{:S(2)}) collective-permute-start(bf16[512,2048]{1,0:T(8,128)(2,1)S(1)} %pad_maximum_fusion.1), channel_id=1, source_target_pairs={{0,2},{2,0},{4,6},{6,4},{8,10},{10,8},{12,14},{14,12},{16,18},{18,... | collective-permute-start | bytes 6291464 | tf_op jit(solution)/shard_map/ppermute | solution.py:71
  480.1 11.8 %collective-permute-start.56 = (f32[128,2048]{1,0:T(8,128)S(1)}, f32[128,2048]{1,0:T(8,128)S(1)}, u32[]{:S(2)}, u32[]{:S(2)}) collective-permute-start(f32[128,2048]{1,0:T(8,128)S(1)} %get-tuple-element.405), channel_id=1, source_target_pairs={{0,2},{2,0},{4,6},{6,4},{8,10},{10,8},{12,14},{14,12},{16,18},{18,... | collective-permute-start | bytes 3145736 | tf_op jit(solution)/shard_map/ppermute | solution.py:71
  492.9 20.6 %collective-permute-start.59 = (bf16[256,512]{1,0:T(8,128)(2,1)}, bf16[256,512]{1,0:T(8,128)(2,1)}, u32[]{:S(2)}, u32[]{:S(2)}) collective-permute-start(bf16[256,512]{1,0:T(8,128)(2,1)} %get-tuple-element.312), channel_id=1, source_target_pairs={{0,24},{2,26},{4,28},{6,30},{8,0},{10,2},{12,4},{14,6},{16,8},{18,... | collective-permute-start | bytes 786440 | tf_op jit(solution)/shard_map/ppermute | solution.py:59
  494.8 18.7 %collective-permute-start.60 = (bf16[256,512]{1,0:T(8,128)(2,1)}, bf16[256,512]{1,0:T(8,128)(2,1)}, u32[]{:S(2)}, u32[]{:S(2)}) collective-permute-start(bf16[256,512]{1,0:T(8,128)(2,1)} %get-tuple-element.314), channel_id=1, source_target_pairs={{0,8},{2,10},{4,12},{6,14},{8,16},{10,18},{12,20},{14,22},{16,24},... | collective-permute-start | bytes 786440 | tf_op jit(solution)/shard_map/ppermute | solution.py:59
  495.1 18.4 %collective-permute-start.58 = (bf16[256,1536]{1,0:T(8,128)(2,1)}, bf16[256,1536]{1,0:T(8,128)(2,1)}, u32[]{:S(2)}, u32[]{:S(2)}) collective-permute-start(bf16[256,1536]{1,0:T(8,128)(2,1)} %get-tuple-element.310), channel_id=1, source_target_pairs={{0,4},{2,6},{4,0},{6,2},{8,12},{10,14},{12,8},{14,10},{16,20},{18,... | collective-permute-start | bytes 2359304 | tf_op jit(solution)/shard_map/ppermute | solution.py:59
  503.9 43.6 %collective-permute-start.57 = (bf16[512,2048]{1,0:T(8,128)(2,1)S(1)}, bf16[512,2048]{1,0:T(8,128)(2,1)S(1)}, u32[]{:S(2)}, u32[]{:S(2)}) collective-permute-start(bf16[512,2048]{1,0:T(8,128)(2,1)S(1)} %fusion.16), channel_id=1, source_target_pairs={{0,1},{1,0},{2,3},{3,2},{4,5},{5,4},{6,7},{7,6},{8,9},{9,8},{10,11... | collective-permute-start | bytes 6291464 | tf_op jit(solution)/shard_map/ppermute | solution.py:81
  514.8 10.6 %collective-permute-start.64 = (bf16[256,512]{1,0:T(8,128)(2,1)S(1)}, bf16[256,512]{1,0:T(8,128)(2,1)S(1)}, u32[]{:S(2)}, u32[]{:S(2)}) collective-permute-start(bf16[256,512]{1,0:T(8,128)(2,1)S(1)} %add_convert_fusion.13), channel_id=1, source_target_pairs={{0,24},{2,26},{4,28},{6,30},{8,0},{10,2},{12,4},{14,6},{16,8},{18,... | collective-permute-start | bytes 786440 | tf_op jit(solution)/shard_map/ppermute | solution.py:59
  520.0 17.4 %collective-permute-start.63 = (bf16[256,1536]{1,0:T(8,128)(2,1)S(1)}, bf16[256,1536]{1,0:T(8,128)(2,1)S(1)}, u32[]{:S(2)}, u32[]{:S(2)}) collective-permute-start(bf16[256,1536]{1,0:T(8,128)(2,1)S(1)} %add_convert_fusion.9), channel_id=1, source_target_pairs={{0,24},{2,26},{4,28},{6,30},{8,0},{10,2},{12,4},{14,6},{16,8},{18,... | collective-permute-start | bytes 2359304 | tf_op jit(solution)/shard_map/ppermute | solution.py:59
  520.0 17.4 %collective-permute-start.62 = (bf16[256,1536]{1,0:T(8,128)(2,1)S(1)}, bf16[256,1536]{1,0:T(8,128)(2,1)S(1)}, u32[]{:S(2)}, u32[]{:S(2)}) collective-permute-start(bf16[256,1536]{1,0:T(8,128)(2,1)S(1)} %copy-done.46), channel_id=1, source_target_pairs={{0,4},{2,6},{4,0},{6,2},{8,12},{10,14},{12,8},{14,10},{16,20},{18,... | collective-permute-start | bytes 2359304 | tf_op jit(solution)/shard_map/ppermute | solution.py:59
  525.3 12.1 %collective-permute-start.65 = (f32[128,2048]{1,0:T(8,128)S(1)}, f32[128,2048]{1,0:T(8,128)S(1)}, u32[]{:S(2)}, u32[]{:S(2)}) collective-permute-start(f32[128,2048]{1,0:T(8,128)S(1)} %get-tuple-element.403), channel_id=1, source_target_pairs={{0,2},{2,0},{4,6},{6,4},{8,10},{10,8},{12,14},{14,12},{16,18},{18,... | collective-permute-start | bytes 3145736 | tf_op jit(solution)/shard_map/ppermute | solution.py:71
  539.9 18.1 %collective-permute-start.67 = (bf16[256,1536]{1,0:T(8,128)(2,1)}, bf16[256,1536]{1,0:T(8,128)(2,1)S(1)}, u32[]{:S(2)}, u32[]{:S(2)}) collective-permute-start(bf16[256,1536]{1,0:T(8,128)(2,1)} %add_convert_fusion.8), channel_id=1, source_target_pairs={{0,8},{2,10},{4,12},{6,14},{8,16},{10,18},{12,20},{14,22},{16,24},... | collective-permute-start | bytes 2359304 | tf_op jit(solution)/shard_map/ppermute | solution.py:59
  539.9 18.1 %collective-permute-start.66 = (bf16[256,1536]{1,0:T(8,128)(2,1)S(1)}, bf16[256,1536]{1,0:T(8,128)(2,1)}, u32[]{:S(2)}, u32[]{:S(2)}) collective-permute-start(bf16[256,1536]{1,0:T(8,128)(2,1)S(1)} %copy-done.45), channel_id=1, source_target_pairs={{0,4},{2,6},{4,0},{6,2},{8,12},{10,14},{12,8},{14,10},{16,20},{18,... | collective-permute-start | bytes 2359304 | tf_op jit(solution)/shard_map/ppermute | solution.py:59
  561.1 15.8 %collective-permute-start.68 = (bf16[256,1536]{1,0:T(8,128)(2,1)S(1)}, bf16[256,1536]{1,0:T(8,128)(2,1)S(1)}, u32[]{:S(2)}, u32[]{:S(2)}) collective-permute-start(bf16[256,1536]{1,0:T(8,128)(2,1)S(1)} %copy-done.44), channel_id=1, source_target_pairs={{0,4},{2,6},{4,0},{6,2},{8,12},{10,14},{12,8},{14,10},{16,20},{18,... | collective-permute-start | bytes 2359304 | tf_op jit(solution)/shard_map/ppermute | solution.py:59
  562.6 16.9 %collective-permute-start.69 = (bf16[256,1536]{1,0:T(8,128)(2,1)}, bf16[256,1536]{1,0:T(8,128)(2,1)}, u32[]{:S(2)}, u32[]{:S(2)}) collective-permute-start(bf16[256,1536]{1,0:T(8,128)(2,1)} %add_convert_fusion.7), channel_id=1, source_target_pairs={{0,24},{2,26},{4,28},{6,30},{8,0},{10,2},{12,4},{14,6},{16,8},{18,... | collective-permute-start | bytes 2359304 | tf_op jit(solution)/shard_map/ppermute | solution.py:59
  566.0 17.0 %all-to-all-start = ((f32[16,14,128]{2,1,0:T(8,128)}), f32[16,14,128]{2,1,0:T(8,128)S(1)}, u32[]{:S(2)}, u32[]{:S(2)}) async-start(f32[16,14,128]{2,1,0:T(8,128)} %copy.47), calls=%async_computation | async-start | bytes 262144 | tf_op jit(solution)/shard_map/all_to_all | solution.py:763
  (87 other events, 1024.5 us)

commit v8 on v7

--- a/solution.py
+++ b/solution.py
@@ -13,7 +13,7 @@
 F32 = jnp.float32
 BF16 = jnp.bfloat16
 CORES = 2
-TILE = 128
+TILE = 256
 CHUNK = 16
 UNROLL = 8
 

time: 598 us -> 598 us (level)
  no operation moved by 1% of the time
where the time goes in v8:
time: 598 us; the launch traced here: 589 us
  waiting for transfers between devices  221 us (37%)
  matrix products  143 us (24%)
  starting transfers between devices  86.7 us (14%)
  local copies, waits for them, and re-layouts  48 us (8%)
  Pallas kernels  46.3 us (8%)
  other arithmetic  41.6 us (7%)
    ppermute x52, waiting for transfers between devices, send(): out = lax.ppermute(value, 'dp', self.ring(dz, dx, 0))  207 us
    dot_general x16, matrix products, matmul(): lax.dot_general(lhs, rhs, (((1,), (1 if turned else 0,)), ((), ())), pref...  101 us
    ppermute x52, starting transfers between devices, send(): out = lax.ppermute(value, 'dp', self.ring(dz, dx, 0))  74.6 us
    dot_general x8, matrix products, dots(): lax.dot_general(lhs[:, kx * width:(kx + 1) * width], rhs, (((0,), (0,)),...  39.9 us
    unnamed x186, local copies, waits for them, and re-layouts  32.5 us
    pallas_call x6, Pallas kernels, by_rows(): pl.pallas_call(functools.partial(kernel, blocks), grid_spec=pltpu.Prefetc...  28.1 us
    pallas_call x2, Pallas kernels, by_image(): pl.pallas_call(kernel, grid=(rows // length,), in_specs=[block(operand.sh...  13.4 us
  transfers between devices with their start and end apart: 73, of which 32 were waited for; matrix products, arithmetic and copies ran while one was open for 37% of the time, Pallas kernels for 8%

profile of v8, /device:TPU:0, one launch (start us, length us, event | category | flops | bytes accessed | tf_op | source)
XLA Modules:
  0.0 588.9 jit_solution(9882623779632728179)
XLA Ops:
  7.7 2.6 collective-permute-start.2
  14.9 4.8 shard_map.144
  21.7 12.3 %collective-permute-done.4 = bf16[256,512]{1,0:T(8,128)(2,1)S(1)} collective-permute-done((bf16[256,512]{1,0:T(8,128)(2,1)}, bf16[256,512]{1,0:T(8,128)(2,1)S(1)}, u32[]{:S(2)}, u32[]{:S(2)}) %collective-permute-start.4) | collective-permute-done | bytes 262176 | tf_op jit(solution)/shard_map/ppermute | solution.py:59
  34.1 3.9 collective-permute-start.6
  41.1 2.5 shard_map.145
  43.7 2.9 constant_dynamic-update-slice_fusion.8
  46.8 7.7 %collective-permute-done.6 = bf16[256,1536]{0,1:T(8,128)(2,1)S(1)} collective-permute-done((bf16[256,1536]{0,1:T(8,128)(2,1)S(1)}, bf16[256,1536]{0,1:T(8,128)(2,1)S(1)}, u32[]{:S(2)}, u32[]{:S(2)}) %collective-permute-start.6) | collective-permute-done | bytes 786464 | tf_op jit(solution)/shard_map/ppermute | solution.py:59
  54.5 2.4 collective-permute-done.7
  60.9 15.8 %collective-permute-done.9 = bf16[256,1536]{0,1:T(8,128)(2,1)S(1)} collective-permute-done((bf16[256,1536]{0,1:T(8,128)(2,1)}, bf16[256,1536]{0,1:T(8,128)(2,1)S(1)}, u32[]{:S(2)}, u32[]{:S(2)}) %collective-permute-start.9) | collective-permute-done | bytes 786464 | tf_op jit(solution)/shard_map/ppermute | solution.py:59
  78.8 10.9 %collective-permute-done.11 = bf16[2,256,512]{2,1,0:T(8,128)(2,1)S(1)} collective-permute-done((bf16[2,256,512]{2,1,0:T(8,128)(2,1)S(1)}, bf16[2,256,512]{2,1,0:T(8,128)(2,1)S(1)}, u32[]{:S(2)}, u32[]{:S(2)}) %collective-permute-start.11) | collective-permute-done | bytes 524320 | tf_op jit(solution)/shard_map/ppermute | solution.py:59
  91.1 2.5 collective-permute-done.12
  93.6 3.5 collective-permute-start.14
  98.9 7.0 %convolution_convert_fusion.qkv_ref = bf16[1024,1536]{1,0:T(8,128)(2,1)S(1)} fusion(bf16[1024,2048]{1,0:T(8,128)(2,1)S(1)} %constant_dynamic-update-slice_fusion, bf16[2048,1536]{0,1:T(8,128)(2,1)S(1)} %constant_dynamic-update-slice_fusion.2), kind=kOutput, calls=%fused_computation.34 | convolution fusion | flops 6444023808 | bytes 13631488 | tf_op jit(solution)/shard_map/dot_general | solution.py:439
  105.9 4.5 shard_map.146
  110.4 6.3 %collective-permute-done.15 = bf16[2,256,512]{2,1,0:T(8,128)(2,1)S(1)} collective-permute-done((bf16[2,256,512]{2,1,0:T(8,128)(2,1)S(1)}, bf16[2,256,512]{2,1,0:T(8,128)(2,1)S(1)}, u32[]{:S(2)}, u32[]{:S(2)}) %collective-permute-start.15) | collective-permute-done | bytes 524320 | tf_op jit(solution)/shard_map/ppermute | solution.py:59
  118.4 4.1 collective-permute-done.17
  131.8 17.9 %collective-permute-done.19 = bf16[256,2048]{1,0:T(8,128)(2,1)} collective-permute-done((bf16[256,2048]{1,0:T(8,128)(2,1)S(1)}, bf16[256,2048]{1,0:T(8,128)(2,1)}, u32[]{:S(2)}, u32[]{:S(2)}) %collective-permute-start.19) | collective-permute-done | bytes 1048608 | tf_op jit(solution)/shard_map/ppermute | solution.py:59
  152.8 21.3 %collective-permute-done.21 = bf16[256,2048]{1,0:T(8,128)(2,1)} collective-permute-done((bf16[256,2048]{1,0:T(8,128)(2,1)S(1)}, bf16[256,2048]{1,0:T(8,128)(2,1)}, u32[]{:S(2)}, u32[]{:S(2)}) %collective-permute-start.21) | collective-permute-done | bytes 1048608 | tf_op jit(solution)/shard_map/ppermute | solution.py:59
  177.6 3.0 shard_map.148
  180.9 19.5 %collective-permute-done.25 = bf16[256,2048]{1,0:T(8,128)(2,1)} collective-permute-done((bf16[256,2048]{1,0:T(8,128)(2,1)}, bf16[256,2048]{1,0:T(8,128)(2,1)}, u32[]{:S(2)}, u32[]{:S(2)}) %collective-permute-start.25) | collective-permute-done | bytes 1048608 | tf_op jit(solution)/shard_map/ppermute | solution.py:59
  210.1 2.5 constant_dynamic-update-slice_fusion.20
  214.9 10.9 %collective-permute-done.27 = bf16[256,2048]{1,0:T(8,128)(2,1)S(1)} collective-permute-done((bf16[256,2048]{1,0:T(8,128)(2,1)S(1)}, bf16[256,2048]{1,0:T(8,128)(2,1)S(1)}, u32[]{:S(2)}, u32[]{:S(2)}) %collective-permute-start.27) | collective-permute-done | bytes 1048608 | tf_op jit(solution)/shard_map/ppermute | solution.py:59
  232.7 15.3 %fusion.13 = (bf16[1024,2048]{1,0:T(8,128)(2,1)}, f32[1024,2048]{1,0:T(8,128)}) fusion(bf16[1024,2048]{1,0:T(8,128)(2,1)S(1)} %copy-done.30, bf16[2048,2048]{1,0:T(8,128)(2,1)} %constant_dynamic-update-slice_fusion.16), kind=kOutput, calls=%fused_computation.16 | convolution fusion | flops 8608808960 | bytes 25165824 | tf_op jit(solution)/shard_map/dot_general | solution.py:439
  249.9 7.0 %convolution_convert_fusion.6 = bf16[1024,2048]{1,0:T(8,128)(2,1)S(1)} fusion(bf16[1024,2048]{1,0:T(8,128)(2,1)} %get-tuple-element.315, bf16[1024,2048]{1,0:T(8,128)(2,1)S(1)} %constant_dynamic-update-slice_fusion.14), kind=kOutput, calls=%fused_computation.40 | convolution fusion | flops 4297064448 | bytes 10485760 | tf_op jit(solution)/shard_map/dot_general | solution.py:176
  258.4 7.0 %convolution_convert_fusion.5 = bf16[1024,2048]{1,0:T(8,128)(2,1)S(1)} fusion(bf16[1024,2048]{1,0:T(8,128)(2,1)} %get-tuple-element.315, bf16[1024,2048]{1,0:T(8,128)(2,1)S(1)} %constant_dynamic-update-slice_fusion.14), kind=kOutput, calls=%fused_computation.39 | convolution fusion | flops 4297064448 | bytes 10485760 | tf_op jit(solution)/shard_map/dot_general | solution.py:176
  273.7 3.7 collective-permute-start.36
  278.5 7.9 %fusion.81 = f32[512,2048]{1,0:T(8,128)} fusion(bf16[512,1536]{1,0:T(8,128)(2,1)S(1)} %pad_maximum_fusion.3, bf16[1536,2048]{1,0:T(8,128)(2,1)} %constant_dynamic-update-slice_fusion.24), kind=kOutput, calls=%fused_computation.214 | convolution fusion | flops 3221225472 | bytes 12058624 | tf_op jit(solution)/shard_map/dot_general | solution.py:439
  286.5 5.1 fusion.82
  291.6 3.6 collective-permute-done.33
  297.8 11.5 %fusion.15 = bf16[1024,2048]{1,0:T(8,128)(2,1)} fusion(f32[512,2048]{1,0:T(8,128)} %fusion.82, f32[512,2048]{1,0:T(8,128)} %fusion.81, f32[1024,2048]{1,0:T(8,128)} %get-tuple-element.243, bf16[1024,512]{1,0:T(8,128)(2,1)S(1)} %pad_maximum_fusion.5, bf16[512,2048]{1,0:T(8,128)(2,1)S(1)} %constant_dynamic-update-slice_fusion.30), kind=kOutput, calls=%fused_computation.19 | convolution fusion | flops 2191523840 | bytes 24117248 | tf_op jit(solution)/shard_map/dot_general | solution.py:439
  309.3 9.9 %convolution_convert_fusion.9 = bf16[512,2048]{1,0:T(8,128)(2,1)} fusion(bf16[2048,2048]{1,0:T(8,128)(2,1)} %constant_dynamic-update-slice_fusion.16, bf16[1024,2048]{1,0:T(8,128)(2,1)} %fusion.15), kind=kOutput, calls=%fused_computation.43 | convolution fusion | flops 4296015872 | bytes 12582912 | tf_op jit(solution)/shard_map/dot_general | solution.py:439
  319.2 2.8 add_convert_fusion.6
  324.8 4.6 collective-permute-start.40
  329.4 8.5 %add_convert_fusion.1.d_a = bf16[512,2048]{1,0:T(8,128)(2,1)S(1)} fusion(bf16[512,2048]{1,0:T(8,128)(2,1)} %copy-done.70, bf16[512,2048]{1,0:T(8,128)(2,1)S(1)} %slice-done.4, bf16[2048,2048]{1,0:T(8,128)(2,1)} %constant_dynamic-update-slice_fusion.16), kind=kOutput, calls=%fused_computation.32 | convolution fusion | flops 4298113024 | bytes 14680064 | tf_op jit(solution)/shard_map/dot_general | solution.py:439
  339.5 7.4 %convolution_convert_fusion.4 = bf16[1024,2048]{1,0:T(8,128)(2,1)S(1)} fusion(bf16[1024,2048]{1,0:T(8,128)(2,1)} %fusion.15, bf16[1024,2048]{1,0:T(8,128)(2,1)} %copy-done.29), kind=kOutput, calls=%fused_computation.38 | convolution fusion | flops 4297064448 | bytes 10485760 | tf_op jit(solution)/shard_map/dot_general | solution.py:176
  352.5 4.3 collective-permute-start.42
  357.4 6.5 %convolution_convert_fusion.3 = bf16[1024,2048]{1,0:T(8,128)(2,1)S(1)} fusion(bf16[1024,2048]{1,0:T(8,128)(2,1)S(1)} %copy-done.24, bf16[1024,2048]{1,0:T(8,128)(2,1)} %copy-done.29), kind=kOutput, calls=%fused_computation.37 | convolution fusion | flops 4297064448 | bytes 10485760 | tf_op jit(solution)/shard_map/dot_general | solution.py:176
  363.9 2.6 convert_add_fusion.1
  369.1 10.2 %collective-permute-done.43 = bf16[256,1024]{1,0:T(8,128)(2,1)S(1)} collective-permute-done((bf16[256,1024]{1,0:T(8,128)(2,1)S(1)}, bf16[256,1024]{1,0:T(8,128)(2,1)S(1)}, u32[]{:S(2)}, u32[]{:S(2)}) %collective-permute-start.43) | collective-permute-done | bytes 524320 | tf_op jit(solution)/shard_map/ppermute | solution.py:59
  381.3 3.8 collective-permute-start.46
  387.8 11.0 %shard_map.149 = (f32[512,2048]{1,0:T(8,128)}, bf16[512,2048]{1,0:T(8,128)(2,1)S(1)}, f32[2,24,2048]{2,1,0:T(8,128)S(1)}) custom-call(s32[8]{0:T(128)S(1)} %copy-done.8, s32[2]{0:T(128)S(1)} %copy-done.11, f32[512,2048]{1,0:T(8,128)} %copy-done.12, bf16[512,2048]{1,0:T(8,128)(2,1)S(1)} %add_convert_fusion.2.att_a, ...), custom_call_target="tpu_custom_call" | custom-call | flops 6291456000 | bytes 8388608 | tf_op jit(solution)/shard_map/pallas_call | solution.py:422
  399.1 6.3 %collective-permute-done.46 = bf16[256,2048]{1,0:T(8,128)(2,1)S(1)} collective-permute-done((bf16[256,2048]{1,0:T(8,128)(2,1)S(1)}, bf16[256,2048]{1,0:T(8,128)(2,1)S(1)}, u32[]{:S(2)}, u32[]{:S(2)}) %collective-permute-start.46) | collective-permute-done | bytes 1048608 | tf_op jit(solution)/shard_map/ppermute | solution.py:59
  405.5 2.9 collective-permute-done.45
  415.4 8.9 %shard_map.150 = bf16[1024,1536]{1,0:T(8,128)(2,1)S(1)} custom-call(bf16[1024,1536]{1,0:T(8,128)(2,1)S(1)} %copy-done.3, bf16[1024,512]{1,0:T(8,128)(2,1)S(1)} %convolution_convert_fusion.11.d_mixed_ref), custom_call_target="tpu_custom_call" | custom-call | flops 3221225472 | bytes 8388608 | tf_op jit(solution)/shard_map/pallas_call | solution.py:250
  424.3 7.5 %convolution_convert_fusion.8 = bf16[512,2048]{1,0:T(8,128)(2,1)S(1)} fusion(bf16[2048,1536]{0,1:T(8,128)(2,1)} %copy-done.64, bf16[1024,1536]{1,0:T(8,128)(2,1)S(1)} %shard_map.150), kind=kOutput, calls=%fused_computation.42 | convolution fusion | flops 3222274048 | bytes 9961472 | tf_op jit(solution)/shard_map/dot_general | solution.py:439
  432.0 9.6 %collective-permute-done.49 = bf16[256,2048]{1,0:T(8,128)(2,1)S(1)} collective-permute-done((bf16[256,2048]{1,0:T(8,128)(2,1)S(1)}, bf16[256,2048]{1,0:T(8,128)(2,1)S(1)}, u32[]{:S(2)}, u32[]{:S(2)}) %collective-permute-start.49) | collective-permute-done | bytes 1048608 | tf_op jit(solution)/shard_map/ppermute | solution.py:59
  446.3 6.5 %add_convert_fusion.d_a = bf16[512,2048]{1,0:T(8,128)(2,1)S(1)} fusion(bf16[512,2048]{1,0:T(8,128)(2,1)S(1)} %collective-permute-done.51, bf16[512,1536]{1,0:T(8,128)(2,1)S(1)} %slice-done, bf16[2048,1536]{0,1:T(8,128)(2,1)} %copy-done.64), kind=kOutput, calls=%fused_computation.31 | convolution fusion | flops 3224371200 | bytes 12058624 | tf_op jit(solution)/shard_map/dot_general | solution.py:439
  458.6 3.7 convolution_convert_fusion.2
  464.0 4.8 convolution_convert_fusion.1
  469.2 2.9 fusion.42
  472.1 6.9 %convolution_convert_fusion.7 = bf16[512,1536]{1,0:T(8,128)(2,1)S(1)} fusion(bf16[1536,2048]{1,0:T(8,128)(2,1)} %constant_dynamic-update-slice_fusion.24, bf16[1024,2048]{1,0:T(8,128)(2,1)} %get-tuple-element.315), kind=kOutput, calls=%fused_computation.41 | convolution fusion | flops 3222011904 | bytes 9961472 | tf_op jit(solution)/shard_map/dot_general | solution.py:439
  480.8 11.2 %collective-permute-done.54 = bf16[1024,512]{1,0:T(8,128)(2,1)S(1)} collective-permute-done((bf16[1024,512]{1,0:T(8,128)(2,1)}, bf16[1024,512]{1,0:T(8,128)(2,1)S(1)}, u32[]{:S(2)}, u32[]{:S(2)}) %collective-permute-start.54) | collective-permute-done | bytes 1048608 | tf_op jit(solution)/shard_map/ppermute | solution.py:59
  496.9 6.3 %fusion.30 = f32[512,1536]{1,0:T(8,128)S(1)} fusion(bf16[1536,2048]{1,0:T(8,128)(2,1)} %constant_dynamic-update-slice_fusion.24, bf16[1024,2048]{1,0:T(8,128)(2,1)} %get-tuple-element.315), kind=kOutput, calls=%fused_computation.70 | convolution fusion | flops 3221225472 | bytes 11534336 | tf_op jit(solution)/shard_map/dot_general | solution.py:439
  506.2 7.1 %shard_map.151 = (f32[512,2048]{1,0:T(8,128)}, f32[2,16,2048]{2,1,0:T(8,128)S(1)}) custom-call(s32[8]{0:T(128)S(1)} %copy-done.8, s32[2]{0:T(128)S(1)} %copy-done.11, bf16[512,2048]{1,0:T(8,128)(2,1)S(1)} %copy-done.16, bf16[512,2048]{1,0:T(8,128)(2,1)S(1)} %add_convert_fusion.d_a, bf16[512,2048]{1,0:T(8,128)(2,1)S(1)} %collective-permute-done.61.d_b, ...), custom_call_target="tpu_custom_call" | custom-call | flops 6291456000 | bytes 8388608 | tf_op jit(solution)/shard_map/pallas_call | solution.py:422
  514.9 3.6 collective-permute-start.64
  525.5 12.0 %collective-permute-done.63 = bf16[256,1536]{1,0:T(8,128)(2,1)S(1)} collective-permute-done((bf16[256,1536]{1,0:T(8,128)(2,1)S(1)}, bf16[256,1536]{1,0:T(8,128)(2,1)S(1)}, u32[]{:S(2)}, u32[]{:S(2)}) %collective-permute-start.63) | collective-permute-done | bytes 786464 | tf_op jit(solution)/shard_map/ppermute | solution.py:59
  537.5 2.5 add_convert_fusion.8
  543.2 4.4 collective-permute-done.57
  547.9 3.2 shard_map.152
  551.3 6.8 %collective-permute-done.67 = bf16[256,1536]{1,0:T(8,128)(2,1)S(1)} collective-permute-done((bf16[256,1536]{1,0:T(8,128)(2,1)}, bf16[256,1536]{1,0:T(8,128)(2,1)S(1)}, u32[]{:S(2)}, u32[]{:S(2)}) %collective-permute-start.67) | collective-permute-done | bytes 786464 | tf_op jit(solution)/shard_map/ppermute | solution.py:59
  558.1 3.1 add_convert_fusion.7
  566.0 3.5 all-to-all-start
  569.5 7.4 %collective-permute-done.68 = bf16[256,1536]{1,0:T(8,128)(2,1)S(1)} collective-permute-done((bf16[256,1536]{1,0:T(8,128)(2,1)S(1)}, bf16[256,1536]{1,0:T(8,128)(2,1)S(1)}, u32[]{:S(2)}, u32[]{:S(2)}) %collective-permute-start.68) | collective-permute-done | bytes 786464 | tf_op jit(solution)/shard_map/ppermute | solution.py:59
  576.9 2.7 collective-permute-done.69
  (401 shorter events, 151.2 us)
Async XLA Ops:
  7.7 26.4 %collective-permute-start.2 = (bf16[256,1536]{0,1:T(8,128)(2,1)S(1)}, bf16[256,1536]{0,1:T(8,128)(2,1)S(1)}, u32[]{:S(2)}, u32[]{:S(2)}) collective-permute-start(bf16[256,1536]{0,1:T(8,128)(2,1)S(1)} %get-tuple-element.186), channel_id=1, source_target_pairs={{0,4},{2,6},{4,0},{6,2},{8,12},{10,14},{12,8},{14,10},{16,20},{18,... | collective-permute-start | bytes 2359304 | tf_op jit(solution)/shard_map/ppermute | solution.py:59
  10.3 23.7 %collective-permute-start.1 = (bf16[256,1536]{0,1:T(8,128)(2,1)S(1)}, bf16[256,1536]{0,1:T(8,128)(2,1)}, u32[]{:S(2)}, u32[]{:S(2)}) collective-permute-start(bf16[256,1536]{0,1:T(8,128)(2,1)S(1)} %get-tuple-element.186), channel_id=1, source_target_pairs={{0,8},{2,10},{4,12},{6,14},{8,16},{10,18},{12,20},{14,22},{16,24},... | collective-permute-start | bytes 2359304 | tf_op jit(solution)/shard_map/ppermute | solution.py:59
  12.8 21.2 %collective-permute-start.4 = (bf16[256,512]{1,0:T(8,128)(2,1)}, bf16[256,512]{1,0:T(8,128)(2,1)S(1)}, u32[]{:S(2)}, u32[]{:S(2)}) collective-permute-start(bf16[256,512]{1,0:T(8,128)(2,1)} %get-tuple-element.385), channel_id=1, source_target_pairs={{0,4},{2,6},{4,0},{6,2},{8,12},{10,14},{12,8},{14,10},{16,20},{18,... | collective-permute-start | bytes 786440 | tf_op jit(solution)/shard_map/ppermute | solution.py:59
  34.1 20.4 %collective-permute-start.6 = (bf16[256,1536]{0,1:T(8,128)(2,1)S(1)}, bf16[256,1536]{0,1:T(8,128)(2,1)S(1)}, u32[]{:S(2)}, u32[]{:S(2)}) collective-permute-start(bf16[256,1536]{0,1:T(8,128)(2,1)S(1)} %get-tuple-element.186), channel_id=1, source_target_pairs={{0,24},{2,26},{4,28},{6,30},{8,0},{10,2},{12,4},{14,6},{16,8},{18,... | collective-permute-start | bytes 2359304 | tf_op jit(solution)/shard_map/ppermute | solution.py:59
  38.0 18.9 %collective-permute-start.7 = (bf16[256,1536]{0,1:T(8,128)(2,1)}, bf16[256,1536]{0,1:T(8,128)(2,1)S(1)}, u32[]{:S(2)}, u32[]{:S(2)}) collective-permute-start(bf16[256,1536]{0,1:T(8,128)(2,1)} %collective-permute-done.1), channel_id=1, source_target_pairs={{0,4},{2,6},{4,0},{6,2},{8,12},{10,14},{12,8},{14,10},{16,20},{18,... | collective-permute-start | bytes 2359304 | tf_op jit(solution)/shard_map/ppermute | solution.py:59
  43.6 13.3 %collective-permute-start.5 = (bf16[512,2048]{1,0:T(8,128)(2,1)S(1)}, bf16[512,2048]{1,0:T(8,128)(2,1)S(1)}, u32[]{:S(2)}, u32[]{:S(2)}) collective-permute-start(bf16[512,2048]{1,0:T(8,128)(2,1)S(1)} %get-tuple-element.190), channel_id=1, source_target_pairs={{0,2},{2,0},{4,6},{6,4},{8,10},{10,8},{12,14},{14,12},{16,18},{18,... | collective-permute-start | bytes 6291464 | tf_op jit(solution)/shard_map/ppermute | solution.py:71
  56.9 19.8 %collective-permute-start.9 = (bf16[256,1536]{0,1:T(8,128)(2,1)}, bf16[256,1536]{0,1:T(8,128)(2,1)S(1)}, u32[]{:S(2)}, u32[]{:S(2)}) collective-permute-start(bf16[256,1536]{0,1:T(8,128)(2,1)} %collective-permute-done.1), channel_id=1, source_target_pairs={{0,8},{2,10},{4,12},{6,14},{8,16},{10,18},{12,20},{14,22},{16,24},... | collective-permute-start | bytes 2359304 | tf_op jit(solution)/shard_map/ppermute | solution.py:59
  56.9 19.8 %collective-permute-start.10 = (bf16[256,1536]{0,1:T(8,128)(2,1)S(1)}, bf16[256,1536]{0,1:T(8,128)(2,1)S(1)}, u32[]{:S(2)}, u32[]{:S(2)}) collective-permute-start(bf16[256,1536]{0,1:T(8,128)(2,1)S(1)} %collective-permute-done.6), channel_id=1, source_target_pairs={{0,4},{2,6},{4,0},{6,2},{8,12},{10,14},{12,8},{14,10},{16,20},{18,... | collective-permute-start | bytes 2359304 | tf_op jit(solution)/shard_map/ppermute | solution.py:59
  76.7 13.1 %collective-permute-start.11 = (bf16[2,256,512]{2,1,0:T(8,128)(2,1)S(1)}, bf16[2,256,512]{2,1,0:T(8,128)(2,1)S(1)}, u32[]{:S(2)}, u32[]{:S(2)}) collective-permute-start(bf16[2,256,512]{2,1,0:T(8,128)(2,1)S(1)} %pad_maximum_fusion.6), channel_id=1, source_target_pairs={{0,8},{2,10},{4,12},{6,14},{8,16},{10,18},{12,20},{14,22},{16,24},... | collective-permute-start | bytes 1572872 | tf_op jit(solution)/shard_map/ppermute | solution.py:59
  76.7 16.9 %collective-permute-start.12 = (bf16[256,1536]{0,1:T(8,128)(2,1)S(1)}, bf16[256,1536]{0,1:T(8,128)(2,1)S(1)}, u32[]{:S(2)}, u32[]{:S(2)}) collective-permute-start(bf16[256,1536]{0,1:T(8,128)(2,1)S(1)} %collective-permute-done.9), channel_id=1, source_target_pairs={{0,4},{2,6},{4,0},{6,2},{8,12},{10,14},{12,8},{14,10},{16,20},{18,... | collective-permute-start | bytes 2359304 | tf_op jit(solution)/shard_map/ppermute | solution.py:59
  78.3 11.5 %collective-permute-start.13 = (bf16[128,2048]{1,0:T(8,128)(2,1)S(1)}, bf16[128,2048]{1,0:T(8,128)(2,1)S(1)}, u32[]{:S(2)}, u32[]{:S(2)}) collective-permute-start(bf16[128,2048]{1,0:T(8,128)(2,1)S(1)} %get-tuple-element.418), channel_id=1, source_target_pairs={{0,2},{2,0},{4,6},{6,4},{8,10},{10,8},{12,14},{14,12},{16,18},{18,... | collective-permute-start | bytes 1572872 | tf_op jit(solution)/shard_map/ppermute | solution.py:71
  93.6 23.1 %collective-permute-start.14 = (bf16[2,256,512]{2,1,0:T(8,128)(2,1)S(1)}, bf16[2,256,512]{2,1,0:T(8,128)(2,1)S(1)}, u32[]{:S(2)}, u32[]{:S(2)}) collective-permute-start(bf16[2,256,512]{2,1,0:T(8,128)(2,1)S(1)} %pad_maximum_fusion.6), channel_id=1, source_target_pairs={{0,24},{2,26},{4,28},{6,30},{8,0},{10,2},{12,4},{14,6},{16,8},{18,... | collective-permute-start | bytes 1572872 | tf_op jit(solution)/shard_map/ppermute | solution.py:59
  97.2 19.6 %collective-permute-start.15 = (bf16[2,256,512]{2,1,0:T(8,128)(2,1)S(1)}, bf16[2,256,512]{2,1,0:T(8,128)(2,1)S(1)}, u32[]{:S(2)}, u32[]{:S(2)}) collective-permute-start(bf16[2,256,512]{2,1,0:T(8,128)(2,1)S(1)} %collective-permute-done.11), channel_id=1, source_target_pairs={{0,8},{2,10},{4,12},{6,14},{8,16},{10,18},{12,20},{14,22},{16,24},... | collective-permute-start | bytes 1572872 | tf_op jit(solution)/shard_map/ppermute | solution.py:59
  97.2 21.2 %collective-permute-start.16 = (bf16[256,2048]{1,0:T(8,128)(2,1)S(1)}, bf16[256,2048]{1,0:T(8,128)(2,1)S(1)}, u32[]{:S(2)}, u32[]{:S(2)}) collective-permute-start(bf16[256,2048]{1,0:T(8,128)(2,1)S(1)} %maximum_select_fusion.3), channel_id=1, source_target_pairs={{0,4},{2,6},{4,0},{6,2},{8,12},{10,14},{12,8},{14,10},{16,20},{18,... | collective-permute-start | bytes 3145736 | tf_op jit(solution)/shard_map/ppermute | solution.py:59
  122.4 27.3 %collective-permute-start.19 = (bf16[256,2048]{1,0:T(8,128)(2,1)S(1)}, bf16[256,2048]{1,0:T(8,128)(2,1)}, u32[]{:S(2)}, u32[]{:S(2)}) collective-permute-start(bf16[256,2048]{1,0:T(8,128)(2,1)S(1)} %maximum_select_fusion.3), channel_id=1, source_target_pairs={{0,8},{2,10},{4,12},{6,14},{8,16},{10,18},{12,20},{14,22},{16,24},... | collective-permute-start | bytes 3145736 | tf_op jit(solution)/shard_map/ppermute | solution.py:59
  124.4 25.3 %collective-permute-start.20 = (bf16[256,2048]{1,0:T(8,128)(2,1)S(1)}, bf16[256,2048]{1,0:T(8,128)(2,1)S(1)}, u32[]{:S(2)}, u32[]{:S(2)}) collective-permute-start(bf16[256,2048]{1,0:T(8,128)(2,1)S(1)} %get-tuple-element.229), channel_id=1, source_target_pairs={{0,4},{2,6},{4,0},{6,2},{8,12},{10,14},{12,8},{14,10},{16,20},{18,... | collective-permute-start | bytes 3145736 | tf_op jit(solution)/shard_map/ppermute | solution.py:59
  128.6 48.9 %collective-permute-start.18 = (bf16[512,2048]{1,0:T(8,128)(2,1)S(1)}, bf16[512,2048]{1,0:T(8,128)(2,1)S(1)}, u32[]{:S(2)}, u32[]{:S(2)}) collective-permute-start(bf16[512,2048]{1,0:T(8,128)(2,1)S(1)} %add_convert_fusion.2.att_a), channel_id=1, source_target_pairs={{0,1},{1,0},{2,3},{3,2},{4,5},{5,4},{6,7},{7,6},{8,9},{9,8},{10,11... | collective-permute-start | bytes 6291464 | tf_op jit(solution)/shard_map/ppermute | solution.py:81
  149.7 24.5 %collective-permute-start.21 = (bf16[256,2048]{1,0:T(8,128)(2,1)S(1)}, bf16[256,2048]{1,0:T(8,128)(2,1)}, u32[]{:S(2)}, u32[]{:S(2)}) collective-permute-start(bf16[256,2048]{1,0:T(8,128)(2,1)S(1)} %maximum_select_fusion.3), channel_id=1, source_target_pairs={{0,24},{2,26},{4,28},{6,30},{8,0},{10,2},{12,4},{14,6},{16,8},{18,... | collective-permute-start | bytes 3145736 | tf_op jit(solution)/shard_map/ppermute | solution.py:59
  151.3 24.0 %collective-permute-start.22 = (bf16[256,2048]{1,0:T(8,128)(2,1)}, bf16[256,2048]{1,0:T(8,128)(2,1)S(1)}, u32[]{:S(2)}, u32[]{:S(2)}) collective-permute-start(bf16[256,2048]{1,0:T(8,128)(2,1)} %collective-permute-done.19), channel_id=1, source_target_pairs={{0,4},{2,6},{4,0},{6,2},{8,12},{10,14},{12,8},{14,10},{16,20},{18,... | collective-permute-start | bytes 3145736 | tf_op jit(solution)/shard_map/ppermute | solution.py:59
  152.8 22.5 %collective-permute-start.23 = (bf16[512,2048]{1,0:T(8,128)(2,1)S(1)}, bf16[512,2048]{1,0:T(8,128)(2,1)S(1)}, u32[]{:S(2)}, u32[]{:S(2)}) collective-permute-start(bf16[512,2048]{1,0:T(8,128)(2,1)S(1)} %get-tuple-element.216), channel_id=1, source_target_pairs={{0,2},{2,0},{4,6},{6,4},{8,10},{10,8},{12,14},{14,12},{16,18},{18,... | collective-permute-start | bytes 6291464 | tf_op jit(solution)/shard_map/ppermute | solution.py:71
  175.3 25.1 %collective-permute-start.25 = (bf16[256,2048]{1,0:T(8,128)(2,1)}, bf16[256,2048]{1,0:T(8,128)(2,1)}, u32[]{:S(2)}, u32[]{:S(2)}) collective-permute-start(bf16[256,2048]{1,0:T(8,128)(2,1)} %collective-permute-done.19), channel_id=1, source_target_pairs={{0,8},{2,10},{4,12},{6,14},{8,16},{10,18},{12,20},{14,22},{16,24},... | collective-permute-start | bytes 3145736 | tf_op jit(solution)/shard_map/ppermute | solution.py:59
  176.1 24.4 %collective-permute-start.26 = (bf16[256,2048]{1,0:T(8,128)(2,1)}, bf16[256,2048]{1,0:T(8,128)(2,1)}, u32[]{:S(2)}, u32[]{:S(2)}) collective-permute-start(bf16[256,2048]{1,0:T(8,128)(2,1)} %collective-permute-done.21), channel_id=1, source_target_pairs={{0,4},{2,6},{4,0},{6,2},{8,12},{10,14},{12,8},{14,10},{16,20},{18,... | collective-permute-start | bytes 3145736 | tf_op jit(solution)/shard_map/ppermute | solution.py:59
  180.6 19.8 %collective-permute-start.24 = (bf16[512,2048]{1,0:T(8,128)(2,1)S(1)}, bf16[512,2048]{1,0:T(8,128)(2,1)S(1)}, u32[]{:S(2)}, u32[]{:S(2)}) collective-permute-start(bf16[512,2048]{1,0:T(8,128)(2,1)S(1)} %get-tuple-element.222), channel_id=1, source_target_pairs={{0,2},{2,0},{4,6},{6,4},{8,10},{10,8},{12,14},{14,12},{16,18},{18,... | collective-permute-start | bytes 6291464 | tf_op jit(solution)/shard_map/ppermute | solution.py:71
  200.4 25.3 %collective-permute-start.27 = (bf16[256,2048]{1,0:T(8,128)(2,1)S(1)}, bf16[256,2048]{1,0:T(8,128)(2,1)S(1)}, u32[]{:S(2)}, u32[]{:S(2)}) collective-permute-start(bf16[256,2048]{1,0:T(8,128)(2,1)S(1)} %copy-done.33), channel_id=1, source_target_pairs={{0,8},{2,10},{4,12},{6,14},{8,16},{10,18},{12,20},{14,22},{16,24},... | collective-permute-start | bytes 3145736 | tf_op jit(solution)/shard_map/ppermute | solution.py:59
  200.5 25.2 %collective-permute-start.28 = (bf16[256,2048]{1,0:T(8,128)(2,1)}, bf16[256,2048]{1,0:T(8,128)(2,1)S(1)}, u32[]{:S(2)}, u32[]{:S(2)}) collective-permute-start(bf16[256,2048]{1,0:T(8,128)(2,1)} %collective-permute-done.25), channel_id=1, source_target_pairs={{0,4},{2,6},{4,0},{6,2},{8,12},{10,14},{12,8},{14,10},{16,20},{18,... | collective-permute-start | bytes 3145736 | tf_op jit(solution)/shard_map/ppermute | solution.py:59
  225.7 23.4 %collective-permute-start.29 = (bf16[256,2048]{1,0:T(8,128)(2,1)S(1)}, bf16[256,2048]{1,0:T(8,128)(2,1)S(1)}, u32[]{:S(2)}, u32[]{:S(2)}) collective-permute-start(bf16[256,2048]{1,0:T(8,128)(2,1)S(1)} %copy-done.33), channel_id=1, source_target_pairs={{0,24},{2,26},{4,28},{6,30},{8,0},{10,2},{12,4},{14,6},{16,8},{18,... | collective-permute-start | bytes 3145736 | tf_op jit(solution)/shard_map/ppermute | solution.py:59
  227.8 21.3 %collective-permute-start.30 = (bf16[256,2048]{1,0:T(8,128)(2,1)S(1)}, bf16[256,2048]{1,0:T(8,128)(2,1)S(1)}, u32[]{:S(2)}, u32[]{:S(2)}) collective-permute-start(bf16[256,2048]{1,0:T(8,128)(2,1)S(1)} %collective-permute-done.27), channel_id=1, source_target_pairs={{0,4},{2,6},{4,0},{6,2},{8,12},{10,14},{12,8},{14,10},{16,20},{18,... | collective-permute-start | bytes 3145736 | tf_op jit(solution)/shard_map/ppermute | solution.py:59
  249.1 23.1 %collective-permute-start.31 = (bf16[256,2048]{1,0:T(8,128)(2,1)S(1)}, bf16[256,2048]{1,0:T(8,128)(2,1)S(1)}, u32[]{:S(2)}, u32[]{:S(2)}) collective-permute-start(bf16[256,2048]{1,0:T(8,128)(2,1)S(1)} %collective-permute-done.27), channel_id=1, source_target_pairs={{0,8},{2,10},{4,12},{6,14},{8,16},{10,18},{12,20},{14,22},{16,24},... | collective-permute-start | bytes 3145736 | tf_op jit(solution)/shard_map/ppermute | solution.py:59
  249.3 22.9 %collective-permute-start.32 = (bf16[256,2048]{1,0:T(8,128)(2,1)S(1)}, bf16[256,2048]{1,0:T(8,128)(2,1)S(1)}, u32[]{:S(2)}, u32[]{:S(2)}) collective-permute-start(bf16[256,2048]{1,0:T(8,128)(2,1)S(1)} %collective-permute-done.29), channel_id=1, source_target_pairs={{0,4},{2,6},{4,0},{6,2},{8,12},{10,14},{12,8},{14,10},{16,20},{18,... | collective-permute-start | bytes 3145736 | tf_op jit(solution)/shard_map/ppermute | solution.py:59
  272.2 23.0 %collective-permute-start.33 = (bf16[256,2048]{1,0:T(8,128)(2,1)S(1)}, bf16[256,2048]{1,0:T(8,128)(2,1)S(1)}, u32[]{:S(2)}, u32[]{:S(2)}) collective-permute-start(bf16[256,2048]{1,0:T(8,128)(2,1)S(1)} %collective-permute-done.31), channel_id=1, source_target_pairs={{0,4},{2,6},{4,0},{6,2},{8,12},{10,14},{12,8},{14,10},{16,20},{18,... | collective-permute-start | bytes 3145736 | tf_op jit(solution)/shard_map/ppermute | solution.py:59
  273.7 45.5 %collective-permute-start.36 = (bf16[2,256,1024]{2,1,0:T(8,128)(2,1)}, bf16[2,256,1024]{2,1,0:T(8,128)(2,1)}, u32[]{:S(2)}, u32[]{:S(2)}) collective-permute-start(bf16[2,256,1024]{2,1,0:T(8,128)(2,1)} %get-tuple-element.246), channel_id=1, source_target_pairs={{0,24},{2,26},{4,28},{6,30},{8,0},{10,2},{12,4},{14,6},{16,8},{18,... | collective-permute-start | bytes 3145736 | tf_op jit(solution)/shard_map/ppermute | solution.py:59
  295.2 26.7 %collective-permute-start.34 = (bf16[512,1024]{1,0:T(8,128)(2,1)}, bf16[512,1024]{1,0:T(8,128)(2,1)S(1)}, u32[]{:S(2)}, u32[]{:S(2)}) collective-permute-start(bf16[512,1024]{1,0:T(8,128)(2,1)} %get-tuple-element.250), channel_id=1, source_target_pairs={{0,4},{2,6},{4,0},{6,2},{8,12},{10,14},{12,8},{14,10},{16,20},{18,... | collective-permute-start | bytes 3145736 | tf_op jit(solution)/shard_map/ppermute | solution.py:59
  296.0 26.0 %collective-permute-start.35 = (bf16[2,256,1024]{2,1,0:T(8,128)(2,1)}, bf16[2,256,1024]{2,1,0:T(8,128)(2,1)S(1)}, u32[]{:S(2)}, u32[]{:S(2)}) collective-permute-start(bf16[2,256,1024]{2,1,0:T(8,128)(2,1)} %get-tuple-element.251), channel_id=1, source_target_pairs={{0,8},{2,10},{4,12},{6,14},{8,16},{10,18},{12,20},{14,22},{16,24},... | collective-permute-start | bytes 3145736 | tf_op jit(solution)/shard_map/ppermute | solution.py:59
  323.5 26.8 %collective-permute-start.39 = (bf16[512,1024]{1,0:T(8,128)(2,1)}, bf16[512,1024]{1,0:T(8,128)(2,1)S(1)}, u32[]{:S(2)}, u32[]{:S(2)}) collective-permute-start(bf16[512,1024]{1,0:T(8,128)(2,1)} %get-tuple-element.257), channel_id=1, source_target_pairs={{0,4},{2,6},{4,0},{6,2},{8,12},{10,14},{12,8},{14,10},{16,20},{18,... | collective-permute-start | bytes 3145736 | tf_op jit(solution)/shard_map/ppermute | solution.py:59
  324.8 27.6 %collective-permute-start.40 = (bf16[2,256,1024]{2,1,0:T(8,128)(2,1)}, bf16[2,256,1024]{2,1,0:T(8,128)(2,1)}, u32[]{:S(2)}, u32[]{:S(2)}) collective-permute-start(bf16[2,256,1024]{2,1,0:T(8,128)(2,1)} %add_convert_fusion.6), channel_id=1, source_target_pairs={{0,24},{2,26},{4,28},{6,30},{8,0},{10,2},{12,4},{14,6},{16,8},{18,... | collective-permute-start | bytes 3145736 | tf_op jit(solution)/shard_map/ppermute | solution.py:59
  337.9 49.9 %collective-permute-start.38 = (bf16[512,2048]{1,0:T(8,128)(2,1)S(1)}, bf16[512,2048]{1,0:T(8,128)(2,1)S(1)}, u32[]{:S(2)}, u32[]{:S(2)}) collective-permute-start(bf16[512,2048]{1,0:T(8,128)(2,1)S(1)} %add_convert_fusion.1.d_a), channel_id=1, source_target_pairs={{0,1},{1,0},{2,3},{3,2},{4,5},{5,4},{6,7},{7,6},{8,9},{9,8},{10,11... | collective-permute-start | bytes 6291464 | tf_op jit(solution)/shard_map/ppermute | solution.py:81
  352.5 16.7 %collective-permute-start.42 = (bf16[256,1024]{1,0:T(8,128)(2,1)S(1)}, bf16[256,1024]{1,0:T(8,128)(2,1)S(1)}, u32[]{:S(2)}, u32[]{:S(2)}) collective-permute-start(bf16[256,1024]{1,0:T(8,128)(2,1)S(1)} %get-tuple-element.267), channel_id=1, source_target_pairs={{0,24},{2,26},{4,28},{6,30},{8,0},{10,2},{12,4},{14,6},{16,8},{18,... | collective-permute-start | bytes 1572872 | tf_op jit(solution)/shard_map/ppermute | solution.py:59
  356.7 22.6 %collective-permute-start.43 = (bf16[256,1024]{1,0:T(8,128)(2,1)S(1)}, bf16[256,1024]{1,0:T(8,128)(2,1)S(1)}, u32[]{:S(2)}, u32[]{:S(2)}) collective-permute-start(bf16[256,1024]{1,0:T(8,128)(2,1)S(1)} %get-tuple-element.268), channel_id=1, source_target_pairs={{0,8},{2,10},{4,12},{6,14},{8,16},{10,18},{12,20},{14,22},{16,24},... | collective-permute-start | bytes 1572872 | tf_op jit(solution)/shard_map/ppermute | solution.py:59
  356.8 24.1 %collective-permute-start.41 = (bf16[256,2048]{1,0:T(8,128)(2,1)S(1)}, bf16[256,2048]{1,0:T(8,128)(2,1)S(1)}, u32[]{:S(2)}, u32[]{:S(2)}) collective-permute-start(bf16[256,2048]{1,0:T(8,128)(2,1)S(1)} %get-tuple-element.266), channel_id=1, source_target_pairs={{0,4},{2,6},{4,0},{6,2},{8,12},{10,14},{12,8},{14,10},{16,20},{18,... | collective-permute-start | bytes 3145736 | tf_op jit(solution)/shard_map/ppermute | solution.py:59
  381.3 24.2 %collective-permute-start.46 = (bf16[256,2048]{1,0:T(8,128)(2,1)S(1)}, bf16[256,2048]{1,0:T(8,128)(2,1)S(1)}, u32[]{:S(2)}, u32[]{:S(2)}) collective-permute-start(bf16[256,2048]{1,0:T(8,128)(2,1)S(1)} %add_convert_fusion.5), channel_id=1, source_target_pairs={{0,24},{2,26},{4,28},{6,30},{8,0},{10,2},{12,4},{14,6},{16,8},{18,... | collective-permute-start | bytes 3145736 | tf_op jit(solution)/shard_map/ppermute | solution.py:59
  385.1 23.3 %collective-permute-start.45 = (bf16[256,2048]{1,0:T(8,128)(2,1)}, bf16[256,2048]{1,0:T(8,128)(2,1)S(1)}, u32[]{:S(2)}, u32[]{:S(2)}) collective-permute-start(bf16[256,2048]{1,0:T(8,128)(2,1)} %get-tuple-element.274), channel_id=1, source_target_pairs={{0,4},{2,6},{4,0},{6,2},{8,12},{10,14},{12,8},{14,10},{16,20},{18,... | collective-permute-start | bytes 3145736 | tf_op jit(solution)/shard_map/ppermute | solution.py:59
  408.4 23.6 %collective-permute-start.48 = (bf16[256,1024]{1,0:T(8,128)(2,1)}, bf16[256,1024]{1,0:T(8,128)(2,1)S(1)}, u32[]{:S(2)}, u32[]{:S(2)}) collective-permute-start(bf16[256,1024]{1,0:T(8,128)(2,1)} %fusion.49), channel_id=1, source_target_pairs={{0,4},{2,6},{4,0},{6,2},{8,12},{10,14},{12,8},{14,10},{16,20},{18,... | collective-permute-start | bytes 1572872 | tf_op jit(solution)/shard_map/ppermute | solution.py:59
  408.8 23.2 %collective-permute-start.50 = (bf16[256,1024]{1,0:T(8,128)(2,1)}, bf16[256,1024]{1,0:T(8,128)(2,1)S(1)}, u32[]{:S(2)}, u32[]{:S(2)}) collective-permute-start(bf16[256,1024]{1,0:T(8,128)(2,1)} %add_convert_fusion.10), channel_id=1, source_target_pairs={{0,24},{2,26},{4,28},{6,30},{8,0},{10,2},{12,4},{14,6},{16,8},{18,... | collective-permute-start | bytes 1572872 | tf_op jit(solution)/shard_map/ppermute | solution.py:59
  410.6 31.0 %collective-permute-start.49 = (bf16[256,2048]{1,0:T(8,128)(2,1)S(1)}, bf16[256,2048]{1,0:T(8,128)(2,1)S(1)}, u32[]{:S(2)}, u32[]{:S(2)}) collective-permute-start(bf16[256,2048]{1,0:T(8,128)(2,1)S(1)} %add_convert_fusion.4), channel_id=1, source_target_pairs={{0,8},{2,10},{4,12},{6,14},{8,16},{10,18},{12,20},{14,22},{16,24},... | collective-permute-start | bytes 3145736 | tf_op jit(solution)/shard_map/ppermute | solution.py:59
  411.3 31.1 %collective-permute-start.47 = (bf16[256,2048]{1,0:T(8,128)(2,1)S(1)}, bf16[256,2048]{1,0:T(8,128)(2,1)S(1)}, u32[]{:S(2)}, u32[]{:S(2)}) collective-permute-start(bf16[256,2048]{1,0:T(8,128)(2,1)S(1)} %copy-done.41), channel_id=1, source_target_pairs={{0,4},{2,6},{4,0},{6,2},{8,12},{10,14},{12,8},{14,10},{16,20},{18,... | collective-permute-start | bytes 3145736 | tf_op jit(solution)/shard_map/ppermute | solution.py:59
  442.9 25.9 %collective-permute-start.52 = (bf16[256,2048]{1,0:T(8,128)(2,1)S(1)}, bf16[256,2048]{1,0:T(8,128)(2,1)S(1)}, u32[]{:S(2)}, u32[]{:S(2)}) collective-permute-start(bf16[256,2048]{1,0:T(8,128)(2,1)S(1)} %copy-done.40), channel_id=1, source_target_pairs={{0,4},{2,6},{4,0},{6,2},{8,12},{10,14},{12,8},{14,10},{16,20},{18,... | collective-permute-start | bytes 3145736 | tf_op jit(solution)/shard_map/ppermute | solution.py:59
  443.9 24.9 %collective-permute-start.53 = (bf16[256,2048]{1,0:T(8,128)(2,1)S(1)}, bf16[256,2048]{1,0:T(8,128)(2,1)S(1)}, u32[]{:S(2)}, u32[]{:S(2)}) collective-permute-start(bf16[256,2048]{1,0:T(8,128)(2,1)S(1)} %add_convert_fusion.3), channel_id=1, source_target_pairs={{0,24},{2,26},{4,28},{6,30},{8,0},{10,2},{12,4},{14,6},{16,8},{18,... | collective-permute-start | bytes 3145736 | tf_op jit(solution)/shard_map/ppermute | solution.py:59
  456.3 49.2 %collective-permute-start.61 = (bf16[512,2048]{1,0:T(8,128)(2,1)S(1)}, bf16[512,2048]{1,0:T(8,128)(2,1)S(1)}, u32[]{:S(2)}, u32[]{:S(2)}) collective-permute-start(bf16[512,2048]{1,0:T(8,128)(2,1)S(1)} %add_convert_fusion.d_a), channel_id=1, source_target_pairs={{0,1},{1,0},{2,3},{3,2},{4,5},{5,4},{6,7},{7,6},{8,9},{9,8},{10,11... | collective-permute-start | bytes 6291464 | tf_op jit(solution)/shard_map/ppermute | solution.py:81
  468.9 23.1 %collective-permute-start.54 = (bf16[1024,512]{1,0:T(8,128)(2,1)}, bf16[1024,512]{1,0:T(8,128)(2,1)S(1)}, u32[]{:S(2)}, u32[]{:S(2)}) collective-permute-start(bf16[1024,512]{1,0:T(8,128)(2,1)} %fusion.36), channel_id=1, source_target_pairs={{0,4},{2,6},{4,0},{6,2},{8,12},{10,14},{12,8},{14,10},{16,20},{18,... | collective-permute-start | bytes 3145736 | tf_op jit(solution)/shard_map/ppermute | solution.py:59
  479.3 12.7 %collective-permute-start.55 = (bf16[512,2048]{1,0:T(8,128)(2,1)S(1)}, bf16[512,2048]{1,0:T(8,128)(2,1)S(1)}, u32[]{:S(2)}, u32[]{:S(2)}) collective-permute-start(bf16[512,2048]{1,0:T(8,128)(2,1)S(1)} %pad_maximum_fusion.1), channel_id=1, source_target_pairs={{0,2},{2,0},{4,6},{6,4},{8,10},{10,8},{12,14},{14,12},{16,18},{18,... | collective-permute-start | bytes 6291464 | tf_op jit(solution)/shard_map/ppermute | solution.py:71
  480.2 11.8 %collective-permute-start.56 = (f32[128,2048]{1,0:T(8,128)S(1)}, f32[128,2048]{1,0:T(8,128)S(1)}, u32[]{:S(2)}, u32[]{:S(2)}) collective-permute-start(f32[128,2048]{1,0:T(8,128)S(1)} %get-tuple-element.405), channel_id=1, source_target_pairs={{0,2},{2,0},{4,6},{6,4},{8,10},{10,8},{12,14},{14,12},{16,18},{18,... | collective-permute-start | bytes 3145736 | tf_op jit(solution)/shard_map/ppermute | solution.py:71
  493.0 20.6 %collective-permute-start.59 = (bf16[256,512]{1,0:T(8,128)(2,1)}, bf16[256,512]{1,0:T(8,128)(2,1)}, u32[]{:S(2)}, u32[]{:S(2)}) collective-permute-start(bf16[256,512]{1,0:T(8,128)(2,1)} %get-tuple-element.312), channel_id=1, source_target_pairs={{0,24},{2,26},{4,28},{6,30},{8,0},{10,2},{12,4},{14,6},{16,8},{18,... | collective-permute-start | bytes 786440 | tf_op jit(solution)/shard_map/ppermute | solution.py:59
  494.8 18.8 %collective-permute-start.60 = (bf16[256,512]{1,0:T(8,128)(2,1)}, bf16[256,512]{1,0:T(8,128)(2,1)}, u32[]{:S(2)}, u32[]{:S(2)}) collective-permute-start(bf16[256,512]{1,0:T(8,128)(2,1)} %get-tuple-element.314), channel_id=1, source_target_pairs={{0,8},{2,10},{4,12},{6,14},{8,16},{10,18},{12,20},{14,22},{16,24},... | collective-permute-start | bytes 786440 | tf_op jit(solution)/shard_map/ppermute | solution.py:59
  495.1 18.5 %collective-permute-start.58 = (bf16[256,1536]{1,0:T(8,128)(2,1)}, bf16[256,1536]{1,0:T(8,128)(2,1)}, u32[]{:S(2)}, u32[]{:S(2)}) collective-permute-start(bf16[256,1536]{1,0:T(8,128)(2,1)} %get-tuple-element.310), channel_id=1, source_target_pairs={{0,4},{2,6},{4,0},{6,2},{8,12},{10,14},{12,8},{14,10},{16,20},{18,... | collective-permute-start | bytes 2359304 | tf_op jit(solution)/shard_map/ppermute | solution.py:59
  503.9 43.6 %collective-permute-start.57 = (bf16[512,2048]{1,0:T(8,128)(2,1)S(1)}, bf16[512,2048]{1,0:T(8,128)(2,1)S(1)}, u32[]{:S(2)}, u32[]{:S(2)}) collective-permute-start(bf16[512,2048]{1,0:T(8,128)(2,1)S(1)} %fusion.16), channel_id=1, source_target_pairs={{0,1},{1,0},{2,3},{3,2},{4,5},{5,4},{6,7},{7,6},{8,9},{9,8},{10,11... | collective-permute-start | bytes 6291464 | tf_op jit(solution)/shard_map/ppermute | solution.py:81
  514.9 10.6 %collective-permute-start.64 = (bf16[256,512]{1,0:T(8,128)(2,1)S(1)}, bf16[256,512]{1,0:T(8,128)(2,1)S(1)}, u32[]{:S(2)}, u32[]{:S(2)}) collective-permute-start(bf16[256,512]{1,0:T(8,128)(2,1)S(1)} %add_convert_fusion.13), channel_id=1, source_target_pairs={{0,24},{2,26},{4,28},{6,30},{8,0},{10,2},{12,4},{14,6},{16,8},{18,... | collective-permute-start | bytes 786440 | tf_op jit(solution)/shard_map/ppermute | solution.py:59
  520.0 17.4 %collective-permute-start.63 = (bf16[256,1536]{1,0:T(8,128)(2,1)S(1)}, bf16[256,1536]{1,0:T(8,128)(2,1)S(1)}, u32[]{:S(2)}, u32[]{:S(2)}) collective-permute-start(bf16[256,1536]{1,0:T(8,128)(2,1)S(1)} %add_convert_fusion.9), channel_id=1, source_target_pairs={{0,24},{2,26},{4,28},{6,30},{8,0},{10,2},{12,4},{14,6},{16,8},{18,... | collective-permute-start | bytes 2359304 | tf_op jit(solution)/shard_map/ppermute | solution.py:59
  520.1 17.4 %collective-permute-start.62 = (bf16[256,1536]{1,0:T(8,128)(2,1)S(1)}, bf16[256,1536]{1,0:T(8,128)(2,1)S(1)}, u32[]{:S(2)}, u32[]{:S(2)}) collective-permute-start(bf16[256,1536]{1,0:T(8,128)(2,1)S(1)} %copy-done.46), channel_id=1, source_target_pairs={{0,4},{2,6},{4,0},{6,2},{8,12},{10,14},{12,8},{14,10},{16,20},{18,... | collective-permute-start | bytes 2359304 | tf_op jit(solution)/shard_map/ppermute | solution.py:59
  525.4 12.1 %collective-permute-start.65 = (f32[128,2048]{1,0:T(8,128)S(1)}, f32[128,2048]{1,0:T(8,128)S(1)}, u32[]{:S(2)}, u32[]{:S(2)}) collective-permute-start(f32[128,2048]{1,0:T(8,128)S(1)} %get-tuple-element.403), channel_id=1, source_target_pairs={{0,2},{2,0},{4,6},{6,4},{8,10},{10,8},{12,14},{14,12},{16,18},{18,... | collective-permute-start | bytes 3145736 | tf_op jit(solution)/shard_map/ppermute | solution.py:71
  540.0 18.1 %collective-permute-start.67 = (bf16[256,1536]{1,0:T(8,128)(2,1)}, bf16[256,1536]{1,0:T(8,128)(2,1)S(1)}, u32[]{:S(2)}, u32[]{:S(2)}) collective-permute-start(bf16[256,1536]{1,0:T(8,128)(2,1)} %add_convert_fusion.8), channel_id=1, source_target_pairs={{0,8},{2,10},{4,12},{6,14},{8,16},{10,18},{12,20},{14,22},{16,24},... | collective-permute-start | bytes 2359304 | tf_op jit(solution)/shard_map/ppermute | solution.py:59
  540.0 18.1 %collective-permute-start.66 = (bf16[256,1536]{1,0:T(8,128)(2,1)S(1)}, bf16[256,1536]{1,0:T(8,128)(2,1)}, u32[]{:S(2)}, u32[]{:S(2)}) collective-permute-start(bf16[256,1536]{1,0:T(8,128)(2,1)S(1)} %copy-done.45), channel_id=1, source_target_pairs={{0,4},{2,6},{4,0},{6,2},{8,12},{10,14},{12,8},{14,10},{16,20},{18,... | collective-permute-start | bytes 2359304 | tf_op jit(solution)/shard_map/ppermute | solution.py:59
  561.1 15.8 %collective-permute-start.68 = (bf16[256,1536]{1,0:T(8,128)(2,1)S(1)}, bf16[256,1536]{1,0:T(8,128)(2,1)S(1)}, u32[]{:S(2)}, u32[]{:S(2)}) collective-permute-start(bf16[256,1536]{1,0:T(8,128)(2,1)S(1)} %copy-done.44), channel_id=1, source_target_pairs={{0,4},{2,6},{4,0},{6,2},{8,12},{10,14},{12,8},{14,10},{16,20},{18,... | collective-permute-start | bytes 2359304 | tf_op jit(solution)/shard_map/ppermute | solution.py:59
  562.7 16.9 %collective-permute-start.69 = (bf16[256,1536]{1,0:T(8,128)(2,1)}, bf16[256,1536]{1,0:T(8,128)(2,1)}, u32[]{:S(2)}, u32[]{:S(2)}) collective-permute-start(bf16[256,1536]{1,0:T(8,128)(2,1)} %add_convert_fusion.7), channel_id=1, source_target_pairs={{0,24},{2,26},{4,28},{6,30},{8,0},{10,2},{12,4},{14,6},{16,8},{18,... | collective-permute-start | bytes 2359304 | tf_op jit(solution)/shard_map/ppermute | solution.py:59
  566.0 17.0 %all-to-all-start = ((f32[16,14,128]{2,1,0:T(8,128)}), f32[16,14,128]{2,1,0:T(8,128)S(1)}, u32[]{:S(2)}, u32[]{:S(2)}) async-start(f32[16,14,128]{2,1,0:T(8,128)} %copy.47), calls=%async_computation | async-start | bytes 262144 | tf_op jit(solution)/shard_map/all_to_all | solution.py:763
  (87 other events, 1023.2 us)
